TPU v7x, 256 devices: a whole 4x4x8 slice. The times are simulated.
256 devices in a mesh: gx: 32 (over z, x_hi, core), gy: 8 (over x_lo, y).
Axes of the slice: x: 4 (x_hi: 2, x_lo: 2; x = x_hi * 2 + x_lo), y: 4, z: 8, core: 2. Of those that a mesh axis runs over, the one named last changes fastest.
Arguments:
- charges: bfloat16 [640, 160, 128], P('gx', 'gy'), may hold values from -6 to 6
- kernels: bfloat16 [2, 21, 21, 21], replicated, may hold values from -0.0625 to 0.0625
Outputs:
- potential: float32 [640, 160, 128], P('gx', 'gy')
All inputs are finite; a program needn't handle non-finite values.
Results may differ from a plain program's by a relative error of at most 0.0003.
Values may be sent and summed in bfloat16 or wider, within the bound.
No kernel may reach another device: no remote copies, remote signals or barrier semaphores. Data moves between devices by JAX's collectives and lax.ppermute only.
A program may use at most 64 MiB of HBM per device.

v0:
```python
import jax
import jax.numpy as jnp
from jax import lax
from jax.sharding import PartitionSpec as P

spread_norm = 1.2533141


def with_halo(block, sides, width):
    for axis, dim in sides:
        count = lax.axis_size(axis)
        forward = [(i, i + 1) for i in range(count - 1)]
        backward = [(target, source) for source, target in forward]
        low = lax.ppermute(
            lax.slice_in_dim(block, block.shape[dim] - width, None, axis=dim), axis, forward
        )
        high = lax.ppermute(lax.slice_in_dim(block, 0, width, axis=dim), axis, backward)
        block = jnp.concatenate([low, block, high], axis=dim)
    return block


def interp_weight(offset):
    distance = jnp.abs(offset)
    unit = jnp.ones(offset.shape, jnp.float32)
    return jnp.where(
        distance == 0,
        unit,
        jnp.where(
            distance == 1, 0.5625 * unit, jnp.where(distance == 3, -0.0625 * unit, 0.0 * unit)
        ),
    )


def weight_table(rows_idx, cols_idx, margin):
    return interp_weight(cols_idx[None, :] - margin - 2 * rows_idx[:, None])


def gauss_weight(offset, spread):
    scaled = offset.astype(jnp.float32) / spread
    return jnp.exp(-scaled * scaled) / jnp.sqrt(jnp.float32(spread * spread_norm))


def top_block(fine_rows, coarse_cols, coarse_count, spread):
    coarse_all = jnp.arange(coarse_count)
    prolong = interp_weight(fine_rows[:, None] - 2 * coarse_all[None, :])
    gauss = gauss_weight(coarse_all[:, None] - coarse_cols[None, :], spread)
    return jnp.dot(prolong, gauss, precision=lax.Precision.HIGHEST)


def band_select(length):
    cells = jnp.arange(length)
    offset = (cells[:, None] - cells[None, :] + 10).reshape(1, length * length)
    taps = jnp.arange(21)[:, None]
    return (offset == taps).astype(jnp.bfloat16)


def direct_sum(padded, kernel):
    size_x = padded.shape[0] - 20
    size_y = padded.shape[1] - 20
    size_z = padded.shape[2]
    select = band_select(size_z)

    def per_plane(shift_a, total):
        slab = lax.dynamic_slice_in_dim(padded, shift_a, size_x, 0)
        plane = lax.dynamic_index_in_dim(kernel, shift_a, 0, keepdims=False)
        bands = (
            jnp.dot(plane, select, preferred_element_type=jnp.float32)
            .astype(jnp.bfloat16)
            .reshape(21 * size_z, size_z)
        )
        stacked = jnp.stack(
            [slab[:, shift_b : shift_b + size_y, :] for shift_b in range(21)], axis=2
        )
        stacked = stacked.reshape(size_x * size_y, 21 * size_z)
        summed = jnp.dot(stacked, bands, preferred_element_type=jnp.float32)
        return total + summed.reshape(size_x, size_y, size_z)

    return lax.fori_loop(0, 21, per_plane, jnp.zeros((size_x, size_y, size_z), jnp.float32))


def restrict_local(padded):
    width_x, width_y, size_z = padded.shape
    size_x = (width_x - 20) // 2
    size_y = (width_y - 20) // 2
    along_x = weight_table(jnp.arange(size_x), jnp.arange(width_x), 10)
    along_y = weight_table(jnp.arange(size_y), jnp.arange(width_y), 10)
    joint = (
        (along_x[:, None, :, None] * along_y[None, :, None, :])
        .reshape(size_x * size_y, width_x * width_y)
        .astype(jnp.bfloat16)
    )
    plane_sum = jnp.dot(
        joint, padded.reshape(width_x * width_y, size_z), preferred_element_type=jnp.float32
    )
    along_z = weight_table(jnp.arange(size_z // 2), jnp.arange(size_z), 0)
    out = jnp.dot(plane_sum, along_z.T, precision=lax.Precision.HIGHEST)
    return out.reshape(size_x, size_y, size_z // 2)


def per_device(charges, kernels):
    size_x, size_y, size_z = charges.shape
    count_x = lax.axis_size("gx")
    count_y = lax.axis_size("gy")
    index_x = lax.axis_index("gx")
    index_y = lax.axis_index("gy")
    spread = size_x * count_x / 16.0
    padded = with_halo(charges, (("gx", 0), ("gy", 1)), 10)
    fine_part = direct_sum(padded, kernels[0])
    middle = restrict_local(padded).astype(jnp.bfloat16)
    middle_pad = with_halo(middle, (("gx", 0), ("gy", 1)), 10)
    middle_sum = direct_sum(middle_pad, kernels[1])
    coarse = restrict_local(middle_pad)
    quarter_x = size_x // 4
    quarter_y = size_y // 4
    half_x = size_x // 2
    half_y = size_y // 2
    coarse_z = jnp.arange(size_z // 4)
    matrix_z = top_block(jnp.arange(size_z // 2), coarse_z, size_z // 4, spread)
    lifted = jnp.einsum("xyc,kc->xyk", coarse, matrix_z, precision=lax.Precision.HIGHEST)
    own_rows_x = index_x * half_x + jnp.arange(half_x)
    own_rows_y = index_y * half_y + jnp.arange(half_y)
    piece = lax.all_gather(lifted, "gx", axis=0, tiled=True)
    block = top_block(own_rows_x, jnp.arange(piece.shape[0]), quarter_x * count_x, spread)
    partial_x = jnp.einsum("jm,myz->jyz", block, piece, precision=lax.Precision.HIGHEST)
    piece = lax.all_gather(partial_x, "gy", axis=1, tiled=True)
    block = top_block(own_rows_y, jnp.arange(piece.shape[1]), quarter_y * count_y, spread)
    top = jnp.einsum("jm,xmz->xjz", block, piece, precision=lax.Precision.HIGHEST)
    middle_potential = middle_sum + top
    rim_pad = with_halo(middle_potential, (("gx", 0), ("gy", 1)), 2)
    up_x = weight_table(jnp.arange(half_x + 4) - 2, jnp.arange(size_x), 0)
    up_y = weight_table(jnp.arange(half_y + 4) - 2, jnp.arange(size_y), 0)
    up_z = weight_table(jnp.arange(size_z // 2), jnp.arange(size_z), 0)
    lifted_up = jnp.einsum("ip,ijk->pjk", up_x, rim_pad, precision=lax.Precision.HIGHEST)
    lifted_up = jnp.einsum("jq,pjk->pqk", up_y, lifted_up, precision=lax.Precision.HIGHEST)
    lifted_up = jnp.einsum("kz,pqk->pqz", up_z, lifted_up, precision=lax.Precision.HIGHEST)
    return fine_part + lifted_up


def solution(mesh):
    return jax.shard_map(
        per_device,
        mesh=mesh,
        in_specs=(P("gx", "gy", None), P()),
        out_specs=P("gx", "gy", None),
        check_vma=False,
    )
```

profile of v0, /device:TPU:2, one launch (start us, length us, event | category | flops | bytes accessed | tf_op | source)
XLA Modules:
  0.0 448.0 jit_solution(10394244525292175797)
XLA Ops:
  8.1 5.5 %collective-permute-start.3 = (bf16[40,10,128]{2,1,0:T(8,128)(2,1)S(1)}, bf16[40,10,128]{2,1,0:T(8,128)(2,1)S(1)}, u32[]{:S(2)}, u32[]{:S(2)}) collective-permute-start(bf16[40,10,128]{2,1,0:T(8,128)(2,1)S(1)} %get-tuple-element.258), channel_id=1, source_target_pairs={{1,0},{2,1},{3,2},{4,3},{5,4},{6,5},{7,6},{9,8},{10,9},{11,10},{12... | collective-permute-start | bytes 307208 | tf_op jit(solution)/shard_map/ppermute | solution.py:17
  16.4 6.5 %collective-permute-done.2 = bf16[40,10,128]{2,1,0:T(8,128)(2,1)S(1)} collective-permute-done((bf16[40,10,128]{2,1,0:T(8,128)(2,1)S(1)}, bf16[40,10,128]{2,1,0:T(8,128)(2,1)S(1)}, u32[]{:S(2)}, u32[]{:S(2)}) %collective-permute-start.2) | collective-permute-done | bytes 102432 | tf_op jit(solution)/shard_map/ppermute | solution.py:14
  23.8 4.9 %collective-permute-start.4 = (bf16[10,10,64]{2,1,0:T(8,128)(2,1)S(1)}, bf16[10,10,64]{2,1,0:T(8,128)(2,1)S(1)}, u32[]{:S(2)}, u32[]{:S(2)}) collective-permute-start(bf16[10,10,64]{2,1,0:T(8,128)(2,1)S(1)} %convert_element_type.63), channel_id=1, source_target_pairs={{0,8},{8,16},{16,24},{24,32},{32,40},{40,48},{48,56},{56,64},{64,7... | collective-permute-start | bytes 38408 | tf_op jit(solution)/shard_map/ppermute | solution.py:14
  30.2 5.5 %collective-permute-done.5 = bf16[10,10,64]{2,1,0:T(8,128)(2,1)S(1)} collective-permute-done((bf16[10,10,64]{2,1,0:T(8,128)(2,1)S(1)}, bf16[10,10,64]{2,1,0:T(8,128)(2,1)S(1)}, u32[]{:S(2)}, u32[]{:S(2)}) %collective-permute-start.5) | collective-permute-done | bytes 12832 | tf_op jit(solution)/shard_map/ppermute | solution.py:17
  37.8 3.8 collective-permute-start.6
  42.5 4.2 collective-permute-done.6
  46.9 47.0 %while.29 = (s32[]{:T(128)}, f32[10,10,64]{2,1,0:T(8,128)S(1)}, bf16[30,30,64]{2,1,0:T(8,128)(2,1)S(1)}, bf16[21,21,21]{2,1,0:T(8,128)(2,1)S(1)}, s32[4096]{0:T(...) while((s32[]{:T(128)}, f32[10,10,64]{2,1,0:T(8,128)S(1)}, ...), condition=%wide.region_3.4_spmd.clone, body=%wide.region_2.3_spmd.clone.sunk | while | flops 21086744 | bytes 3798679 | solution.py:78
  94.5 46.3 %all_gather.6 = f32[160,5,64]{2,1,0:T(8,128)S(1)} all-gather(f32[5,5,64]{2,1,0:T(8,128)S(1)} %fusion.261), channel_id=1, replica_groups=mesh['gx'=32,'gy'=8] {'gx'}, dimensions={0}, use_global_device_ids=true | all-gather | bytes 211200 | tf_op jit(solution)/shard_map/all_gather | solution.py:122
  141.2 28.5 %all_gather.7 = f32[10,40,64]{2,0,1:T(8,128)S(1)} all-gather(f32[10,5,64]{2,0,1:T(8,128)S(1)} %fusion.38), channel_id=1, replica_groups=mesh['gx'=32,'gy'=8] {'gy'}, dimensions={1}, use_global_device_ids=true | all-gather | bytes 115200 | tf_op jit(solution)/shard_map/all_gather | solution.py:125
  177.9 4.0 collective-permute-start.10
  181.9 263.3 %while.28 = (s32[]{:T(128)}, f32[20,20,128]{2,1,0:T(8,128)S(1)}, bf16[40,40,128]{2,1,0:T(8,128)(2,1)S(1)}, bf16[21,21,21]{2,1,0:T(8,128)(2,1)S(1)}, s32[16384]{0...) while((s32[]{:T(128)}, f32[20,20,128]{2,1,0:T(8,128)S(1)}, ...), condition=%wide.region_1.2_spmd.clone, body=%wide.region_0.1_spmd.clone.sunk | while | flops 290836512 | bytes 19126936 | solution.py:78
  185.5 3.4 dot_general.88
  210.6 3.4 dot_general.88
  223.1 3.4 dot_general.88
  248.2 3.4 dot_general.88
  273.2 3.4 dot_general.88
  285.8 3.4 dot_general.88
  323.4 3.4 dot_general.88
  348.5 3.4 dot_general.88
  361.0 3.4 dot_general.88
  373.5 3.4 dot_general.88
  386.1 3.4 dot_general.88
  398.6 3.4 dot_general.88
  436.2 3.4 dot_general.88
  (1157 shorter events, 289.9 us)
Async XLA Ops:
  0.0 8.0 %copy-start.1 = (bf16[20,20,128]{2,1,0:T(8,128)(2,1)S(1)}, bf16[20,20,128]{2,1,0:T(8,128)(2,1)}, u32[]{:S(2)}) copy-start(bf16[20,20,128]{2,1,0:T(8,128)(2,1)} %param.6) | copy-start | bytes 307204
  0.9 7.0 %collective-permute-start = (bf16[10,20,128]{2,1,0:T(8,128)(2,1)S(1)}, bf16[10,20,128]{2,1,0:T(8,128)(2,1)S(1)}, u32[]{:S(2)}, u32[]{:S(2)}) collective-permute-start(bf16[10,20,128]{2,1,0:T(8,128)(2,1)S(1)} %get-tuple-element.262), channel_id=1, source_target_pairs={{0,8},{8,16},{16,24},{24,32},{32,40},{40,48},{48,56},{56,64},{64,7... | collective-permute-start | bytes 153608 | tf_op jit(solution)/shard_map/ppermute | solution.py:14
  2.7 5.3 %collective-permute-start.1 = (bf16[10,20,128]{2,1,0:T(8,128)(2,1)S(1)}, bf16[10,20,128]{2,1,0:T(8,128)(2,1)S(1)}, u32[]{:S(2)}, u32[]{:S(2)}) collective-permute-start(bf16[10,20,128]{2,1,0:T(8,128)(2,1)S(1)} %get-tuple-element.261), channel_id=1, source_target_pairs={{8,0},{16,8},{24,16},{32,24},{40,32},{48,40},{56,48},{64,56},{72,6... | collective-permute-start | bytes 153608 | tf_op jit(solution)/shard_map/ppermute | solution.py:17
  8.1 8.3 %collective-permute-start.3 = (bf16[40,10,128]{2,1,0:T(8,128)(2,1)S(1)}, bf16[40,10,128]{2,1,0:T(8,128)(2,1)S(1)}, u32[]{:S(2)}, u32[]{:S(2)}) collective-permute-start(bf16[40,10,128]{2,1,0:T(8,128)(2,1)S(1)} %get-tuple-element.258), channel_id=1, source_target_pairs={{1,0},{2,1},{3,2},{4,3},{5,4},{6,5},{7,6},{9,8},{10,9},{11,10},{12... | collective-permute-start | bytes 307208 | tf_op jit(solution)/shard_map/ppermute | solution.py:17
  13.6 9.3 %collective-permute-start.2 = (bf16[40,10,128]{2,1,0:T(8,128)(2,1)S(1)}, bf16[40,10,128]{2,1,0:T(8,128)(2,1)S(1)}, u32[]{:S(2)}, u32[]{:S(2)}) collective-permute-start(bf16[40,10,128]{2,1,0:T(8,128)(2,1)S(1)} %get-tuple-element.257), channel_id=1, source_target_pairs={{0,1},{1,2},{2,3},{3,4},{4,5},{5,6},{6,7},{8,9},{9,10},{10,11},{11... | collective-permute-start | bytes 307208 | tf_op jit(solution)/shard_map/ppermute | solution.py:14
  23.8 6.4 %collective-permute-start.4 = (bf16[10,10,64]{2,1,0:T(8,128)(2,1)S(1)}, bf16[10,10,64]{2,1,0:T(8,128)(2,1)S(1)}, u32[]{:S(2)}, u32[]{:S(2)}) collective-permute-start(bf16[10,10,64]{2,1,0:T(8,128)(2,1)S(1)} %convert_element_type.63), channel_id=1, source_target_pairs={{0,8},{8,16},{16,24},{24,32},{32,40},{40,48},{48,56},{56,64},{64,7... | collective-permute-start | bytes 38408 | tf_op jit(solution)/shard_map/ppermute | solution.py:14
  28.9 6.8 %collective-permute-start.5 = (bf16[10,10,64]{2,1,0:T(8,128)(2,1)S(1)}, bf16[10,10,64]{2,1,0:T(8,128)(2,1)S(1)}, u32[]{:S(2)}, u32[]{:S(2)}) collective-permute-start(bf16[10,10,64]{2,1,0:T(8,128)(2,1)S(1)} %convert_element_type.63), channel_id=1, source_target_pairs={{8,0},{16,8},{24,16},{32,24},{40,32},{48,40},{56,48},{64,56},{72,6... | collective-permute-start | bytes 38408 | tf_op jit(solution)/shard_map/ppermute | solution.py:17
  35.7 6.8 %collective-permute-start.7 = (bf16[30,10,64]{2,1,0:T(8,128)(2,1)S(1)}, bf16[30,10,64]{2,1,0:T(8,128)(2,1)S(1)}, u32[]{:S(2)}, u32[]{:S(2)}) collective-permute-start(bf16[30,10,64]{2,1,0:T(8,128)(2,1)S(1)} %constant_dynamic-update-slice_fusion.24), channel_id=1, source_target_pairs={{1,0},{2,1},{3,2},{4,3},{5,4},{6,5},{7,6},{9,8},{10,9},{11,10},{12... | collective-permute-start | bytes 115208 | tf_op jit(solution)/shard_map/ppermute | solution.py:17
  37.8 8.9 %collective-permute-start.6 = (bf16[30,10,64]{2,1,0:T(8,128)(2,1)S(1)}, bf16[30,10,64]{2,1,0:T(8,128)(2,1)S(1)}, u32[]{:S(2)}, u32[]{:S(2)}) collective-permute-start(bf16[30,10,64]{2,1,0:T(8,128)(2,1)S(1)} %constant_dynamic-update-slice_fusion.24), channel_id=1, source_target_pairs={{0,1},{1,2},{2,3},{3,4},{4,5},{5,6},{6,7},{8,9},{9,10},{10,11},{11... | collective-permute-start | bytes 115208 | tf_op jit(solution)/shard_map/ppermute | solution.py:14
  93.9 80.5 %copy-start = (bf16[1,21,21,21]{3,0,2,1:T(2,128)(2,1)S(1)}, bf16[1,21,21,21]{3,0,2,1:T(2,128)(2,1)}, u32[]{:S(2)}) copy-start(bf16[1,21,21,21]{3,0,2,1:T(2,128)(2,1)} %get-tuple-element.260) | copy-start | bytes 55570
  170.0 4.4 collective-permute-start.9
  171.3 3.9 collective-permute-start.8
  175.8 269.3 %collective-permute-start.11 = (f32[14,2,64]{2,1,0:T(2,128)}, f32[14,2,64]{2,1,0:T(2,128)}, u32[]{:S(2)}, u32[]{:S(2)}) collective-permute-start(f32[14,2,64]{2,1,0:T(2,128)} %get-tuple-element.264), channel_id=1, source_target_pairs={{1,0},{2,1},{3,2},{4,3},{5,4},{6,5},{7,6},{9,8},{10,9},{11,10},{12... | collective-permute-start | bytes 21512 | tf_op jit(solution)/shard_map/ppermute | solution.py:17
  177.9 267.3 %collective-permute-start.10 = (f32[14,2,64]{2,1,0:T(2,128)}, f32[14,2,64]{2,1,0:T(2,128)}, u32[]{:S(2)}, u32[]{:S(2)}) collective-permute-start(f32[14,2,64]{2,1,0:T(2,128)} %get-tuple-element.263), channel_id=1, source_target_pairs={{0,1},{1,2},{2,3},{3,4},{4,5},{5,6},{6,7},{8,9},{9,10},{10,11},{11... | collective-permute-start | bytes 21512 | tf_op jit(solution)/shard_map/ppermute | solution.py:14
where the time goes:
time: 454 us; the launch traced here: 448 us
  local copies, waits for them, and re-layouts  232 us (51%)
  matrix products  82.1 us (18%)
  blocking collectives  74.8 us (16%)
  starting transfers between devices  32.8 us (7%)
  waiting for transfers between devices  18.3 us (4%)
  loops' own time  4.55 us (1%)
    dot_general x42, local copies, waits for them, and re-layouts, per_plane(): summed = jnp.dot(stacked, bands, preferred_element_type=jnp.float32)  79.4 us
    another operation x84, local copies, waits for them, and re-layouts, per_plane(): jnp.stack([slab[:, shift_b:shift_b + size_y, :] for shift_b in range(21)]...  56.6 us
    reshape x42, local copies, waits for them, and re-layouts, per_plane(): bands = jnp.dot(plane, select, preferred_element_type=jnp.float32).astype...  54 us
    dot_general x42, matrix products, per_plane(): summed = jnp.dot(stacked, bands, preferred_element_type=jnp.float32)  47.8 us
    all_gather x1, blocking collectives, per_device(): piece = lax.all_gather(lifted, 'gx', axis=0, tiled=True)  46.3 us
    while x840, local copies, waits for them, and re-layouts  37.3 us
    dot_general x42, matrix products, per_plane(): jnp.dot(plane, select, preferred_element_type=jnp.float32)  30.6 us
    all_gather x1, blocking collectives, per_device(): piece = lax.all_gather(partial_x, 'gy', axis=1, tiled=True)  28.5 us
  transfers between devices with their start and end apart: 12, of which 6 were waited for; matrix products, arithmetic and copies ran while one was open for 59% of the time, Pallas kernels for 0%

commit v1 on v0

v1 whole, which is shorter than its diff:
```python
import functools
import numpy as np
import jax
import jax.numpy as jnp
from jax import lax
from jax.experimental import pallas as pl
from jax.experimental.pallas import tpu as pltpu
from jax.sharding import PartitionSpec as P

f32 = jnp.float32
bf16 = jnp.bfloat16
spread_norm = 1.2533141
HIGHEST = lax.Precision.HIGHEST
REACH = 10
TAPS = 21


def weight_np(offset):
    d = np.abs(offset)
    return np.where(d == 0, 1.0, np.where(d == 1, 0.5625, np.where(d == 3, -0.0625, 0.0)))


def top_matrix_np(n, spread):
    prolong = weight_np(np.arange(2 * n)[:, None] - 2 * np.arange(n)[None, :])
    offset = (np.arange(n)[:, None] - np.arange(n)[None, :]) / spread
    return prolong @ (np.exp(-offset * offset) / np.sqrt(spread * spread_norm))


def lane_tiles(m):
    return m.reshape(m.shape[0], -1, 128).transpose(1, 0, 2).astype(np.float32)


def matrix_x_np(spread):
    m = top_matrix_np(160, spread).reshape(320, 32, 5)
    out = np.zeros((328, 32, 8))
    out[1:321, :, :5] = m
    return lane_tiles(out.reshape(328, 256))


def matrix_y_np(spread):
    m = top_matrix_np(40, spread).reshape(80, 8, 5)
    out = np.zeros((88, 8, 8))
    out[2:82, :, :5] = m
    return lane_tiles(np.repeat(out.reshape(88, 64), 32, axis=1))


def matrix_z_np(spread):
    m = top_matrix_np(32, spread).T
    out = np.zeros((2, 8, 32, 2, 64))
    for par in range(2):
        out[par, :, :, par, :] = m[None]
    return out.reshape(512, 128).astype(np.float32)


def spots_np():
    taps = np.arange(TAPS)[:, None]
    lanes = np.arange(128)[None, :]
    near = lanes == (REACH - taps) % 128
    far = lanes == (64 + REACH - taps) % 128
    return near, far


def weight(d):
    d = jnp.abs(d)
    return jnp.where(d == 0, 1.0, jnp.where(d == 1, 0.5625, jnp.where(d == 3, -0.0625, 0.0))).astype(f32)


def iota2(shape):
    return (lax.broadcasted_iota(jnp.int32, shape, 0), lax.broadcasted_iota(jnp.int32, shape, 1))


def vmem_call(body, out_shape, scratch, name, args, smem=0, flops=0):
    specs = [pl.BlockSpec(memory_space=pltpu.SMEM)] * smem
    specs += [pl.BlockSpec(memory_space=pltpu.VMEM)] * (len(args) - smem)
    return pl.pallas_call(
        body,
        out_shape=out_shape,
        in_specs=specs,
        out_specs=jax.tree.map(lambda _: pl.BlockSpec(memory_space=pltpu.VMEM), out_shape),
        scratch_shapes=scratch,
        compiler_params=pltpu.CompilerParams(vmem_limit_bytes=32 << 20),
        cost_estimate=pl.CostEstimate(flops=flops, bytes_accessed=1 << 16, transcendentals=0),
        name=name,
    )(*args)


def rim_kernel(blk_ref, ylo_ref, yhi_ref, xlo_ref, xhi_ref, wide):
    for out_ref, start in ((xlo_ref, 0), (xhi_ref, 10)):
        wide[:, 0:10, :] = ylo_ref[start : start + 10].astype(f32)
        wide[:, 10:30, :] = blk_ref[start : start + 10].astype(f32)
        wide[:, 30:40, :] = yhi_ref[start : start + 10].astype(f32)
        out_ref[...] = wide[...].astype(bf16)


def restrict_kernel(
    where_ref, blk_ref, ylo_ref, yhi_ref, xlo_ref, xhi_ref,
    d_ref, right_ref, left_ref, own_ref, coarse_ref,
    planes, cells, mid, row,
):
    for x in range(40):
        p, i = x % 2, x // 2
        if x < 10:
            d_ref[p, i, 0:40, :] = xlo_ref[x].astype(f32)
        elif x >= 30:
            d_ref[p, i, 0:40, :] = xhi_ref[x - 30].astype(f32)
        else:
            d_ref[p, i, 0:10, :] = ylo_ref[x - 10].astype(f32)
            d_ref[p, i, 10:30, :] = blk_ref[x - 10].astype(f32)
            d_ref[p, i, 30:40, :] = yhi_ref[x - 10].astype(f32)
        d_ref[p, i, 40:48, :] = jnp.zeros((8, 128), f32)

    def fine(x):
        return d_ref[x % 2, x // 2]

    for i in range(16):
        c = 2 * i + 4
        planes[i] = (
            fine(c) + 0.5625 * (fine(c - 1) + fine(c + 1)) - 0.0625 * (fine(c - 3) + fine(c + 3))
        )
    for i in range(16):
        def tap(o):
            return planes[i, pl.ds(4 + o, 16, stride=2), :]
        cells[16 * i : 16 * i + 16, :] = (
            tap(0) + 0.5625 * (tap(-1) + tap(1)) - 0.0625 * (tap(-3) + tap(3))
        )
    zero = jnp.zeros((16, 128), f32)
    rows = []
    for n in range(9):
        pair = []
        for y in (2 * n - 4, 2 * n - 3):
            inside = -3 <= y <= 12
            pair.append(cells[pl.ds(y + 3, 16, stride=16), :] if inside else zero)
        rows.append(jnp.concatenate(pair, axis=1))
    r, c = iota2((256, 128))
    down_z = jnp.where(r // 128 == c // 64, weight(r % 128 - 2 * (c % 64)), 0.0)
    value = jnp.dot(
        jnp.concatenate(rows, axis=0), down_z, precision=HIGHEST, preferred_element_type=f32
    )
    r, c = iota2((144, 128))
    cell_x = 10 * where_ref[0] - 3 + r % 16
    cell_y = 10 * where_ref[1] - 4 + 2 * (r // 16) + c // 64
    inside = (cell_x >= 0) & (cell_x < 320) & (cell_y >= 0) & (cell_y < 80)
    value = jnp.where(inside, value, 0.0).astype(bf16).astype(f32)
    for n in range(9):
        mid[n, 0:16, :] = value[16 * n : 16 * n + 16]
        mid[n, 16:24, :] = jnp.zeros((8, 128), f32)
    for n in range(5):
        own_ref[n] = value[16 * n + 32 : 16 * n + 48].astype(bf16)
        right_ref[n] = mid[n + 2, 2:10, :].astype(bf16)
        left_ref[n] = mid[n + 2, 6:15, :].astype(bf16)

    lane = lax.broadcasted_iota(jnp.int32, (1, 128), 1)
    odd = lane >= 64
    weight_0 = jnp.where(odd, 0.5625, 1.0)
    weight_1 = jnp.where(odd, 0.5625, 0.0)
    weight_3 = jnp.where(odd, -0.0625, 0.0)
    r, c = iota2((128, 32))
    down_z = weight(r % 64 - 2 * c)
    row[...] = jnp.zeros((8, 256), f32)
    sums = []
    for y in range(5):
        n = y + 2
        def tap(o):
            def part(k):
                return mid[k, pl.ds(3 + o, 8, stride=2), :]
            return (
                weight_0 * part(n) + weight_1 * part(n - 1) + weight_3 * (part(n - 2) + part(n + 1))
            )
        sums.append(tap(0) + 0.5625 * (tap(-1) + tap(1)) - 0.0625 * (tap(-3) + tap(3)))
    out = jnp.dot(
        jnp.concatenate(sums, axis=0), down_z, precision=HIGHEST, preferred_element_type=f32
    )
    for y in range(5):
        row[:, 32 * y : 32 * y + 32] = out[8 * y : 8 * y + 8]
    for k in range(coarse_ref.shape[0]):
        coarse_ref[k] = row[...]


def fine_kernel(lo, hi, first, d_ref, v_ref, *refs):
    if first:
        out_ref, w0, w1, e0, e1 = refs
        out_ref[...] = jnp.zeros((240, 256), f32)
    else:
        acc_ref, out_ref, w0, w1, e0, e1 = refs
        out_ref[...] = acc_ref[...]
    r, c = iota2((128, 128))
    mask = jnp.abs(r - c) <= REACH
    zero = jnp.zeros((128, 128), bf16)
    for w in (w0, w1):
        w[0:128, 128:256] = zero
        w[2688:2816, 0:128] = zero

    def build(w, b):
        for a in range(TAPS):
            line = jnp.broadcast_to(v_ref[pl.ds(a * TAPS + b, 1), :], (128, 128))
            line = pltpu.roll(line, 0, 1, stride=1, stride_axis=0)
            band = jnp.where(mask, line, 0.0).astype(bf16)
            w[a * 128 : (a + 1) * 128, 0:128] = band
            w[(a + 1) * 128 : (a + 2) * 128, 128:256] = band

    def dot(w, e, b):
        for p in range(2):
            for q in range(10):
                part = d_ref[p, 2 * q : 2 * q + 2, pl.ds(b, 24), :].reshape(48, 128)
                e[0, 48 * q : 48 * q + 48, p * 128 : (p + 1) * 128] = part.astype(bf16)
            for q in range(9):
                part = d_ref[p, 2 * q + 1 : 2 * q + 3, pl.ds(b, 24), :].reshape(48, 128)
                e[1, 48 * q : 48 * q + 48, p * 128 : (p + 1) * 128] = part.astype(bf16)
        lhs = jnp.concatenate(
            [e[k % 2, 24 * (k - k % 2) : 24 * (k - k % 2) + 240, :] for k in range(11)], axis=1
        )
        out_ref[...] += jnp.dot(lhs, w[...], preferred_element_type=f32)

    build(w0, lo)

    def step(t, _):
        b = lo + 2 * t
        build(w1, b + 1)
        dot(w0, e0, b)
        build(w0, jnp.minimum(b + 2, TAPS - 1))
        dot(w1, e1, b + 1)
        return 0

    lax.fori_loop(0, (hi - lo) // 2, step, 0)
    if (hi - lo) % 2:
        dot(w0, e0, hi - 1)


def fine_sum(lo, hi, d, v, acc=None):
    args = (d, v) if acc is None else (d, v, acc)
    return vmem_call(
        functools.partial(fine_kernel, lo, hi, acc is None),
        jax.ShapeDtypeStruct((240, 256), f32),
        [pltpu.VMEM((2816, 256), bf16)] * 2 + [pltpu.VMEM((2, 480, 256), bf16)] * 2,
        "fine_sum",
        args,
        flops=(hi - lo) * 2 * 240 * 2816 * 256,
    )


def spread_kernel(where_ref, coarse_ref, mx_ref, own_ref, lo_ref, hi_ref, out_ref, buf):
    start = 10 * where_ref[0]
    rows = jnp.concatenate([mx_ref[h, pl.ds(start, 16), :] for h in range(2)], axis=1)
    part = jnp.dot(rows, coarse_ref[...], precision=HIGHEST, preferred_element_type=f32)
    for n in range(5):
        buf[33 * n : 33 * n + 8, :] = lo_ref[n].astype(f32)
        buf[33 * n + 8 : 33 * n + 24, :] = own_ref[n].astype(f32)
        buf[33 * n + 24 : 33 * n + 33, :] = hi_ref[n].astype(f32)
    buf[165:176, :] = jnp.zeros((11, 128), f32)
    high = part.astype(bf16)
    low = (part - high.astype(f32)).astype(bf16)
    cells = buf[...].astype(bf16)
    for k in range(out_ref.shape[0]):
        out_ref[k, 0:176, :] = cells
        out_ref[k, 176:192, :] = high[:, 0:128]
        out_ref[k, 192:208, :] = high[:, 128:256]
        out_ref[k, 208:224, :] = low[:, 0:128]
        out_ref[k, 224:240, :] = low[:, 128:256]


def final_kernel(
    where_ref, recv_ref, my_ref, mz_ref, near_ref, far_ref, fine_ref, out_ref,
    cells, w0, w1, acc, moved, wide, line,
):
    index_x = where_ref[0]
    index_y = where_ref[1]
    count = recv_ref.shape[0]
    cells[:, 32:40, :] = jnp.zeros((18, 8, 128), f32)
    for step in range(-2, 3):
        source = index_y + step
        inside = (source >= 0) & (source < count)
        got = recv_ref[jnp.clip(source, 0, count - 1), 0:176, :].astype(f32)
        line[...] = jnp.where(inside, got, 0.0)
        for p in range(5):
            n = 5 * step + 6 + p
            if 0 <= n < 18:
                cells[n, 0:33, :] = line[33 * p : 33 * p + 33, :]

    r, c = iota2((128, 128))
    mask = jnp.abs(r % 64 - c % 64) <= REACH
    zero = jnp.zeros((128, 128), bf16)
    for w in (w0, w1):
        w[0:128, 128:256] = zero
        w[1408:1536, 0:128] = zero

    def build(w, a):
        base = TAPS * TAPS + a * TAPS
        for j in range(11):
            same = near_ref[pl.ds(base + 2 * j, 1), :]
            upper = same
            lower = same
            if j > 0:
                upper = same + far_ref[pl.ds(base + 2 * j - 1, 1), :]
            if j < 10:
                lower = same + far_ref[pl.ds(base + 2 * j + 1, 1), :]
            upper = pltpu.roll(jnp.broadcast_to(upper, (64, 128)), 0, 1, stride=1, stride_axis=0)
            lower = pltpu.roll(jnp.broadcast_to(lower, (64, 128)), 64, 1, stride=1, stride_axis=0)
            band = jnp.where(mask, jnp.concatenate([upper, lower], axis=0), 0.0).astype(bf16)
            w[128 * j : 128 * j + 128, 0:128] = band
            w[128 * j + 128 : 128 * j + 256, 128:256] = band

    def dot(w, a):
        part = [cells[n, pl.ds(a, 16), :].astype(bf16) for n in range(18)]
        lhs = jnp.concatenate(
            [jnp.concatenate(part[2 * g : 2 * g + 12], axis=1) for g in range(4)], axis=0
        )
        acc[...] += jnp.dot(lhs, w[...], preferred_element_type=f32)

    acc[...] = jnp.zeros((64, 256), f32)
    build(w0, 0)

    def step(t, _):
        a = 2 * t
        build(w1, a + 1)
        dot(w0, a)
        build(w0, a + 2)
        dot(w1, a + 1)
        return 0

    lax.fori_loop(0, 10, step, 0)
    dot(w0, TAPS - 1)

    start = 10 * index_y
    sums = [[None] * 16, [None] * 16]
    for k in range(count):
        high = [recv_ref[k, 176 + 16 * h : 192 + 16 * h, :].astype(f32) for h in range(2)]
        low = [recv_ref[k, 208 + 16 * h : 224 + 16 * h, :].astype(f32) for h in range(2)]
        for h in range(2):
            value = high[h] + low[h]
            rows_y = my_ref[2 * k + h, pl.ds(start, 16), :]
            for y in range(16):
                term = value * rows_y[y : y + 1, :]
                sums[h][y] = term if k == 0 else sums[h][y] + term
    rows = [
        jnp.concatenate([sums[h][2 * n + p] for p in range(2) for h in range(2)], axis=1)
        for n in range(8)
    ]
    top = jnp.dot(
        jnp.concatenate(rows, axis=0), mz_ref[...], precision=HIGHEST, preferred_element_type=f32
    )
    both = []
    for n in range(8):
        g, u = n // 2, n % 2
        both.append(acc[16 * g : 16 * g + 16, 128 * u : 128 * u + 128])
    total = jnp.concatenate(both, axis=0) + top
    r, c = iota2((128, 128))
    cell_x = 10 * index_x - 1 + r % 16
    cell_y = 10 * index_y - 2 + 2 * (r // 16) + c // 64
    inside = (cell_x >= 0) & (cell_x < 320) & (cell_y >= 0) & (cell_y < 80)
    total = jnp.where(inside, total, 0.0)
    r, c = iota2((128, 256))
    up_z = jnp.where(r // 64 == c // 128, weight(c % 128 - 2 * (r % 64)), 0.0)
    wide[...] = jnp.dot(total, up_z, precision=HIGHEST, preferred_element_type=f32)

    def middle_y(y):
        n, par = (y + 2) // 2, y % 2
        return wide[16 * n : 16 * n + 16, 128 * par : 128 * par + 128]

    for y in range(20):
        m = y // 2
        if y % 2 == 0:
            value = middle_y(m)
        else:
            value = 0.5625 * (middle_y(m) + middle_y(m + 1)) - 0.0625 * (
                middle_y(m - 1) + middle_y(m + 2)
            )
        moved[16 * y : 16 * y + 16, :] = value
    planes = [moved[pl.ds(k, 20, stride=16), :] for k in range(13)]
    for x in range(20):
        m = x // 2
        if x % 2 == 0:
            value = planes[m + 1]
        else:
            value = 0.5625 * (planes[m + 1] + planes[m + 2]) - 0.0625 * (planes[m] + planes[m + 3])
        out_ref[x] = value + fine_ref[24 * m : 24 * m + 20, 128 * (x % 2) : 128 * (x % 2) + 128]


def halo(low_edge, high_edge, axis):
    count = lax.axis_size(axis)
    forward = [(i, i + 1) for i in range(count - 1)]
    backward = [(i + 1, i) for i in range(count - 1)]
    return lax.ppermute(high_edge, axis, forward), lax.ppermute(low_edge, axis, backward)


def per_device(charges, kernels):
    count_x = lax.axis_size("gx")
    count_y = lax.axis_size("gy")
    where = jnp.stack([lax.axis_index("gx"), lax.axis_index("gy")]).astype(jnp.int32)
    spread = charges.shape[0] * count_x / 16.0
    shape = jax.ShapeDtypeStruct
    near, far = (
        jnp.dot(kernels.reshape(-1, TAPS), jnp.asarray(m, bf16), preferred_element_type=f32)
        for m in spots_np()
    )
    y_lo, y_hi = halo(charges[:, :10], charges[:, 10:], "gy")
    edge_lo, edge_hi = vmem_call(
        rim_kernel,
        [shape((10, 40, 128), bf16)] * 2,
        [pltpu.VMEM((10, 40, 128), f32)],
        "rim",
        (charges, y_lo, y_hi),
    )
    x_lo, x_hi = halo(edge_lo, edge_hi, "gx")
    d, right, left, own, coarse = vmem_call(
        restrict_kernel,
        [
            shape((2, 20, 48, 128), f32),
            shape((5, 8, 128), bf16),
            shape((5, 9, 128), bf16),
            shape((5, 16, 128), bf16),
            shape((count_x, 8, 256), f32),
        ],
        [
            pltpu.VMEM((16, 48, 128), f32),
            pltpu.VMEM((256, 128), f32),
            pltpu.VMEM((9, 24, 128), f32),
            pltpu.VMEM((8, 256), f32),
        ],
        "restrict",
        (where, charges, y_lo, y_hi, x_lo, x_hi),
        smem=1,
    )
    mid_lo, mid_hi = halo(left, right, "gx")
    coarse = lax.all_to_all(coarse, "gx", 0, 0).reshape(256, 256)
    fine = fine_sum(0, 11, d, near)
    parts = vmem_call(
        spread_kernel,
        shape((count_y, 240, 128), bf16),
        [pltpu.VMEM((176, 128), f32)],
        "spread",
        (where, coarse, jnp.asarray(matrix_x_np(spread)), own, mid_lo, mid_hi),
        smem=1,
    )
    parts = lax.all_to_all(parts, "gy", 0, 0)
    fine = fine_sum(11, 21, d, near, fine)
    return vmem_call(
        final_kernel,
        shape((20, 20, 128), f32),
        [
            pltpu.VMEM((18, 40, 128), f32),
            pltpu.VMEM((1536, 256), bf16),
            pltpu.VMEM((1536, 256), bf16),
            pltpu.VMEM((64, 256), f32),
            pltpu.VMEM((320, 128), f32),
            pltpu.VMEM((128, 256), f32),
            pltpu.VMEM((176, 128), f32),
        ],
        "final",
        (
            where,
            parts,
            jnp.asarray(matrix_y_np(spread)),
            jnp.asarray(matrix_z_np(spread)),
            near,
            far,
            fine,
        ),
        smem=1,
    )


def solution(mesh):
    return jax.shard_map(
        per_device,
        mesh=mesh,
        in_specs=(P("gx", "gy", None), P()),
        out_specs=P("gx", "gy", None),
        check_vma=False,
    )
```

time: 454 us -> 77.6 us (0.17); the launches traced: 448 us -> 76.7 us
  local copies, waits for them, and re-layouts: 232 us -> 3.2 us
  matrix products: 82.1 us -> 0.63 us
  blocking collectives: 74.8 us -> 0 us
  Pallas kernels: 0 us -> 21.8 us
  waiting for transfers between devices: 18.3 us -> 13 us
  starting transfers between devices: 32.8 us -> 37.8 us
  loops' own time: 4.55 us -> 0 us
    dot_general x97 -> x2, matrix products: 82.1 us -> 0.63 us  [per_device(): jnp.dot(kernels.reshape(-1, TAPS), jnp.asarray(m, bf16), preferred_elemen...]
    dot_general x42 -> x0, local copies, waits for them, and re-layouts: 79.4 us -> none  [per_plane(): summed = jnp.dot(stacked, bands, preferred_element_type=jnp.float32)]
    all_gather x2 -> x0, blocking collectives: 74.8 us -> none  [the longest x1 46.3 us: per_device(): piece = lax.all_gather(lifted, 'gx', axis=0, tiled=True)]
    another operation x84 -> x0, local copies, waits for them, and re-layouts: 56.6 us -> none  [per_plane(): jnp.stack([slab[:, shift_b:shift_b + size_y, :] for shift_b in range(21)]...]
    reshape x44 -> x1, local copies, waits for them, and re-layouts: 54.1 us -> 0.26 us  [per_device(): kernels.reshape(-1, TAPS)]
    while x840 -> x0, local copies, waits for them, and re-layouts: 37.3 us -> none
    all_to_all x0 -> x2, starting transfers between devices: none -> 22.8 us  [the longest x1 16.3 us: per_device(): coarse = lax.all_to_all(coarse, 'gx', 0, 0).reshape(256, 256)]
    pallas_call x0 -> x6, Pallas kernels: none -> 21.8 us  [vmem_call(): pl.pallas_call(body, out_shape=out_shape, in_specs=specs, out_specs=jax.t...]
  transfers between devices with their start and end apart: 12 -> 8, of which waited for: 6 -> 5; matrix products, arithmetic and copies ran while one was open for 59% -> 2% of each run, Pallas kernels for 0% -> 14%
where the time goes in v1:
time: 77.6 us; the launch traced here: 76.7 us
  starting transfers between devices  37.8 us (49%)
  Pallas kernels  21.8 us (28%)
  waiting for transfers between devices  13 us (17%)
  local copies, waits for them, and re-layouts  3.2 us (4%)
    pallas_call x6, Pallas kernels, vmem_call(): pl.pallas_call(body, out_shape=out_shape, in_specs=specs, out_specs=jax.t...  21.8 us
    all_to_all x1, starting transfers between devices, per_device(): coarse = lax.all_to_all(coarse, 'gx', 0, 0).reshape(256, 256)  16.3 us
    ppermute x3, starting transfers between devices, halo(): lax.ppermute(high_edge, axis, forward)  7.81 us
    ppermute x3, starting transfers between devices, halo(): lax.ppermute(low_edge, axis, backward)  7.18 us
    all_to_all x1, starting transfers between devices, per_device(): parts = lax.all_to_all(parts, 'gy', 0, 0)  6.46 us
    all_to_all x1, waiting for transfers between devices, per_device(): coarse = lax.all_to_all(coarse, 'gx', 0, 0).reshape(256, 256)  6.31 us
    ppermute x3, waiting for transfers between devices, halo(): lax.ppermute(low_edge, axis, backward)  5.74 us
    unnamed x21, local copies, waits for them, and re-layouts  1.88 us
  transfers between devices with their start and end apart: 8, of which 5 were waited for; matrix products, arithmetic and copies ran while one was open for 2% of the time, Pallas kernels for 14%

profile of v1, /device:TPU:2, one launch (start us, length us, event | category | flops | bytes accessed | tf_op | source)
XLA Modules:
  0.0 76.7 jit_solution(3189054641318059855)
XLA Ops:
  0.0 1.1 %fusion = (bf16[20,10,128]{2,1,0:T(8,128)(2,1)S(1)}, bf16[20,10,128]{2,1,0:T(8,128)(2,1)S(1)}) fusion(bf16[20,20,128]{2,1,0:T(8,128)(2,1)} %blk_ref.3), kind=kLoop, calls=%fused_computation.3 | loop fusion | bytes 204800 | tf_op jit(solution)/shard_map/slice | solution.py:395
  1.1 3.5 %collective-permute-start = (bf16[20,10,128]{2,1,0:T(8,128)(2,1)S(1)}, bf16[20,10,128]{2,1,0:T(8,128)(2,1)S(1)}, u32[]{:S(2)}, u32[]{:S(2)}) collective-permute-start(bf16[20,10,128]{2,1,0:T(8,128)(2,1)S(1)} %get-tuple-element.20), channel_id=1, source_target_pairs={{0,1},{1,2},{2,3},{3,4},{4,5},{5,6},{6,7},{8,9},{9,10},{10,11},{11... | collective-permute-start | bytes 153608 | tf_op jit(solution)/shard_map/ppermute | solution.py:382
  4.6 4.5 %collective-permute-start.1 = (bf16[20,10,128]{2,1,0:T(8,128)(2,1)S(1)}, bf16[20,10,128]{2,1,0:T(8,128)(2,1)S(1)}, u32[]{:S(2)}, u32[]{:S(2)}) collective-permute-start(bf16[20,10,128]{2,1,0:T(8,128)(2,1)S(1)} %get-tuple-element.19), channel_id=1, source_target_pairs={{1,0},{2,1},{3,2},{4,3},{5,4},{6,5},{7,6},{9,8},{10,9},{11,10},{12... | collective-permute-start | bytes 153608 | tf_op jit(solution)/shard_map/ppermute | solution.py:382
  9.0 0.5 collective-permute-done.ylo_ref
  9.5 1.6 %collective-permute-done.1.yhi_ref = bf16[20,10,128]{2,1,0:T(8,128)(2,1)S(1)} collective-permute-done((bf16[20,10,128]{2,1,0:T(8,128)(2,1)S(1)}, bf16[20,10,128]{2,1,0:T(8,128)(2,1)S(1)}, u32[]{:S(2)}, u32[]{:S(2)}) %collective-permute-start.1) | collective-permute-done | bytes 51232 | tf_op jit(solution)/shard_map/ppermute | solution.py:382
  11.1 1.3 %collective-permute-start.2 = (bf16[10,40,128]{2,1,0:T(8,128)(2,1)S(1)}, bf16[10,40,128]{2,1,0:T(8,128)(2,1)S(1)}, u32[]{:S(2)}, u32[]{:S(2)}) collective-permute-start(bf16[10,40,128]{2,1,0:T(8,128)(2,1)S(1)} %get-tuple-element.12), channel_id=1, source_target_pairs={{0,8},{8,16},{16,24},{24,32},{32,40},{40,48},{48,56},{56,64},{64,7... | collective-permute-start | bytes 307208 | tf_op jit(solution)/shard_map/ppermute | solution.py:382
  12.4 1.3 %collective-permute-start.3 = (bf16[10,40,128]{2,1,0:T(8,128)(2,1)S(1)}, bf16[10,40,128]{2,1,0:T(8,128)(2,1)S(1)}, u32[]{:S(2)}, u32[]{:S(2)}) collective-permute-start(bf16[10,40,128]{2,1,0:T(8,128)(2,1)S(1)} %get-tuple-element.13), channel_id=1, source_target_pairs={{8,0},{16,8},{24,16},{32,24},{40,32},{48,40},{56,48},{64,56},{72,6... | collective-permute-start | bytes 307208 | tf_op jit(solution)/shard_map/ppermute | solution.py:382
  13.8 4.2 %collective-permute-done.3.xhi_ref = bf16[10,40,128]{2,1,0:T(8,128)(2,1)S(1)} collective-permute-done((bf16[10,40,128]{2,1,0:T(8,128)(2,1)S(1)}, bf16[10,40,128]{2,1,0:T(8,128)(2,1)S(1)}, u32[]{:S(2)}, u32[]{:S(2)}) %collective-permute-start.3) | collective-permute-done | bytes 102432 | tf_op jit(solution)/shard_map/ppermute | solution.py:382
  18.0 2.1 %restrict.1 = (f32[2,20,48,128]{3,2,1,0:T(8,128)S(1)}, bf16[5,8,128]{2,1,0:T(8,128)(2,1)S(1)}, bf16[5,9,128]{2,1,0:T(8,128)(2,1)S(1)}, bf16[5,16,128]{2,1,0:T(8,128)(2,1)S(1)}, f32[32,8,256]{2,1,0:T(8,128)}) custom-call(s32[2]{0:T(128)S(1)} %pad_add_fusion.where_ref, bf16[20,20,128]{2,1,0:T(8,128)(2,1)S(1)} %copy-done, ...), custom_call_target="tpu_custom_call" | custom-call | bytes 65536 | tf_op jit(solution)/shard_map/restrict/pallas_call | solution.py:75
  20.1 1.0 %copy-done.4 = f32[2,20,48,128]{3,2,1,0:T(8,128)} copy-done((f32[2,20,48,128]{3,2,1,0:T(8,128)}, f32[2,20,48,128]{3,2,1,0:T(8,128)S(1)}, u32[]{:S(2)}) %copy-start.4) | copy-done | bytes 983064
  21.1 16.3 %all-to-all-start = ((f32[32,8,256]{2,1,0:T(8,128)}), f32[32,8,256]{2,1,0:T(8,128)S(1)}, u32[]{:S(2)}, u32[]{:S(2)}) async-start(f32[32,8,256]{2,1,0:T(8,128)} %get-tuple-element.14), calls=%async_computation | async-start | bytes 524288 | tf_op jit(solution)/shard_map/all_to_all | solution.py:424
  37.4 0.5 copy.8
  38.1 0.4 copy-done.9
  38.6 0.3 convolution_bitcast_fusion.1.v_ref.near_ref
  38.9 1.4 %collective-permute-start.5 = (bf16[5,9,128]{2,1,0:T(8,128)(2,1)S(1)}, bf16[5,9,128]{2,1,0:T(8,128)(2,1)S(1)}, u32[]{:S(2)}, u32[]{:S(2)}) collective-permute-start(bf16[5,9,128]{2,1,0:T(8,128)(2,1)S(1)} %get-tuple-element.17), channel_id=1, source_target_pairs={{8,0},{16,8},{24,16},{32,24},{40,32},{48,40},{56,48},{64,56},{72,6... | collective-permute-start | bytes 34568 | tf_op jit(solution)/shard_map/ppermute | solution.py:382
  40.3 3.0 %collective-permute-start.4 = (bf16[5,8,128]{2,1,0:T(8,128)(2,1)S(1)}, bf16[5,8,128]{2,1,0:T(8,128)(2,1)S(1)}, u32[]{:S(2)}, u32[]{:S(2)}) collective-permute-start(bf16[5,8,128]{2,1,0:T(8,128)(2,1)S(1)} %get-tuple-element.16), channel_id=1, source_target_pairs={{0,8},{8,16},{16,24},{24,32},{32,40},{40,48},{48,56},{56,64},{64,7... | collective-permute-start | bytes 30728 | tf_op jit(solution)/shard_map/ppermute | solution.py:382
  43.4 0.3 convolution_bitcast_fusion.far_ref
  43.7 0.5 collective-permute-done.4.lo_ref
  44.2 6.3 %all-to-all-done = f32[32,8,256]{2,1,0:T(8,128)S(1)} async-done(((f32[32,8,256]{2,1,0:T(8,128)}), f32[32,8,256]{2,1,0:T(8,128)S(1)}, u32[]{:S(2)}, u32[]{:S(2)}) %all-to-all-start) | async-done | bytes 262176 | tf_op jit(solution)/shard_map/all_to_all | solution.py:424
  50.5 1.6 %spread.1 = bf16[8,240,128]{2,1,0:T(8,128)(2,1)} custom-call(s32[2]{0:T(128)S(1)} %pad_add_fusion.where_ref, f32[256,256]{1,0:T(8,128)S(1)} %bitcast.13, f32[2,328,128]{2,1,0:T(8,128)S(1)} %copy-done.2, bf16[5,16,128]{2,1,0:T(8,128)(2,1)S(1)} %get-tuple-element.15.own_ref, bf16[5,8,128]{2,1,0:T(8,128)(2,1)S(1)} %collective-permute-done.4.lo_ref, ...), custom_call_target="tpu_custom_call" | custom-call | bytes 65536 | tf_op jit(solution)/shard_map/spread/pallas_call | solution.py:75
  52.1 6.5 %all-to-all-start.1 = ((bf16[8,240,128]{2,1,0:T(8,128)(2,1)}), bf16[8,240,128]{2,1,0:T(8,128)(2,1)S(1)}, u32[]{:S(2)}, u32[]{:S(2)}) async-start(bf16[8,240,128]{2,1,0:T(8,128)(2,1)} %spread.1), calls=%async_computation.1 | async-start | bytes 983040 | tf_op jit(solution)/shard_map/all_to_all | solution.py:434
  58.6 5.8 %fine_sum.2.refs_0_ = f32[240,256]{1,0:T(8,128)S(1)} custom-call(f32[2,20,48,128]{3,2,1,0:T(8,128)S(1)} %copy-done.5, f32[882,128]{1,0:T(8,128)S(1)} %convolution_bitcast_fusion.1.v_ref.near_ref), custom_call_target="tpu_custom_call" | custom-call | flops 3806330880 | bytes 65536 | tf_op jit(solution)/shard_map/fine_sum/pallas_call | solution.py:75
  64.4 5.2 %fine_sum.3.fine_ref = f32[240,256]{1,0:T(8,128)S(1)} custom-call(f32[2,20,48,128]{3,2,1,0:T(8,128)S(1)} %copy-done.6, f32[882,128]{1,0:T(8,128)S(1)} %convolution_bitcast_fusion.1.v_ref.near_ref, f32[240,256]{1,0:T(8,128)S(1)} %fine_sum.2.refs_0_), custom_call_target="tpu_custom_call" | custom-call | flops 3460300800 | bytes 65536 | tf_op jit(solution)/shard_map/fine_sum/pallas_call | solution.py:75
  69.6 7.1 %final.1 = f32[20,20,128]{2,1,0:T(8,128)} custom-call(s32[2]{0:T(128)S(1)} %pad_add_fusion.where_ref, bf16[8,240,128]{2,1,0:T(8,128)(2,1)S(1)} %all-to-all-done.1.recv_ref, f32[16,88,128]{2,1,0:T(8,128)S(1)} %copy-done.1, f32[512,128]{1,0:T(8,128)S(1)} %copy-done.3, f32[882,128]{1,0:T(8,128)S(1)} %convolution_bitcast_fusion.1.v_ref.near_ref, ...), custom_call_target="tpu_custom_call" | custom-call | bytes 65536 | tf_op jit(solution)/shard_map/final/pallas_call | solution.py:75
  (24 shorter events, 0.5 us)
Async XLA Ops:
  0.0 11.1 %copy-start = (bf16[20,20,128]{2,1,0:T(8,128)(2,1)S(1)}, bf16[20,20,128]{2,1,0:T(8,128)(2,1)}, u32[]{:S(2)}) copy-start(bf16[20,20,128]{2,1,0:T(8,128)(2,1)} %blk_ref.3) | copy-start | bytes 307204
  1.1 8.4 %collective-permute-start = (bf16[20,10,128]{2,1,0:T(8,128)(2,1)S(1)}, bf16[20,10,128]{2,1,0:T(8,128)(2,1)S(1)}, u32[]{:S(2)}, u32[]{:S(2)}) collective-permute-start(bf16[20,10,128]{2,1,0:T(8,128)(2,1)S(1)} %get-tuple-element.20), channel_id=1, source_target_pairs={{0,1},{1,2},{2,3},{3,4},{4,5},{5,6},{6,7},{8,9},{9,10},{10,11},{11... | collective-permute-start | bytes 153608 | tf_op jit(solution)/shard_map/ppermute | solution.py:382
  4.6 6.5 %collective-permute-start.1 = (bf16[20,10,128]{2,1,0:T(8,128)(2,1)S(1)}, bf16[20,10,128]{2,1,0:T(8,128)(2,1)S(1)}, u32[]{:S(2)}, u32[]{:S(2)}) collective-permute-start(bf16[20,10,128]{2,1,0:T(8,128)(2,1)S(1)} %get-tuple-element.19), channel_id=1, source_target_pairs={{1,0},{2,1},{3,2},{4,3},{5,4},{6,5},{7,6},{9,8},{10,9},{11,10},{12... | collective-permute-start | bytes 153608 | tf_op jit(solution)/shard_map/ppermute | solution.py:382
  11.1 2.7 %collective-permute-start.2 = (bf16[10,40,128]{2,1,0:T(8,128)(2,1)S(1)}, bf16[10,40,128]{2,1,0:T(8,128)(2,1)S(1)}, u32[]{:S(2)}, u32[]{:S(2)}) collective-permute-start(bf16[10,40,128]{2,1,0:T(8,128)(2,1)S(1)} %get-tuple-element.12), channel_id=1, source_target_pairs={{0,8},{8,16},{16,24},{24,32},{32,40},{40,48},{48,56},{56,64},{64,7... | collective-permute-start | bytes 307208 | tf_op jit(solution)/shard_map/ppermute | solution.py:382
  12.4 5.6 %collective-permute-start.3 = (bf16[10,40,128]{2,1,0:T(8,128)(2,1)S(1)}, bf16[10,40,128]{2,1,0:T(8,128)(2,1)S(1)}, u32[]{:S(2)}, u32[]{:S(2)}) collective-permute-start(bf16[10,40,128]{2,1,0:T(8,128)(2,1)S(1)} %get-tuple-element.13), channel_id=1, source_target_pairs={{8,0},{16,8},{24,16},{32,24},{40,32},{48,40},{56,48},{64,56},{72,6... | collective-permute-start | bytes 307208 | tf_op jit(solution)/shard_map/ppermute | solution.py:382
  20.1 1.0 %copy-start.4 = (f32[2,20,48,128]{3,2,1,0:T(8,128)}, f32[2,20,48,128]{3,2,1,0:T(8,128)S(1)}, u32[]{:S(2)}) copy-start(f32[2,20,48,128]{3,2,1,0:T(8,128)S(1)} %get-tuple-element.18.d_ref) | copy-start | bytes 2949124
  21.1 16.3 %copy-start.7 = (bf16[2,21,21,21]{3,0,2,1:T(2,128)(2,1)S(1)}, bf16[2,21,21,21]{3,0,2,1:T(2,128)(2,1)}, u32[]{:S(2)}) copy-start(bf16[2,21,21,21]{3,0,2,1:T(2,128)(2,1)} %param.8) | copy-start | bytes 111136
  21.1 29.4 %all-to-all-start = ((f32[32,8,256]{2,1,0:T(8,128)}), f32[32,8,256]{2,1,0:T(8,128)S(1)}, u32[]{:S(2)}, u32[]{:S(2)}) async-start(f32[32,8,256]{2,1,0:T(8,128)} %get-tuple-element.14), calls=%async_computation | async-start | bytes 524288 | tf_op jit(solution)/shard_map/all_to_all | solution.py:424
  37.9 0.7 copy-start.9
  38.6 4.8 %copy-start.8 = (bf16[21,128]{1,0:T(8,128)(2,1)S(1)}, bf16[21,128]{1,0:T(8,128)(2,1)}, u32[]{:S(2)}) copy-start(bf16[21,128]{1,0:T(8,128)(2,1)} %constant.20.clone) | copy-start | bytes 16132
  38.9 11.6 %copy-start.2 = (f32[2,328,128]{2,1,0:T(8,128)S(1)}, f32[2,328,128]{2,1,0:T(8,128)}, u32[]{:S(2)}) copy-start(f32[2,328,128]{2,1,0:T(8,128)} %constant.21.clone.mx_ref) | copy-start | bytes 1007620
  38.9 5.3 %collective-permute-start.5 = (bf16[5,9,128]{2,1,0:T(8,128)(2,1)S(1)}, bf16[5,9,128]{2,1,0:T(8,128)(2,1)S(1)}, u32[]{:S(2)}, u32[]{:S(2)}) collective-permute-start(bf16[5,9,128]{2,1,0:T(8,128)(2,1)S(1)} %get-tuple-element.17), channel_id=1, source_target_pairs={{8,0},{16,8},{24,16},{32,24},{40,32},{48,40},{56,48},{64,56},{72,6... | collective-permute-start | bytes 34568 | tf_op jit(solution)/shard_map/ppermute | solution.py:382
  40.3 3.9 %collective-permute-start.4 = (bf16[5,8,128]{2,1,0:T(8,128)(2,1)S(1)}, bf16[5,8,128]{2,1,0:T(8,128)(2,1)S(1)}, u32[]{:S(2)}, u32[]{:S(2)}) collective-permute-start(bf16[5,8,128]{2,1,0:T(8,128)(2,1)S(1)} %get-tuple-element.16), channel_id=1, source_target_pairs={{0,8},{8,16},{16,24},{24,32},{32,40},{40,48},{48,56},{56,64},{64,7... | collective-permute-start | bytes 30728 | tf_op jit(solution)/shard_map/ppermute | solution.py:382
  52.1 6.5 %copy-start.5 = (f32[2,20,48,128]{3,2,1,0:T(8,128)S(1)}, f32[2,20,48,128]{3,2,1,0:T(8,128)}, u32[]{:S(2)}) copy-start(f32[2,20,48,128]{3,2,1,0:T(8,128)} %copy-done.4) | copy-start | bytes 2949124
  52.1 17.4 %all-to-all-start.1 = ((bf16[8,240,128]{2,1,0:T(8,128)(2,1)}), bf16[8,240,128]{2,1,0:T(8,128)(2,1)S(1)}, u32[]{:S(2)}, u32[]{:S(2)}) async-start(bf16[8,240,128]{2,1,0:T(8,128)(2,1)} %spread.1), calls=%async_computation.1 | async-start | bytes 983040 | tf_op jit(solution)/shard_map/all_to_all | solution.py:434
  58.6 5.8 %copy-start.6 = (f32[2,20,48,128]{3,2,1,0:T(8,128)S(1)}, f32[2,20,48,128]{3,2,1,0:T(8,128)}, u32[]{:S(2)}) copy-start(f32[2,20,48,128]{3,2,1,0:T(8,128)} %copy-done.4) | copy-start | bytes 2949124
  64.4 5.2 %copy-start.1 = (f32[16,88,128]{2,1,0:T(8,128)S(1)}, f32[16,88,128]{2,1,0:T(8,128)}, u32[]{:S(2)}) copy-start(f32[16,88,128]{2,1,0:T(8,128)} %constant.22.clone.my_ref) | copy-start | bytes 2162692
  64.4 5.2 %copy-start.3 = (f32[512,128]{1,0:T(8,128)S(1)}, f32[512,128]{1,0:T(8,128)}, u32[]{:S(2)}) copy-start(f32[512,128]{1,0:T(8,128)} %constant.23.clone.mz_ref) | copy-start | bytes 786436

commit v2 on v1

--- a/solution.py
+++ b/solution.py
@@ -13,6 +13,7 @@
 HIGHEST = lax.Precision.HIGHEST
 REACH = 10
 TAPS = 21
+SPLIT = 15
 
 
 def weight_np(offset):
@@ -94,8 +95,8 @@
 
 def restrict_kernel(
     where_ref, blk_ref, ylo_ref, yhi_ref, xlo_ref, xhi_ref,
-    d_ref, right_ref, left_ref, own_ref, coarse_ref,
-    planes, cells, mid, row,
+    d_ref, out_ref,
+    planes, cells, mid, pay,
 ):
     for x in range(40):
         p, i = x % 2, x // 2
@@ -144,10 +145,9 @@
     for n in range(9):
         mid[n, 0:16, :] = value[16 * n : 16 * n + 16]
         mid[n, 16:24, :] = jnp.zeros((8, 128), f32)
+    pay[48:56, :] = jnp.zeros((8, 128), f32)
     for n in range(5):
-        own_ref[n] = value[16 * n + 32 : 16 * n + 48].astype(bf16)
-        right_ref[n] = mid[n + 2, 2:10, :].astype(bf16)
-        left_ref[n] = mid[n + 2, 6:15, :].astype(bf16)
+        pay[10 * n : 10 * n + 10, :] = mid[n + 2, 3:13, :]
 
     lane = lax.broadcasted_iota(jnp.int32, (1, 128), 1)
     odd = lane >= 64
@@ -156,7 +156,6 @@
     weight_3 = jnp.where(odd, -0.0625, 0.0)
     r, c = iota2((128, 32))
     down_z = weight(r % 64 - 2 * c)
-    row[...] = jnp.zeros((8, 256), f32)
     sums = []
     for y in range(5):
         n = y + 2
@@ -170,10 +169,18 @@
     out = jnp.dot(
         jnp.concatenate(sums, axis=0), down_z, precision=HIGHEST, preferred_element_type=f32
     )
-    for y in range(5):
-        row[:, 32 * y : 32 * y + 32] = out[8 * y : 8 * y + 8]
-    for k in range(coarse_ref.shape[0]):
-        coarse_ref[k] = row[...]
+    wide = jnp.concatenate([out[8 * y : 8 * y + 8] for y in range(4)], axis=1)
+    last = out[32:40]
+    high = wide.astype(bf16).astype(f32)
+    last_high = last.astype(bf16).astype(f32)
+    pay[56:64, :] = jnp.concatenate(
+        [last_high, last - last_high, jnp.zeros((8, 64), f32)], axis=1
+    )
+    pay[64:72, :] = high
+    pay[72:80, :] = wide - high
+    packed = pay[...].astype(bf16)
+    for k in range(out_ref.shape[0]):
+        out_ref[k] = packed
 
 
 def fine_kernel(lo, hi, first, d_ref, v_ref, *refs):
@@ -238,14 +245,25 @@
     )
 
 
-def spread_kernel(where_ref, coarse_ref, mx_ref, own_ref, lo_ref, hi_ref, out_ref, buf):
-    start = 10 * where_ref[0]
+def spread_kernel(where_ref, recv_ref, mx_ref, out_ref, buf, line):
+    index_x = where_ref[0]
+    count = recv_ref.shape[0]
+    start = 10 * index_x
     rows = jnp.concatenate([mx_ref[h, pl.ds(start, 16), :] for h in range(2)], axis=1)
-    part = jnp.dot(rows, coarse_ref[...], precision=HIGHEST, preferred_element_type=f32)
-    for n in range(5):
-        buf[33 * n : 33 * n + 8, :] = lo_ref[n].astype(f32)
-        buf[33 * n + 8 : 33 * n + 24, :] = own_ref[n].astype(f32)
-        buf[33 * n + 24 : 33 * n + 33, :] = hi_ref[n].astype(f32)
+    coarse = recv_ref[:, 48:80, :].astype(f32)
+    last = coarse[:, 8:16, :].reshape(8 * count, 128)
+    wide = (coarse[:, 16:24, :] + coarse[:, 24:32, :]).reshape(8 * count, 128)
+    wide = jnp.dot(rows, wide, precision=HIGHEST, preferred_element_type=f32)
+    last = jnp.dot(rows, last, precision=HIGHEST, preferred_element_type=f32)
+    last = last[:, 0:32] + last[:, 32:64]
+    part = jnp.concatenate([wide, last, jnp.zeros((16, 96), f32)], axis=1)
+    for step, first, size, at in ((-2, 9, 1, 0), (-1, 0, 10, 1), (0, 0, 10, 11), (1, 0, 10, 21), (2, 0, 2, 31)):
+        source = index_x + step
+        inside = (source >= 0) & (source < count)
+        got = recv_ref[jnp.clip(source, 0, count - 1), 0:64, :].astype(f32)
+        line[...] = jnp.where(inside, got, 0.0)
+        for n in range(5):
+            buf[33 * n + at : 33 * n + at + size, :] = line[10 * n + first : 10 * n + first + size, :]
     buf[165:176, :] = jnp.zeros((11, 128), f32)
     high = part.astype(bf16)
     low = (part - high.astype(f32)).astype(bf16)
@@ -265,7 +283,7 @@
     index_x = where_ref[0]
     index_y = where_ref[1]
     count = recv_ref.shape[0]
-    cells[:, 32:40, :] = jnp.zeros((18, 8, 128), f32)
+    cells[:, 32:40, :] = jnp.zeros((17, 8, 128), f32)
     for step in range(-2, 3):
         source = index_y + step
         inside = (source >= 0) & (source < count)
@@ -273,15 +291,11 @@
         line[...] = jnp.where(inside, got, 0.0)
         for p in range(5):
             n = 5 * step + 6 + p
-            if 0 <= n < 18:
+            if 0 <= n < 17:
                 cells[n, 0:33, :] = line[33 * p : 33 * p + 33, :]
 
     r, c = iota2((128, 128))
     mask = jnp.abs(r % 64 - c % 64) <= REACH
-    zero = jnp.zeros((128, 128), bf16)
-    for w in (w0, w1):
-        w[0:128, 128:256] = zero
-        w[1408:1536, 0:128] = zero
 
     def build(w, a):
         base = TAPS * TAPS + a * TAPS
@@ -296,17 +310,16 @@
             upper = pltpu.roll(jnp.broadcast_to(upper, (64, 128)), 0, 1, stride=1, stride_axis=0)
             lower = pltpu.roll(jnp.broadcast_to(lower, (64, 128)), 64, 1, stride=1, stride_axis=0)
             band = jnp.where(mask, jnp.concatenate([upper, lower], axis=0), 0.0).astype(bf16)
-            w[128 * j : 128 * j + 128, 0:128] = band
-            w[128 * j + 128 : 128 * j + 256, 128:256] = band
+            w[128 * j : 128 * j + 128, :] = band
 
     def dot(w, a):
-        part = [cells[n, pl.ds(a, 16), :].astype(bf16) for n in range(18)]
+        part = [cells[n, pl.ds(a, 16), :].astype(bf16) for n in range(17)]
         lhs = jnp.concatenate(
-            [jnp.concatenate(part[2 * g : 2 * g + 12], axis=1) for g in range(4)], axis=0
+            [jnp.concatenate(part[g : g + 11], axis=1) for g in range(7)], axis=0
         )
         acc[...] += jnp.dot(lhs, w[...], preferred_element_type=f32)
 
-    acc[...] = jnp.zeros((64, 256), f32)
+    acc[...] = jnp.zeros((112, 128), f32)
     build(w0, 0)
 
     def step(t, _):
@@ -321,29 +334,25 @@
     dot(w0, TAPS - 1)
 
     start = 10 * index_y
-    sums = [[None] * 16, [None] * 16]
+    sums = [[None] * 14, [None] * 14]
     for k in range(count):
         high = [recv_ref[k, 176 + 16 * h : 192 + 16 * h, :].astype(f32) for h in range(2)]
         low = [recv_ref[k, 208 + 16 * h : 224 + 16 * h, :].astype(f32) for h in range(2)]
         for h in range(2):
             value = high[h] + low[h]
             rows_y = my_ref[2 * k + h, pl.ds(start, 16), :]
-            for y in range(16):
+            for y in range(14):
                 term = value * rows_y[y : y + 1, :]
                 sums[h][y] = term if k == 0 else sums[h][y] + term
     rows = [
         jnp.concatenate([sums[h][2 * n + p] for p in range(2) for h in range(2)], axis=1)
-        for n in range(8)
+        for n in range(7)
     ]
     top = jnp.dot(
         jnp.concatenate(rows, axis=0), mz_ref[...], precision=HIGHEST, preferred_element_type=f32
     )
-    both = []
-    for n in range(8):
-        g, u = n // 2, n % 2
-        both.append(acc[16 * g : 16 * g + 16, 128 * u : 128 * u + 128])
-    total = jnp.concatenate(both, axis=0) + top
-    r, c = iota2((128, 128))
+    total = acc[...] + top
+    r, c = iota2((112, 128))
     cell_x = 10 * index_x - 1 + r % 16
     cell_y = 10 * index_y - 2 + 2 * (r // 16) + c // 64
     inside = (cell_x >= 0) & (cell_x < 320) & (cell_y >= 0) & (cell_y < 80)
@@ -393,6 +402,7 @@
         for m in spots_np()
     )
     y_lo, y_hi = halo(charges[:, :10], charges[:, 10:], "gy")
+    y_lo, y_hi, near, far = lax.optimization_barrier((y_lo, y_hi, near, far))
     edge_lo, edge_hi = vmem_call(
         rim_kernel,
         [shape((10, 40, 128), bf16)] * 2,
@@ -401,48 +411,42 @@
         (charges, y_lo, y_hi),
     )
     x_lo, x_hi = halo(edge_lo, edge_hi, "gx")
-    d, right, left, own, coarse = vmem_call(
+    d, blocks = vmem_call(
         restrict_kernel,
-        [
-            shape((2, 20, 48, 128), f32),
-            shape((5, 8, 128), bf16),
-            shape((5, 9, 128), bf16),
-            shape((5, 16, 128), bf16),
-            shape((count_x, 8, 256), f32),
-        ],
+        [shape((2, 20, 48, 128), f32), shape((count_x, 80, 128), bf16)],
         [
             pltpu.VMEM((16, 48, 128), f32),
             pltpu.VMEM((256, 128), f32),
             pltpu.VMEM((9, 24, 128), f32),
-            pltpu.VMEM((8, 256), f32),
+            pltpu.VMEM((80, 128), f32),
         ],
         "restrict",
         (where, charges, y_lo, y_hi, x_lo, x_hi),
         smem=1,
     )
-    mid_lo, mid_hi = halo(left, right, "gx")
-    coarse = lax.all_to_all(coarse, "gx", 0, 0).reshape(256, 256)
-    fine = fine_sum(0, 11, d, near)
+    blocks = lax.all_to_all(blocks, "gx", 0, 0)
+    fine = fine_sum(0, SPLIT, d, near)
+    blocks, fine = lax.optimization_barrier((blocks, fine))
     parts = vmem_call(
         spread_kernel,
         shape((count_y, 240, 128), bf16),
-        [pltpu.VMEM((176, 128), f32)],
+        [pltpu.VMEM((176, 128), f32), pltpu.VMEM((64, 128), f32)],
         "spread",
-        (where, coarse, jnp.asarray(matrix_x_np(spread)), own, mid_lo, mid_hi),
+        (where, blocks, jnp.asarray(matrix_x_np(spread))),
         smem=1,
     )
     parts = lax.all_to_all(parts, "gy", 0, 0)
-    fine = fine_sum(11, 21, d, near, fine)
+    fine = fine_sum(SPLIT, TAPS, d, near, fine)
     return vmem_call(
         final_kernel,
         shape((20, 20, 128), f32),
         [
-            pltpu.VMEM((18, 40, 128), f32),
-            pltpu.VMEM((1536, 256), bf16),
-            pltpu.VMEM((1536, 256), bf16),
-            pltpu.VMEM((64, 256), f32),
+            pltpu.VMEM((17, 40, 128), f32),
+            pltpu.VMEM((1408, 128), bf16),
+            pltpu.VMEM((1408, 128), bf16),
+            pltpu.VMEM((112, 128), f32),
             pltpu.VMEM((320, 128), f32),
-            pltpu.VMEM((128, 256), f32),
+            pltpu.VMEM((112, 256), f32),
             pltpu.VMEM((176, 128), f32),
         ],
         "final",

time: 77.6 us -> 82.7 us (1.066)
  the two profiles are of different devices: /device:TPU:2 before, /device:TPU:4 now
where the time goes in v2:
time: 82.7 us; the launch traced here: 82.2 us
  starting transfers between devices  35 us (42%)
  Pallas kernels  21.1 us (26%)
  waiting for transfers between devices  18.7 us (23%)
  local copies, waits for them, and re-layouts  6.42 us (8%)
    pallas_call x6, Pallas kernels, vmem_call(): pl.pallas_call(body, out_shape=out_shape, in_specs=specs, out_specs=jax.t...  21.1 us
    all_to_all x1, starting transfers between devices, per_device(): blocks = lax.all_to_all(blocks, 'gx', 0, 0)  14 us
    all_to_all x1, waiting for transfers between devices, per_device(): blocks = lax.all_to_all(blocks, 'gx', 0, 0)  11.7 us
    all_to_all x1, starting transfers between devices, per_device(): parts = lax.all_to_all(parts, 'gy', 0, 0)  8.11 us
    ppermute x2, starting transfers between devices, halo(): lax.ppermute(high_edge, axis, forward)  6.47 us
    ppermute x2, starting transfers between devices, halo(): lax.ppermute(low_edge, axis, backward)  6.44 us
    unnamed x21, local copies, waits for them, and re-layouts  5.16 us
    all_to_all x1, waiting for transfers between devices, per_device(): parts = lax.all_to_all(parts, 'gy', 0, 0)  4.85 us
  transfers between devices with their start and end apart: 6, of which 4 were waited for; matrix products, arithmetic and copies ran while one was open for 2% of the time, Pallas kernels for 13%

profile of v2, /device:TPU:4, one launch (start us, length us, event | category | flops | bytes accessed | tf_op | source)
XLA Modules:
  0.0 82.2 jit_solution(15609240031348686907)
XLA Ops:
  0.0 1.0 %fusion = (bf16[20,10,128]{2,1,0:T(8,128)(2,1)S(1)}, bf16[20,10,128]{2,1,0:T(8,128)(2,1)S(1)}) fusion(bf16[20,20,128]{2,1,0:T(8,128)(2,1)} %blk_ref.3), kind=kLoop, calls=%fused_computation.3 | loop fusion | bytes 204800 | tf_op jit(solution)/shard_map/slice | solution.py:404
  1.0 1.3 %collective-permute-start.1 = (bf16[20,10,128]{2,1,0:T(8,128)(2,1)S(1)}, bf16[20,10,128]{2,1,0:T(8,128)(2,1)S(1)}, u32[]{:S(2)}, u32[]{:S(2)}) collective-permute-start(bf16[20,10,128]{2,1,0:T(8,128)(2,1)S(1)} %get-tuple-element.25), channel_id=1, source_target_pairs={{1,0},{2,1},{3,2},{4,3},{5,4},{6,5},{7,6},{9,8},{10,9},{11,10},{12... | collective-permute-start | bytes 153608 | tf_op jit(solution)/shard_map/ppermute | solution.py:391
  2.3 4.6 %collective-permute-start = (bf16[20,10,128]{2,1,0:T(8,128)(2,1)S(1)}, bf16[20,10,128]{2,1,0:T(8,128)(2,1)S(1)}, u32[]{:S(2)}, u32[]{:S(2)}) collective-permute-start(bf16[20,10,128]{2,1,0:T(8,128)(2,1)S(1)} %get-tuple-element.26), channel_id=1, source_target_pairs={{0,1},{1,2},{2,3},{3,4},{4,5},{5,6},{6,7},{8,9},{9,10},{10,11},{11... | collective-permute-start | bytes 153608 | tf_op jit(solution)/shard_map/ppermute | solution.py:391
  6.9 0.5 copy.8
  7.6 0.4 copy-done.8
  8.3 0.4 copy-done.9
  8.7 0.3 convolution_bitcast_fusion.1.v_ref.near_ref
  9.1 0.6 copy-done
  9.7 1.9 %collective-permute-start.2 = (bf16[10,40,128]{2,1,0:T(8,128)(2,1)S(1)}, bf16[10,40,128]{2,1,0:T(8,128)(2,1)S(1)}, u32[]{:S(2)}, u32[]{:S(2)}) collective-permute-start(bf16[10,40,128]{2,1,0:T(8,128)(2,1)S(1)} %get-tuple-element.17), channel_id=1, source_target_pairs={{0,8},{8,16},{16,24},{24,32},{32,40},{40,48},{48,56},{56,64},{64,7... | collective-permute-start | bytes 307208 | tf_op jit(solution)/shard_map/ppermute | solution.py:391
  11.6 5.1 %collective-permute-start.3 = (bf16[10,40,128]{2,1,0:T(8,128)(2,1)S(1)}, bf16[10,40,128]{2,1,0:T(8,128)(2,1)S(1)}, u32[]{:S(2)}, u32[]{:S(2)}) collective-permute-start(bf16[10,40,128]{2,1,0:T(8,128)(2,1)S(1)} %get-tuple-element.18), channel_id=1, source_target_pairs={{8,0},{16,8},{24,16},{32,24},{40,32},{48,40},{56,48},{64,56},{72,6... | collective-permute-start | bytes 307208 | tf_op jit(solution)/shard_map/ppermute | solution.py:391
  16.8 0.3 collective-permute-done.2.xlo_ref
  17.2 1.8 %collective-permute-done.3.xhi_ref = bf16[10,40,128]{2,1,0:T(8,128)(2,1)S(1)} collective-permute-done((bf16[10,40,128]{2,1,0:T(8,128)(2,1)S(1)}, bf16[10,40,128]{2,1,0:T(8,128)(2,1)S(1)}, u32[]{:S(2)}, u32[]{:S(2)}) %collective-permute-start.3) | collective-permute-done | bytes 102432 | tf_op jit(solution)/shard_map/ppermute | solution.py:391
  19.0 2.3 %restrict.1 = (f32[2,20,48,128]{3,2,1,0:T(8,128)S(1)}, bf16[32,80,128]{2,1,0:T(8,128)(2,1)}) custom-call(s32[2]{0:T(128)S(1)} %pad_add_fusion.where_ref, bf16[20,20,128]{2,1,0:T(8,128)(2,1)S(1)} %copy-done, bf16[20,10,128]{2,1,0:T(8,128)(2,1)S(1)} %collective-permute-done.ylo_ref, bf16[20,10,128]{2,1,0:T(8,128)(2,1)S(1)} %collective-permute-done.1.yhi_ref, ...), custom_call_target="tpu_custom_call" | custom-call | bytes 65536 | tf_op jit(solution)/shard_map/restrict/pallas_call | solution.py:76
  21.3 1.0 %copy-done.4 = f32[2,20,48,128]{3,2,1,0:T(8,128)} copy-done((f32[2,20,48,128]{3,2,1,0:T(8,128)}, f32[2,20,48,128]{3,2,1,0:T(8,128)S(1)}, u32[]{:S(2)}) %copy-start.4) | copy-done | bytes 983064
  22.2 14.0 %all-to-all-start = ((bf16[32,80,128]{2,1,0:T(8,128)(2,1)}), bf16[32,80,128]{2,1,0:T(8,128)(2,1)S(1)}, u32[]{:S(2)}, u32[]{:S(2)}) async-start(bf16[32,80,128]{2,1,0:T(8,128)(2,1)} %get-tuple-element.19), calls=%async_computation | async-start | bytes 1310720 | tf_op jit(solution)/shard_map/all_to_all | solution.py:427
  36.3 1.2 %copy-done.5 = f32[2,20,48,128]{3,2,1,0:T(8,128)S(1)} copy-done((f32[2,20,48,128]{3,2,1,0:T(8,128)S(1)}, f32[2,20,48,128]{3,2,1,0:T(8,128)}, u32[]{:S(2)}) %copy-start.5) | copy-done | bytes 983064
  37.5 7.6 %fine_sum.2.refs_0_ = f32[240,256]{1,0:T(8,128)S(1)} custom-call(f32[2,20,48,128]{3,2,1,0:T(8,128)S(1)} %copy-done.5, f32[882,128]{1,0:T(8,128)S(1)} %convolution_bitcast_fusion.1.v_ref.near_ref), custom_call_target="tpu_custom_call" | custom-call | flops 5190451200 | bytes 65536 | tf_op jit(solution)/shard_map/fine_sum/pallas_call | solution.py:76
  45.1 11.7 %all-to-all-done.recv_ref = bf16[32,80,128]{2,1,0:T(8,128)(2,1)S(1)} async-done(((bf16[32,80,128]{2,1,0:T(8,128)(2,1)}), bf16[32,80,128]{2,1,0:T(8,128)(2,1)S(1)}, u32[]{:S(2)}, u32[]{:S(2)}) %all-to-all-start) | async-done | bytes 655392 | tf_op jit(solution)/shard_map/all_to_all | solution.py:427
  56.8 1.7 %spread.1 = bf16[8,240,128]{2,1,0:T(8,128)(2,1)} custom-call(s32[2]{0:T(128)S(1)} %pad_add_fusion.where_ref, bf16[32,80,128]{2,1,0:T(8,128)(2,1)S(1)} %all-to-all-done.recv_ref, f32[2,328,128]{2,1,0:T(8,128)S(1)} %copy-done.2), custom_call_target="tpu_custom_call" | custom-call | bytes 65536 | tf_op jit(solution)/shard_map/spread/pallas_call | solution.py:76
  58.5 8.1 %all-to-all-start.1 = ((bf16[8,240,128]{2,1,0:T(8,128)(2,1)}), bf16[8,240,128]{2,1,0:T(8,128)(2,1)S(1)}, u32[]{:S(2)}, u32[]{:S(2)}) async-start(bf16[8,240,128]{2,1,0:T(8,128)(2,1)} %spread.1), calls=%async_computation.1 | async-start | bytes 983040 | tf_op jit(solution)/shard_map/all_to_all | solution.py:438
  66.6 1.2 %copy-done.6 = f32[2,20,48,128]{3,2,1,0:T(8,128)S(1)} copy-done((f32[2,20,48,128]{3,2,1,0:T(8,128)S(1)}, f32[2,20,48,128]{3,2,1,0:T(8,128)}, u32[]{:S(2)}) %copy-start.6) | copy-done | bytes 983064
  67.8 3.2 %fine_sum.3.fine_ref = f32[240,256]{1,0:T(8,128)S(1)} custom-call(f32[2,20,48,128]{3,2,1,0:T(8,128)S(1)} %copy-done.6, f32[882,128]{1,0:T(8,128)S(1)} %convolution_bitcast_fusion.1.v_ref.near_ref, f32[240,256]{1,0:T(8,128)S(1)} %fine_sum.2.refs_0_), custom_call_target="tpu_custom_call" | custom-call | flops 2076180480 | bytes 65536 | tf_op jit(solution)/shard_map/fine_sum/pallas_call | solution.py:76
  71.0 4.8 %all-to-all-done.1.recv_ref = bf16[8,240,128]{2,1,0:T(8,128)(2,1)S(1)} async-done(((bf16[8,240,128]{2,1,0:T(8,128)(2,1)}), bf16[8,240,128]{2,1,0:T(8,128)(2,1)S(1)}, u32[]{:S(2)}, u32[]{:S(2)}) %all-to-all-start.1) | async-done | bytes 491552 | tf_op jit(solution)/shard_map/all_to_all | solution.py:438
  75.8 6.3 %final.1 = f32[20,20,128]{2,1,0:T(8,128)} custom-call(s32[2]{0:T(128)S(1)} %pad_add_fusion.where_ref, bf16[8,240,128]{2,1,0:T(8,128)(2,1)S(1)} %all-to-all-done.1.recv_ref, f32[16,88,128]{2,1,0:T(8,128)S(1)} %copy-done.1, f32[512,128]{1,0:T(8,128)S(1)} %copy-done.3, f32[882,128]{1,0:T(8,128)S(1)} %convolution_bitcast_fusion.1.v_ref.near_ref, ...), custom_call_target="tpu_custom_call" | custom-call | bytes 65536 | tf_op jit(solution)/shard_map/final/pallas_call | solution.py:76
  (20 shorter events, 0.7 us)
Async XLA Ops:
  0.0 6.9 %copy-start.7 = (bf16[2,21,21,21]{3,0,2,1:T(2,128)(2,1)S(1)}, bf16[2,21,21,21]{3,0,2,1:T(2,128)(2,1)}, u32[]{:S(2)}) copy-start(bf16[2,21,21,21]{3,0,2,1:T(2,128)(2,1)} %param.8) | copy-start | bytes 111136
  1.0 8.0 %collective-permute-start.1 = (bf16[20,10,128]{2,1,0:T(8,128)(2,1)S(1)}, bf16[20,10,128]{2,1,0:T(8,128)(2,1)S(1)}, u32[]{:S(2)}, u32[]{:S(2)}) collective-permute-start(bf16[20,10,128]{2,1,0:T(8,128)(2,1)S(1)} %get-tuple-element.25), channel_id=1, source_target_pairs={{1,0},{2,1},{3,2},{4,3},{5,4},{6,5},{7,6},{9,8},{10,9},{11,10},{12... | collective-permute-start | bytes 153608 | tf_op jit(solution)/shard_map/ppermute | solution.py:391
  2.3 6.8 %collective-permute-start = (bf16[20,10,128]{2,1,0:T(8,128)(2,1)S(1)}, bf16[20,10,128]{2,1,0:T(8,128)(2,1)S(1)}, u32[]{:S(2)}, u32[]{:S(2)}) collective-permute-start(bf16[20,10,128]{2,1,0:T(8,128)(2,1)S(1)} %get-tuple-element.26), channel_id=1, source_target_pairs={{0,1},{1,2},{2,3},{3,4},{4,5},{5,6},{6,7},{8,9},{9,10},{10,11},{11... | collective-permute-start | bytes 153608 | tf_op jit(solution)/shard_map/ppermute | solution.py:391
  7.3 0.7 copy-start.8
  8.0 0.7 copy-start.9
  8.7 0.9 %copy-start = (bf16[20,20,128]{2,1,0:T(8,128)(2,1)S(1)}, bf16[20,20,128]{2,1,0:T(8,128)(2,1)}, u32[]{:S(2)}) copy-start(bf16[20,20,128]{2,1,0:T(8,128)(2,1)} %blk_ref.3) | copy-start | bytes 307204
  9.7 7.5 %collective-permute-start.2 = (bf16[10,40,128]{2,1,0:T(8,128)(2,1)S(1)}, bf16[10,40,128]{2,1,0:T(8,128)(2,1)S(1)}, u32[]{:S(2)}, u32[]{:S(2)}) collective-permute-start(bf16[10,40,128]{2,1,0:T(8,128)(2,1)S(1)} %get-tuple-element.17), channel_id=1, source_target_pairs={{0,8},{8,16},{16,24},{24,32},{32,40},{40,48},{48,56},{56,64},{64,7... | collective-permute-start | bytes 307208 | tf_op jit(solution)/shard_map/ppermute | solution.py:391
  11.6 7.4 %collective-permute-start.3 = (bf16[10,40,128]{2,1,0:T(8,128)(2,1)S(1)}, bf16[10,40,128]{2,1,0:T(8,128)(2,1)S(1)}, u32[]{:S(2)}, u32[]{:S(2)}) collective-permute-start(bf16[10,40,128]{2,1,0:T(8,128)(2,1)S(1)} %get-tuple-element.18), channel_id=1, source_target_pairs={{8,0},{16,8},{24,16},{32,24},{40,32},{48,40},{56,48},{64,56},{72,6... | collective-permute-start | bytes 307208 | tf_op jit(solution)/shard_map/ppermute | solution.py:391
  21.3 1.0 %copy-start.4 = (f32[2,20,48,128]{3,2,1,0:T(8,128)}, f32[2,20,48,128]{3,2,1,0:T(8,128)S(1)}, u32[]{:S(2)}) copy-start(f32[2,20,48,128]{3,2,1,0:T(8,128)S(1)} %get-tuple-element.20.d_ref) | copy-start | bytes 2949124
  22.2 34.5 %all-to-all-start = ((bf16[32,80,128]{2,1,0:T(8,128)(2,1)}), bf16[32,80,128]{2,1,0:T(8,128)(2,1)S(1)}, u32[]{:S(2)}, u32[]{:S(2)}) async-start(bf16[32,80,128]{2,1,0:T(8,128)(2,1)} %get-tuple-element.19), calls=%async_computation | async-start | bytes 1310720 | tf_op jit(solution)/shard_map/all_to_all | solution.py:427
  36.2 1.2 %copy-start.5 = (f32[2,20,48,128]{3,2,1,0:T(8,128)S(1)}, f32[2,20,48,128]{3,2,1,0:T(8,128)}, u32[]{:S(2)}) copy-start(f32[2,20,48,128]{3,2,1,0:T(8,128)} %copy-done.4) | copy-start | bytes 2949124
  37.5 19.3 %copy-start.2 = (f32[2,328,128]{2,1,0:T(8,128)S(1)}, f32[2,328,128]{2,1,0:T(8,128)}, u32[]{:S(2)}) copy-start(f32[2,328,128]{2,1,0:T(8,128)} %constant.21.clone.mx_ref) | copy-start | bytes 1007620
  58.5 17.3 %all-to-all-start.1 = ((bf16[8,240,128]{2,1,0:T(8,128)(2,1)}), bf16[8,240,128]{2,1,0:T(8,128)(2,1)S(1)}, u32[]{:S(2)}, u32[]{:S(2)}) async-start(bf16[8,240,128]{2,1,0:T(8,128)(2,1)} %spread.1), calls=%async_computation.1 | async-start | bytes 983040 | tf_op jit(solution)/shard_map/all_to_all | solution.py:438
  66.6 1.2 %copy-start.6 = (f32[2,20,48,128]{3,2,1,0:T(8,128)S(1)}, f32[2,20,48,128]{3,2,1,0:T(8,128)}, u32[]{:S(2)}) copy-start(f32[2,20,48,128]{3,2,1,0:T(8,128)} %copy-done.4) | copy-start | bytes 2949124
  67.8 8.0 %copy-start.1 = (f32[16,88,128]{2,1,0:T(8,128)S(1)}, f32[16,88,128]{2,1,0:T(8,128)}, u32[]{:S(2)}) copy-start(f32[16,88,128]{2,1,0:T(8,128)} %constant.22.clone.my_ref) | copy-start | bytes 2162692
  67.8 8.0 %copy-start.3 = (f32[512,128]{1,0:T(8,128)S(1)}, f32[512,128]{1,0:T(8,128)}, u32[]{:S(2)}) copy-start(f32[512,128]{1,0:T(8,128)} %constant.23.clone.mz_ref) | copy-start | bytes 786436

commit v3 on v2

--- a/solution.py
+++ b/solution.py
@@ -13,7 +13,6 @@
 HIGHEST = lax.Precision.HIGHEST
 REACH = 10
 TAPS = 21
-SPLIT = 15
 
 
 def weight_np(offset):
@@ -70,45 +69,66 @@
     return (lax.broadcasted_iota(jnp.int32, shape, 0), lax.broadcasted_iota(jnp.int32, shape, 1))
 
 
-def vmem_call(body, out_shape, scratch, name, args, smem=0, flops=0):
-    specs = [pl.BlockSpec(memory_space=pltpu.SMEM)] * smem
-    specs += [pl.BlockSpec(memory_space=pltpu.VMEM)] * (len(args) - smem)
+def vmem_call(body, out_shape, scratch, name, args, smem=0, flops=0, hbm_in=(), hbm_out=()):
+    def spec(space):
+        return pl.BlockSpec(memory_space=space)
+
+    in_specs = [spec(pltpu.SMEM)] * smem + [spec(pltpu.VMEM)] * (len(args) - smem)
+    for k in hbm_in:
+        in_specs[k] = spec(pl.ANY)
+    out_specs = [spec(pltpu.VMEM)] * len(out_shape)
+    for k in hbm_out:
+        out_specs[k] = spec(pl.ANY)
     return pl.pallas_call(
         body,
         out_shape=out_shape,
-        in_specs=specs,
-        out_specs=jax.tree.map(lambda _: pl.BlockSpec(memory_space=pltpu.VMEM), out_shape),
+        in_specs=in_specs,
+        out_specs=out_specs,
         scratch_shapes=scratch,
-        compiler_params=pltpu.CompilerParams(vmem_limit_bytes=32 << 20),
+        compiler_params=pltpu.CompilerParams(vmem_limit_bytes=24 << 20),
         cost_estimate=pl.CostEstimate(flops=flops, bytes_accessed=1 << 16, transcendentals=0),
         name=name,
     )(*args)
 
 
-def rim_kernel(blk_ref, ylo_ref, yhi_ref, xlo_ref, xhi_ref, wide):
-    for out_ref, start in ((xlo_ref, 0), (xhi_ref, 10)):
-        wide[:, 0:10, :] = ylo_ref[start : start + 10].astype(f32)
-        wide[:, 10:30, :] = blk_ref[start : start + 10].astype(f32)
-        wide[:, 30:40, :] = yhi_ref[start : start + 10].astype(f32)
-        out_ref[...] = wide[...].astype(bf16)
+def even(index):
+    return index % 2 == 0
+
+
+def rim_kernel(where_ref, blk_ref, near_ref, next_ref, first_ref, second_ref, wide):
+    even_x = even(where_ref[0])
+    even_y = even(where_ref[1])
+    near, other = near_ref[...].astype(f32), next_ref[...].astype(f32)
+    wide[0:10] = jnp.where(even_x, other, near)
+    wide[10:30] = blk_ref[...].astype(f32)
+    wide[30:40] = jnp.where(even_x, near, other)
+    low, high = wide[:, 0:10, :], wide[:, 10:20, :]
+    first_ref[...] = jnp.where(even_y, high, low).astype(bf16)
+    second_ref[...] = jnp.where(even_y, low, high).astype(bf16)
 
 
 def restrict_kernel(
-    where_ref, blk_ref, ylo_ref, yhi_ref, xlo_ref, xhi_ref,
-    d_ref, out_ref,
-    planes, cells, mid, pay,
+    where_ref, blk_ref, near_x_ref, next_x_ref, near_y_ref, next_y_ref,
+    d_out_ref, first_ref, second_ref, own_ref, out_ref,
+    d_ref, planes, cells, mid, pay, sem,
 ):
+    even_x = even(where_ref[0])
+    even_y = even(where_ref[1])
     for x in range(40):
         p, i = x % 2, x // 2
-        if x < 10:
-            d_ref[p, i, 0:40, :] = xlo_ref[x].astype(f32)
-        elif x >= 30:
-            d_ref[p, i, 0:40, :] = xhi_ref[x - 30].astype(f32)
+        near, other = near_y_ref[x].astype(f32), next_y_ref[x].astype(f32)
+        d_ref[p, i, 0:10, :] = jnp.where(even_y, other, near)
+        d_ref[p, i, 30:40, :] = jnp.where(even_y, near, other)
+        if 10 <= x < 30:
+            centre = blk_ref[x - 10].astype(f32)
         else:
-            d_ref[p, i, 0:10, :] = ylo_ref[x - 10].astype(f32)
-            d_ref[p, i, 10:30, :] = blk_ref[x - 10].astype(f32)
-            d_ref[p, i, 30:40, :] = yhi_ref[x - 10].astype(f32)
+            near, other = near_x_ref[x % 30].astype(f32), next_x_ref[x % 30].astype(f32)
+            low, high = (other, near) if x < 10 else (near, other)
+            centre = jnp.where(even_x, low, high)
+        d_ref[p, i, 10:30, :] = centre
         d_ref[p, i, 40:48, :] = jnp.zeros((8, 128), f32)
+    save = pltpu.make_async_copy(d_ref, d_out_ref, sem)
+    save.start()
 
     def fine(x):
         return d_ref[x % 2, x // 2]
@@ -145,9 +165,11 @@
     for n in range(9):
         mid[n, 0:16, :] = value[16 * n : 16 * n + 16]
         mid[n, 16:24, :] = jnp.zeros((8, 128), f32)
-    pay[48:56, :] = jnp.zeros((8, 128), f32)
     for n in range(5):
-        pay[10 * n : 10 * n + 10, :] = mid[n + 2, 3:13, :]
+        right, left = mid[n + 2, 1:10, :], mid[n + 2, 6:15, :]
+        first_ref[n] = jnp.where(even_x, right, left).astype(bf16)
+        second_ref[n] = jnp.where(even_x, left, right).astype(bf16)
+        own_ref[n] = mid[n + 2, 0:16, :].astype(bf16)
 
     lane = lax.broadcasted_iota(jnp.int32, (1, 128), 1)
     odd = lane >= 64
@@ -169,27 +191,20 @@
     out = jnp.dot(
         jnp.concatenate(sums, axis=0), down_z, precision=HIGHEST, preferred_element_type=f32
     )
-    wide = jnp.concatenate([out[8 * y : 8 * y + 8] for y in range(4)], axis=1)
-    last = out[32:40]
-    high = wide.astype(bf16).astype(f32)
-    last_high = last.astype(bf16).astype(f32)
-    pay[56:64, :] = jnp.concatenate(
-        [last_high, last - last_high, jnp.zeros((8, 64), f32)], axis=1
-    )
-    pay[64:72, :] = high
-    pay[72:80, :] = wide - high
-    packed = pay[...].astype(bf16)
+    pay[...] = jnp.concatenate([out[8 * y : 8 * y + 8] for y in range(4)], axis=1)
+    pay[5:6, :] = jnp.concatenate([out[32 + x : 33 + x] for x in range(4)], axis=1)
+    pay[6:8, :] = jnp.zeros((2, 128), f32)
+    pay[6:7, 0:32] = out[36:37]
+    row = pay[...]
     for k in range(out_ref.shape[0]):
-        out_ref[k] = packed
-
-
-def fine_kernel(lo, hi, first, d_ref, v_ref, *refs):
-    if first:
-        out_ref, w0, w1, e0, e1 = refs
-        out_ref[...] = jnp.zeros((240, 256), f32)
-    else:
-        acc_ref, out_ref, w0, w1, e0, e1 = refs
-        out_ref[...] = acc_ref[...]
+        out_ref[k] = row
+    save.wait()
+
+
+def fine_kernel(lo, hi, d_in_ref, v_ref, out_ref, w0, w1, e0, e1, d_ref, sem):
+    load = pltpu.make_async_copy(d_in_ref, d_ref, sem)
+    load.start()
+    out_ref[...] = jnp.zeros((240, 256), f32)
     r, c = iota2((128, 128))
     mask = jnp.abs(r - c) <= REACH
     zero = jnp.zeros((128, 128), bf16)
@@ -219,6 +234,7 @@
         out_ref[...] += jnp.dot(lhs, w[...], preferred_element_type=f32)
 
     build(w0, lo)
+    load.wait()
 
     def step(t, _):
         b = lo + 2 * t
@@ -233,38 +249,44 @@
         dot(w0, e0, hi - 1)
 
 
-def fine_sum(lo, hi, d, v, acc=None):
-    args = (d, v) if acc is None else (d, v, acc)
+def fine_sum(lo, hi, d, v):
     return vmem_call(
-        functools.partial(fine_kernel, lo, hi, acc is None),
-        jax.ShapeDtypeStruct((240, 256), f32),
-        [pltpu.VMEM((2816, 256), bf16)] * 2 + [pltpu.VMEM((2, 480, 256), bf16)] * 2,
+        functools.partial(fine_kernel, lo, hi),
+        [jax.ShapeDtypeStruct((240, 256), f32)],
+        [pltpu.VMEM((2816, 256), bf16)] * 2
+        + [pltpu.VMEM((2, 480, 256), bf16)] * 2
+        + [pltpu.VMEM((2, 20, 48, 128), f32), pltpu.SemaphoreType.DMA(())],
         "fine_sum",
-        args,
+        (d, v),
         flops=(hi - lo) * 2 * 240 * 2816 * 256,
-    )
-
-
-def spread_kernel(where_ref, recv_ref, mx_ref, out_ref, buf, line):
-    index_x = where_ref[0]
-    count = recv_ref.shape[0]
-    start = 10 * index_x
-    rows = jnp.concatenate([mx_ref[h, pl.ds(start, 16), :] for h in range(2)], axis=1)
-    coarse = recv_ref[:, 48:80, :].astype(f32)
-    last = coarse[:, 8:16, :].reshape(8 * count, 128)
-    wide = (coarse[:, 16:24, :] + coarse[:, 24:32, :]).reshape(8 * count, 128)
-    wide = jnp.dot(rows, wide, precision=HIGHEST, preferred_element_type=f32)
-    last = jnp.dot(rows, last, precision=HIGHEST, preferred_element_type=f32)
-    last = last[:, 0:32] + last[:, 32:64]
-    part = jnp.concatenate([wide, last, jnp.zeros((16, 96), f32)], axis=1)
-    for step, first, size, at in ((-2, 9, 1, 0), (-1, 0, 10, 1), (0, 0, 10, 11), (1, 0, 10, 21), (2, 0, 2, 31)):
-        source = index_x + step
-        inside = (source >= 0) & (source < count)
-        got = recv_ref[jnp.clip(source, 0, count - 1), 0:64, :].astype(f32)
-        line[...] = jnp.where(inside, got, 0.0)
-        for n in range(5):
-            buf[33 * n + at : 33 * n + at + size, :] = line[10 * n + first : 10 * n + first + size, :]
-    buf[165:176, :] = jnp.zeros((11, 128), f32)
+        hbm_in=(0,),
+    )[0]
+
+
+def spread_kernel(where_ref, recv_ref, mx_ref, own_ref, near_ref, next_ref, out_ref, buf):
+    even_x = even(where_ref[0])
+    start = 10 * where_ref[0]
+    halves = [mx_ref[h, pl.ds(start, 16), :] for h in range(2)]
+    lane = lax.broadcasted_iota(jnp.int32, (16, 128), 1) % 8
+    rows = [jnp.concatenate(halves, axis=1)]
+    for x in range(5):
+        at = 5 if x < 4 else 6
+        moved = [jnp.where(lane == at, pltpu.roll(h, at - x, 1), 0.0) for h in halves]
+        rows.append(jnp.concatenate(moved, axis=1))
+    coarse = recv_ref[...].reshape(8 * recv_ref.shape[0], 128)
+    value = jnp.dot(
+        jnp.concatenate(rows, axis=0), coarse, precision=HIGHEST, preferred_element_type=f32
+    )
+    last = value[80:96, 0:32]
+    for x in range(4):
+        last = last + value[16 * x + 16 : 16 * x + 32, 32 * x : 32 * x + 32]
+    part = jnp.concatenate([value[0:16], last, jnp.zeros((16, 96), f32)], axis=1)
+    for n in range(5):
+        near, other = near_ref[n].astype(f32), next_ref[n].astype(f32)
+        buf[34 * n : 34 * n + 9, :] = jnp.where(even_x, other, near)
+        buf[34 * n + 9 : 34 * n + 25, :] = own_ref[n].astype(f32)
+        buf[34 * n + 25 : 34 * n + 34, :] = jnp.where(even_x, near, other)
+    buf[170:176, :] = jnp.zeros((6, 128), f32)
     high = part.astype(bf16)
     low = (part - high.astype(f32)).astype(bf16)
     cells = buf[...].astype(bf16)
@@ -292,12 +314,12 @@
         for p in range(5):
             n = 5 * step + 6 + p
             if 0 <= n < 17:
-                cells[n, 0:33, :] = line[33 * p : 33 * p + 33, :]
+                cells[n, 0:34, :] = line[34 * p : 34 * p + 34, :]
 
     r, c = iota2((128, 128))
     mask = jnp.abs(r % 64 - c % 64) <= REACH
 
-    def build(w, a):
+    def band_rows(w, a, at):
         base = TAPS * TAPS + a * TAPS
         for j in range(11):
             same = near_ref[pl.ds(base + 2 * j, 1), :]
@@ -310,12 +332,19 @@
             upper = pltpu.roll(jnp.broadcast_to(upper, (64, 128)), 0, 1, stride=1, stride_axis=0)
             lower = pltpu.roll(jnp.broadcast_to(lower, (64, 128)), 64, 1, stride=1, stride_axis=0)
             band = jnp.where(mask, jnp.concatenate([upper, lower], axis=0), 0.0).astype(bf16)
-            w[128 * j : 128 * j + 128, :] = band
+            w[at + 128 * j : at + 128 * j + 128, :] = band
+
+    def build(w, a):
+        for k in range(3):
+            band_rows(w, a + k, 1408 * k)
 
     def dot(w, a):
-        part = [cells[n, pl.ds(a, 16), :].astype(bf16) for n in range(17)]
+        rows = []
+        for k in range(3):
+            part = [cells[n, pl.ds(a + k + 1, 16), :].astype(bf16) for n in range(17)]
+            rows.append([jnp.concatenate(part[g : g + 11], axis=1) for g in range(7)])
         lhs = jnp.concatenate(
-            [jnp.concatenate(part[g : g + 11], axis=1) for g in range(7)], axis=0
+            [jnp.concatenate([rows[k][g] for k in range(3)], axis=1) for g in range(7)], axis=0
         )
         acc[...] += jnp.dot(lhs, w[...], preferred_element_type=f32)
 
@@ -323,15 +352,15 @@
     build(w0, 0)
 
     def step(t, _):
-        a = 2 * t
-        build(w1, a + 1)
+        a = 6 * t
+        build(w1, a + 3)
         dot(w0, a)
-        build(w0, a + 2)
-        dot(w1, a + 1)
+        build(w0, a + 6)
+        dot(w1, a + 3)
         return 0
 
-    lax.fori_loop(0, 10, step, 0)
-    dot(w0, TAPS - 1)
+    lax.fori_loop(0, 3, step, 0)
+    dot(w0, 18)
 
     start = 10 * index_y
     sums = [[None] * 14, [None] * 14]
@@ -384,11 +413,15 @@
         out_ref[x] = value + fine_ref[24 * m : 24 * m + 20, 128 * (x % 2) : 128 * (x % 2) + 128]
 
 
-def halo(low_edge, high_edge, axis):
+def swap(first, second, axis):
     count = lax.axis_size(axis)
-    forward = [(i, i + 1) for i in range(count - 1)]
-    backward = [(i + 1, i) for i in range(count - 1)]
-    return lax.ppermute(high_edge, axis, forward), lax.ppermute(low_edge, axis, backward)
+    pairs = [(k, k + 1) for k in range(0, count - 1, 2)]
+    others = [(k, k + 1) for k in range(1, count - 1, 2)]
+
+    def both(ends):
+        return ends + [(b, a) for a, b in ends]
+
+    return lax.ppermute(first, axis, both(pairs)), lax.ppermute(second, axis, both(others))
 
 
 def per_device(charges, kernels):
@@ -401,49 +434,61 @@
         jnp.dot(kernels.reshape(-1, TAPS), jnp.asarray(m, bf16), preferred_element_type=f32)
         for m in spots_np()
     )
-    y_lo, y_hi = halo(charges[:, :10], charges[:, 10:], "gy")
-    y_lo, y_hi, near, far = lax.optimization_barrier((y_lo, y_hi, near, far))
-    edge_lo, edge_hi = vmem_call(
+    low, high = charges[:10], charges[10:]
+    even_x = even(lax.axis_index("gx"))
+    near_x, next_x = swap(jnp.where(even_x, high, low), jnp.where(even_x, low, high), "gx")
+    first, second = vmem_call(
         rim_kernel,
-        [shape((10, 40, 128), bf16)] * 2,
-        [pltpu.VMEM((10, 40, 128), f32)],
+        [shape((40, 10, 128), bf16)] * 2,
+        [pltpu.VMEM((40, 20, 128), f32)],
         "rim",
-        (charges, y_lo, y_hi),
-    )
-    x_lo, x_hi = halo(edge_lo, edge_hi, "gx")
-    d, blocks = vmem_call(
+        (where, charges, near_x, next_x),
+        smem=1,
+    )
+    near_y, next_y = swap(first, second, "gy")
+    near_y, next_y, near, far = lax.optimization_barrier((near_y, next_y, near, far))
+    d, first, second, own, coarse = vmem_call(
         restrict_kernel,
-        [shape((2, 20, 48, 128), f32), shape((count_x, 80, 128), bf16)],
         [
+            shape((2, 20, 48, 128), f32),
+            shape((5, 9, 128), bf16),
+            shape((5, 9, 128), bf16),
+            shape((5, 16, 128), bf16),
+            shape((count_x, 8, 128), f32),
+        ],
+        [
+            pltpu.VMEM((2, 20, 48, 128), f32),
             pltpu.VMEM((16, 48, 128), f32),
             pltpu.VMEM((256, 128), f32),
             pltpu.VMEM((9, 24, 128), f32),
-            pltpu.VMEM((80, 128), f32),
+            pltpu.VMEM((8, 128), f32),
+            pltpu.SemaphoreType.DMA(()),
         ],
         "restrict",
-        (where, charges, y_lo, y_hi, x_lo, x_hi),
+        (where, charges, near_x, next_x, near_y, next_y),
         smem=1,
-    )
-    blocks = lax.all_to_all(blocks, "gx", 0, 0)
-    fine = fine_sum(0, SPLIT, d, near)
-    blocks, fine = lax.optimization_barrier((blocks, fine))
+        hbm_out=(0,),
+    )
+    near_m, next_m = swap(first, second, "gx")
+    coarse = lax.all_to_all(coarse, "gx", 0, 0)
     parts = vmem_call(
         spread_kernel,
-        shape((count_y, 240, 128), bf16),
-        [pltpu.VMEM((176, 128), f32), pltpu.VMEM((64, 128), f32)],
+        [shape((count_y, 240, 128), bf16)],
+        [pltpu.VMEM((176, 128), f32)],
         "spread",
-        (where, blocks, jnp.asarray(matrix_x_np(spread))),
+        (where, coarse, jnp.asarray(matrix_x_np(spread)), own, near_m, next_m),
         smem=1,
-    )
+    )[0]
+    parts, near = lax.optimization_barrier((parts, near))
     parts = lax.all_to_all(parts, "gy", 0, 0)
-    fine = fine_sum(SPLIT, TAPS, d, near, fine)
+    fine = fine_sum(0, TAPS, d, near)
     return vmem_call(
         final_kernel,
-        shape((20, 20, 128), f32),
+        [shape((20, 20, 128), f32)],
         [
             pltpu.VMEM((17, 40, 128), f32),
-            pltpu.VMEM((1408, 128), bf16),
-            pltpu.VMEM((1408, 128), bf16),
+            pltpu.VMEM((4224, 128), bf16),
+            pltpu.VMEM((4224, 128), bf16),
             pltpu.VMEM((112, 128), f32),
             pltpu.VMEM((320, 128), f32),
             pltpu.VMEM((112, 256), f32),
@@ -460,7 +505,7 @@
             fine,
         ),
         smem=1,
-    )
+    )[0]
 
 
 def solution(mesh):

time: 82.7 us -> 70 us (0.85)
  the two profiles are of different devices: /device:TPU:4 before, /device:TPU:2 now
where the time goes in v3:
time: 70 us; the launch traced here: 69.1 us
  starting transfers between devices  28.1 us (40%)
  Pallas kernels  20.6 us (29%)
  waiting for transfers between devices  14.8 us (21%)
  local copies, waits for them, and re-layouts  3.82 us (5%)
  other arithmetic  0.99 us (1%)
    pallas_call x5, Pallas kernels, vmem_call(): pl.pallas_call(body, out_shape=out_shape, in_specs=in_specs, out_specs=ou...  20.6 us
    all_to_all x1, starting transfers between devices, per_device(): coarse = lax.all_to_all(coarse, 'gx', 0, 0)  11.3 us
    all_to_all x1, waiting for transfers between devices, per_device(): coarse = lax.all_to_all(coarse, 'gx', 0, 0)  9.48 us
    ppermute x3, starting transfers between devices, swap(): lax.ppermute(second, axis, both(others))  6.26 us
    ppermute x3, starting transfers between devices, swap(): lax.ppermute(first, axis, both(pairs))  5.59 us
    ppermute x3, waiting for transfers between devices, swap(): lax.ppermute(second, axis, both(others))  5.1 us
    all_to_all x1, starting transfers between devices, per_device(): parts = lax.all_to_all(parts, 'gy', 0, 0)  4.89 us
    unnamed x19, local copies, waits for them, and re-layouts  3.55 us
  transfers between devices with their start and end apart: 8, of which 3 were waited for; matrix products, arithmetic and copies ran while one was open for 2% of the time, Pallas kernels for 16%

profile of v3, /device:TPU:2, one launch (start us, length us, event | category | flops | bytes accessed | tf_op | source)
XLA Modules:
  0.0 69.1 jit_solution(8197257893791448382)
XLA Ops:
  0.0 0.9 %broadcast_select_fusion = (bf16[10,20,128]{2,1,0:T(8,128)(2,1)S(1)}, bf16[10,20,128]{2,1,0:T(8,128)(2,1)S(1)}) fusion(pred[]{:T(512)S(6)} %eq.5, bf16[20,20,128]{2,1,0:T(8,128)(2,1)} %blk_ref.3), kind=kLoop, calls=%fused_computation.2 | loop fusion | flops 51200 | bytes 204801 | tf_op jit(solution)/shard_map/jit(_where)/select_n | solution.py:439
  0.9 0.7 collective-permute-start.1
  1.6 3.6 %collective-permute-start = (bf16[10,20,128]{2,1,0:T(8,128)(2,1)S(1)}, bf16[10,20,128]{2,1,0:T(8,128)(2,1)S(1)}, u32[]{:S(2)}, u32[]{:S(2)}) collective-permute-start(bf16[10,20,128]{2,1,0:T(8,128)(2,1)S(1)} %get-tuple-element.32), channel_id=1, source_target_pairs={{0,8},{16,24},{32,40},{48,56},{64,72},{80,88},{96,104},{112,120},{... | collective-permute-start | bytes 153608 | tf_op jit(solution)/shard_map/ppermute | solution.py:424
  5.2 0.4 copy.8
  5.6 0.3 reshape.4
  5.9 0.4 copy-done.8
  6.3 0.3 convolution_bitcast_fusion.far_ref
  6.7 0.5 copy-done
  7.2 0.7 rim.1
  7.9 1.7 %collective-permute-start.2 = (bf16[40,10,128]{2,1,0:T(8,128)(2,1)S(1)}, bf16[40,10,128]{2,1,0:T(8,128)(2,1)S(1)}, u32[]{:S(2)}, u32[]{:S(2)}) collective-permute-start(bf16[40,10,128]{2,1,0:T(8,128)(2,1)S(1)} %get-tuple-element.18), channel_id=1, source_target_pairs={{0,1},{2,3},{4,5},{6,7},{1,0},{3,2},{5,4},{7,6},{8,9},{10,11},{12,... | collective-permute-start | bytes 307208 | tf_op jit(solution)/shard_map/ppermute | solution.py:424
  9.6 4.9 %collective-permute-start.3 = (bf16[40,10,128]{2,1,0:T(8,128)(2,1)S(1)}, bf16[40,10,128]{2,1,0:T(8,128)(2,1)S(1)}, u32[]{:S(2)}, u32[]{:S(2)}) collective-permute-start(bf16[40,10,128]{2,1,0:T(8,128)(2,1)S(1)} %get-tuple-element.19), channel_id=1, source_target_pairs={{1,2},{3,4},{5,6},{2,1},{4,3},{6,5},{9,10},{11,12},{13,14},{10,9},... | collective-permute-start | bytes 307208 | tf_op jit(solution)/shard_map/ppermute | solution.py:424
  14.5 0.3 convolution_bitcast_fusion.1.v_ref.near_ref
  14.9 5.1 %collective-permute-done.3.next_y_ref = bf16[40,10,128]{2,1,0:T(8,128)(2,1)S(1)} collective-permute-done((bf16[40,10,128]{2,1,0:T(8,128)(2,1)S(1)}, bf16[40,10,128]{2,1,0:T(8,128)(2,1)S(1)}, u32[]{:S(2)}, u32[]{:S(2)}) %collective-permute-start.3) | collective-permute-done | bytes 102432 | tf_op jit(solution)/shard_map/ppermute | solution.py:424
  20.0 2.5 %restrict.1 = (f32[2,20,48,128]{3,2,1,0:T(8,128)S(1)}, bf16[5,9,128]{2,1,0:T(8,128)(2,1)S(1)}, bf16[5,9,128]{2,1,0:T(8,128)(2,1)S(1)}, bf16[5,16,128]{2,1,0:T(8,128)(2,1)S(1)}, f32[32,8,128]{2,1,0:T(8,128)}) custom-call(s32[2]{0:T(128)S(1)} %pad_add_fusion.where_ref, bf16[20,20,128]{2,1,0:T(8,128)(2,1)S(1)} %copy-done, ...), custom_call_target="tpu_custom_call" | custom-call | bytes 65536 | tf_op jit(solution)/shard_map/restrict/pallas_call | solution.py:82
  22.5 1.0 %copy-done.4 = f32[2,20,48,128]{3,2,1,0:T(8,128)} copy-done((f32[2,20,48,128]{3,2,1,0:T(8,128)}, f32[2,20,48,128]{3,2,1,0:T(8,128)S(1)}, u32[]{:S(2)}) %copy-start.4) | copy-done | bytes 983064
  23.4 11.3 %all-to-all-start = ((f32[32,8,128]{2,1,0:T(8,128)}), f32[32,8,128]{2,1,0:T(8,128)S(1)}, u32[]{:S(2)}, u32[]{:S(2)}) async-start(f32[32,8,128]{2,1,0:T(8,128)} %get-tuple-element.22), calls=%async_computation | async-start | bytes 262144 | tf_op jit(solution)/shard_map/all_to_all | solution.py:473
  34.7 0.4 collective-permute-start.4
  35.1 0.7 collective-permute-start.5
  36.0 9.5 %all-to-all-done.recv_ref = f32[32,8,128]{2,1,0:T(8,128)S(1)} async-done(((f32[32,8,128]{2,1,0:T(8,128)}), f32[32,8,128]{2,1,0:T(8,128)S(1)}, u32[]{:S(2)}, u32[]{:S(2)}) %all-to-all-start) | async-done | bytes 131104 | tf_op jit(solution)/shard_map/all_to_all | solution.py:473
  45.5 1.7 %spread.1 = bf16[8,240,128]{2,1,0:T(8,128)(2,1)} custom-call(s32[2]{0:T(128)S(1)} %pad_add_fusion.where_ref, f32[32,8,128]{2,1,0:T(8,128)S(1)} %all-to-all-done.recv_ref, f32[2,328,128]{2,1,0:T(8,128)S(1)} %copy-done.2, bf16[5,16,128]{2,1,0:T(8,128)(2,1)S(1)} %get-tuple-element.23.own_ref, bf16[5,9,128]{2,1,0:T(8,128)(2,1)S(1)} %collective-permute-done.4.near_ref, ...), custom_call_target="tpu_custom_call" | custom-call | bytes 65536 | tf_op jit(solution)/shard_map/spread/pallas_call | solution.py:82
  47.2 4.9 %all-to-all-start.1 = ((bf16[8,240,128]{2,1,0:T(8,128)(2,1)}), bf16[8,240,128]{2,1,0:T(8,128)(2,1)S(1)}, u32[]{:S(2)}, u32[]{:S(2)}) async-start(bf16[8,240,128]{2,1,0:T(8,128)(2,1)} %spread.1), calls=%async_computation.1 | async-start | bytes 983040 | tf_op jit(solution)/shard_map/all_to_all | solution.py:483
  52.1 1.2 %copy-done.5 = f32[2,20,48,128]{3,2,1,0:T(8,128)S(1)} copy-done((f32[2,20,48,128]{3,2,1,0:T(8,128)S(1)}, f32[2,20,48,128]{3,2,1,0:T(8,128)}, u32[]{:S(2)}) %copy-start.5) | copy-done | bytes 983064
  53.3 10.9 %fine_sum.1.fine_ref = f32[240,256]{1,0:T(8,128)S(1)} custom-call(f32[2,20,48,128]{3,2,1,0:T(8,128)S(1)} %copy-done.5, f32[882,128]{1,0:T(8,128)S(1)} %convolution_bitcast_fusion.1.v_ref.near_ref), custom_call_target="tpu_custom_call" | custom-call | flops 7266631680 | bytes 65536 | tf_op jit(solution)/shard_map/fine_sum/pallas_call | solution.py:82
  64.3 4.9 %final.1 = f32[20,20,128]{2,1,0:T(8,128)} custom-call(s32[2]{0:T(128)S(1)} %pad_add_fusion.where_ref, bf16[8,240,128]{2,1,0:T(8,128)(2,1)S(1)} %all-to-all-done.1.recv_ref, f32[16,88,128]{2,1,0:T(8,128)S(1)} %copy-done.1, f32[512,128]{1,0:T(8,128)S(1)} %copy-done.3, f32[882,128]{1,0:T(8,128)S(1)} %convolution_bitcast_fusion.1.v_ref.near_ref, ...), custom_call_target="tpu_custom_call" | custom-call | bytes 65536 | tf_op jit(solution)/shard_map/final/pallas_call | solution.py:82
  (21 shorter events, 0.4 us)
Async XLA Ops:
  0.0 5.2 %copy-start.6 = (bf16[2,21,21,21]{3,0,2,1:T(2,128)(2,1)S(1)}, bf16[2,21,21,21]{3,0,2,1:T(2,128)(2,1)}, u32[]{:S(2)}) copy-start(bf16[2,21,21,21]{3,0,2,1:T(2,128)(2,1)} %param.8) | copy-start | bytes 111136
  0.9 5.8 %collective-permute-start.1 = (bf16[10,20,128]{2,1,0:T(8,128)(2,1)S(1)}, bf16[10,20,128]{2,1,0:T(8,128)(2,1)S(1)}, u32[]{:S(2)}, u32[]{:S(2)}) collective-permute-start(bf16[10,20,128]{2,1,0:T(8,128)(2,1)S(1)} %get-tuple-element.31), channel_id=1, source_target_pairs={{8,16},{24,32},{40,48},{56,64},{72,80},{88,96},{104,112},{120,128}... | collective-permute-start | bytes 153608 | tf_op jit(solution)/shard_map/ppermute | solution.py:424
  1.6 5.1 %collective-permute-start = (bf16[10,20,128]{2,1,0:T(8,128)(2,1)S(1)}, bf16[10,20,128]{2,1,0:T(8,128)(2,1)S(1)}, u32[]{:S(2)}, u32[]{:S(2)}) collective-permute-start(bf16[10,20,128]{2,1,0:T(8,128)(2,1)S(1)} %get-tuple-element.32), channel_id=1, source_target_pairs={{0,8},{16,24},{32,40},{48,56},{64,72},{80,88},{96,104},{112,120},{... | collective-permute-start | bytes 153608 | tf_op jit(solution)/shard_map/ppermute | solution.py:424
  5.6 0.7 %copy-start.8 = (bf16[21,128]{1,0:T(8,128)(2,1)S(1)}, bf16[21,128]{1,0:T(8,128)(2,1)}, u32[]{:S(2)}) copy-start(bf16[21,128]{1,0:T(8,128)(2,1)} %constant.34.clone) | copy-start | bytes 16132
  6.3 0.9 %copy-start = (bf16[20,20,128]{2,1,0:T(8,128)(2,1)S(1)}, bf16[20,20,128]{2,1,0:T(8,128)(2,1)}, u32[]{:S(2)}) copy-start(bf16[20,20,128]{2,1,0:T(8,128)(2,1)} %blk_ref.3) | copy-start | bytes 307204
  7.2 7.3 %copy-start.7 = (bf16[21,128]{1,0:T(8,128)(2,1)S(1)}, bf16[21,128]{1,0:T(8,128)(2,1)}, u32[]{:S(2)}) copy-start(bf16[21,128]{1,0:T(8,128)(2,1)} %constant.33.clone) | copy-start | bytes 16132
  7.9 7.0 %collective-permute-start.2 = (bf16[40,10,128]{2,1,0:T(8,128)(2,1)S(1)}, bf16[40,10,128]{2,1,0:T(8,128)(2,1)S(1)}, u32[]{:S(2)}, u32[]{:S(2)}) collective-permute-start(bf16[40,10,128]{2,1,0:T(8,128)(2,1)S(1)} %get-tuple-element.18), channel_id=1, source_target_pairs={{0,1},{2,3},{4,5},{6,7},{1,0},{3,2},{5,4},{7,6},{8,9},{10,11},{12,... | collective-permute-start | bytes 307208 | tf_op jit(solution)/shard_map/ppermute | solution.py:424
  9.6 10.4 %collective-permute-start.3 = (bf16[40,10,128]{2,1,0:T(8,128)(2,1)S(1)}, bf16[40,10,128]{2,1,0:T(8,128)(2,1)S(1)}, u32[]{:S(2)}, u32[]{:S(2)}) collective-permute-start(bf16[40,10,128]{2,1,0:T(8,128)(2,1)S(1)} %get-tuple-element.19), channel_id=1, source_target_pairs={{1,2},{3,4},{5,6},{2,1},{4,3},{6,5},{9,10},{11,12},{13,14},{10,9},... | collective-permute-start | bytes 307208 | tf_op jit(solution)/shard_map/ppermute | solution.py:424
  14.9 30.6 %copy-start.2 = (f32[2,328,128]{2,1,0:T(8,128)S(1)}, f32[2,328,128]{2,1,0:T(8,128)}, u32[]{:S(2)}) copy-start(f32[2,328,128]{2,1,0:T(8,128)} %constant.35.clone.mx_ref) | copy-start | bytes 1007620
  22.4 1.0 %copy-start.4 = (f32[2,20,48,128]{3,2,1,0:T(8,128)}, f32[2,20,48,128]{3,2,1,0:T(8,128)S(1)}, u32[]{:S(2)}) copy-start(f32[2,20,48,128]{3,2,1,0:T(8,128)S(1)} %get-tuple-element.30.d_in_ref) | copy-start | bytes 2949124
  23.4 22.1 %all-to-all-start = ((f32[32,8,128]{2,1,0:T(8,128)}), f32[32,8,128]{2,1,0:T(8,128)S(1)}, u32[]{:S(2)}, u32[]{:S(2)}) async-start(f32[32,8,128]{2,1,0:T(8,128)} %get-tuple-element.22), calls=%async_computation | async-start | bytes 262144 | tf_op jit(solution)/shard_map/all_to_all | solution.py:473
  34.7 1.3 %collective-permute-start.4 = (bf16[5,9,128]{2,1,0:T(8,128)(2,1)S(1)}, bf16[5,9,128]{2,1,0:T(8,128)(2,1)S(1)}, u32[]{:S(2)}, u32[]{:S(2)}) collective-permute-start(bf16[5,9,128]{2,1,0:T(8,128)(2,1)S(1)} %get-tuple-element.24), channel_id=1, source_target_pairs={{0,8},{16,24},{32,40},{48,56},{64,72},{80,88},{96,104},{112,120},{... | collective-permute-start | bytes 34568 | tf_op jit(solution)/shard_map/ppermute | solution.py:424
  35.1 0.9 %collective-permute-start.5 = (bf16[5,9,128]{2,1,0:T(8,128)(2,1)S(1)}, bf16[5,9,128]{2,1,0:T(8,128)(2,1)S(1)}, u32[]{:S(2)}, u32[]{:S(2)}) collective-permute-start(bf16[5,9,128]{2,1,0:T(8,128)(2,1)S(1)} %get-tuple-element.25), channel_id=1, source_target_pairs={{8,16},{24,32},{40,48},{56,64},{72,80},{88,96},{104,112},{120,128}... | collective-permute-start | bytes 34568 | tf_op jit(solution)/shard_map/ppermute | solution.py:424
  47.2 17.0 %all-to-all-start.1 = ((bf16[8,240,128]{2,1,0:T(8,128)(2,1)}), bf16[8,240,128]{2,1,0:T(8,128)(2,1)S(1)}, u32[]{:S(2)}, u32[]{:S(2)}) async-start(bf16[8,240,128]{2,1,0:T(8,128)(2,1)} %spread.1), calls=%async_computation.1 | async-start | bytes 983040 | tf_op jit(solution)/shard_map/all_to_all | solution.py:483
  52.1 1.2 %copy-start.5 = (f32[2,20,48,128]{3,2,1,0:T(8,128)S(1)}, f32[2,20,48,128]{3,2,1,0:T(8,128)}, u32[]{:S(2)}) copy-start(f32[2,20,48,128]{3,2,1,0:T(8,128)} %copy-done.4) | copy-start | bytes 2949124
  53.3 10.9 %copy-start.1 = (f32[16,88,128]{2,1,0:T(8,128)S(1)}, f32[16,88,128]{2,1,0:T(8,128)}, u32[]{:S(2)}) copy-start(f32[16,88,128]{2,1,0:T(8,128)} %constant.36.clone.my_ref) | copy-start | bytes 2162692
  53.3 10.9 %copy-start.3 = (f32[512,128]{1,0:T(8,128)S(1)}, f32[512,128]{1,0:T(8,128)}, u32[]{:S(2)}) copy-start(f32[512,128]{1,0:T(8,128)} %constant.37.clone.mz_ref) | copy-start | bytes 786436

commit v4 on v3

--- a/solution.py
+++ b/solution.py
@@ -13,6 +13,8 @@
 HIGHEST = lax.Precision.HIGHEST
 REACH = 10
 TAPS = 21
+GROUP = 3
+SPLIT = 9
 
 
 def weight_np(offset):
@@ -65,6 +67,20 @@
     return jnp.where(d == 0, 1.0, jnp.where(d == 1, 0.5625, jnp.where(d == 3, -0.0625, 0.0))).astype(f32)
 
 
+def exact_dot(rows, weights):
+    count = rows.shape[0]
+    high = rows.astype(bf16)
+    rest = rows - high.astype(f32)
+    middle = rest.astype(bf16)
+    low = (rest - middle.astype(f32)).astype(bf16)
+    out = jnp.dot(
+        jnp.concatenate([high, middle, low], axis=0),
+        weights.astype(bf16),
+        preferred_element_type=f32,
+    )
+    return out[0:count] + (out[count : 2 * count] + out[2 * count :])
+
+
 def iota2(shape):
     return (lax.broadcasted_iota(jnp.int32, shape, 0), lax.broadcasted_iota(jnp.int32, shape, 1))
 
@@ -75,10 +91,10 @@
 
     in_specs = [spec(pltpu.SMEM)] * smem + [spec(pltpu.VMEM)] * (len(args) - smem)
     for k in hbm_in:
-        in_specs[k] = spec(pl.ANY)
+        in_specs[k] = spec(pltpu.HBM)
     out_specs = [spec(pltpu.VMEM)] * len(out_shape)
     for k in hbm_out:
-        out_specs[k] = spec(pl.ANY)
+        out_specs[k] = spec(pltpu.HBM)
     return pl.pallas_call(
         body,
         out_shape=out_shape,
@@ -154,9 +170,7 @@
         rows.append(jnp.concatenate(pair, axis=1))
     r, c = iota2((256, 128))
     down_z = jnp.where(r // 128 == c // 64, weight(r % 128 - 2 * (c % 64)), 0.0)
-    value = jnp.dot(
-        jnp.concatenate(rows, axis=0), down_z, precision=HIGHEST, preferred_element_type=f32
-    )
+    value = exact_dot(jnp.concatenate(rows, axis=0), down_z)
     r, c = iota2((144, 128))
     cell_x = 10 * where_ref[0] - 3 + r % 16
     cell_y = 10 * where_ref[1] - 4 + 2 * (r // 16) + c // 64
@@ -188,9 +202,7 @@
                 weight_0 * part(n) + weight_1 * part(n - 1) + weight_3 * (part(n - 2) + part(n + 1))
             )
         sums.append(tap(0) + 0.5625 * (tap(-1) + tap(1)) - 0.0625 * (tap(-3) + tap(3)))
-    out = jnp.dot(
-        jnp.concatenate(sums, axis=0), down_z, precision=HIGHEST, preferred_element_type=f32
-    )
+    out = exact_dot(jnp.concatenate(sums, axis=0), down_z)
     pay[...] = jnp.concatenate([out[8 * y : 8 * y + 8] for y in range(4)], axis=1)
     pay[5:6, :] = jnp.concatenate([out[32 + x : 33 + x] for x in range(4)], axis=1)
     pay[6:8, :] = jnp.zeros((2, 128), f32)
@@ -201,63 +213,74 @@
     save.wait()
 
 
-def fine_kernel(lo, hi, d_in_ref, v_ref, out_ref, w0, w1, e0, e1, d_ref, sem):
+def fine_kernel(lo, hi, first, d_in_ref, v_ref, *refs):
+    if first:
+        out_ref, w0, w1, e0, e1, d_ref, sem = refs
+    else:
+        acc_ref, out_ref, w0, w1, e0, e1, d_ref, sem = refs
     load = pltpu.make_async_copy(d_in_ref, d_ref, sem)
     load.start()
-    out_ref[...] = jnp.zeros((240, 256), f32)
     r, c = iota2((128, 128))
     mask = jnp.abs(r - c) <= REACH
     zero = jnp.zeros((128, 128), bf16)
     for w in (w0, w1):
-        w[0:128, 128:256] = zero
-        w[2688:2816, 0:128] = zero
-
-    def build(w, b):
-        for a in range(TAPS):
-            line = jnp.broadcast_to(v_ref[pl.ds(a * TAPS + b, 1), :], (128, 128))
-            line = pltpu.roll(line, 0, 1, stride=1, stride_axis=0)
-            band = jnp.where(mask, line, 0.0).astype(bf16)
-            w[a * 128 : (a + 1) * 128, 0:128] = band
-            w[(a + 1) * 128 : (a + 2) * 128, 128:256] = band
-
-    def dot(w, e, b):
-        for p in range(2):
-            for q in range(10):
-                part = d_ref[p, 2 * q : 2 * q + 2, pl.ds(b, 24), :].reshape(48, 128)
-                e[0, 48 * q : 48 * q + 48, p * 128 : (p + 1) * 128] = part.astype(bf16)
-            for q in range(9):
-                part = d_ref[p, 2 * q + 1 : 2 * q + 3, pl.ds(b, 24), :].reshape(48, 128)
-                e[1, 48 * q : 48 * q + 48, p * 128 : (p + 1) * 128] = part.astype(bf16)
-        lhs = jnp.concatenate(
-            [e[k % 2, 24 * (k - k % 2) : 24 * (k - k % 2) + 240, :] for k in range(11)], axis=1
-        )
+        for k in range(GROUP):
+            w[2816 * k : 2816 * k + 128, 128:256] = zero
+            w[2816 * k + 2688 : 2816 * k + 2816, 0:128] = zero
+
+    def build(w, start):
+        for k in range(GROUP):
+            for a in range(TAPS):
+                line = jnp.broadcast_to(v_ref[pl.ds(a * TAPS + start + k, 1), :], (128, 128))
+                line = pltpu.roll(line, 0, 1, stride=1, stride_axis=0)
+                band = jnp.where(mask, line, 0.0).astype(bf16)
+                at = 2816 * k + 128 * a
+                w[at : at + 128, 0:128] = band
+                w[at + 128 : at + 256, 128:256] = band
+
+    def dot(w, e, start):
+        tiles = []
+        for k in range(GROUP):
+            for p in range(2):
+                for q in range(10):
+                    part = d_ref[p, 2 * q : 2 * q + 2, pl.ds(start + k, 24), :].reshape(48, 128)
+                    e[k, 0, 48 * q : 48 * q + 48, p * 128 : (p + 1) * 128] = part.astype(bf16)
+                for q in range(9):
+                    part = d_ref[p, 2 * q + 1 : 2 * q + 3, pl.ds(start + k, 24), :].reshape(48, 128)
+                    e[k, 1, 48 * q : 48 * q + 48, p * 128 : (p + 1) * 128] = part.astype(bf16)
+            tiles += [
+                e[k, m % 2, 24 * (m - m % 2) : 24 * (m - m % 2) + 240, :] for m in range(11)
+            ]
+        lhs = jnp.concatenate(tiles, axis=1)
         out_ref[...] += jnp.dot(lhs, w[...], preferred_element_type=f32)
 
     build(w0, lo)
     load.wait()
+    out_ref[...] = jnp.zeros((240, 256), f32) if first else acc_ref[...]
 
     def step(t, _):
-        b = lo + 2 * t
-        build(w1, b + 1)
+        b = lo + 2 * GROUP * t
+        build(w1, b + GROUP)
         dot(w0, e0, b)
-        build(w0, jnp.minimum(b + 2, TAPS - 1))
-        dot(w1, e1, b + 1)
+        build(w0, jnp.minimum(b + 2 * GROUP, TAPS - GROUP))
+        dot(w1, e1, b + GROUP)
         return 0
 
-    lax.fori_loop(0, (hi - lo) // 2, step, 0)
-    if (hi - lo) % 2:
-        dot(w0, e0, hi - 1)
-
-
-def fine_sum(lo, hi, d, v):
+    groups = (hi - lo) // GROUP
+    lax.fori_loop(0, groups // 2, step, 0)
+    if groups % 2:
+        dot(w0, e0, hi - GROUP)
+
+
+def fine_sum(lo, hi, d, v, acc=None):
     return vmem_call(
-        functools.partial(fine_kernel, lo, hi),
+        functools.partial(fine_kernel, lo, hi, acc is None),
         [jax.ShapeDtypeStruct((240, 256), f32)],
-        [pltpu.VMEM((2816, 256), bf16)] * 2
-        + [pltpu.VMEM((2, 480, 256), bf16)] * 2
+        [pltpu.VMEM((GROUP * 2816, 256), bf16)] * 2
+        + [pltpu.VMEM((GROUP, 2, 480, 256), bf16)] * 2
         + [pltpu.VMEM((2, 20, 48, 128), f32), pltpu.SemaphoreType.DMA(())],
         "fine_sum",
-        (d, v),
+        (d, v) if acc is None else (d, v, acc),
         flops=(hi - lo) * 2 * 240 * 2816 * 256,
         hbm_in=(0,),
     )[0]
@@ -388,7 +411,7 @@
     total = jnp.where(inside, total, 0.0)
     r, c = iota2((128, 256))
     up_z = jnp.where(r // 64 == c // 128, weight(c % 128 - 2 * (r % 64)), 0.0)
-    wide[...] = jnp.dot(total, up_z, precision=HIGHEST, preferred_element_type=f32)
+    wide[...] = exact_dot(total, up_z)
 
     def middle_y(y):
         n, par = (y + 2) // 2, y % 2
@@ -430,10 +453,6 @@
     where = jnp.stack([lax.axis_index("gx"), lax.axis_index("gy")]).astype(jnp.int32)
     spread = charges.shape[0] * count_x / 16.0
     shape = jax.ShapeDtypeStruct
-    near, far = (
-        jnp.dot(kernels.reshape(-1, TAPS), jnp.asarray(m, bf16), preferred_element_type=f32)
-        for m in spots_np()
-    )
     low, high = charges[:10], charges[10:]
     even_x = even(lax.axis_index("gx"))
     near_x, next_x = swap(jnp.where(even_x, high, low), jnp.where(even_x, low, high), "gx")
@@ -444,6 +463,11 @@
         "rim",
         (where, charges, near_x, next_x),
         smem=1,
+    )
+    first, second, kernels = lax.optimization_barrier((first, second, kernels))
+    near, far = (
+        jnp.dot(kernels.reshape(-1, TAPS), jnp.asarray(m, bf16), preferred_element_type=f32)
+        for m in spots_np()
     )
     near_y, next_y = swap(first, second, "gy")
     near_y, next_y, near, far = lax.optimization_barrier((near_y, next_y, near, far))
@@ -470,7 +494,10 @@
         hbm_out=(0,),
     )
     near_m, next_m = swap(first, second, "gx")
+    coarse, near_m, next_m = lax.optimization_barrier((coarse, near_m, next_m))
     coarse = lax.all_to_all(coarse, "gx", 0, 0)
+    fine = fine_sum(0, SPLIT, d, near)
+    coarse, fine = lax.optimization_barrier((coarse, fine))
     parts = vmem_call(
         spread_kernel,
         [shape((count_y, 240, 128), bf16)],
@@ -481,7 +508,7 @@
     )[0]
     parts, near = lax.optimization_barrier((parts, near))
     parts = lax.all_to_all(parts, "gy", 0, 0)
-    fine = fine_sum(0, TAPS, d, near)
+    fine = fine_sum(SPLIT, TAPS, d, near, fine)
     return vmem_call(
         final_kernel,
         [shape((20, 20, 128), f32)],

time: 70 us -> 72.6 us (1.037)
  starting transfers between devices: 28.1 us -> 35.4 us
  waiting for transfers between devices: 14.8 us -> 12 us
  local copies, waits for them, and re-layouts: 3.82 us -> 2.74 us
    all_to_all x1, starting transfers between devices: 11.3 us -> 19.1 us  [per_device(): coarse = lax.all_to_all(coarse, 'gx', 0, 0)]
    all_to_all x1, waiting for transfers between devices: 9.48 us -> 5.88 us  [per_device(): coarse = lax.all_to_all(coarse, 'gx', 0, 0)]
    ppermute x3, waiting for transfers between devices: 5.1 us -> 3.51 us  [swap(): lax.ppermute(second, axis, both(others))]
    all_to_all x1, waiting for transfers between devices: 0.01 us -> 1.53 us  [per_device(): parts = lax.all_to_all(parts, 'gy', 0, 0)]
    unnamed x19 -> x18, local copies, waits for them, and re-layouts: 3.55 us -> 2.03 us
    ppermute x3, waiting for transfers between devices: 0.26 us -> 1.11 us  [swap(): lax.ppermute(first, axis, both(pairs))]
    pallas_call x5 -> x6, Pallas kernels: 20.6 us -> 20.3 us  [vmem_call(): pl.pallas_call(body, out_shape=out_shape, in_specs=in_specs, out_specs=ou...]
  transfers between devices with their start and end apart: 8 -> 8, of which waited for: 3 -> 5; matrix products, arithmetic and copies ran while one was open for 2% -> 2% of each run, Pallas kernels for 16% -> 15%
where the time goes in v4:
time: 72.6 us; the launch traced here: 72.1 us
  starting transfers between devices  35.4 us (49%)
  Pallas kernels  20.3 us (28%)
  waiting for transfers between devices  12 us (17%)
  local copies, waits for them, and re-layouts  2.74 us (4%)
  other arithmetic  0.99 us (1%)
    pallas_call x6, Pallas kernels, vmem_call(): pl.pallas_call(body, out_shape=out_shape, in_specs=in_specs, out_specs=ou...  20.3 us
    all_to_all x1, starting transfers between devices, per_device(): coarse = lax.all_to_all(coarse, 'gx', 0, 0)  19.1 us
    ppermute x3, starting transfers between devices, swap(): lax.ppermute(second, axis, both(others))  6.26 us
    all_to_all x1, waiting for transfers between devices, per_device(): coarse = lax.all_to_all(coarse, 'gx', 0, 0)  5.88 us
    ppermute x3, starting transfers between devices, swap(): lax.ppermute(first, axis, both(pairs))  5.56 us
    all_to_all x1, starting transfers between devices, per_device(): parts = lax.all_to_all(parts, 'gy', 0, 0)  4.46 us
    ppermute x3, waiting for transfers between devices, swap(): lax.ppermute(second, axis, both(others))  3.51 us
    unnamed x18, local copies, waits for them, and re-layouts  2.03 us
  transfers between devices with their start and end apart: 8, of which 5 were waited for; matrix products, arithmetic and copies ran while one was open for 2% of the time, Pallas kernels for 15%

profile of v4, /device:TPU:2, one launch (start us, length us, event | category | flops | bytes accessed | tf_op | source)
XLA Modules:
  0.0 72.1 jit_solution(1470698897684266448)
XLA Ops:
  0.0 0.9 %broadcast_select_fusion = (bf16[10,20,128]{2,1,0:T(8,128)(2,1)S(1)}, bf16[10,20,128]{2,1,0:T(8,128)(2,1)S(1)}) fusion(pred[]{:T(512)S(6)} %eq.5, bf16[20,20,128]{2,1,0:T(8,128)(2,1)} %blk_ref.3), kind=kLoop, calls=%fused_computation | loop fusion | flops 51200 | bytes 204801 | tf_op jit(solution)/shard_map/jit(_where)/select_n | solution.py:458
  0.9 0.7 collective-permute-start.1
  1.6 3.6 %collective-permute-start = (bf16[10,20,128]{2,1,0:T(8,128)(2,1)S(1)}, bf16[10,20,128]{2,1,0:T(8,128)(2,1)S(1)}, u32[]{:S(2)}, u32[]{:S(2)}) collective-permute-start(bf16[10,20,128]{2,1,0:T(8,128)(2,1)S(1)} %get-tuple-element.48), channel_id=1, source_target_pairs={{0,8},{16,24},{32,40},{48,56},{64,72},{80,88},{96,104},{112,120},{... | collective-permute-start | bytes 153608 | tf_op jit(solution)/shard_map/ppermute | solution.py:447
  5.2 0.8 %collective-permute-done.near_ref.near_x_ref = bf16[10,20,128]{2,1,0:T(8,128)(2,1)S(1)} collective-permute-done((bf16[10,20,128]{2,1,0:T(8,128)(2,1)S(1)}, bf16[10,20,128]{2,1,0:T(8,128)(2,1)S(1)}, u32[]{:S(2)}, u32[]{:S(2)}) %collective-permute-start) | collective-permute-done | bytes 51232 | tf_op jit(solution)/shard_map/ppermute | solution.py:447
  6.1 0.7 rim.1
  6.8 1.7 %collective-permute-start.2 = (bf16[40,10,128]{2,1,0:T(8,128)(2,1)S(1)}, bf16[40,10,128]{2,1,0:T(8,128)(2,1)S(1)}, u32[]{:S(2)}, u32[]{:S(2)}) collective-permute-start(bf16[40,10,128]{2,1,0:T(8,128)(2,1)S(1)} %get-tuple-element.28), channel_id=1, source_target_pairs={{0,1},{2,3},{4,5},{6,7},{1,0},{3,2},{5,4},{7,6},{8,9},{10,11},{12,... | collective-permute-start | bytes 307208 | tf_op jit(solution)/shard_map/ppermute | solution.py:447
  8.4 4.9 %collective-permute-start.3 = (bf16[40,10,128]{2,1,0:T(8,128)(2,1)S(1)}, bf16[40,10,128]{2,1,0:T(8,128)(2,1)S(1)}, u32[]{:S(2)}, u32[]{:S(2)}) collective-permute-start(bf16[40,10,128]{2,1,0:T(8,128)(2,1)S(1)} %get-tuple-element.29), channel_id=1, source_target_pairs={{1,2},{3,4},{5,6},{2,1},{4,3},{6,5},{9,10},{11,12},{13,14},{10,9},... | collective-permute-start | bytes 307208 | tf_op jit(solution)/shard_map/ppermute | solution.py:447
  13.4 0.5 copy.8
  14.1 0.4 copy-done.8
  14.5 0.3 fusion.1.far_ref
  14.9 0.4 copy-done.7
  15.6 3.5 %collective-permute-done.3.next_y_ref = bf16[40,10,128]{2,1,0:T(8,128)(2,1)S(1)} collective-permute-done((bf16[40,10,128]{2,1,0:T(8,128)(2,1)S(1)}, bf16[40,10,128]{2,1,0:T(8,128)(2,1)S(1)}, u32[]{:S(2)}, u32[]{:S(2)}) %collective-permute-start.3) | collective-permute-done | bytes 102432 | tf_op jit(solution)/shard_map/ppermute | solution.py:447
  19.1 2.2 %restrict.1 = (f32[2,20,48,128]{3,2,1,0:T(8,128)S(1)}, bf16[5,9,128]{2,1,0:T(8,128)(2,1)S(1)}, bf16[5,9,128]{2,1,0:T(8,128)(2,1)S(1)}, bf16[5,16,128]{2,1,0:T(8,128)(2,1)S(1)}, f32[32,8,128]{2,1,0:T(8,128)}) custom-call(s32[2]{0:T(128)S(1)} %pad_add_fusion.where_ref, bf16[20,20,128]{2,1,0:T(8,128)(2,1)S(1)} %copy-done, ...), custom_call_target="tpu_custom_call" | custom-call | bytes 65536 | tf_op jit(solution)/shard_map/restrict/pallas_call | solution.py:98
  21.3 0.3 collective-permute-start.4
  21.7 0.7 collective-permute-start.5
  22.6 19.1 %all-to-all-start = ((f32[32,8,128]{2,1,0:T(8,128)}), f32[32,8,128]{2,1,0:T(8,128)S(1)}, u32[]{:S(2)}, u32[]{:S(2)}) async-start(f32[32,8,128]{2,1,0:T(8,128)} %get-tuple-element.36), calls=%async_computation | async-start | bytes 262144 | tf_op jit(solution)/shard_map/all_to_all | solution.py:498
  41.7 4.9 %fine_sum.2.refs_0_ = f32[240,256]{1,0:T(8,128)S(1)} custom-call(f32[2,20,48,128]{3,2,1,0:T(8,128)S(1)} %get-tuple-element.37.d_in_ref, f32[882,128]{1,0:T(8,128)S(1)} %fusion.v_ref.near_ref), custom_call_target="tpu_custom_call" | custom-call | flops 3114270720 | bytes 65536 | tf_op jit(solution)/shard_map/fine_sum/pallas_call | solution.py:98
  46.6 5.9 %all-to-all-done.recv_ref = f32[32,8,128]{2,1,0:T(8,128)S(1)} async-done(((f32[32,8,128]{2,1,0:T(8,128)}), f32[32,8,128]{2,1,0:T(8,128)S(1)}, u32[]{:S(2)}, u32[]{:S(2)}) %all-to-all-start) | async-done | bytes 131104 | tf_op jit(solution)/shard_map/all_to_all | solution.py:498
  52.5 1.7 %spread.1 = bf16[8,240,128]{2,1,0:T(8,128)(2,1)} custom-call(s32[2]{0:T(128)S(1)} %pad_add_fusion.where_ref, f32[32,8,128]{2,1,0:T(8,128)S(1)} %all-to-all-done.recv_ref, f32[2,328,128]{2,1,0:T(8,128)S(1)} %copy-done.2, bf16[5,16,128]{2,1,0:T(8,128)(2,1)S(1)} %get-tuple-element.40.own_ref, bf16[5,9,128]{2,1,0:T(8,128)(2,1)S(1)} %collective-permute-done.4.near_ref, ...), custom_call_target="tpu_custom_call" | custom-call | bytes 65536 | tf_op jit(solution)/shard_map/spread/pallas_call | solution.py:98
  54.2 4.5 %all-to-all-start.1 = ((bf16[8,240,128]{2,1,0:T(8,128)(2,1)}), bf16[8,240,128]{2,1,0:T(8,128)(2,1)S(1)}, u32[]{:S(2)}, u32[]{:S(2)}) async-start(bf16[8,240,128]{2,1,0:T(8,128)(2,1)} %spread.1), calls=%async_computation.1 | async-start | bytes 983040 | tf_op jit(solution)/shard_map/all_to_all | solution.py:510
  58.6 1.2 %copy-done.5 = f32[2,20,48,128]{3,2,1,0:T(8,128)S(1)} copy-done((f32[2,20,48,128]{3,2,1,0:T(8,128)S(1)}, f32[2,20,48,128]{3,2,1,0:T(8,128)}, u32[]{:S(2)}) %copy-start.5) | copy-done | bytes 983064
  59.9 6.0 %fine_sum.3.fine_ref = f32[240,256]{1,0:T(8,128)S(1)} custom-call(f32[2,20,48,128]{3,2,1,0:T(8,128)S(1)} %copy-done.5, f32[882,128]{1,0:T(8,128)S(1)} %fusion.v_ref.near_ref, f32[240,256]{1,0:T(8,128)S(1)} %fine_sum.2.refs_0_), custom_call_target="tpu_custom_call" | custom-call | flops 4152360960 | bytes 65536 | tf_op jit(solution)/shard_map/fine_sum/pallas_call | solution.py:98
  65.8 1.5 %all-to-all-done.1.recv_ref = bf16[8,240,128]{2,1,0:T(8,128)(2,1)S(1)} async-done(((bf16[8,240,128]{2,1,0:T(8,128)(2,1)}), bf16[8,240,128]{2,1,0:T(8,128)(2,1)S(1)}, u32[]{:S(2)}, u32[]{:S(2)}) %all-to-all-start.1) | async-done | bytes 491552 | tf_op jit(solution)/shard_map/all_to_all | solution.py:510
  67.4 4.8 %final.1 = f32[20,20,128]{2,1,0:T(8,128)} custom-call(s32[2]{0:T(128)S(1)} %pad_add_fusion.where_ref, bf16[8,240,128]{2,1,0:T(8,128)(2,1)S(1)} %all-to-all-done.1.recv_ref, f32[16,88,128]{2,1,0:T(8,128)S(1)} %copy-done.1, f32[512,128]{1,0:T(8,128)S(1)} %copy-done.3, f32[882,128]{1,0:T(8,128)S(1)} %fusion.v_ref.near_ref, f32[882,128]{1,0:T(8,128)S(1)} %fusion.1.far_ref, ...), custom_call_target="tpu_custom_call" | custom-call | bytes 65536 | tf_op jit(solution)/shard_map/final/pallas_call | solution.py:98
  (22 shorter events, 1.0 us)
Async XLA Ops:
  0.0 6.1 %copy-start = (bf16[20,20,128]{2,1,0:T(8,128)(2,1)S(1)}, bf16[20,20,128]{2,1,0:T(8,128)(2,1)}, u32[]{:S(2)}) copy-start(bf16[20,20,128]{2,1,0:T(8,128)(2,1)} %blk_ref.3) | copy-start | bytes 307204
  0.0 13.4 %copy-start.6 = (bf16[2,21,21,21]{3,0,2,1:T(2,128)(2,1)S(1)}, bf16[2,21,21,21]{3,0,2,1:T(2,128)(2,1)}, u32[]{:S(2)}) copy-start(bf16[2,21,21,21]{3,0,2,1:T(2,128)(2,1)} %param.8) | copy-start | bytes 111136
  0.9 4.3 %collective-permute-start.1 = (bf16[10,20,128]{2,1,0:T(8,128)(2,1)S(1)}, bf16[10,20,128]{2,1,0:T(8,128)(2,1)S(1)}, u32[]{:S(2)}, u32[]{:S(2)}) collective-permute-start(bf16[10,20,128]{2,1,0:T(8,128)(2,1)S(1)} %get-tuple-element.47), channel_id=1, source_target_pairs={{8,16},{24,32},{40,48},{56,64},{72,80},{88,96},{104,112},{120,128}... | collective-permute-start | bytes 153608 | tf_op jit(solution)/shard_map/ppermute | solution.py:447
  1.6 4.5 %collective-permute-start = (bf16[10,20,128]{2,1,0:T(8,128)(2,1)S(1)}, bf16[10,20,128]{2,1,0:T(8,128)(2,1)S(1)}, u32[]{:S(2)}, u32[]{:S(2)}) collective-permute-start(bf16[10,20,128]{2,1,0:T(8,128)(2,1)S(1)} %get-tuple-element.48), channel_id=1, source_target_pairs={{0,8},{16,24},{32,40},{48,56},{64,72},{80,88},{96,104},{112,120},{... | collective-permute-start | bytes 153608 | tf_op jit(solution)/shard_map/ppermute | solution.py:447
  6.8 8.8 %collective-permute-start.2 = (bf16[40,10,128]{2,1,0:T(8,128)(2,1)S(1)}, bf16[40,10,128]{2,1,0:T(8,128)(2,1)S(1)}, u32[]{:S(2)}, u32[]{:S(2)}) collective-permute-start(bf16[40,10,128]{2,1,0:T(8,128)(2,1)S(1)} %get-tuple-element.28), channel_id=1, source_target_pairs={{0,1},{2,3},{4,5},{6,7},{1,0},{3,2},{5,4},{7,6},{8,9},{10,11},{12,... | collective-permute-start | bytes 307208 | tf_op jit(solution)/shard_map/ppermute | solution.py:447
  8.4 10.6 %collective-permute-start.3 = (bf16[40,10,128]{2,1,0:T(8,128)(2,1)S(1)}, bf16[40,10,128]{2,1,0:T(8,128)(2,1)S(1)}, u32[]{:S(2)}, u32[]{:S(2)}) collective-permute-start(bf16[40,10,128]{2,1,0:T(8,128)(2,1)S(1)} %get-tuple-element.29), channel_id=1, source_target_pairs={{1,2},{3,4},{5,6},{2,1},{4,3},{6,5},{9,10},{11,12},{13,14},{10,9},... | collective-permute-start | bytes 307208 | tf_op jit(solution)/shard_map/ppermute | solution.py:447
  13.8 0.7 copy-start.8
  14.5 0.7 copy-start.7
  21.3 25.2 %copy-start.4 = (f32[2,20,48,128]{3,2,1,0:T(8,128)}, f32[2,20,48,128]{3,2,1,0:T(8,128)S(1)}, u32[]{:S(2)}) copy-start(f32[2,20,48,128]{3,2,1,0:T(8,128)S(1)} %get-tuple-element.37.d_in_ref) | copy-start | bytes 2949124
  21.3 1.3 %collective-permute-start.4 = (bf16[5,9,128]{2,1,0:T(8,128)(2,1)S(1)}, bf16[5,9,128]{2,1,0:T(8,128)(2,1)S(1)}, u32[]{:S(2)}, u32[]{:S(2)}) collective-permute-start(bf16[5,9,128]{2,1,0:T(8,128)(2,1)S(1)} %get-tuple-element.34), channel_id=1, source_target_pairs={{0,8},{16,24},{32,40},{48,56},{64,72},{80,88},{96,104},{112,120},{... | collective-permute-start | bytes 34568 | tf_op jit(solution)/shard_map/ppermute | solution.py:447
  21.7 1.0 %collective-permute-start.5 = (bf16[5,9,128]{2,1,0:T(8,128)(2,1)S(1)}, bf16[5,9,128]{2,1,0:T(8,128)(2,1)S(1)}, u32[]{:S(2)}, u32[]{:S(2)}) collective-permute-start(bf16[5,9,128]{2,1,0:T(8,128)(2,1)S(1)} %get-tuple-element.35), channel_id=1, source_target_pairs={{8,16},{24,32},{40,48},{56,64},{72,80},{88,96},{104,112},{120,128}... | collective-permute-start | bytes 34568 | tf_op jit(solution)/shard_map/ppermute | solution.py:447
  22.6 29.8 %all-to-all-start = ((f32[32,8,128]{2,1,0:T(8,128)}), f32[32,8,128]{2,1,0:T(8,128)S(1)}, u32[]{:S(2)}, u32[]{:S(2)}) async-start(f32[32,8,128]{2,1,0:T(8,128)} %get-tuple-element.36), calls=%async_computation | async-start | bytes 262144 | tf_op jit(solution)/shard_map/all_to_all | solution.py:498
  41.7 10.8 %copy-start.2 = (f32[2,328,128]{2,1,0:T(8,128)S(1)}, f32[2,328,128]{2,1,0:T(8,128)}, u32[]{:S(2)}) copy-start(f32[2,328,128]{2,1,0:T(8,128)} %constant.35.clone.mx_ref) | copy-start | bytes 1007620
  54.2 13.2 %all-to-all-start.1 = ((bf16[8,240,128]{2,1,0:T(8,128)(2,1)}), bf16[8,240,128]{2,1,0:T(8,128)(2,1)S(1)}, u32[]{:S(2)}, u32[]{:S(2)}) async-start(bf16[8,240,128]{2,1,0:T(8,128)(2,1)} %spread.1), calls=%async_computation.1 | async-start | bytes 983040 | tf_op jit(solution)/shard_map/all_to_all | solution.py:510
  58.6 1.2 %copy-start.5 = (f32[2,20,48,128]{3,2,1,0:T(8,128)S(1)}, f32[2,20,48,128]{3,2,1,0:T(8,128)}, u32[]{:S(2)}) copy-start(f32[2,20,48,128]{3,2,1,0:T(8,128)} %copy-done.4) | copy-start | bytes 2949124
  59.8 7.5 %copy-start.1 = (f32[16,88,128]{2,1,0:T(8,128)S(1)}, f32[16,88,128]{2,1,0:T(8,128)}, u32[]{:S(2)}) copy-start(f32[16,88,128]{2,1,0:T(8,128)} %constant.36.clone.my_ref) | copy-start | bytes 2162692
  59.8 7.5 %copy-start.3 = (f32[512,128]{1,0:T(8,128)S(1)}, f32[512,128]{1,0:T(8,128)}, u32[]{:S(2)}) copy-start(f32[512,128]{1,0:T(8,128)} %constant.37.clone.mz_ref) | copy-start | bytes 786436

commit v5 on v4

--- a/solution.py
+++ b/solution.py
@@ -14,7 +14,6 @@
 REACH = 10
 TAPS = 21
 GROUP = 3
-SPLIT = 9
 
 
 def weight_np(offset):
@@ -85,23 +84,17 @@
     return (lax.broadcasted_iota(jnp.int32, shape, 0), lax.broadcasted_iota(jnp.int32, shape, 1))
 
 
-def vmem_call(body, out_shape, scratch, name, args, smem=0, flops=0, hbm_in=(), hbm_out=()):
+def vmem_call(body, out_shape, scratch, name, args, smem=0, flops=0, limit=8):
     def spec(space):
         return pl.BlockSpec(memory_space=space)
 
-    in_specs = [spec(pltpu.SMEM)] * smem + [spec(pltpu.VMEM)] * (len(args) - smem)
-    for k in hbm_in:
-        in_specs[k] = spec(pltpu.HBM)
-    out_specs = [spec(pltpu.VMEM)] * len(out_shape)
-    for k in hbm_out:
-        out_specs[k] = spec(pltpu.HBM)
     return pl.pallas_call(
         body,
         out_shape=out_shape,
-        in_specs=in_specs,
-        out_specs=out_specs,
+        in_specs=[spec(pltpu.SMEM)] * smem + [spec(pltpu.VMEM)] * (len(args) - smem),
+        out_specs=[spec(pltpu.VMEM)] * len(out_shape),
         scratch_shapes=scratch,
-        compiler_params=pltpu.CompilerParams(vmem_limit_bytes=24 << 20),
+        compiler_params=pltpu.CompilerParams(vmem_limit_bytes=limit << 20),
         cost_estimate=pl.CostEstimate(flops=flops, bytes_accessed=1 << 16, transcendentals=0),
         name=name,
     )(*args)
@@ -111,30 +104,35 @@
     return index % 2 == 0
 
 
-def rim_kernel(where_ref, blk_ref, near_ref, next_ref, first_ref, second_ref, wide):
+def rim_kernel(where_ref, blk_ref, near_ref, next_ref, first_ref, second_ref, wide, dense):
     even_x = even(where_ref[0])
     even_y = even(where_ref[1])
     near, other = near_ref[...].astype(f32), next_ref[...].astype(f32)
     wide[0:10] = jnp.where(even_x, other, near)
     wide[10:30] = blk_ref[...].astype(f32)
     wide[30:40] = jnp.where(even_x, near, other)
-    low, high = wide[:, 0:10, :], wide[:, 10:20, :]
-    first_ref[...] = jnp.where(even_y, high, low).astype(bf16)
-    second_ref[...] = jnp.where(even_y, low, high).astype(bf16)
+    for x in range(40):
+        low, high = wide[x, 0:10, :], wide[x, 10:20, :]
+        dense[0, 10 * x : 10 * x + 10, :] = jnp.where(even_y, high, low)
+        dense[1, 10 * x : 10 * x + 10, :] = jnp.where(even_y, low, high)
+    first_ref[...] = dense[0].astype(bf16)
+    second_ref[...] = dense[1].astype(bf16)
 
 
 def restrict_kernel(
     where_ref, blk_ref, near_x_ref, next_x_ref, near_y_ref, next_y_ref,
     d_out_ref, first_ref, second_ref, own_ref, out_ref,
-    d_ref, planes, cells, mid, pay, sem,
+    d_ref, dense, planes, cells, mid, pay,
 ):
     even_x = even(where_ref[0])
     even_y = even(where_ref[1])
+    near, other = near_y_ref[...].astype(f32), next_y_ref[...].astype(f32)
+    dense[0] = jnp.where(even_y, other, near)
+    dense[1] = jnp.where(even_y, near, other)
     for x in range(40):
         p, i = x % 2, x // 2
-        near, other = near_y_ref[x].astype(f32), next_y_ref[x].astype(f32)
-        d_ref[p, i, 0:10, :] = jnp.where(even_y, other, near)
-        d_ref[p, i, 30:40, :] = jnp.where(even_y, near, other)
+        d_ref[p, i, 0:10, :] = dense[0, 10 * x : 10 * x + 10, :]
+        d_ref[p, i, 30:40, :] = dense[1, 10 * x : 10 * x + 10, :]
         if 10 <= x < 30:
             centre = blk_ref[x - 10].astype(f32)
         else:
@@ -142,9 +140,7 @@
             low, high = (other, near) if x < 10 else (near, other)
             centre = jnp.where(even_x, low, high)
         d_ref[p, i, 10:30, :] = centre
-        d_ref[p, i, 40:48, :] = jnp.zeros((8, 128), f32)
-    save = pltpu.make_async_copy(d_ref, d_out_ref, sem)
-    save.start()
+        d_out_ref[x] = d_ref[p, i, 0:40, :].astype(bf16)
 
     def fine(x):
         return d_ref[x % 2, x // 2]
@@ -210,16 +206,16 @@
     row = pay[...]
     for k in range(out_ref.shape[0]):
         out_ref[k] = row
-    save.wait()
 
 
 def fine_kernel(lo, hi, first, d_in_ref, v_ref, *refs):
     if first:
-        out_ref, w0, w1, e0, e1, d_ref, sem = refs
+        out_ref, w0, w1, e0, e1, d_ref = refs
     else:
-        acc_ref, out_ref, w0, w1, e0, e1, d_ref, sem = refs
-    load = pltpu.make_async_copy(d_in_ref, d_ref, sem)
-    load.start()
+        acc_ref, out_ref, w0, w1, e0, e1, d_ref = refs
+    for x in range(40):
+        d_ref[x % 2, x // 2, 0:40, :] = d_in_ref[x].astype(f32)
+        d_ref[x % 2, x // 2, 40:48, :] = jnp.zeros((8, 128), f32)
     r, c = iota2((128, 128))
     mask = jnp.abs(r - c) <= REACH
     zero = jnp.zeros((128, 128), bf16)
@@ -255,7 +251,6 @@
         out_ref[...] += jnp.dot(lhs, w[...], preferred_element_type=f32)
 
     build(w0, lo)
-    load.wait()
     out_ref[...] = jnp.zeros((240, 256), f32) if first else acc_ref[...]
 
     def step(t, _):
@@ -278,11 +273,11 @@
         [jax.ShapeDtypeStruct((240, 256), f32)],
         [pltpu.VMEM((GROUP * 2816, 256), bf16)] * 2
         + [pltpu.VMEM((GROUP, 2, 480, 256), bf16)] * 2
-        + [pltpu.VMEM((2, 20, 48, 128), f32), pltpu.SemaphoreType.DMA(())],
+        + [pltpu.VMEM((2, 20, 48, 128), f32)],
         "fine_sum",
         (d, v) if acc is None else (d, v, acc),
         flops=(hi - lo) * 2 * 240 * 2816 * 256,
-        hbm_in=(0,),
+        limit=20,
     )[0]
 
 
@@ -458,8 +453,8 @@
     near_x, next_x = swap(jnp.where(even_x, high, low), jnp.where(even_x, low, high), "gx")
     first, second = vmem_call(
         rim_kernel,
-        [shape((40, 10, 128), bf16)] * 2,
-        [pltpu.VMEM((40, 20, 128), f32)],
+        [shape((400, 128), bf16)] * 2,
+        [pltpu.VMEM((40, 20, 128), f32), pltpu.VMEM((2, 400, 128), f32)],
         "rim",
         (where, charges, near_x, next_x),
         smem=1,
@@ -474,7 +469,7 @@
     d, first, second, own, coarse = vmem_call(
         restrict_kernel,
         [
-            shape((2, 20, 48, 128), f32),
+            shape((40, 40, 128), bf16),
             shape((5, 9, 128), bf16),
             shape((5, 9, 128), bf16),
             shape((5, 16, 128), bf16),
@@ -482,22 +477,18 @@
         ],
         [
             pltpu.VMEM((2, 20, 48, 128), f32),
+            pltpu.VMEM((2, 400, 128), f32),
             pltpu.VMEM((16, 48, 128), f32),
             pltpu.VMEM((256, 128), f32),
             pltpu.VMEM((9, 24, 128), f32),
             pltpu.VMEM((8, 128), f32),
-            pltpu.SemaphoreType.DMA(()),
         ],
         "restrict",
         (where, charges, near_x, next_x, near_y, next_y),
         smem=1,
-        hbm_out=(0,),
     )
     near_m, next_m = swap(first, second, "gx")
-    coarse, near_m, next_m = lax.optimization_barrier((coarse, near_m, next_m))
     coarse = lax.all_to_all(coarse, "gx", 0, 0)
-    fine = fine_sum(0, SPLIT, d, near)
-    coarse, fine = lax.optimization_barrier((coarse, fine))
     parts = vmem_call(
         spread_kernel,
         [shape((count_y, 240, 128), bf16)],
@@ -508,7 +499,7 @@
     )[0]
     parts, near = lax.optimization_barrier((parts, near))
     parts = lax.all_to_all(parts, "gy", 0, 0)
-    fine = fine_sum(SPLIT, TAPS, d, near, fine)
+    fine = fine_sum(0, TAPS, d, near)
     return vmem_call(
         final_kernel,
         [shape((20, 20, 128), f32)],

time: 72.6 us -> 64.4 us (0.89)
  starting transfers between devices: 35.4 us -> 29 us
  Pallas kernels: 20.3 us -> 18.6 us
  local copies, waits for them, and re-layouts: 2.74 us -> 1.54 us
    all_to_all x1, starting transfers between devices: 19.1 us -> 12.2 us  [per_device(): coarse = lax.all_to_all(coarse, 'gx', 0, 0)]
    all_to_all x1, waiting for transfers between devices: 5.88 us -> 9.48 us  [per_device(): coarse = lax.all_to_all(coarse, 'gx', 0, 0)]
    pallas_call x6 -> x5, Pallas kernels: 20.3 us -> 18.6 us  [vmem_call(): pl.pallas_call(body, out_shape=out_shape, in_specs=[spec(pltpu.SMEM)] * s...]
    all_to_all x1, waiting for transfers between devices: 1.53 us -> 0.01 us  [per_device(): parts = lax.all_to_all(parts, 'gy', 0, 0)]
    ppermute x3, waiting for transfers between devices: 3.51 us -> 2.18 us  [swap(): lax.ppermute(second, axis, both(others))]
    unnamed x18 -> x14, local copies, waits for them, and re-layouts: 2.03 us -> 0.82 us
  transfers between devices with their start and end apart: 8 -> 8, of which waited for: 5 -> 4; matrix products, arithmetic and copies ran while one was open for 2% -> 2% of each run, Pallas kernels for 15% -> 15%
where the time goes in v5:
time: 64.4 us; the launch traced here: 63.6 us
  starting transfers between devices  29 us (45%)
  Pallas kernels  18.6 us (29%)
  waiting for transfers between devices  12.7 us (20%)
  local copies, waits for them, and re-layouts  1.54 us (2%)
  other arithmetic  0.99 us (2%)
    pallas_call x5, Pallas kernels, vmem_call(): pl.pallas_call(body, out_shape=out_shape, in_specs=[spec(pltpu.SMEM)] * s...  18.6 us
    all_to_all x1, starting transfers between devices, per_device(): coarse = lax.all_to_all(coarse, 'gx', 0, 0)  12.2 us
    all_to_all x1, waiting for transfers between devices, per_device(): coarse = lax.all_to_all(coarse, 'gx', 0, 0)  9.48 us
    ppermute x3, starting transfers between devices, swap(): lax.ppermute(second, axis, both(others))  6.26 us
    ppermute x3, starting transfers between devices, swap(): lax.ppermute(first, axis, both(pairs))  5.59 us
    all_to_all x1, starting transfers between devices, per_device(): parts = lax.all_to_all(parts, 'gy', 0, 0)  4.89 us
    ppermute x3, waiting for transfers between devices, swap(): lax.ppermute(second, axis, both(others))  2.18 us
  transfers between devices with their start and end apart: 8, of which 4 were waited for; matrix products, arithmetic and copies ran while one was open for 2% of the time, Pallas kernels for 15%

profile of v5, /device:TPU:2, one launch (start us, length us, event | category | flops | bytes accessed | tf_op | source)
XLA Modules:
  0.0 63.6 jit_solution(17475412841950393584)
XLA Ops:
  0.0 0.9 %broadcast_select_fusion = (bf16[10,20,128]{2,1,0:T(8,128)(2,1)S(1)}, bf16[10,20,128]{2,1,0:T(8,128)(2,1)S(1)}) fusion(pred[]{:T(512)S(6)} %eq.5, bf16[20,20,128]{2,1,0:T(8,128)(2,1)} %blk_ref.3), kind=kLoop, calls=%fused_computation | loop fusion | flops 51200 | bytes 204801 | tf_op jit(solution)/shard_map/jit(_where)/select_n | solution.py:453
  0.9 0.7 %collective-permute-start.1 = (bf16[10,20,128]{2,1,0:T(8,128)(2,1)S(1)}, bf16[10,20,128]{2,1,0:T(8,128)(2,1)S(1)}, u32[]{:S(2)}, u32[]{:S(2)}) collective-permute-start(bf16[10,20,128]{2,1,0:T(8,128)(2,1)S(1)} %get-tuple-element.37), channel_id=1, source_target_pairs={{8,16},{24,32},{40,48},{56,64},{72,80},{88,96},{104,112},{120,128}... | collective-permute-start | bytes 153608 | tf_op jit(solution)/shard_map/ppermute | solution.py:442
  1.6 3.6 %collective-permute-start = (bf16[10,20,128]{2,1,0:T(8,128)(2,1)S(1)}, bf16[10,20,128]{2,1,0:T(8,128)(2,1)S(1)}, u32[]{:S(2)}, u32[]{:S(2)}) collective-permute-start(bf16[10,20,128]{2,1,0:T(8,128)(2,1)S(1)} %get-tuple-element.38), channel_id=1, source_target_pairs={{0,8},{16,24},{32,40},{48,56},{64,72},{80,88},{96,104},{112,120},{... | collective-permute-start | bytes 153608 | tf_op jit(solution)/shard_map/ppermute | solution.py:442
  5.2 0.8 %collective-permute-done.near_ref.near_x_ref = bf16[10,20,128]{2,1,0:T(8,128)(2,1)S(1)} collective-permute-done((bf16[10,20,128]{2,1,0:T(8,128)(2,1)S(1)}, bf16[10,20,128]{2,1,0:T(8,128)(2,1)S(1)}, u32[]{:S(2)}, u32[]{:S(2)}) %collective-permute-start) | collective-permute-done | bytes 51232 | tf_op jit(solution)/shard_map/ppermute | solution.py:442
  6.1 0.6 %rim.1 = (bf16[400,128]{1,0:T(8,128)(2,1)S(1)}, bf16[400,128]{1,0:T(8,128)(2,1)S(1)}) custom-call(s32[2]{0:T(128)S(1)} %pad_add_fusion.where_ref, bf16[20,20,128]{2,1,0:T(8,128)(2,1)S(1)} %copy-done, bf16[10,20,128]{2,1,0:T(8,128)(2,1)S(1)} %collective-permute-done.near_ref.near_x_ref, bf16[10,20,128]{2,1,0:T(8,128)(2,1)S(1)} %collective-permute-done.1.next_ref.next_x_ref), custom_call_target="tpu_custom_call" | custom-call | bytes 65536 | tf_op jit(solution)/shard_map/rim/pallas_call | solution.py:91
  6.7 1.7 %collective-permute-start.2 = (bf16[400,128]{1,0:T(8,128)(2,1)S(1)}, bf16[400,128]{1,0:T(8,128)(2,1)S(1)}, u32[]{:S(2)}, u32[]{:S(2)}) collective-permute-start(bf16[400,128]{1,0:T(8,128)(2,1)S(1)} %get-tuple-element.23), channel_id=1, source_target_pairs={{0,1},{2,3},{4,5},{6,7},{1,0},{3,2},{5,4},{7,6},{8,9},{10,11},{12,... | collective-permute-start | bytes 307208 | tf_op jit(solution)/shard_map/ppermute | solution.py:442
  8.4 4.9 %collective-permute-start.3 = (bf16[400,128]{1,0:T(8,128)(2,1)S(1)}, bf16[400,128]{1,0:T(8,128)(2,1)S(1)}, u32[]{:S(2)}, u32[]{:S(2)}) collective-permute-start(bf16[400,128]{1,0:T(8,128)(2,1)S(1)} %get-tuple-element.24), channel_id=1, source_target_pairs={{1,2},{3,4},{5,6},{2,1},{4,3},{6,5},{9,10},{11,12},{13,14},{10,9},... | collective-permute-start | bytes 307208 | tf_op jit(solution)/shard_map/ppermute | solution.py:442
  13.3 0.5 copy.8
  13.8 0.3 reshape.4
  14.1 0.4 copy-done.6
  14.5 0.3 fusion.1.far_ref
  14.8 0.4 copy-done.5
  15.2 0.3 fusion.v_ref.near_ref
  15.5 2.2 %collective-permute-done.3.next_y_ref = bf16[400,128]{1,0:T(8,128)(2,1)S(1)} collective-permute-done((bf16[400,128]{1,0:T(8,128)(2,1)S(1)}, bf16[400,128]{1,0:T(8,128)(2,1)S(1)}, u32[]{:S(2)}, u32[]{:S(2)}) %collective-permute-start.3) | collective-permute-done | bytes 102432 | tf_op jit(solution)/shard_map/ppermute | solution.py:442
  17.7 2.0 %restrict.1 = (bf16[40,40,128]{2,1,0:T(8,128)(2,1)S(1)}, bf16[5,9,128]{2,1,0:T(8,128)(2,1)S(1)}, bf16[5,9,128]{2,1,0:T(8,128)(2,1)S(1)}, bf16[5,16,128]{2,1,0:T(8,128)(2,1)S(1)}, f32[32,8,128]{2,1,0:T(8,128)}) custom-call(s32[2]{0:T(128)S(1)} %pad_add_fusion.where_ref, bf16[20,20,128]{2,1,0:T(8,128)(2,1)S(1)} %copy-done, ...), custom_call_target="tpu_custom_call" | custom-call | bytes 65536 | tf_op jit(solution)/shard_map/restrict/pallas_call | solution.py:91
  19.7 12.2 %all-to-all-start = ((f32[32,8,128]{2,1,0:T(8,128)}), f32[32,8,128]{2,1,0:T(8,128)S(1)}, u32[]{:S(2)}, u32[]{:S(2)}) async-start(f32[32,8,128]{2,1,0:T(8,128)} %get-tuple-element.28), calls=%async_computation | async-start | bytes 262144 | tf_op jit(solution)/shard_map/all_to_all | solution.py:491
  31.9 0.4 collective-permute-start.4
  32.3 0.7 %collective-permute-start.5 = (bf16[5,9,128]{2,1,0:T(8,128)(2,1)S(1)}, bf16[5,9,128]{2,1,0:T(8,128)(2,1)S(1)}, u32[]{:S(2)}, u32[]{:S(2)}) collective-permute-start(bf16[5,9,128]{2,1,0:T(8,128)(2,1)S(1)} %get-tuple-element.31), channel_id=1, source_target_pairs={{8,16},{24,32},{40,48},{56,64},{72,80},{88,96},{104,112},{120,128}... | collective-permute-start | bytes 34568 | tf_op jit(solution)/shard_map/ppermute | solution.py:442
  32.9 0.3 collective-permute-done.4.near_ref
  33.2 9.5 %all-to-all-done.recv_ref = f32[32,8,128]{2,1,0:T(8,128)S(1)} async-done(((f32[32,8,128]{2,1,0:T(8,128)}), f32[32,8,128]{2,1,0:T(8,128)S(1)}, u32[]{:S(2)}, u32[]{:S(2)}) %all-to-all-start) | async-done | bytes 131104 | tf_op jit(solution)/shard_map/all_to_all | solution.py:491
  42.7 1.7 %spread.1 = bf16[8,240,128]{2,1,0:T(8,128)(2,1)} custom-call(s32[2]{0:T(128)S(1)} %pad_add_fusion.where_ref, f32[32,8,128]{2,1,0:T(8,128)S(1)} %all-to-all-done.recv_ref, f32[2,328,128]{2,1,0:T(8,128)S(1)} %copy-done.2, bf16[5,16,128]{2,1,0:T(8,128)(2,1)S(1)} %get-tuple-element.29.own_ref, bf16[5,9,128]{2,1,0:T(8,128)(2,1)S(1)} %collective-permute-done.4.near_ref, ...), custom_call_target="tpu_custom_call" | custom-call | bytes 65536 | tf_op jit(solution)/shard_map/spread/pallas_call | solution.py:91
  44.4 4.9 %all-to-all-start.1 = ((bf16[8,240,128]{2,1,0:T(8,128)(2,1)}), bf16[8,240,128]{2,1,0:T(8,128)(2,1)S(1)}, u32[]{:S(2)}, u32[]{:S(2)}) async-start(bf16[8,240,128]{2,1,0:T(8,128)(2,1)} %spread.1), calls=%async_computation.1 | async-start | bytes 983040 | tf_op jit(solution)/shard_map/all_to_all | solution.py:501
  49.3 9.5 %fine_sum.1.fine_ref = f32[240,256]{1,0:T(8,128)S(1)} custom-call(bf16[40,40,128]{2,1,0:T(8,128)(2,1)S(1)} %get-tuple-element.36.d_in_ref, f32[882,128]{1,0:T(8,128)S(1)} %fusion.v_ref.near_ref), custom_call_target="tpu_custom_call" | custom-call | flops 7266631680 | bytes 65536 | tf_op jit(solution)/shard_map/fine_sum/pallas_call | solution.py:91
  58.8 4.8 %final.1 = f32[20,20,128]{2,1,0:T(8,128)} custom-call(s32[2]{0:T(128)S(1)} %pad_add_fusion.where_ref, bf16[8,240,128]{2,1,0:T(8,128)(2,1)S(1)} %all-to-all-done.1.recv_ref, f32[16,88,128]{2,1,0:T(8,128)S(1)} %copy-done.1, f32[512,128]{1,0:T(8,128)S(1)} %copy-done.3, f32[882,128]{1,0:T(8,128)S(1)} %fusion.v_ref.near_ref, f32[882,128]{1,0:T(8,128)S(1)} %fusion.1.far_ref, ...), custom_call_target="tpu_custom_call" | custom-call | bytes 65536 | tf_op jit(solution)/shard_map/final/pallas_call | solution.py:91
  (17 shorter events, 0.1 us)
Async XLA Ops:
  0.0 6.1 %copy-start = (bf16[20,20,128]{2,1,0:T(8,128)(2,1)S(1)}, bf16[20,20,128]{2,1,0:T(8,128)(2,1)}, u32[]{:S(2)}) copy-start(bf16[20,20,128]{2,1,0:T(8,128)(2,1)} %blk_ref.3) | copy-start | bytes 307204
  0.0 13.3 %copy-start.4 = (bf16[2,21,21,21]{3,0,2,1:T(2,128)(2,1)S(1)}, bf16[2,21,21,21]{3,0,2,1:T(2,128)(2,1)}, u32[]{:S(2)}) copy-start(bf16[2,21,21,21]{3,0,2,1:T(2,128)(2,1)} %param.8) | copy-start | bytes 111136
  0.9 4.3 %collective-permute-start.1 = (bf16[10,20,128]{2,1,0:T(8,128)(2,1)S(1)}, bf16[10,20,128]{2,1,0:T(8,128)(2,1)S(1)}, u32[]{:S(2)}, u32[]{:S(2)}) collective-permute-start(bf16[10,20,128]{2,1,0:T(8,128)(2,1)S(1)} %get-tuple-element.37), channel_id=1, source_target_pairs={{8,16},{24,32},{40,48},{56,64},{72,80},{88,96},{104,112},{120,128}... | collective-permute-start | bytes 153608 | tf_op jit(solution)/shard_map/ppermute | solution.py:442
  1.6 4.5 %collective-permute-start = (bf16[10,20,128]{2,1,0:T(8,128)(2,1)S(1)}, bf16[10,20,128]{2,1,0:T(8,128)(2,1)S(1)}, u32[]{:S(2)}, u32[]{:S(2)}) collective-permute-start(bf16[10,20,128]{2,1,0:T(8,128)(2,1)S(1)} %get-tuple-element.38), channel_id=1, source_target_pairs={{0,8},{16,24},{32,40},{48,56},{64,72},{80,88},{96,104},{112,120},{... | collective-permute-start | bytes 153608 | tf_op jit(solution)/shard_map/ppermute | solution.py:442
  6.7 8.8 %collective-permute-start.2 = (bf16[400,128]{1,0:T(8,128)(2,1)S(1)}, bf16[400,128]{1,0:T(8,128)(2,1)S(1)}, u32[]{:S(2)}, u32[]{:S(2)}) collective-permute-start(bf16[400,128]{1,0:T(8,128)(2,1)S(1)} %get-tuple-element.23), channel_id=1, source_target_pairs={{0,1},{2,3},{4,5},{6,7},{1,0},{3,2},{5,4},{7,6},{8,9},{10,11},{12,... | collective-permute-start | bytes 307208 | tf_op jit(solution)/shard_map/ppermute | solution.py:442
  8.4 9.3 %collective-permute-start.3 = (bf16[400,128]{1,0:T(8,128)(2,1)S(1)}, bf16[400,128]{1,0:T(8,128)(2,1)S(1)}, u32[]{:S(2)}, u32[]{:S(2)}) collective-permute-start(bf16[400,128]{1,0:T(8,128)(2,1)S(1)} %get-tuple-element.24), channel_id=1, source_target_pairs={{1,2},{3,4},{5,6},{2,1},{4,3},{6,5},{9,10},{11,12},{13,14},{10,9},... | collective-permute-start | bytes 307208 | tf_op jit(solution)/shard_map/ppermute | solution.py:442
  13.8 0.7 %copy-start.6 = (bf16[21,128]{1,0:T(8,128)(2,1)S(1)}, bf16[21,128]{1,0:T(8,128)(2,1)}, u32[]{:S(2)}) copy-start(bf16[21,128]{1,0:T(8,128)(2,1)} %constant.34.clone) | copy-start | bytes 16132
  14.5 0.7 %copy-start.5 = (bf16[21,128]{1,0:T(8,128)(2,1)S(1)}, bf16[21,128]{1,0:T(8,128)(2,1)}, u32[]{:S(2)}) copy-start(bf16[21,128]{1,0:T(8,128)(2,1)} %constant.33.clone) | copy-start | bytes 16132
  15.5 27.2 %copy-start.2 = (f32[2,328,128]{2,1,0:T(8,128)S(1)}, f32[2,328,128]{2,1,0:T(8,128)}, u32[]{:S(2)}) copy-start(f32[2,328,128]{2,1,0:T(8,128)} %constant.35.clone.mx_ref) | copy-start | bytes 1007620
  19.7 23.0 %all-to-all-start = ((f32[32,8,128]{2,1,0:T(8,128)}), f32[32,8,128]{2,1,0:T(8,128)S(1)}, u32[]{:S(2)}, u32[]{:S(2)}) async-start(f32[32,8,128]{2,1,0:T(8,128)} %get-tuple-element.28), calls=%async_computation | async-start | bytes 262144 | tf_op jit(solution)/shard_map/all_to_all | solution.py:491
  31.9 1.3 %collective-permute-start.4 = (bf16[5,9,128]{2,1,0:T(8,128)(2,1)S(1)}, bf16[5,9,128]{2,1,0:T(8,128)(2,1)S(1)}, u32[]{:S(2)}, u32[]{:S(2)}) collective-permute-start(bf16[5,9,128]{2,1,0:T(8,128)(2,1)S(1)} %get-tuple-element.30), channel_id=1, source_target_pairs={{0,8},{16,24},{32,40},{48,56},{64,72},{80,88},{96,104},{112,120},{... | collective-permute-start | bytes 34568 | tf_op jit(solution)/shard_map/ppermute | solution.py:442
  32.3 0.9 %collective-permute-start.5 = (bf16[5,9,128]{2,1,0:T(8,128)(2,1)S(1)}, bf16[5,9,128]{2,1,0:T(8,128)(2,1)S(1)}, u32[]{:S(2)}, u32[]{:S(2)}) collective-permute-start(bf16[5,9,128]{2,1,0:T(8,128)(2,1)S(1)} %get-tuple-element.31), channel_id=1, source_target_pairs={{8,16},{24,32},{40,48},{56,64},{72,80},{88,96},{104,112},{120,128}... | collective-permute-start | bytes 34568 | tf_op jit(solution)/shard_map/ppermute | solution.py:442
  44.4 14.4 %all-to-all-start.1 = ((bf16[8,240,128]{2,1,0:T(8,128)(2,1)}), bf16[8,240,128]{2,1,0:T(8,128)(2,1)S(1)}, u32[]{:S(2)}, u32[]{:S(2)}) async-start(bf16[8,240,128]{2,1,0:T(8,128)(2,1)} %spread.1), calls=%async_computation.1 | async-start | bytes 983040 | tf_op jit(solution)/shard_map/all_to_all | solution.py:501
  49.2 9.6 %copy-start.1 = (f32[16,88,128]{2,1,0:T(8,128)S(1)}, f32[16,88,128]{2,1,0:T(8,128)}, u32[]{:S(2)}) copy-start(f32[16,88,128]{2,1,0:T(8,128)} %constant.36.clone.my_ref) | copy-start | bytes 2162692
  49.3 9.6 %copy-start.3 = (f32[512,128]{1,0:T(8,128)S(1)}, f32[512,128]{1,0:T(8,128)}, u32[]{:S(2)}) copy-start(f32[512,128]{1,0:T(8,128)} %constant.37.clone.mz_ref) | copy-start | bytes 786436

commit v6 on v5

--- a/solution.py
+++ b/solution.py
@@ -14,6 +14,7 @@
 REACH = 10
 TAPS = 21
 GROUP = 3
+SPLIT = 6
 
 
 def weight_np(offset):
@@ -104,7 +105,7 @@
     return index % 2 == 0
 
 
-def rim_kernel(where_ref, blk_ref, near_ref, next_ref, first_ref, second_ref, wide, dense):
+def rim_kernel(where_ref, blk_ref, near_ref, next_ref, second_ref, first_ref, wide, dense):
     even_x = even(where_ref[0])
     even_y = even(where_ref[1])
     near, other = near_ref[...].astype(f32), next_ref[...].astype(f32)
@@ -120,8 +121,8 @@
 
 
 def restrict_kernel(
-    where_ref, blk_ref, near_x_ref, next_x_ref, near_y_ref, next_y_ref,
-    d_out_ref, first_ref, second_ref, own_ref, out_ref,
+    where_ref, blk_ref, near_x_ref, next_x_ref, next_y_ref, near_y_ref,
+    d_out_ref, second_ref, first_ref, own_ref, out_ref,
     d_ref, dense, planes, cells, mid, pay,
 ):
     even_x = even(where_ref[0])
@@ -281,7 +282,7 @@
     )[0]
 
 
-def spread_kernel(where_ref, recv_ref, mx_ref, own_ref, near_ref, next_ref, out_ref, buf):
+def spread_kernel(where_ref, recv_ref, mx_ref, own_ref, next_ref, near_ref, out_ref, buf):
     even_x = even(where_ref[0])
     start = 10 * where_ref[0]
     halves = [mx_ref[h, pl.ds(start, 16), :] for h in range(2)]
@@ -439,7 +440,8 @@
     def both(ends):
         return ends + [(b, a) for a, b in ends]
 
-    return lax.ppermute(first, axis, both(pairs)), lax.ppermute(second, axis, both(others))
+    second = lax.ppermute(second, axis, both(others))
+    return lax.ppermute(first, axis, both(pairs)), second
 
 
 def per_device(charges, kernels):
@@ -451,7 +453,7 @@
     low, high = charges[:10], charges[10:]
     even_x = even(lax.axis_index("gx"))
     near_x, next_x = swap(jnp.where(even_x, high, low), jnp.where(even_x, low, high), "gx")
-    first, second = vmem_call(
+    second, first = vmem_call(
         rim_kernel,
         [shape((400, 128), bf16)] * 2,
         [pltpu.VMEM((40, 20, 128), f32), pltpu.VMEM((2, 400, 128), f32)],
@@ -465,8 +467,8 @@
         for m in spots_np()
     )
     near_y, next_y = swap(first, second, "gy")
-    near_y, next_y, near, far = lax.optimization_barrier((near_y, next_y, near, far))
-    d, first, second, own, coarse = vmem_call(
+    next_y, near_y, near, far = lax.optimization_barrier((next_y, near_y, near, far))
+    d, second, first, own, coarse = vmem_call(
         restrict_kernel,
         [
             shape((40, 40, 128), bf16),
@@ -484,22 +486,25 @@
             pltpu.VMEM((8, 128), f32),
         ],
         "restrict",
-        (where, charges, near_x, next_x, near_y, next_y),
+        (where, charges, near_x, next_x, next_y, near_y),
         smem=1,
     )
     near_m, next_m = swap(first, second, "gx")
     coarse = lax.all_to_all(coarse, "gx", 0, 0)
+    near, near_m = lax.optimization_barrier((near, near_m))
+    fine = fine_sum(0, SPLIT, d, near)
+    coarse, fine = lax.optimization_barrier((coarse, fine))
     parts = vmem_call(
         spread_kernel,
         [shape((count_y, 240, 128), bf16)],
         [pltpu.VMEM((176, 128), f32)],
         "spread",
-        (where, coarse, jnp.asarray(matrix_x_np(spread)), own, near_m, next_m),
+        (where, coarse, jnp.asarray(matrix_x_np(spread)), own, next_m, near_m),
         smem=1,
     )[0]
     parts, near = lax.optimization_barrier((parts, near))
     parts = lax.all_to_all(parts, "gy", 0, 0)
-    fine = fine_sum(0, TAPS, d, near)
+    fine = fine_sum(SPLIT, TAPS, d, near, fine)
     return vmem_call(
         final_kernel,
         [shape((20, 20, 128), f32)],

time: 64.4 us -> 62.6 us (0.972)
  starting transfers between devices: 29 us -> 27.4 us
    all_to_all x1, waiting for transfers between devices: 9.48 us -> 6.45 us  [per_device(): coarse = lax.all_to_all(coarse, 'gx', 0, 0)]
    all_to_all x1, waiting for transfers between devices: 0.01 us -> 1.74 us  [per_device(): parts = lax.all_to_all(parts, 'gy', 0, 0)]
    ppermute x6, waiting for transfers between devices: 3.26 us -> 4.32 us  [the longest x3 3.36 us: swap(): return (lax.ppermute(first, axis, both(pairs)), second)]
    ppermute x6, starting transfers between devices: 11.9 us -> 11.1 us  [the longest x3 7.11 us: swap(): second = lax.ppermute(second, axis, both(others))]
    all_to_all x1, starting transfers between devices: 12.2 us -> 11.5 us  [per_device(): coarse = lax.all_to_all(coarse, 'gx', 0, 0)]
    pallas_call x5 -> x6, Pallas kernels: 18.6 us -> 19 us  [vmem_call(): pl.pallas_call(body, out_shape=out_shape, in_specs=[spec(pltpu.SMEM)] * s...]
  transfers between devices with their start and end apart: 8 -> 8, of which waited for: 4 -> 6; matrix products, arithmetic and copies ran while one was open for 2% -> 2% of each run, Pallas kernels for 15% -> 16%
where the time goes in v6:
time: 62.6 us; the launch traced here: 62.2 us
  starting transfers between devices  27.4 us (44%)
  Pallas kernels  19 us (30%)
  waiting for transfers between devices  12.5 us (20%)
  local copies, waits for them, and re-layouts  1.54 us (2%)
  other arithmetic  0.99 us (2%)
    pallas_call x6, Pallas kernels, vmem_call(): pl.pallas_call(body, out_shape=out_shape, in_specs=[spec(pltpu.SMEM)] * s...  19 us
    all_to_all x1, starting transfers between devices, per_device(): coarse = lax.all_to_all(coarse, 'gx', 0, 0)  11.5 us
    ppermute x3, starting transfers between devices, swap(): second = lax.ppermute(second, axis, both(others))  7.11 us
    all_to_all x1, waiting for transfers between devices, per_device(): coarse = lax.all_to_all(coarse, 'gx', 0, 0)  6.45 us
    all_to_all x1, starting transfers between devices, per_device(): parts = lax.all_to_all(parts, 'gy', 0, 0)  4.73 us
    ppermute x3, starting transfers between devices, swap(): return (lax.ppermute(first, axis, both(pairs)), second)  4.02 us
    ppermute x3, waiting for transfers between devices, swap(): return (lax.ppermute(first, axis, both(pairs)), second)  3.36 us
    all_to_all x1, waiting for transfers between devices, per_device(): parts = lax.all_to_all(parts, 'gy', 0, 0)  1.74 us
  transfers between devices with their start and end apart: 8, of which 6 were waited for; matrix products, arithmetic and copies ran while one was open for 2% of the time, Pallas kernels for 16%

profile of v6, /device:TPU:2, one launch (start us, length us, event | category | flops | bytes accessed | tf_op | source)
XLA Modules:
  0.0 62.2 jit_solution(15349098331528102268)
XLA Ops:
  0.0 0.9 %broadcast_select_fusion = (bf16[10,20,128]{2,1,0:T(8,128)(2,1)S(1)}, bf16[10,20,128]{2,1,0:T(8,128)(2,1)S(1)}) fusion(pred[]{:T(512)S(6)} %eq.5, bf16[20,20,128]{2,1,0:T(8,128)(2,1)} %blk_ref.3), kind=kLoop, calls=%fused_computation | loop fusion | flops 51200 | bytes 204801 | tf_op jit(solution)/shard_map/jit(_where)/select_n | solution.py:455
  0.9 0.7 %collective-permute-start.1 = (bf16[10,20,128]{2,1,0:T(8,128)(2,1)S(1)}, bf16[10,20,128]{2,1,0:T(8,128)(2,1)S(1)}, u32[]{:S(2)}, u32[]{:S(2)}) collective-permute-start(bf16[10,20,128]{2,1,0:T(8,128)(2,1)S(1)} %get-tuple-element.45), channel_id=1, source_target_pairs={{8,16},{24,32},{40,48},{56,64},{72,80},{88,96},{104,112},{120,128}... | collective-permute-start | bytes 153608 | tf_op jit(solution)/shard_map/ppermute | solution.py:443
  1.6 3.6 %collective-permute-start = (bf16[10,20,128]{2,1,0:T(8,128)(2,1)S(1)}, bf16[10,20,128]{2,1,0:T(8,128)(2,1)S(1)}, u32[]{:S(2)}, u32[]{:S(2)}) collective-permute-start(bf16[10,20,128]{2,1,0:T(8,128)(2,1)S(1)} %get-tuple-element.46), channel_id=1, source_target_pairs={{0,8},{16,24},{32,40},{48,56},{64,72},{80,88},{96,104},{112,120},{... | collective-permute-start | bytes 153608 | tf_op jit(solution)/shard_map/ppermute | solution.py:444
  5.2 0.8 %collective-permute-done.near_ref.near_x_ref = bf16[10,20,128]{2,1,0:T(8,128)(2,1)S(1)} collective-permute-done((bf16[10,20,128]{2,1,0:T(8,128)(2,1)S(1)}, bf16[10,20,128]{2,1,0:T(8,128)(2,1)S(1)}, u32[]{:S(2)}, u32[]{:S(2)}) %collective-permute-start) | collective-permute-done | bytes 51232 | tf_op jit(solution)/shard_map/ppermute | solution.py:444
  6.1 0.6 %rim.1 = (bf16[400,128]{1,0:T(8,128)(2,1)S(1)}, bf16[400,128]{1,0:T(8,128)(2,1)S(1)}) custom-call(s32[2]{0:T(128)S(1)} %pad_add_fusion.where_ref, bf16[20,20,128]{2,1,0:T(8,128)(2,1)S(1)} %copy-done, bf16[10,20,128]{2,1,0:T(8,128)(2,1)S(1)} %collective-permute-done.near_ref.near_x_ref, bf16[10,20,128]{2,1,0:T(8,128)(2,1)S(1)} %collective-permute-done.1.next_ref.next_x_ref), custom_call_target="tpu_custom_call" | custom-call | bytes 65536 | tf_op jit(solution)/shard_map/rim/pallas_call | solution.py:92
  6.7 5.8 %collective-permute-start.2 = (bf16[400,128]{1,0:T(8,128)(2,1)S(1)}, bf16[400,128]{1,0:T(8,128)(2,1)S(1)}, u32[]{:S(2)}, u32[]{:S(2)}) collective-permute-start(bf16[400,128]{1,0:T(8,128)(2,1)S(1)} %get-tuple-element.27), channel_id=1, source_target_pairs={{1,2},{3,4},{5,6},{2,1},{4,3},{6,5},{9,10},{11,12},{13,14},{10,9},... | collective-permute-start | bytes 307208 | tf_op jit(solution)/shard_map/ppermute | solution.py:443
  12.6 0.5 copy.8
  13.3 0.4 copy-done.6
  13.8 0.3 fusion.1.far_ref
  14.1 0.4 copy-done.5
  14.5 0.3 fusion.v_ref.near_ref
  14.8 0.9 %collective-permute-done.2.next_y_ref = bf16[400,128]{1,0:T(8,128)(2,1)S(1)} collective-permute-done((bf16[400,128]{1,0:T(8,128)(2,1)S(1)}, bf16[400,128]{1,0:T(8,128)(2,1)S(1)}, u32[]{:S(2)}, u32[]{:S(2)}) %collective-permute-start.2) | collective-permute-done | bytes 102432 | tf_op jit(solution)/shard_map/ppermute | solution.py:443
  15.7 2.3 %collective-permute-done.3.near_y_ref = bf16[400,128]{1,0:T(8,128)(2,1)S(1)} collective-permute-done((bf16[400,128]{1,0:T(8,128)(2,1)S(1)}, bf16[400,128]{1,0:T(8,128)(2,1)S(1)}, u32[]{:S(2)}, u32[]{:S(2)}) %collective-permute-start.3) | collective-permute-done | bytes 102432 | tf_op jit(solution)/shard_map/ppermute | solution.py:444
  18.0 2.0 %restrict.1 = (bf16[40,40,128]{2,1,0:T(8,128)(2,1)S(1)}, bf16[5,9,128]{2,1,0:T(8,128)(2,1)S(1)}, bf16[5,9,128]{2,1,0:T(8,128)(2,1)S(1)}, bf16[5,16,128]{2,1,0:T(8,128)(2,1)S(1)}, f32[32,8,128]{2,1,0:T(8,128)}) custom-call(s32[2]{0:T(128)S(1)} %pad_add_fusion.where_ref, bf16[20,20,128]{2,1,0:T(8,128)(2,1)S(1)} %copy-done, ...), custom_call_target="tpu_custom_call" | custom-call | bytes 65536 | tf_op jit(solution)/shard_map/restrict/pallas_call | solution.py:92
  20.0 11.5 %all-to-all-start = ((f32[32,8,128]{2,1,0:T(8,128)}), f32[32,8,128]{2,1,0:T(8,128)S(1)}, u32[]{:S(2)}, u32[]{:S(2)}) async-start(f32[32,8,128]{2,1,0:T(8,128)} %get-tuple-element.32), calls=%async_computation | async-start | bytes 262144 | tf_op jit(solution)/shard_map/all_to_all | solution.py:493
  31.6 0.4 collective-permute-start.4
  31.9 0.7 %collective-permute-start.5 = (bf16[5,9,128]{2,1,0:T(8,128)(2,1)S(1)}, bf16[5,9,128]{2,1,0:T(8,128)(2,1)S(1)}, u32[]{:S(2)}, u32[]{:S(2)}) collective-permute-start(bf16[5,9,128]{2,1,0:T(8,128)(2,1)S(1)} %get-tuple-element.39), channel_id=1, source_target_pairs={{8,16},{24,32},{40,48},{56,64},{72,80},{88,96},{104,112},{120,128}... | collective-permute-start | bytes 34568 | tf_op jit(solution)/shard_map/ppermute | solution.py:443
  32.8 3.0 %fine_sum.2.refs_0_ = f32[240,256]{1,0:T(8,128)S(1)} custom-call(bf16[40,40,128]{2,1,0:T(8,128)(2,1)S(1)} %get-tuple-element.33.d_in_ref, f32[882,128]{1,0:T(8,128)S(1)} %fusion.v_ref.near_ref), custom_call_target="tpu_custom_call" | custom-call | flops 2076180480 | bytes 65536 | tf_op jit(solution)/shard_map/fine_sum/pallas_call | solution.py:92
  35.9 6.5 %all-to-all-done.recv_ref = f32[32,8,128]{2,1,0:T(8,128)S(1)} async-done(((f32[32,8,128]{2,1,0:T(8,128)}), f32[32,8,128]{2,1,0:T(8,128)S(1)}, u32[]{:S(2)}, u32[]{:S(2)}) %all-to-all-start) | async-done | bytes 131104 | tf_op jit(solution)/shard_map/all_to_all | solution.py:493
  42.3 1.7 %spread.1 = bf16[8,240,128]{2,1,0:T(8,128)(2,1)} custom-call(s32[2]{0:T(128)S(1)} %pad_add_fusion.where_ref, f32[32,8,128]{2,1,0:T(8,128)S(1)} %all-to-all-done.recv_ref, f32[2,328,128]{2,1,0:T(8,128)S(1)} %copy-done.2, bf16[5,16,128]{2,1,0:T(8,128)(2,1)S(1)} %get-tuple-element.38.own_ref, bf16[5,9,128]{2,1,0:T(8,128)(2,1)S(1)} %collective-permute-done.5.next_ref, ...), custom_call_target="tpu_custom_call" | custom-call | bytes 65536 | tf_op jit(solution)/shard_map/spread/pallas_call | solution.py:92
  44.0 4.7 %all-to-all-start.1 = ((bf16[8,240,128]{2,1,0:T(8,128)(2,1)}), bf16[8,240,128]{2,1,0:T(8,128)(2,1)S(1)}, u32[]{:S(2)}, u32[]{:S(2)}) async-start(bf16[8,240,128]{2,1,0:T(8,128)(2,1)} %spread.1), calls=%async_computation.1 | async-start | bytes 983040 | tf_op jit(solution)/shard_map/all_to_all | solution.py:506
  48.7 7.0 %fine_sum.3.fine_ref = f32[240,256]{1,0:T(8,128)S(1)} custom-call(bf16[40,40,128]{2,1,0:T(8,128)(2,1)S(1)} %get-tuple-element.33.d_in_ref, f32[882,128]{1,0:T(8,128)S(1)} %fusion.v_ref.near_ref, f32[240,256]{1,0:T(8,128)S(1)} %fine_sum.2.refs_0_), custom_call_target="tpu_custom_call" | custom-call | flops 5190451200 | bytes 65536 | tf_op jit(solution)/shard_map/fine_sum/pallas_call | solution.py:92
  55.7 1.7 %all-to-all-done.1.recv_ref = bf16[8,240,128]{2,1,0:T(8,128)(2,1)S(1)} async-done(((bf16[8,240,128]{2,1,0:T(8,128)(2,1)}), bf16[8,240,128]{2,1,0:T(8,128)(2,1)S(1)}, u32[]{:S(2)}, u32[]{:S(2)}) %all-to-all-start.1) | async-done | bytes 491552 | tf_op jit(solution)/shard_map/all_to_all | solution.py:506
  57.4 4.8 %final.1 = f32[20,20,128]{2,1,0:T(8,128)} custom-call(s32[2]{0:T(128)S(1)} %pad_add_fusion.where_ref, bf16[8,240,128]{2,1,0:T(8,128)(2,1)S(1)} %all-to-all-done.1.recv_ref, f32[16,88,128]{2,1,0:T(8,128)S(1)} %copy-done.1, f32[512,128]{1,0:T(8,128)S(1)} %copy-done.3, f32[882,128]{1,0:T(8,128)S(1)} %fusion.v_ref.near_ref, f32[882,128]{1,0:T(8,128)S(1)} %fusion.1.far_ref, ...), custom_call_target="tpu_custom_call" | custom-call | bytes 65536 | tf_op jit(solution)/shard_map/final/pallas_call | solution.py:92
  (18 shorter events, 0.7 us)
Async XLA Ops:
  0.0 6.1 %copy-start = (bf16[20,20,128]{2,1,0:T(8,128)(2,1)S(1)}, bf16[20,20,128]{2,1,0:T(8,128)(2,1)}, u32[]{:S(2)}) copy-start(bf16[20,20,128]{2,1,0:T(8,128)(2,1)} %blk_ref.3) | copy-start | bytes 307204
  0.0 12.6 %copy-start.4 = (bf16[2,21,21,21]{3,0,2,1:T(2,128)(2,1)S(1)}, bf16[2,21,21,21]{3,0,2,1:T(2,128)(2,1)}, u32[]{:S(2)}) copy-start(bf16[2,21,21,21]{3,0,2,1:T(2,128)(2,1)} %param.8) | copy-start | bytes 111136
  0.9 4.3 %collective-permute-start.1 = (bf16[10,20,128]{2,1,0:T(8,128)(2,1)S(1)}, bf16[10,20,128]{2,1,0:T(8,128)(2,1)S(1)}, u32[]{:S(2)}, u32[]{:S(2)}) collective-permute-start(bf16[10,20,128]{2,1,0:T(8,128)(2,1)S(1)} %get-tuple-element.45), channel_id=1, source_target_pairs={{8,16},{24,32},{40,48},{56,64},{72,80},{88,96},{104,112},{120,128}... | collective-permute-start | bytes 153608 | tf_op jit(solution)/shard_map/ppermute | solution.py:443
  1.6 4.5 %collective-permute-start = (bf16[10,20,128]{2,1,0:T(8,128)(2,1)S(1)}, bf16[10,20,128]{2,1,0:T(8,128)(2,1)S(1)}, u32[]{:S(2)}, u32[]{:S(2)}) collective-permute-start(bf16[10,20,128]{2,1,0:T(8,128)(2,1)S(1)} %get-tuple-element.46), channel_id=1, source_target_pairs={{0,8},{16,24},{32,40},{48,56},{64,72},{80,88},{96,104},{112,120},{... | collective-permute-start | bytes 153608 | tf_op jit(solution)/shard_map/ppermute | solution.py:444
  6.7 9.0 %collective-permute-start.2 = (bf16[400,128]{1,0:T(8,128)(2,1)S(1)}, bf16[400,128]{1,0:T(8,128)(2,1)S(1)}, u32[]{:S(2)}, u32[]{:S(2)}) collective-permute-start(bf16[400,128]{1,0:T(8,128)(2,1)S(1)} %get-tuple-element.27), channel_id=1, source_target_pairs={{1,2},{3,4},{5,6},{2,1},{4,3},{6,5},{9,10},{11,12},{13,14},{10,9},... | collective-permute-start | bytes 307208 | tf_op jit(solution)/shard_map/ppermute | solution.py:443
  12.5 5.5 %collective-permute-start.3 = (bf16[400,128]{1,0:T(8,128)(2,1)S(1)}, bf16[400,128]{1,0:T(8,128)(2,1)S(1)}, u32[]{:S(2)}, u32[]{:S(2)}) collective-permute-start(bf16[400,128]{1,0:T(8,128)(2,1)S(1)} %get-tuple-element.28), channel_id=1, source_target_pairs={{0,1},{2,3},{4,5},{6,7},{1,0},{3,2},{5,4},{7,6},{8,9},{10,11},{12,... | collective-permute-start | bytes 307208 | tf_op jit(solution)/shard_map/ppermute | solution.py:444
  13.1 0.7 %copy-start.6 = (bf16[21,128]{1,0:T(8,128)(2,1)S(1)}, bf16[21,128]{1,0:T(8,128)(2,1)}, u32[]{:S(2)}) copy-start(bf16[21,128]{1,0:T(8,128)(2,1)} %constant.34.clone) | copy-start | bytes 16132
  13.8 0.7 %copy-start.5 = (bf16[21,128]{1,0:T(8,128)(2,1)S(1)}, bf16[21,128]{1,0:T(8,128)(2,1)}, u32[]{:S(2)}) copy-start(bf16[21,128]{1,0:T(8,128)(2,1)} %constant.33.clone) | copy-start | bytes 16132
  20.0 22.3 %all-to-all-start = ((f32[32,8,128]{2,1,0:T(8,128)}), f32[32,8,128]{2,1,0:T(8,128)S(1)}, u32[]{:S(2)}, u32[]{:S(2)}) async-start(f32[32,8,128]{2,1,0:T(8,128)} %get-tuple-element.32), calls=%async_computation | async-start | bytes 262144 | tf_op jit(solution)/shard_map/all_to_all | solution.py:493
  31.6 1.3 %collective-permute-start.4 = (bf16[5,9,128]{2,1,0:T(8,128)(2,1)S(1)}, bf16[5,9,128]{2,1,0:T(8,128)(2,1)S(1)}, u32[]{:S(2)}, u32[]{:S(2)}) collective-permute-start(bf16[5,9,128]{2,1,0:T(8,128)(2,1)S(1)} %get-tuple-element.35), channel_id=1, source_target_pairs={{0,8},{16,24},{32,40},{48,56},{64,72},{80,88},{96,104},{112,120},{... | collective-permute-start | bytes 34568 | tf_op jit(solution)/shard_map/ppermute | solution.py:444
  31.9 10.4 %collective-permute-start.5 = (bf16[5,9,128]{2,1,0:T(8,128)(2,1)S(1)}, bf16[5,9,128]{2,1,0:T(8,128)(2,1)S(1)}, u32[]{:S(2)}, u32[]{:S(2)}) collective-permute-start(bf16[5,9,128]{2,1,0:T(8,128)(2,1)S(1)} %get-tuple-element.39), channel_id=1, source_target_pairs={{8,16},{24,32},{40,48},{56,64},{72,80},{88,96},{104,112},{120,128}... | collective-permute-start | bytes 34568 | tf_op jit(solution)/shard_map/ppermute | solution.py:443
  32.8 9.5 %copy-start.2 = (f32[2,328,128]{2,1,0:T(8,128)S(1)}, f32[2,328,128]{2,1,0:T(8,128)}, u32[]{:S(2)}) copy-start(f32[2,328,128]{2,1,0:T(8,128)} %constant.35.clone.mx_ref) | copy-start | bytes 1007620
  44.0 13.4 %all-to-all-start.1 = ((bf16[8,240,128]{2,1,0:T(8,128)(2,1)}), bf16[8,240,128]{2,1,0:T(8,128)(2,1)S(1)}, u32[]{:S(2)}, u32[]{:S(2)}) async-start(bf16[8,240,128]{2,1,0:T(8,128)(2,1)} %spread.1), calls=%async_computation.1 | async-start | bytes 983040 | tf_op jit(solution)/shard_map/all_to_all | solution.py:506
  48.7 8.7 %copy-start.1 = (f32[16,88,128]{2,1,0:T(8,128)S(1)}, f32[16,88,128]{2,1,0:T(8,128)}, u32[]{:S(2)}) copy-start(f32[16,88,128]{2,1,0:T(8,128)} %constant.36.clone.my_ref) | copy-start | bytes 2162692
  48.7 8.7 %copy-start.3 = (f32[512,128]{1,0:T(8,128)S(1)}, f32[512,128]{1,0:T(8,128)}, u32[]{:S(2)}) copy-start(f32[512,128]{1,0:T(8,128)} %constant.37.clone.mz_ref) | copy-start | bytes 786436

commit v7 on v6

--- a/solution.py
+++ b/solution.py
@@ -123,7 +123,7 @@
 def restrict_kernel(
     where_ref, blk_ref, near_x_ref, next_x_ref, next_y_ref, near_y_ref,
     d_out_ref, second_ref, first_ref, own_ref, out_ref,
-    d_ref, dense, planes, cells, mid, pay,
+    d_ref, dense, planes, cells, mid,
 ):
     even_x = even(where_ref[0])
     even_y = even(where_ref[1])
@@ -200,13 +200,10 @@
             )
         sums.append(tap(0) + 0.5625 * (tap(-1) + tap(1)) - 0.0625 * (tap(-3) + tap(3)))
     out = exact_dot(jnp.concatenate(sums, axis=0), down_z)
-    pay[...] = jnp.concatenate([out[8 * y : 8 * y + 8] for y in range(4)], axis=1)
-    pay[5:6, :] = jnp.concatenate([out[32 + x : 33 + x] for x in range(4)], axis=1)
-    pay[6:8, :] = jnp.zeros((2, 128), f32)
-    pay[6:7, 0:32] = out[36:37]
-    row = pay[...]
-    for k in range(out_ref.shape[0]):
-        out_ref[k] = row
+    out_ref[...] = jnp.concatenate([out[8 * y : 8 * y + 8] for y in range(4)], axis=1)
+    out_ref[5:6, :] = jnp.concatenate([out[32 + x : 33 + x] for x in range(4)], axis=1)
+    out_ref[6:8, :] = jnp.zeros((2, 128), f32)
+    out_ref[6:7, 0:32] = out[36:37]
 
 
 def fine_kernel(lo, hi, first, d_in_ref, v_ref, *refs):
@@ -251,20 +248,20 @@
         lhs = jnp.concatenate(tiles, axis=1)
         out_ref[...] += jnp.dot(lhs, w[...], preferred_element_type=f32)
 
-    build(w0, lo)
     out_ref[...] = jnp.zeros((240, 256), f32) if first else acc_ref[...]
 
     def step(t, _):
         b = lo + 2 * GROUP * t
+        build(w0, b)
+        dot(w0, e0, b)
         build(w1, b + GROUP)
-        dot(w0, e0, b)
-        build(w0, jnp.minimum(b + 2 * GROUP, TAPS - GROUP))
         dot(w1, e1, b + GROUP)
         return 0
 
     groups = (hi - lo) // GROUP
     lax.fori_loop(0, groups // 2, step, 0)
     if groups % 2:
+        build(w0, hi - GROUP)
         dot(w0, e0, hi - GROUP)
 
 
@@ -282,7 +279,7 @@
     )[0]
 
 
-def spread_kernel(where_ref, recv_ref, mx_ref, own_ref, next_ref, near_ref, out_ref, buf):
+def spread_kernel(where_ref, recv_ref, mx_ref, own_ref, next_ref, near_ref, out_ref, buf, tail):
     even_x = even(where_ref[0])
     start = 10 * where_ref[0]
     halves = [mx_ref[h, pl.ds(start, 16), :] for h in range(2)]
@@ -299,27 +296,27 @@
     last = value[80:96, 0:32]
     for x in range(4):
         last = last + value[16 * x + 16 : 16 * x + 32, 32 * x : 32 * x + 32]
-    part = jnp.concatenate([value[0:16], last, jnp.zeros((16, 96), f32)], axis=1)
+    tail[...] = jnp.concatenate([last, jnp.zeros((16, 96), f32)], axis=1)
+    last = tail[pl.ds(0, 4, stride=4), :]
+    for k in range(1, 4):
+        last = last + pltpu.roll(tail[pl.ds(k, 4, stride=4), :], 32 * k, 1)
     for n in range(5):
         near, other = near_ref[n].astype(f32), next_ref[n].astype(f32)
-        buf[34 * n : 34 * n + 9, :] = jnp.where(even_x, other, near)
-        buf[34 * n + 9 : 34 * n + 25, :] = own_ref[n].astype(f32)
-        buf[34 * n + 25 : 34 * n + 34, :] = jnp.where(even_x, near, other)
-    buf[170:176, :] = jnp.zeros((6, 128), f32)
-    high = part.astype(bf16)
-    low = (part - high.astype(f32)).astype(bf16)
-    cells = buf[...].astype(bf16)
-    for k in range(out_ref.shape[0]):
-        out_ref[k, 0:176, :] = cells
-        out_ref[k, 176:192, :] = high[:, 0:128]
-        out_ref[k, 192:208, :] = high[:, 128:256]
-        out_ref[k, 208:224, :] = low[:, 0:128]
-        out_ref[k, 224:240, :] = low[:, 128:256]
+        buf[33 * n : 33 * n + 8, :] = jnp.where(even_x, other, near)[1:9]
+        buf[33 * n + 8 : 33 * n + 24, :] = own_ref[n].astype(f32)
+        buf[33 * n + 24 : 33 * n + 33, :] = jnp.where(even_x, near, other)
+    for at, part in ((165, last), (176, value[0:16])):
+        rows = part.shape[0]
+        high = part.astype(bf16).astype(f32)
+        buf[at : at + rows, :] = high
+        buf[at + rows : at + 2 * rows, :] = part - high
+    buf[173:176, :] = jnp.zeros((3, 128), f32)
+    out_ref[...] = buf[...].astype(bf16)
 
 
 def final_kernel(
-    where_ref, recv_ref, my_ref, mz_ref, near_ref, far_ref, fine_ref, out_ref,
-    cells, w0, w1, acc, moved, wide, line,
+    where_ref, recv_ref, my_ref, mz_ref, near_ref, far_ref, fine_ref, out_ref, same_ref,
+    cells, w0, w1, acc, moved, wide, line, tail,
 ):
     index_x = where_ref[0]
     index_y = where_ref[1]
@@ -333,7 +330,7 @@
         for p in range(5):
             n = 5 * step + 6 + p
             if 0 <= n < 17:
-                cells[n, 0:34, :] = line[34 * p : 34 * p + 34, :]
+                cells[n, 0:33, :] = line[33 * p : 33 * p + 33, :]
 
     r, c = iota2((128, 128))
     mask = jnp.abs(r % 64 - c % 64) <= REACH
@@ -360,7 +357,7 @@
     def dot(w, a):
         rows = []
         for k in range(3):
-            part = [cells[n, pl.ds(a + k + 1, 16), :].astype(bf16) for n in range(17)]
+            part = [cells[n, pl.ds(a + k, 16), :].astype(bf16) for n in range(17)]
             rows.append([jnp.concatenate(part[g : g + 11], axis=1) for g in range(7)])
         lhs = jnp.concatenate(
             [jnp.concatenate([rows[k][g] for k in range(3)], axis=1) for g in range(7)], axis=0
@@ -384,10 +381,13 @@
     start = 10 * index_y
     sums = [[None] * 14, [None] * 14]
     for k in range(count):
-        high = [recv_ref[k, 176 + 16 * h : 192 + 16 * h, :].astype(f32) for h in range(2)]
-        low = [recv_ref[k, 208 + 16 * h : 224 + 16 * h, :].astype(f32) for h in range(2)]
-        for h in range(2):
-            value = high[h] + low[h]
+        main = recv_ref[k, 176:192, :].astype(f32) + recv_ref[k, 192:208, :].astype(f32)
+        last = recv_ref[k, 160:176, :].astype(f32)
+        last = last[5:9] + last[9:13]
+        tail[k, pl.ds(0, 4, stride=4), :] = last
+        for r in range(1, 4):
+            tail[k, pl.ds(r, 4, stride=4), :] = pltpu.roll(last, 128 - 32 * r, 1)
+        for h, value in ((0, main), (1, tail[k])):
             rows_y = my_ref[2 * k + h, pl.ds(start, 16), :]
             for y in range(14):
                 term = value * rows_y[y : y + 1, :]
@@ -429,7 +429,8 @@
             value = planes[m + 1]
         else:
             value = 0.5625 * (planes[m + 1] + planes[m + 2]) - 0.0625 * (planes[m] + planes[m + 3])
-        out_ref[x] = value + fine_ref[24 * m : 24 * m + 20, 128 * (x % 2) : 128 * (x % 2) + 128]
+        out_ref[x] = value
+        same_ref[x] = fine_ref[24 * m : 24 * m + 20, 128 * (x % 2) : 128 * (x % 2) + 128]
 
 
 def swap(first, second, axis):
@@ -475,7 +476,7 @@
             shape((5, 9, 128), bf16),
             shape((5, 9, 128), bf16),
             shape((5, 16, 128), bf16),
-            shape((count_x, 8, 128), f32),
+            shape((8, 128), f32),
         ],
         [
             pltpu.VMEM((2, 20, 48, 128), f32),
@@ -483,31 +484,30 @@
             pltpu.VMEM((16, 48, 128), f32),
             pltpu.VMEM((256, 128), f32),
             pltpu.VMEM((9, 24, 128), f32),
-            pltpu.VMEM((8, 128), f32),
         ],
         "restrict",
         (where, charges, near_x, next_x, next_y, near_y),
         smem=1,
     )
     near_m, next_m = swap(first, second, "gx")
-    coarse = lax.all_to_all(coarse, "gx", 0, 0)
+    coarse = lax.all_to_all(jnp.broadcast_to(coarse, (count_x, 8, 128)), "gx", 0, 0)
     near, near_m = lax.optimization_barrier((near, near_m))
     fine = fine_sum(0, SPLIT, d, near)
     coarse, fine = lax.optimization_barrier((coarse, fine))
     parts = vmem_call(
         spread_kernel,
-        [shape((count_y, 240, 128), bf16)],
-        [pltpu.VMEM((176, 128), f32)],
+        [shape((208, 128), bf16)],
+        [pltpu.VMEM((208, 128), f32), pltpu.VMEM((16, 128), f32)],
         "spread",
         (where, coarse, jnp.asarray(matrix_x_np(spread)), own, next_m, near_m),
         smem=1,
     )[0]
     parts, near = lax.optimization_barrier((parts, near))
-    parts = lax.all_to_all(parts, "gy", 0, 0)
+    parts = lax.all_to_all(jnp.broadcast_to(parts, (count_y, 208, 128)), "gy", 0, 0)
     fine = fine_sum(SPLIT, TAPS, d, near, fine)
-    return vmem_call(
+    total, fine = vmem_call(
         final_kernel,
-        [shape((20, 20, 128), f32)],
+        [shape((20, 20, 128), f32)] * 2,
         [
             pltpu.VMEM((17, 40, 128), f32),
             pltpu.VMEM((4224, 128), bf16),
@@ -516,6 +516,7 @@
             pltpu.VMEM((320, 128), f32),
             pltpu.VMEM((112, 256), f32),
             pltpu.VMEM((176, 128), f32),
+            pltpu.VMEM((count_y, 16, 128), f32),
         ],
         "final",
         (
@@ -528,7 +529,8 @@
             fine,
         ),
         smem=1,
-    )[0]
+    )
+    return total + fine
 
 
 def solution(mesh):

time: 62.6 us -> 62 us (level)
  Pallas kernels: 19 us -> 16.1 us
  local copies, waits for them, and re-layouts: 1.54 us -> 3.04 us
  other arithmetic: 0.99 us -> 1.72 us
    pallas_call x6, Pallas kernels: 19 us -> 16.1 us  [vmem_call(): pl.pallas_call(body, out_shape=out_shape, in_specs=[spec(pltpu.SMEM)] * s...]
    broadcast_in_dim x0 -> x2, local copies, waits for them, and re-layouts: none -> 1.5 us  [the longest x1 0.82 us: per_device(): jnp.broadcast_to(parts, (count_y, 208, 128))]
    add x0 -> x1, other arithmetic: none -> 0.73 us  [per_device(): return total + fine]
  transfers between devices with their start and end apart: 8 -> 8, of which waited for: 6 -> 6; matrix products, arithmetic and copies ran while one was open for 2% -> 2% of each run, Pallas kernels for 16% -> 15%
where the time goes in v7:
time: 62 us; the launch traced here: 61.6 us
  starting transfers between devices  27.4 us (44%)
  Pallas kernels  16.1 us (26%)
  waiting for transfers between devices  12.7 us (20%)
  local copies, waits for them, and re-layouts  3.04 us (5%)
  other arithmetic  1.72 us (3%)
  matrix products  0.62 us (1%)
    pallas_call x6, Pallas kernels, vmem_call(): pl.pallas_call(body, out_shape=out_shape, in_specs=[spec(pltpu.SMEM)] * s...  16.1 us
    all_to_all x1, starting transfers between devices, per_device(): lax.all_to_all(jnp.broadcast_to(coarse, (count_x, 8, 128)), 'gx', 0, 0)  11.5 us
    ppermute x3, starting transfers between devices, swap(): second = lax.ppermute(second, axis, both(others))  7.11 us
    all_to_all x1, waiting for transfers between devices, per_device(): lax.all_to_all(jnp.broadcast_to(coarse, (count_x, 8, 128)), 'gx', 0, 0)  6.91 us
    all_to_all x1, starting transfers between devices, per_device(): lax.all_to_all(jnp.broadcast_to(parts, (count_y, 208, 128)), 'gy', 0, 0)  4.72 us
    ppermute x3, starting transfers between devices, swap(): return (lax.ppermute(first, axis, both(pairs)), second)  4.02 us
    ppermute x3, waiting for transfers between devices, swap(): return (lax.ppermute(first, axis, both(pairs)), second)  3.36 us
    all_to_all x1, waiting for transfers between devices, per_device(): lax.all_to_all(jnp.broadcast_to(parts, (count_y, 208, 128)), 'gy', 0, 0)  1.44 us
  transfers between devices with their start and end apart: 8, of which 6 were waited for; matrix products, arithmetic and copies ran while one was open for 2% of the time, Pallas kernels for 15%

profile of v7, /device:TPU:2, one launch (start us, length us, event | category | flops | bytes accessed | tf_op | source)
XLA Modules:
  0.0 61.6 jit_solution(2125341794714813485)
XLA Ops:
  0.0 0.9 %broadcast_select_fusion = (bf16[10,20,128]{2,1,0:T(8,128)(2,1)S(1)}, bf16[10,20,128]{2,1,0:T(8,128)(2,1)S(1)}) fusion(pred[]{:T(512)S(6)} %eq.5, bf16[20,20,128]{2,1,0:T(8,128)(2,1)} %blk_ref.3), kind=kLoop, calls=%fused_computation | loop fusion | flops 51200 | bytes 204801 | tf_op jit(solution)/shard_map/jit(_where)/select_n | solution.py:456
  0.9 0.7 %collective-permute-start.1 = (bf16[10,20,128]{2,1,0:T(8,128)(2,1)S(1)}, bf16[10,20,128]{2,1,0:T(8,128)(2,1)S(1)}, u32[]{:S(2)}, u32[]{:S(2)}) collective-permute-start(bf16[10,20,128]{2,1,0:T(8,128)(2,1)S(1)} %get-tuple-element.49), channel_id=1, source_target_pairs={{8,16},{24,32},{40,48},{56,64},{72,80},{88,96},{104,112},{120,128}... | collective-permute-start | bytes 153608 | tf_op jit(solution)/shard_map/ppermute | solution.py:444
  1.6 3.6 %collective-permute-start = (bf16[10,20,128]{2,1,0:T(8,128)(2,1)S(1)}, bf16[10,20,128]{2,1,0:T(8,128)(2,1)S(1)}, u32[]{:S(2)}, u32[]{:S(2)}) collective-permute-start(bf16[10,20,128]{2,1,0:T(8,128)(2,1)S(1)} %get-tuple-element.50), channel_id=1, source_target_pairs={{0,8},{16,24},{32,40},{48,56},{64,72},{80,88},{96,104},{112,120},{... | collective-permute-start | bytes 153608 | tf_op jit(solution)/shard_map/ppermute | solution.py:445
  5.2 0.8 %collective-permute-done.near_ref.near_x_ref = bf16[10,20,128]{2,1,0:T(8,128)(2,1)S(1)} collective-permute-done((bf16[10,20,128]{2,1,0:T(8,128)(2,1)S(1)}, bf16[10,20,128]{2,1,0:T(8,128)(2,1)S(1)}, u32[]{:S(2)}, u32[]{:S(2)}) %collective-permute-start) | collective-permute-done | bytes 51232 | tf_op jit(solution)/shard_map/ppermute | solution.py:445
  6.1 0.6 %rim.1 = (bf16[400,128]{1,0:T(8,128)(2,1)S(1)}, bf16[400,128]{1,0:T(8,128)(2,1)S(1)}) custom-call(s32[2]{0:T(128)S(1)} %pad_add_fusion.where_ref, bf16[20,20,128]{2,1,0:T(8,128)(2,1)S(1)} %copy-done, bf16[10,20,128]{2,1,0:T(8,128)(2,1)S(1)} %collective-permute-done.near_ref.near_x_ref, bf16[10,20,128]{2,1,0:T(8,128)(2,1)S(1)} %collective-permute-done.1.next_ref.next_x_ref), custom_call_target="tpu_custom_call" | custom-call | bytes 65536 | tf_op jit(solution)/shard_map/rim/pallas_call | solution.py:92
  6.7 5.8 %collective-permute-start.2 = (bf16[400,128]{1,0:T(8,128)(2,1)S(1)}, bf16[400,128]{1,0:T(8,128)(2,1)S(1)}, u32[]{:S(2)}, u32[]{:S(2)}) collective-permute-start(bf16[400,128]{1,0:T(8,128)(2,1)S(1)} %get-tuple-element.29), channel_id=1, source_target_pairs={{1,2},{3,4},{5,6},{2,1},{4,3},{6,5},{9,10},{11,12},{13,14},{10,9},... | collective-permute-start | bytes 307208 | tf_op jit(solution)/shard_map/ppermute | solution.py:444
  12.6 0.5 copy.8
  13.3 0.4 copy-done.6
  14.1 0.4 copy-done.5
  14.8 0.9 %collective-permute-done.2.next_y_ref = bf16[400,128]{1,0:T(8,128)(2,1)S(1)} collective-permute-done((bf16[400,128]{1,0:T(8,128)(2,1)S(1)}, bf16[400,128]{1,0:T(8,128)(2,1)S(1)}, u32[]{:S(2)}, u32[]{:S(2)}) %collective-permute-start.2) | collective-permute-done | bytes 102432 | tf_op jit(solution)/shard_map/ppermute | solution.py:444
  15.7 2.3 %collective-permute-done.3.near_y_ref = bf16[400,128]{1,0:T(8,128)(2,1)S(1)} collective-permute-done((bf16[400,128]{1,0:T(8,128)(2,1)S(1)}, bf16[400,128]{1,0:T(8,128)(2,1)S(1)}, u32[]{:S(2)}, u32[]{:S(2)}) %collective-permute-start.3) | collective-permute-done | bytes 102432 | tf_op jit(solution)/shard_map/ppermute | solution.py:445
  18.0 1.3 %restrict.1 = (bf16[40,40,128]{2,1,0:T(8,128)(2,1)S(1)}, bf16[5,9,128]{2,1,0:T(8,128)(2,1)S(1)}, bf16[5,9,128]{2,1,0:T(8,128)(2,1)S(1)}, bf16[5,16,128]{2,1,0:T(8,128)(2,1)S(1)}, f32[8,128]{1,0:T(8,128)S(1)}) custom-call(s32[2]{0:T(128)S(1)} %pad_add_fusion.where_ref, bf16[20,20,128]{2,1,0:T(8,128)(2,1)S(1)} %copy-done, ...), custom_call_target="tpu_custom_call" | custom-call | bytes 65536 | tf_op jit(solution)/shard_map/restrict/pallas_call | solution.py:92
  19.3 0.7 %broadcast_in_dim.6 = f32[32,8,128]{2,1,0:T(8,128)} broadcast(f32[8,128]{1,0:T(8,128)S(1)} %get-tuple-element.34), dimensions={1,2} | broadcast | bytes 135168 | tf_op jit(solution)/shard_map/broadcast_in_dim | solution.py:493
  20.0 11.5 %all-to-all-start = ((f32[32,8,128]{2,1,0:T(8,128)}), f32[32,8,128]{2,1,0:T(8,128)S(1)}, u32[]{:S(2)}, u32[]{:S(2)}) async-start(f32[32,8,128]{2,1,0:T(8,128)} %broadcast_in_dim.6), calls=%async_computation | async-start | bytes 262144 | tf_op jit(solution)/shard_map/all_to_all | solution.py:493
  31.9 0.7 %collective-permute-start.5 = (bf16[5,9,128]{2,1,0:T(8,128)(2,1)S(1)}, bf16[5,9,128]{2,1,0:T(8,128)(2,1)S(1)}, u32[]{:S(2)}, u32[]{:S(2)}) collective-permute-start(bf16[5,9,128]{2,1,0:T(8,128)(2,1)S(1)} %get-tuple-element.41), channel_id=1, source_target_pairs={{8,16},{24,32},{40,48},{56,64},{72,80},{88,96},{104,112},{120,128}... | collective-permute-start | bytes 34568 | tf_op jit(solution)/shard_map/ppermute | solution.py:444
  32.8 2.6 %fine_sum.2.refs_0_ = f32[240,256]{1,0:T(8,128)S(1)} custom-call(bf16[40,40,128]{2,1,0:T(8,128)(2,1)S(1)} %get-tuple-element.35.d_in_ref, f32[882,128]{1,0:T(8,128)S(1)} %fusion.v_ref.near_ref), custom_call_target="tpu_custom_call" | custom-call | flops 2076180480 | bytes 65536 | tf_op jit(solution)/shard_map/fine_sum/pallas_call | solution.py:92
  35.4 6.9 %all-to-all-done.recv_ref = f32[32,8,128]{2,1,0:T(8,128)S(1)} async-done(((f32[32,8,128]{2,1,0:T(8,128)}), f32[32,8,128]{2,1,0:T(8,128)S(1)}, u32[]{:S(2)}, u32[]{:S(2)}) %all-to-all-start) | async-done | bytes 131104 | tf_op jit(solution)/shard_map/all_to_all | solution.py:493
  42.3 1.0 %spread.1 = bf16[208,128]{1,0:T(8,128)(2,1)S(1)} custom-call(s32[2]{0:T(128)S(1)} %pad_add_fusion.where_ref, f32[32,8,128]{2,1,0:T(8,128)S(1)} %all-to-all-done.recv_ref, f32[2,328,128]{2,1,0:T(8,128)S(1)} %copy-done.2, bf16[5,16,128]{2,1,0:T(8,128)(2,1)S(1)} %get-tuple-element.40.own_ref, bf16[5,9,128]{2,1,0:T(8,128)(2,1)S(1)} %collective-permute-done.5.next_ref, ...), custom_call_target="tpu_custom_call" | custom-call | bytes 65536 | tf_op jit(solution)/shard_map/spread/pallas_call | solution.py:92
  43.3 0.8 %broadcast_in_dim.7 = bf16[8,208,128]{2,1,0:T(8,128)(2,1)} broadcast(bf16[208,128]{1,0:T(8,128)(2,1)S(1)} %spread.1), dimensions={1,2} | broadcast | bytes 479232 | tf_op jit(solution)/shard_map/broadcast_in_dim | solution.py:506
  44.1 4.7 %all-to-all-start.1 = ((bf16[8,208,128]{2,1,0:T(8,128)(2,1)}), bf16[8,208,128]{2,1,0:T(8,128)(2,1)S(1)}, u32[]{:S(2)}, u32[]{:S(2)}) async-start(bf16[8,208,128]{2,1,0:T(8,128)(2,1)} %broadcast_in_dim.7), calls=%async_computation.1 | async-start | bytes 851968 | tf_op jit(solution)/shard_map/all_to_all | solution.py:506
  48.8 6.6 %fine_sum.3.fine_ref = f32[240,256]{1,0:T(8,128)S(1)} custom-call(bf16[40,40,128]{2,1,0:T(8,128)(2,1)S(1)} %get-tuple-element.35.d_in_ref, f32[882,128]{1,0:T(8,128)S(1)} %fusion.v_ref.near_ref, f32[240,256]{1,0:T(8,128)S(1)} %fine_sum.2.refs_0_), custom_call_target="tpu_custom_call" | custom-call | flops 5190451200 | bytes 65536 | tf_op jit(solution)/shard_map/fine_sum/pallas_call | solution.py:92
  55.4 1.4 %all-to-all-done.1.recv_ref = bf16[8,208,128]{2,1,0:T(8,128)(2,1)S(1)} async-done(((bf16[8,208,128]{2,1,0:T(8,128)(2,1)}), bf16[8,208,128]{2,1,0:T(8,128)(2,1)S(1)}, u32[]{:S(2)}, u32[]{:S(2)}) %all-to-all-start.1) | async-done | bytes 426016 | tf_op jit(solution)/shard_map/all_to_all | solution.py:506
  56.9 4.0 %final.1 = (f32[20,20,128]{2,1,0:T(8,128)S(1)}, f32[20,20,128]{2,1,0:T(8,128)S(1)}) custom-call(s32[2]{0:T(128)S(1)} %pad_add_fusion.where_ref, bf16[8,208,128]{2,1,0:T(8,128)(2,1)S(1)} %all-to-all-done.1.recv_ref, f32[16,88,128]{2,1,0:T(8,128)S(1)} %copy-done.1, f32[512,128]{1,0:T(8,128)S(1)} %copy-done.3, f32[882,128]{1,0:T(8,128)S(1)} %fusion.v_ref.near_ref, ...), custom_call_target="tpu_custom_call" | custom-call | bytes 65536 | tf_op jit(solution)/shard_map/final/pallas_call | solution.py:92
  60.9 0.7 %add.8 = f32[20,20,128]{2,1,0:T(8,128)} add(f32[20,20,128]{2,1,0:T(8,128)S(1)} %get-tuple-element.47, f32[20,20,128]{2,1,0:T(8,128)S(1)} %get-tuple-element.48) | non-fusion elementwise | flops 51200 | bytes 614400 | tf_op jit(solution)/shard_map/add | solution.py:533
  (21 shorter events, 1.7 us)
Async XLA Ops:
  0.0 6.1 %copy-start = (bf16[20,20,128]{2,1,0:T(8,128)(2,1)S(1)}, bf16[20,20,128]{2,1,0:T(8,128)(2,1)}, u32[]{:S(2)}) copy-start(bf16[20,20,128]{2,1,0:T(8,128)(2,1)} %blk_ref.3) | copy-start | bytes 307204
  0.0 12.6 %copy-start.4 = (bf16[2,21,21,21]{3,0,2,1:T(2,128)(2,1)S(1)}, bf16[2,21,21,21]{3,0,2,1:T(2,128)(2,1)}, u32[]{:S(2)}) copy-start(bf16[2,21,21,21]{3,0,2,1:T(2,128)(2,1)} %param.8) | copy-start | bytes 111136
  0.9 4.3 %collective-permute-start.1 = (bf16[10,20,128]{2,1,0:T(8,128)(2,1)S(1)}, bf16[10,20,128]{2,1,0:T(8,128)(2,1)S(1)}, u32[]{:S(2)}, u32[]{:S(2)}) collective-permute-start(bf16[10,20,128]{2,1,0:T(8,128)(2,1)S(1)} %get-tuple-element.49), channel_id=1, source_target_pairs={{8,16},{24,32},{40,48},{56,64},{72,80},{88,96},{104,112},{120,128}... | collective-permute-start | bytes 153608 | tf_op jit(solution)/shard_map/ppermute | solution.py:444
  1.6 4.5 %collective-permute-start = (bf16[10,20,128]{2,1,0:T(8,128)(2,1)S(1)}, bf16[10,20,128]{2,1,0:T(8,128)(2,1)S(1)}, u32[]{:S(2)}, u32[]{:S(2)}) collective-permute-start(bf16[10,20,128]{2,1,0:T(8,128)(2,1)S(1)} %get-tuple-element.50), channel_id=1, source_target_pairs={{0,8},{16,24},{32,40},{48,56},{64,72},{80,88},{96,104},{112,120},{... | collective-permute-start | bytes 153608 | tf_op jit(solution)/shard_map/ppermute | solution.py:445
  6.7 9.0 %collective-permute-start.2 = (bf16[400,128]{1,0:T(8,128)(2,1)S(1)}, bf16[400,128]{1,0:T(8,128)(2,1)S(1)}, u32[]{:S(2)}, u32[]{:S(2)}) collective-permute-start(bf16[400,128]{1,0:T(8,128)(2,1)S(1)} %get-tuple-element.29), channel_id=1, source_target_pairs={{1,2},{3,4},{5,6},{2,1},{4,3},{6,5},{9,10},{11,12},{13,14},{10,9},... | collective-permute-start | bytes 307208 | tf_op jit(solution)/shard_map/ppermute | solution.py:444
  12.5 5.5 %collective-permute-start.3 = (bf16[400,128]{1,0:T(8,128)(2,1)S(1)}, bf16[400,128]{1,0:T(8,128)(2,1)S(1)}, u32[]{:S(2)}, u32[]{:S(2)}) collective-permute-start(bf16[400,128]{1,0:T(8,128)(2,1)S(1)} %get-tuple-element.30), channel_id=1, source_target_pairs={{0,1},{2,3},{4,5},{6,7},{1,0},{3,2},{5,4},{7,6},{8,9},{10,11},{12,... | collective-permute-start | bytes 307208 | tf_op jit(solution)/shard_map/ppermute | solution.py:445
  13.1 0.7 %copy-start.6 = (bf16[21,128]{1,0:T(8,128)(2,1)S(1)}, bf16[21,128]{1,0:T(8,128)(2,1)}, u32[]{:S(2)}) copy-start(bf16[21,128]{1,0:T(8,128)(2,1)} %constant.34.clone) | copy-start | bytes 16132
  13.8 0.7 %copy-start.5 = (bf16[21,128]{1,0:T(8,128)(2,1)S(1)}, bf16[21,128]{1,0:T(8,128)(2,1)}, u32[]{:S(2)}) copy-start(bf16[21,128]{1,0:T(8,128)(2,1)} %constant.33.clone) | copy-start | bytes 16132
  20.0 22.3 %all-to-all-start = ((f32[32,8,128]{2,1,0:T(8,128)}), f32[32,8,128]{2,1,0:T(8,128)S(1)}, u32[]{:S(2)}, u32[]{:S(2)}) async-start(f32[32,8,128]{2,1,0:T(8,128)} %broadcast_in_dim.6), calls=%async_computation | async-start | bytes 262144 | tf_op jit(solution)/shard_map/all_to_all | solution.py:493
  31.5 1.3 %collective-permute-start.4 = (bf16[5,9,128]{2,1,0:T(8,128)(2,1)S(1)}, bf16[5,9,128]{2,1,0:T(8,128)(2,1)S(1)}, u32[]{:S(2)}, u32[]{:S(2)}) collective-permute-start(bf16[5,9,128]{2,1,0:T(8,128)(2,1)S(1)} %get-tuple-element.37), channel_id=1, source_target_pairs={{0,8},{16,24},{32,40},{48,56},{64,72},{80,88},{96,104},{112,120},{... | collective-permute-start | bytes 34568 | tf_op jit(solution)/shard_map/ppermute | solution.py:445
  31.9 10.4 %collective-permute-start.5 = (bf16[5,9,128]{2,1,0:T(8,128)(2,1)S(1)}, bf16[5,9,128]{2,1,0:T(8,128)(2,1)S(1)}, u32[]{:S(2)}, u32[]{:S(2)}) collective-permute-start(bf16[5,9,128]{2,1,0:T(8,128)(2,1)S(1)} %get-tuple-element.41), channel_id=1, source_target_pairs={{8,16},{24,32},{40,48},{56,64},{72,80},{88,96},{104,112},{120,128}... | collective-permute-start | bytes 34568 | tf_op jit(solution)/shard_map/ppermute | solution.py:444
  32.8 9.5 %copy-start.2 = (f32[2,328,128]{2,1,0:T(8,128)S(1)}, f32[2,328,128]{2,1,0:T(8,128)}, u32[]{:S(2)}) copy-start(f32[2,328,128]{2,1,0:T(8,128)} %constant.35.clone.mx_ref) | copy-start | bytes 1007620
  44.1 12.7 %all-to-all-start.1 = ((bf16[8,208,128]{2,1,0:T(8,128)(2,1)}), bf16[8,208,128]{2,1,0:T(8,128)(2,1)S(1)}, u32[]{:S(2)}, u32[]{:S(2)}) async-start(bf16[8,208,128]{2,1,0:T(8,128)(2,1)} %broadcast_in_dim.7), calls=%async_computation.1 | async-start | bytes 851968 | tf_op jit(solution)/shard_map/all_to_all | solution.py:506
  48.8 8.0 %copy-start.1 = (f32[16,88,128]{2,1,0:T(8,128)S(1)}, f32[16,88,128]{2,1,0:T(8,128)}, u32[]{:S(2)}) copy-start(f32[16,88,128]{2,1,0:T(8,128)} %constant.36.clone.my_ref) | copy-start | bytes 2162692
  48.8 8.0 %copy-start.3 = (f32[512,128]{1,0:T(8,128)S(1)}, f32[512,128]{1,0:T(8,128)}, u32[]{:S(2)}) copy-start(f32[512,128]{1,0:T(8,128)} %constant.37.clone.mz_ref) | copy-start | bytes 786436

commit v8 on v7

--- a/solution.py
+++ b/solution.py
@@ -14,7 +14,7 @@
 REACH = 10
 TAPS = 21
 GROUP = 3
-SPLIT = 6
+SPLIT = 9
 
 
 def weight_np(offset):
@@ -36,7 +36,7 @@
     m = top_matrix_np(160, spread).reshape(320, 32, 5)
     out = np.zeros((328, 32, 8))
     out[1:321, :, :5] = m
-    return lane_tiles(out.reshape(328, 256))
+    return out.reshape(328, 16, 2, 8).transpose(2, 0, 1, 3).reshape(2, 328, 128).astype(np.float32)
 
 
 def matrix_y_np(spread):
@@ -108,7 +108,8 @@
 def rim_kernel(where_ref, blk_ref, near_ref, next_ref, second_ref, first_ref, wide, dense):
     even_x = even(where_ref[0])
     even_y = even(where_ref[1])
-    near, other = near_ref[...].astype(f32), next_ref[...].astype(f32)
+    near = jnp.where(even_x, near_ref[0:10].astype(f32), near_ref[10:20].astype(f32))
+    other = next_ref[...].astype(f32)
     wide[0:10] = jnp.where(even_x, other, near)
     wide[10:30] = blk_ref[...].astype(f32)
     wide[30:40] = jnp.where(even_x, near, other)
@@ -137,9 +138,11 @@
         if 10 <= x < 30:
             centre = blk_ref[x - 10].astype(f32)
         else:
-            near, other = near_x_ref[x % 30].astype(f32), next_x_ref[x % 30].astype(f32)
-            low, high = (other, near) if x < 10 else (near, other)
-            centre = jnp.where(even_x, low, high)
+            other = next_x_ref[x % 30].astype(f32)
+            if x < 10:
+                centre = jnp.where(even_x, other, near_x_ref[x + 10].astype(f32))
+            else:
+                centre = jnp.where(even_x, near_x_ref[x - 30].astype(f32), other)
         d_ref[p, i, 10:30, :] = centre
         d_out_ref[x] = d_ref[p, i, 0:40, :].astype(bf16)
 
@@ -279,17 +282,20 @@
     )[0]
 
 
-def spread_kernel(where_ref, recv_ref, mx_ref, own_ref, next_ref, near_ref, out_ref, buf, tail):
+def spread_kernel(
+    where_ref, recv_ref, other_ref, mx_ref, own_ref, next_ref, near_ref, out_ref, buf, tail
+):
     even_x = even(where_ref[0])
     start = 10 * where_ref[0]
-    halves = [mx_ref[h, pl.ds(start, 16), :] for h in range(2)]
+    core = where_ref[0] % 2
+    halves = [mx_ref[h, pl.ds(start, 16), :] for h in (core, 1 - core)]
     lane = lax.broadcasted_iota(jnp.int32, (16, 128), 1) % 8
     rows = [jnp.concatenate(halves, axis=1)]
     for x in range(5):
         at = 5 if x < 4 else 6
         moved = [jnp.where(lane == at, pltpu.roll(h, at - x, 1), 0.0) for h in halves]
         rows.append(jnp.concatenate(moved, axis=1))
-    coarse = recv_ref[...].reshape(8 * recv_ref.shape[0], 128)
+    coarse = jnp.concatenate([recv_ref[...], other_ref[...]], axis=0).reshape(256, 128)
     value = jnp.dot(
         jnp.concatenate(rows, axis=0), coarse, precision=HIGHEST, preferred_element_type=f32
     )
@@ -433,16 +439,18 @@
         same_ref[x] = fine_ref[24 * m : 24 * m + 20, 128 * (x % 2) : 128 * (x % 2) + 128]
 
 
+def partners(count, first):
+    return [(k, k + 1) for k in range(first, count - 1, 2)]
+
+
+def both_ways(pairs):
+    return pairs + [(b, a) for a, b in pairs]
+
+
 def swap(first, second, axis):
     count = lax.axis_size(axis)
-    pairs = [(k, k + 1) for k in range(0, count - 1, 2)]
-    others = [(k, k + 1) for k in range(1, count - 1, 2)]
-
-    def both(ends):
-        return ends + [(b, a) for a, b in ends]
-
-    second = lax.ppermute(second, axis, both(others))
-    return lax.ppermute(first, axis, both(pairs)), second
+    second = lax.ppermute(second, axis, both_ways(partners(count, 1)))
+    return lax.ppermute(first, axis, both_ways(partners(count, 0))), second
 
 
 def per_device(charges, kernels):
@@ -453,7 +461,8 @@
     shape = jax.ShapeDtypeStruct
     low, high = charges[:10], charges[10:]
     even_x = even(lax.axis_index("gx"))
-    near_x, next_x = swap(jnp.where(even_x, high, low), jnp.where(even_x, low, high), "gx")
+    edge, block = lax.optimization_barrier((jnp.where(even_x, low, high), charges))
+    near_x, next_x = swap(block, edge, "gx")
     second, first = vmem_call(
         rim_kernel,
         [shape((400, 128), bf16)] * 2,
@@ -490,16 +499,21 @@
         smem=1,
     )
     near_m, next_m = swap(first, second, "gx")
-    coarse = lax.all_to_all(jnp.broadcast_to(coarse, (count_x, 8, 128)), "gx", 0, 0)
+    chips = count_x // 2
+    groups = [[2 * q + core for q in range(chips)] for core in range(2)]
+    coarse = lax.all_to_all(
+        jnp.broadcast_to(coarse, (chips, 8, 128)), "gx", 0, 0, axis_index_groups=groups
+    )
     near, near_m = lax.optimization_barrier((near, near_m))
     fine = fine_sum(0, SPLIT, d, near)
-    coarse, fine = lax.optimization_barrier((coarse, fine))
+    coarse, fine, next_m = lax.optimization_barrier((coarse, fine, next_m))
+    other = lax.ppermute(coarse, "gx", both_ways(partners(count_x, 0)))
     parts = vmem_call(
         spread_kernel,
         [shape((208, 128), bf16)],
         [pltpu.VMEM((208, 128), f32), pltpu.VMEM((16, 128), f32)],
         "spread",
-        (where, coarse, jnp.asarray(matrix_x_np(spread)), own, next_m, near_m),
+        (where, coarse, other, jnp.asarray(matrix_x_np(spread)), own, next_m, near_m),
         smem=1,
     )[0]
     parts, near = lax.optimization_barrier((parts, near))

time: 62 us -> 66.4 us (1.071)
  starting transfers between devices: 27.4 us -> 29.9 us
  waiting for transfers between devices: 12.7 us -> 14.1 us
    all_to_all x1, starting transfers between devices: 11.5 us -> 15.2 us  [per_device(): lax.all_to_all(jnp.broadcast_to(coarse, (chips, 8, 128)), 'gx', 0, 0, axi...]
    all_to_all x1, waiting for transfers between devices: 1.44 us -> 2.73 us  [per_device(): lax.all_to_all(jnp.broadcast_to(parts, (count_y, 208, 128)), 'gy', 0, 0)]
    ppermute x6 -> x7, waiting for transfers between devices: 4.31 us -> 5.3 us  [the longest x3 3 us: swap(): return (lax.ppermute(first, axis, both_ways(partners(count, 0))), second)]
    all_to_all x1, starting transfers between devices: 4.72 us -> 3.84 us  [per_device(): lax.all_to_all(jnp.broadcast_to(parts, (count_y, 208, 128)), 'gy', 0, 0)]
    all_to_all x1, waiting for transfers between devices: 6.91 us -> 6.06 us  [per_device(): lax.all_to_all(jnp.broadcast_to(coarse, (chips, 8, 128)), 'gx', 0, 0, axi...]
    ppermute x6 -> x7, starting transfers between devices: 11.1 us -> 10.8 us  [the longest x3 7.12 us: swap(): second = lax.ppermute(second, axis, both_ways(partners(count, 1)))]
  transfers between devices with their start and end apart: 8 -> 9, of which waited for: 6 -> 6; matrix products, arithmetic and copies ran while one was open for 2% -> 3% of each run, Pallas kernels for 15% -> 15%
where the time goes in v8:
time: 66.4 us; the launch traced here: 66.1 us
  starting transfers between devices  29.9 us (45%)
  Pallas kernels  16.6 us (25%)
  waiting for transfers between devices  14.1 us (21%)
  local copies, waits for them, and re-layouts  3 us (5%)
  other arithmetic  1.72 us (3%)
    pallas_call x6, Pallas kernels, vmem_call(): pl.pallas_call(body, out_shape=out_shape, in_specs=[spec(pltpu.SMEM)] * s...  16.6 us
    all_to_all x1, starting transfers between devices, per_device(): lax.all_to_all(jnp.broadcast_to(coarse, (chips, 8, 128)), 'gx', 0, 0, axi...  15.2 us
    ppermute x3, starting transfers between devices, swap(): second = lax.ppermute(second, axis, both_ways(partners(count, 1)))  7.12 us
    all_to_all x1, waiting for transfers between devices, per_device(): lax.all_to_all(jnp.broadcast_to(coarse, (chips, 8, 128)), 'gx', 0, 0, axi...  6.06 us
    all_to_all x1, starting transfers between devices, per_device(): lax.all_to_all(jnp.broadcast_to(parts, (count_y, 208, 128)), 'gy', 0, 0)  3.84 us
    ppermute x3, starting transfers between devices, swap(): return (lax.ppermute(first, axis, both_ways(partners(count, 0))), second)  3.71 us
    ppermute x3, waiting for transfers between devices, swap(): return (lax.ppermute(first, axis, both_ways(partners(count, 0))), second)  3 us
    all_to_all x1, waiting for transfers between devices, per_device(): lax.all_to_all(jnp.broadcast_to(parts, (count_y, 208, 128)), 'gy', 0, 0)  2.73 us
  transfers between devices with their start and end apart: 9, of which 6 were waited for; matrix products, arithmetic and copies ran while one was open for 3% of the time, Pallas kernels for 15%

profile of v8, /device:TPU:2, one launch (start us, length us, event | category | flops | bytes accessed | tf_op | source)
XLA Modules:
  0.0 66.1 jit_solution(6839793216838632779)
XLA Ops:
  0.0 0.9 %slice_select_fusion = bf16[10,20,128]{2,1,0:T(8,128)(2,1)S(1)} fusion(bf16[20,20,128]{2,1,0:T(8,128)(2,1)} %blk_ref.3, pred[]{:T(512)S(6)} %eq.5), kind=kLoop, calls=%fused_computation | loop fusion | flops 25600 | bytes 153601 | tf_op jit(solution)/shard_map/jit(_where)/select_n | solution.py:464
  0.9 0.7 %collective-permute-start.1 = (bf16[10,20,128]{2,1,0:T(8,128)(2,1)S(1)}, bf16[10,20,128]{2,1,0:T(8,128)(2,1)S(1)}, u32[]{:S(2)}, u32[]{:S(2)}) collective-permute-start(bf16[10,20,128]{2,1,0:T(8,128)(2,1)S(1)} %slice_select_fusion), channel_id=1, source_target_pairs={{8,16},{24,32},{40,48},{56,64},{72,80},{88,96},{104,112},{120,128}... | collective-permute-start | bytes 153608 | tf_op jit(solution)/shard_map/ppermute | solution.py:452
  1.6 3.6 %collective-permute-start = (bf16[20,20,128]{2,1,0:T(8,128)(2,1)S(1)}, bf16[20,20,128]{2,1,0:T(8,128)(2,1)S(1)}, u32[]{:S(2)}, u32[]{:S(2)}) collective-permute-start(bf16[20,20,128]{2,1,0:T(8,128)(2,1)S(1)} %copy-done), channel_id=1, source_target_pairs={{0,8},{16,24},{32,40},{48,56},{64,72},{80,88},{96,104},{112,120},{... | collective-permute-start | bytes 307208 | tf_op jit(solution)/shard_map/ppermute | solution.py:453
  5.2 0.9 %collective-permute-done.near_ref.near_x_ref = bf16[20,20,128]{2,1,0:T(8,128)(2,1)S(1)} collective-permute-done((bf16[20,20,128]{2,1,0:T(8,128)(2,1)S(1)}, bf16[20,20,128]{2,1,0:T(8,128)(2,1)S(1)}, u32[]{:S(2)}, u32[]{:S(2)}) %collective-permute-start) | collective-permute-done | bytes 102432 | tf_op jit(solution)/shard_map/ppermute | solution.py:453
  6.1 0.6 rim.1
  6.8 5.8 %collective-permute-start.2 = (bf16[400,128]{1,0:T(8,128)(2,1)S(1)}, bf16[400,128]{1,0:T(8,128)(2,1)S(1)}, u32[]{:S(2)}, u32[]{:S(2)}) collective-permute-start(bf16[400,128]{1,0:T(8,128)(2,1)S(1)} %get-tuple-element.34), channel_id=1, source_target_pairs={{1,2},{3,4},{5,6},{2,1},{4,3},{6,5},{9,10},{11,12},{13,14},{10,9},... | collective-permute-start | bytes 307208 | tf_op jit(solution)/shard_map/ppermute | solution.py:452
  12.7 0.5 copy.8
  13.4 0.4 copy-done.6
  14.9 1.0 %collective-permute-done.2.next_y_ref = bf16[400,128]{1,0:T(8,128)(2,1)S(1)} collective-permute-done((bf16[400,128]{1,0:T(8,128)(2,1)S(1)}, bf16[400,128]{1,0:T(8,128)(2,1)S(1)}, u32[]{:S(2)}, u32[]{:S(2)}) %collective-permute-start.2) | collective-permute-done | bytes 102432 | tf_op jit(solution)/shard_map/ppermute | solution.py:452
  15.9 2.1 %collective-permute-done.3.near_y_ref = bf16[400,128]{1,0:T(8,128)(2,1)S(1)} collective-permute-done((bf16[400,128]{1,0:T(8,128)(2,1)S(1)}, bf16[400,128]{1,0:T(8,128)(2,1)S(1)}, u32[]{:S(2)}, u32[]{:S(2)}) %collective-permute-start.3) | collective-permute-done | bytes 102432 | tf_op jit(solution)/shard_map/ppermute | solution.py:453
  18.0 1.3 %restrict.1 = (bf16[40,40,128]{2,1,0:T(8,128)(2,1)S(1)}, bf16[5,9,128]{2,1,0:T(8,128)(2,1)S(1)}, bf16[5,9,128]{2,1,0:T(8,128)(2,1)S(1)}, bf16[5,16,128]{2,1,0:T(8,128)(2,1)S(1)}, f32[8,128]{1,0:T(8,128)S(1)}) custom-call(s32[2]{0:T(128)S(1)} %pad_add_fusion.where_ref, bf16[20,20,128]{2,1,0:T(8,128)(2,1)S(1)} %copy-done, ...), custom_call_target="tpu_custom_call" | custom-call | bytes 65536 | tf_op jit(solution)/shard_map/restrict/pallas_call | solution.py:92
  19.4 0.7 %collective-permute-start.5 = (bf16[5,9,128]{2,1,0:T(8,128)(2,1)S(1)}, bf16[5,9,128]{2,1,0:T(8,128)(2,1)S(1)}, u32[]{:S(2)}, u32[]{:S(2)}) collective-permute-start(bf16[5,9,128]{2,1,0:T(8,128)(2,1)S(1)} %get-tuple-element.44), channel_id=1, source_target_pairs={{8,16},{24,32},{40,48},{56,64},{72,80},{88,96},{104,112},{120,128}... | collective-permute-start | bytes 34568 | tf_op jit(solution)/shard_map/ppermute | solution.py:452
  20.0 0.6 broadcast_in_dim.6
  20.7 15.2 %all-to-all-start = ((f32[16,8,128]{2,1,0:T(8,128)}), f32[16,8,128]{2,1,0:T(8,128)S(1)}, u32[]{:S(2)}, u32[]{:S(2)}) async-start(f32[16,8,128]{2,1,0:T(8,128)} %broadcast_in_dim.6), calls=%async_computation | async-start | bytes 131072 | tf_op jit(solution)/shard_map/all_to_all | solution.py:504
  35.9 4.4 %fine_sum.2.refs_0_ = f32[240,256]{1,0:T(8,128)S(1)} custom-call(bf16[40,40,128]{2,1,0:T(8,128)(2,1)S(1)} %get-tuple-element.40.d_in_ref, f32[882,128]{1,0:T(8,128)S(1)} %fusion.v_ref.near_ref), custom_call_target="tpu_custom_call" | custom-call | flops 3114270720 | bytes 65536 | tf_op jit(solution)/shard_map/fine_sum/pallas_call | solution.py:92
  40.4 6.1 %all-to-all-done.recv_ref = f32[16,8,128]{2,1,0:T(8,128)S(1)} async-done(((f32[16,8,128]{2,1,0:T(8,128)}), f32[16,8,128]{2,1,0:T(8,128)S(1)}, u32[]{:S(2)}, u32[]{:S(2)}) %all-to-all-start) | async-done | bytes 65568 | tf_op jit(solution)/shard_map/all_to_all | solution.py:504
  46.5 1.3 %collective-permute-done.6.other_ref = f32[16,8,128]{2,1,0:T(8,128)S(1)} collective-permute-done((f32[16,8,128]{2,1,0:T(8,128)S(1)}, f32[16,8,128]{2,1,0:T(8,128)S(1)}, u32[]{:S(2)}, u32[]{:S(2)}) %collective-permute-start.6) | collective-permute-done | bytes 65568 | tf_op jit(solution)/shard_map/ppermute | solution.py:510
  47.7 1.0 %spread.1 = bf16[208,128]{1,0:T(8,128)(2,1)S(1)} custom-call(s32[2]{0:T(128)S(1)} %pad_add_fusion.where_ref, f32[16,8,128]{2,1,0:T(8,128)S(1)} %all-to-all-done.recv_ref, f32[16,8,128]{2,1,0:T(8,128)S(1)} %collective-permute-done.6.other_ref, f32[2,328,128]{2,1,0:T(8,128)S(1)} %copy-done.2, bf16[5,16,128]{2,1,0:T(8,128)(2,1)S(1)} %get-tuple-element.46.own_ref, ...), custom_call_target="tpu_custom_call" | custom-call | bytes 65536 | tf_op jit(solution)/shard_map/spread/pallas_call | solution.py:92
  48.7 0.8 %broadcast_in_dim.7 = bf16[8,208,128]{2,1,0:T(8,128)(2,1)} broadcast(bf16[208,128]{1,0:T(8,128)(2,1)S(1)} %spread.1), dimensions={1,2} | broadcast | bytes 479232 | tf_op jit(solution)/shard_map/broadcast_in_dim | solution.py:520
  49.5 3.8 %all-to-all-start.1 = ((bf16[8,208,128]{2,1,0:T(8,128)(2,1)}), bf16[8,208,128]{2,1,0:T(8,128)(2,1)S(1)}, u32[]{:S(2)}, u32[]{:S(2)}) async-start(bf16[8,208,128]{2,1,0:T(8,128)(2,1)} %broadcast_in_dim.7), calls=%async_computation.1 | async-start | bytes 851968 | tf_op jit(solution)/shard_map/all_to_all | solution.py:520
  53.4 5.1 %fine_sum.3.fine_ref = f32[240,256]{1,0:T(8,128)S(1)} custom-call(bf16[40,40,128]{2,1,0:T(8,128)(2,1)S(1)} %get-tuple-element.40.d_in_ref, f32[882,128]{1,0:T(8,128)S(1)} %fusion.v_ref.near_ref, f32[240,256]{1,0:T(8,128)S(1)} %fine_sum.2.refs_0_), custom_call_target="tpu_custom_call" | custom-call | flops 4152360960 | bytes 65536 | tf_op jit(solution)/shard_map/fine_sum/pallas_call | solution.py:92
  58.5 2.7 %all-to-all-done.1.recv_ref = bf16[8,208,128]{2,1,0:T(8,128)(2,1)S(1)} async-done(((bf16[8,208,128]{2,1,0:T(8,128)(2,1)}), bf16[8,208,128]{2,1,0:T(8,128)(2,1)S(1)}, u32[]{:S(2)}, u32[]{:S(2)}) %all-to-all-start.1) | async-done | bytes 426016 | tf_op jit(solution)/shard_map/all_to_all | solution.py:520
  61.3 4.0 %final.1 = (f32[20,20,128]{2,1,0:T(8,128)S(1)}, f32[20,20,128]{2,1,0:T(8,128)S(1)}) custom-call(s32[2]{0:T(128)S(1)} %pad_add_fusion.where_ref, bf16[8,208,128]{2,1,0:T(8,128)(2,1)S(1)} %all-to-all-done.1.recv_ref, f32[16,88,128]{2,1,0:T(8,128)S(1)} %copy-done.1, f32[512,128]{1,0:T(8,128)S(1)} %copy-done.3, f32[882,128]{1,0:T(8,128)S(1)} %fusion.v_ref.near_ref, ...), custom_call_target="tpu_custom_call" | custom-call | bytes 65536 | tf_op jit(solution)/shard_map/final/pallas_call | solution.py:92
  65.3 0.7 %add.8 = f32[20,20,128]{2,1,0:T(8,128)} add(f32[20,20,128]{2,1,0:T(8,128)S(1)} %get-tuple-element.53, f32[20,20,128]{2,1,0:T(8,128)S(1)} %get-tuple-element.54) | non-fusion elementwise | flops 51200 | bytes 614400 | tf_op jit(solution)/shard_map/add | solution.py:547
  (23 shorter events, 1.5 us)
Async XLA Ops:
  0.0 1.6 %copy-start = (bf16[20,20,128]{2,1,0:T(8,128)(2,1)S(1)}, bf16[20,20,128]{2,1,0:T(8,128)(2,1)}, u32[]{:S(2)}) copy-start(bf16[20,20,128]{2,1,0:T(8,128)(2,1)} %blk_ref.3) | copy-start | bytes 307204
  0.0 12.7 %copy-start.4 = (bf16[2,21,21,21]{3,0,2,1:T(2,128)(2,1)S(1)}, bf16[2,21,21,21]{3,0,2,1:T(2,128)(2,1)}, u32[]{:S(2)}) copy-start(bf16[2,21,21,21]{3,0,2,1:T(2,128)(2,1)} %param.8) | copy-start | bytes 111136
  0.9 4.3 %collective-permute-start.1 = (bf16[10,20,128]{2,1,0:T(8,128)(2,1)S(1)}, bf16[10,20,128]{2,1,0:T(8,128)(2,1)S(1)}, u32[]{:S(2)}, u32[]{:S(2)}) collective-permute-start(bf16[10,20,128]{2,1,0:T(8,128)(2,1)S(1)} %slice_select_fusion), channel_id=1, source_target_pairs={{8,16},{24,32},{40,48},{56,64},{72,80},{88,96},{104,112},{120,128}... | collective-permute-start | bytes 153608 | tf_op jit(solution)/shard_map/ppermute | solution.py:452
  1.6 4.5 %collective-permute-start = (bf16[20,20,128]{2,1,0:T(8,128)(2,1)S(1)}, bf16[20,20,128]{2,1,0:T(8,128)(2,1)S(1)}, u32[]{:S(2)}, u32[]{:S(2)}) collective-permute-start(bf16[20,20,128]{2,1,0:T(8,128)(2,1)S(1)} %copy-done), channel_id=1, source_target_pairs={{0,8},{16,24},{32,40},{48,56},{64,72},{80,88},{96,104},{112,120},{... | collective-permute-start | bytes 307208 | tf_op jit(solution)/shard_map/ppermute | solution.py:453
  6.8 9.1 %collective-permute-start.2 = (bf16[400,128]{1,0:T(8,128)(2,1)S(1)}, bf16[400,128]{1,0:T(8,128)(2,1)S(1)}, u32[]{:S(2)}, u32[]{:S(2)}) collective-permute-start(bf16[400,128]{1,0:T(8,128)(2,1)S(1)} %get-tuple-element.34), channel_id=1, source_target_pairs={{1,2},{3,4},{5,6},{2,1},{4,3},{6,5},{9,10},{11,12},{13,14},{10,9},... | collective-permute-start | bytes 307208 | tf_op jit(solution)/shard_map/ppermute | solution.py:452
  12.6 5.4 %collective-permute-start.3 = (bf16[400,128]{1,0:T(8,128)(2,1)S(1)}, bf16[400,128]{1,0:T(8,128)(2,1)S(1)}, u32[]{:S(2)}, u32[]{:S(2)}) collective-permute-start(bf16[400,128]{1,0:T(8,128)(2,1)S(1)} %get-tuple-element.35), channel_id=1, source_target_pairs={{0,1},{2,3},{4,5},{6,7},{1,0},{3,2},{5,4},{7,6},{8,9},{10,11},{12,... | collective-permute-start | bytes 307208 | tf_op jit(solution)/shard_map/ppermute | solution.py:453
  13.2 0.7 %copy-start.6 = (bf16[21,128]{1,0:T(8,128)(2,1)S(1)}, bf16[21,128]{1,0:T(8,128)(2,1)}, u32[]{:S(2)}) copy-start(bf16[21,128]{1,0:T(8,128)(2,1)} %constant.34.clone) | copy-start | bytes 16132
  13.9 0.7 %copy-start.5 = (bf16[21,128]{1,0:T(8,128)(2,1)S(1)}, bf16[21,128]{1,0:T(8,128)(2,1)}, u32[]{:S(2)}) copy-start(bf16[21,128]{1,0:T(8,128)(2,1)} %constant.33.clone) | copy-start | bytes 16132
  19.3 16.6 %collective-permute-start.4 = (bf16[5,9,128]{2,1,0:T(8,128)(2,1)S(1)}, bf16[5,9,128]{2,1,0:T(8,128)(2,1)S(1)}, u32[]{:S(2)}, u32[]{:S(2)}) collective-permute-start(bf16[5,9,128]{2,1,0:T(8,128)(2,1)S(1)} %get-tuple-element.42), channel_id=1, source_target_pairs={{0,8},{16,24},{32,40},{48,56},{64,72},{80,88},{96,104},{112,120},{... | collective-permute-start | bytes 34568 | tf_op jit(solution)/shard_map/ppermute | solution.py:453
  19.4 21.0 %collective-permute-start.5 = (bf16[5,9,128]{2,1,0:T(8,128)(2,1)S(1)}, bf16[5,9,128]{2,1,0:T(8,128)(2,1)S(1)}, u32[]{:S(2)}, u32[]{:S(2)}) collective-permute-start(bf16[5,9,128]{2,1,0:T(8,128)(2,1)S(1)} %get-tuple-element.44), channel_id=1, source_target_pairs={{8,16},{24,32},{40,48},{56,64},{72,80},{88,96},{104,112},{120,128}... | collective-permute-start | bytes 34568 | tf_op jit(solution)/shard_map/ppermute | solution.py:452
  20.7 25.8 %all-to-all-start = ((f32[16,8,128]{2,1,0:T(8,128)}), f32[16,8,128]{2,1,0:T(8,128)S(1)}, u32[]{:S(2)}, u32[]{:S(2)}) async-start(f32[16,8,128]{2,1,0:T(8,128)} %broadcast_in_dim.6), calls=%async_computation | async-start | bytes 131072 | tf_op jit(solution)/shard_map/all_to_all | solution.py:504
  35.9 11.8 %copy-start.2 = (f32[2,328,128]{2,1,0:T(8,128)S(1)}, f32[2,328,128]{2,1,0:T(8,128)}, u32[]{:S(2)}) copy-start(f32[2,328,128]{2,1,0:T(8,128)} %constant.35.clone.mx_ref) | copy-start | bytes 1007620
  46.5 1.3 %collective-permute-start.6 = (f32[16,8,128]{2,1,0:T(8,128)S(1)}, f32[16,8,128]{2,1,0:T(8,128)S(1)}, u32[]{:S(2)}, u32[]{:S(2)}) collective-permute-start(f32[16,8,128]{2,1,0:T(8,128)S(1)} %all-to-all-done.recv_ref), channel_id=1, source_target_pairs={{0,8},{16,24},{32,40},{48,56},{64,72},{80,88},{96,104},{112,120},{... | collective-permute-start | bytes 196616 | tf_op jit(solution)/shard_map/ppermute | solution.py:510
  49.5 11.7 %all-to-all-start.1 = ((bf16[8,208,128]{2,1,0:T(8,128)(2,1)}), bf16[8,208,128]{2,1,0:T(8,128)(2,1)S(1)}, u32[]{:S(2)}, u32[]{:S(2)}) async-start(bf16[8,208,128]{2,1,0:T(8,128)(2,1)} %broadcast_in_dim.7), calls=%async_computation.1 | async-start | bytes 851968 | tf_op jit(solution)/shard_map/all_to_all | solution.py:520
  53.4 7.9 %copy-start.1 = (f32[16,88,128]{2,1,0:T(8,128)S(1)}, f32[16,88,128]{2,1,0:T(8,128)}, u32[]{:S(2)}) copy-start(f32[16,88,128]{2,1,0:T(8,128)} %constant.36.clone.my_ref) | copy-start | bytes 2162692
  53.4 7.9 %copy-start.3 = (f32[512,128]{1,0:T(8,128)S(1)}, f32[512,128]{1,0:T(8,128)}, u32[]{:S(2)}) copy-start(f32[512,128]{1,0:T(8,128)} %constant.37.clone.mz_ref) | copy-start | bytes 786436

commit v9 on v7

--- a/solution.py
+++ b/solution.py
@@ -10,7 +10,6 @@
 f32 = jnp.float32
 bf16 = jnp.bfloat16
 spread_norm = 1.2533141
-HIGHEST = lax.Precision.HIGHEST
 REACH = 10
 TAPS = 21
 GROUP = 3
@@ -81,6 +80,21 @@
     return out[0:count] + (out[count : 2 * count] + out[2 * count :])
 
 
+def parts_of(value):
+    high = value.astype(bf16)
+    return high, (value - high.astype(f32)).astype(bf16)
+
+
+def two_part_dot(rows, weights):
+    high, low = parts_of(rows)
+    w_high, w_low = parts_of(weights)
+    return jnp.dot(
+        jnp.concatenate([high, high, low], axis=1),
+        jnp.concatenate([w_high, w_low, w_high], axis=0),
+        preferred_element_type=f32,
+    )
+
+
 def iota2(shape):
     return (lax.broadcasted_iota(jnp.int32, shape, 0), lax.broadcasted_iota(jnp.int32, shape, 1))
 
@@ -107,15 +121,13 @@
 
 def rim_kernel(where_ref, blk_ref, near_ref, next_ref, second_ref, first_ref, wide, dense):
     even_x = even(where_ref[0])
-    even_y = even(where_ref[1])
-    near, other = near_ref[...].astype(f32), next_ref[...].astype(f32)
-    wide[0:10] = jnp.where(even_x, other, near)
-    wide[10:30] = blk_ref[...].astype(f32)
-    wide[30:40] = jnp.where(even_x, near, other)
+    wide[pl.ds(jnp.where(even_x, 30, 0), 10), 0:20, :] = near_ref[...].astype(f32)
+    wide[pl.ds(jnp.where(even_x, 0, 30), 10), 0:20, :] = next_ref[...].astype(f32)
+    wide[10:30, 0:20, :] = blk_ref[...].astype(f32)
+    start = jnp.where(even(where_ref[1]), 10, 0)
     for x in range(40):
-        low, high = wide[x, 0:10, :], wide[x, 10:20, :]
-        dense[0, 10 * x : 10 * x + 10, :] = jnp.where(even_y, high, low)
-        dense[1, 10 * x : 10 * x + 10, :] = jnp.where(even_y, low, high)
+        dense[0, 10 * x : 10 * x + 10, :] = wide[x, pl.ds(start, 10), :]
+        dense[1, 10 * x : 10 * x + 10, :] = wide[x, pl.ds(10 - start, 10), :]
     first_ref[...] = dense[0].astype(bf16)
     second_ref[...] = dense[1].astype(bf16)
 
@@ -123,13 +135,16 @@
 def restrict_kernel(
     where_ref, blk_ref, near_x_ref, next_x_ref, next_y_ref, near_y_ref,
     d_out_ref, second_ref, first_ref, own_ref, out_ref,
-    d_ref, dense, planes, cells, mid,
+    d_ref, dense, sides, planes, cells, mid,
 ):
     even_x = even(where_ref[0])
     even_y = even(where_ref[1])
-    near, other = near_y_ref[...].astype(f32), next_y_ref[...].astype(f32)
-    dense[0] = jnp.where(even_y, other, near)
-    dense[1] = jnp.where(even_y, near, other)
+    upper = jnp.where(even_y, 1, 0)
+    dense[upper] = near_y_ref[...].astype(f32)
+    dense[1 - upper] = next_y_ref[...].astype(f32)
+    upper = jnp.where(even_x, 1, 0)
+    sides[upper, :, 0:20, :] = near_x_ref[...].astype(f32)
+    sides[1 - upper, :, 0:20, :] = next_x_ref[...].astype(f32)
     for x in range(40):
         p, i = x % 2, x // 2
         d_ref[p, i, 0:10, :] = dense[0, 10 * x : 10 * x + 10, :]
@@ -137,9 +152,7 @@
         if 10 <= x < 30:
             centre = blk_ref[x - 10].astype(f32)
         else:
-            near, other = near_x_ref[x % 30].astype(f32), next_x_ref[x % 30].astype(f32)
-            low, high = (other, near) if x < 10 else (near, other)
-            centre = jnp.where(even_x, low, high)
+            centre = sides[x // 30, x % 30, 0:20, :]
         d_ref[p, i, 10:30, :] = centre
         d_out_ref[x] = d_ref[p, i, 0:40, :].astype(bf16)
 
@@ -200,10 +213,12 @@
             )
         sums.append(tap(0) + 0.5625 * (tap(-1) + tap(1)) - 0.0625 * (tap(-3) + tap(3)))
     out = exact_dot(jnp.concatenate(sums, axis=0), down_z)
-    out_ref[...] = jnp.concatenate([out[8 * y : 8 * y + 8] for y in range(4)], axis=1)
-    out_ref[5:6, :] = jnp.concatenate([out[32 + x : 33 + x] for x in range(4)], axis=1)
-    out_ref[6:8, :] = jnp.zeros((2, 128), f32)
-    out_ref[6:7, 0:32] = out[36:37]
+    main = jnp.concatenate([out[8 * y : 8 * y + 8] for y in range(4)], axis=1)[0:5]
+    last = jnp.concatenate([out[32 + x : 33 + x] for x in range(4)], axis=1)
+    rest = jnp.concatenate([out[36:37], jnp.zeros((1, 96), f32)], axis=1)
+    row = jnp.concatenate([main, last, rest, jnp.zeros((1, 128), f32)], axis=0)
+    for k in range(out_ref.shape[0]):
+        out_ref[k] = row
 
 
 def fine_kernel(lo, hi, first, d_in_ref, v_ref, *refs):
@@ -290,9 +305,7 @@
         moved = [jnp.where(lane == at, pltpu.roll(h, at - x, 1), 0.0) for h in halves]
         rows.append(jnp.concatenate(moved, axis=1))
     coarse = recv_ref[...].reshape(8 * recv_ref.shape[0], 128)
-    value = jnp.dot(
-        jnp.concatenate(rows, axis=0), coarse, precision=HIGHEST, preferred_element_type=f32
-    )
+    value = two_part_dot(jnp.concatenate(rows, axis=0), coarse)
     last = value[80:96, 0:32]
     for x in range(4):
         last = last + value[16 * x + 16 : 16 * x + 32, 32 * x : 32 * x + 32]
@@ -311,11 +324,13 @@
         buf[at : at + rows, :] = high
         buf[at + rows : at + 2 * rows, :] = part - high
     buf[173:176, :] = jnp.zeros((3, 128), f32)
-    out_ref[...] = buf[...].astype(bf16)
+    packed = buf[...].astype(bf16)
+    for k in range(out_ref.shape[0]):
+        out_ref[k] = packed
 
 
 def final_kernel(
-    where_ref, recv_ref, my_ref, mz_ref, near_ref, far_ref, fine_ref, out_ref, same_ref,
+    where_ref, recv_ref, my_ref, mz_ref, near_ref, far_ref, fine_ref, out_ref,
     cells, w0, w1, acc, moved, wide, line, tail,
 ):
     index_x = where_ref[0]
@@ -396,9 +411,7 @@
         jnp.concatenate([sums[h][2 * n + p] for p in range(2) for h in range(2)], axis=1)
         for n in range(7)
     ]
-    top = jnp.dot(
-        jnp.concatenate(rows, axis=0), mz_ref[...], precision=HIGHEST, preferred_element_type=f32
-    )
+    top = two_part_dot(jnp.concatenate(rows, axis=0), mz_ref[...])
     total = acc[...] + top
     r, c = iota2((112, 128))
     cell_x = 10 * index_x - 1 + r % 16
@@ -429,8 +442,7 @@
             value = planes[m + 1]
         else:
             value = 0.5625 * (planes[m + 1] + planes[m + 2]) - 0.0625 * (planes[m] + planes[m + 3])
-        out_ref[x] = value
-        same_ref[x] = fine_ref[24 * m : 24 * m + 20, 128 * (x % 2) : 128 * (x % 2) + 128]
+        out_ref[x] = value + fine_ref[24 * m : 24 * m + 20, 128 * (x % 2) : 128 * (x % 2) + 128]
 
 
 def swap(first, second, axis):
@@ -457,7 +469,7 @@
     second, first = vmem_call(
         rim_kernel,
         [shape((400, 128), bf16)] * 2,
-        [pltpu.VMEM((40, 20, 128), f32), pltpu.VMEM((2, 400, 128), f32)],
+        [pltpu.VMEM((40, 24, 128), f32), pltpu.VMEM((2, 400, 128), f32)],
         "rim",
         (where, charges, near_x, next_x),
         smem=1,
@@ -476,11 +488,12 @@
             shape((5, 9, 128), bf16),
             shape((5, 9, 128), bf16),
             shape((5, 16, 128), bf16),
-            shape((8, 128), f32),
+            shape((count_x, 8, 128), f32),
         ],
         [
             pltpu.VMEM((2, 20, 48, 128), f32),
             pltpu.VMEM((2, 400, 128), f32),
+            pltpu.VMEM((2, 10, 24, 128), f32),
             pltpu.VMEM((16, 48, 128), f32),
             pltpu.VMEM((256, 128), f32),
             pltpu.VMEM((9, 24, 128), f32),
@@ -490,24 +503,24 @@
         smem=1,
     )
     near_m, next_m = swap(first, second, "gx")
-    coarse = lax.all_to_all(jnp.broadcast_to(coarse, (count_x, 8, 128)), "gx", 0, 0)
+    coarse = lax.all_to_all(coarse, "gx", 0, 0)
     near, near_m = lax.optimization_barrier((near, near_m))
     fine = fine_sum(0, SPLIT, d, near)
     coarse, fine = lax.optimization_barrier((coarse, fine))
     parts = vmem_call(
         spread_kernel,
-        [shape((208, 128), bf16)],
+        [shape((count_y, 208, 128), bf16)],
         [pltpu.VMEM((208, 128), f32), pltpu.VMEM((16, 128), f32)],
         "spread",
         (where, coarse, jnp.asarray(matrix_x_np(spread)), own, next_m, near_m),
         smem=1,
     )[0]
     parts, near = lax.optimization_barrier((parts, near))
-    parts = lax.all_to_all(jnp.broadcast_to(parts, (count_y, 208, 128)), "gy", 0, 0)
+    parts = lax.all_to_all(parts, "gy", 0, 0)
     fine = fine_sum(SPLIT, TAPS, d, near, fine)
-    total, fine = vmem_call(
+    return vmem_call(
         final_kernel,
-        [shape((20, 20, 128), f32)] * 2,
+        [shape((20, 20, 128), f32)],
         [
             pltpu.VMEM((17, 40, 128), f32),
             pltpu.VMEM((4224, 128), bf16),
@@ -529,8 +542,7 @@
             fine,
         ),
         smem=1,
-    )
-    return total + fine
+    )[0]
 
 
 def solution(mesh):

time: 62 us -> 61.8 us (level)
  Pallas kernels: 16.1 us -> 18.1 us
  local copies, waits for them, and re-layouts: 3.04 us -> 1.54 us
  other arithmetic: 1.72 us -> 0.99 us
    pallas_call x6, Pallas kernels: 16.1 us -> 18.1 us  [vmem_call(): pl.pallas_call(body, out_shape=out_shape, in_specs=[spec(pltpu.SMEM)] * s...]
    broadcast_in_dim x2 -> x0, local copies, waits for them, and re-layouts: 1.5 us -> none  [the longest x1 0.82 us: per_device(): jnp.broadcast_to(parts, (count_y, 208, 128))]
    add x1 -> x0, other arithmetic: 0.73 us -> none  [per_device(): return total + fine]
where the time goes in v9:
time: 61.8 us; the launch traced here: 61.4 us
  starting transfers between devices  27.4 us (44%)
  Pallas kernels  18.1 us (29%)
  waiting for transfers between devices  12.7 us (21%)
  local copies, waits for them, and re-layouts  1.54 us (2%)
  other arithmetic  0.99 us (2%)
    pallas_call x6, Pallas kernels, vmem_call(): pl.pallas_call(body, out_shape=out_shape, in_specs=[spec(pltpu.SMEM)] * s...  18.1 us
    all_to_all x1, starting transfers between devices, per_device(): coarse = lax.all_to_all(coarse, 'gx', 0, 0)  11.5 us
    ppermute x3, starting transfers between devices, swap(): second = lax.ppermute(second, axis, both(others))  7.1 us
    all_to_all x1, waiting for transfers between devices, per_device(): coarse = lax.all_to_all(coarse, 'gx', 0, 0)  6.91 us
    all_to_all x1, starting transfers between devices, per_device(): parts = lax.all_to_all(parts, 'gy', 0, 0)  4.73 us
    ppermute x3, starting transfers between devices, swap(): return (lax.ppermute(first, axis, both(pairs)), second)  4.02 us
    ppermute x3, waiting for transfers between devices, swap(): return (lax.ppermute(first, axis, both(pairs)), second)  3.36 us
    all_to_all x1, waiting for transfers between devices, per_device(): parts = lax.all_to_all(parts, 'gy', 0, 0)  1.44 us
  transfers between devices with their start and end apart: 8, of which 6 were waited for; matrix products, arithmetic and copies ran while one was open for 2% of the time, Pallas kernels for 15%

profile of v9, /device:TPU:2, one launch (start us, length us, event | category | flops | bytes accessed | tf_op | source)
XLA Modules:
  0.0 61.4 jit_solution(8634100188043422156)
XLA Ops:
  0.0 0.9 %broadcast_select_fusion = (bf16[10,20,128]{2,1,0:T(8,128)(2,1)S(1)}, bf16[10,20,128]{2,1,0:T(8,128)(2,1)S(1)}) fusion(pred[]{:T(512)S(6)} %eq.5, bf16[20,20,128]{2,1,0:T(8,128)(2,1)} %blk_ref.3), kind=kLoop, calls=%fused_computation | loop fusion | flops 51200 | bytes 204801 | tf_op jit(solution)/shard_map/jit(_where)/select_n | solution.py:468
  0.9 0.7 %collective-permute-start.1 = (bf16[10,20,128]{2,1,0:T(8,128)(2,1)S(1)}, bf16[10,20,128]{2,1,0:T(8,128)(2,1)S(1)}, u32[]{:S(2)}, u32[]{:S(2)}) collective-permute-start(bf16[10,20,128]{2,1,0:T(8,128)(2,1)S(1)} %get-tuple-element.45), channel_id=1, source_target_pairs={{8,16},{24,32},{40,48},{56,64},{72,80},{88,96},{104,112},{120,128}... | collective-permute-start | bytes 153608 | tf_op jit(solution)/shard_map/ppermute | solution.py:456
  1.6 3.6 %collective-permute-start = (bf16[10,20,128]{2,1,0:T(8,128)(2,1)S(1)}, bf16[10,20,128]{2,1,0:T(8,128)(2,1)S(1)}, u32[]{:S(2)}, u32[]{:S(2)}) collective-permute-start(bf16[10,20,128]{2,1,0:T(8,128)(2,1)S(1)} %get-tuple-element.46), channel_id=1, source_target_pairs={{0,8},{16,24},{32,40},{48,56},{64,72},{80,88},{96,104},{112,120},{... | collective-permute-start | bytes 153608 | tf_op jit(solution)/shard_map/ppermute | solution.py:457
  5.2 0.8 %collective-permute-done.near_ref.near_x_ref = bf16[10,20,128]{2,1,0:T(8,128)(2,1)S(1)} collective-permute-done((bf16[10,20,128]{2,1,0:T(8,128)(2,1)S(1)}, bf16[10,20,128]{2,1,0:T(8,128)(2,1)S(1)}, u32[]{:S(2)}, u32[]{:S(2)}) %collective-permute-start) | collective-permute-done | bytes 51232 | tf_op jit(solution)/shard_map/ppermute | solution.py:457
  6.1 0.6 %rim.1 = (bf16[400,128]{1,0:T(8,128)(2,1)S(1)}, bf16[400,128]{1,0:T(8,128)(2,1)S(1)}) custom-call(s32[2]{0:T(128)S(1)} %pad_add_fusion.where_ref, bf16[20,20,128]{2,1,0:T(8,128)(2,1)S(1)} %copy-done, bf16[10,20,128]{2,1,0:T(8,128)(2,1)S(1)} %collective-permute-done.near_ref.near_x_ref, bf16[10,20,128]{2,1,0:T(8,128)(2,1)S(1)} %collective-permute-done.1.next_ref.next_x_ref), custom_call_target="tpu_custom_call" | custom-call | bytes 65536 | tf_op jit(solution)/shard_map/rim/pallas_call | solution.py:106
  6.7 5.8 %collective-permute-start.2 = (bf16[400,128]{1,0:T(8,128)(2,1)S(1)}, bf16[400,128]{1,0:T(8,128)(2,1)S(1)}, u32[]{:S(2)}, u32[]{:S(2)}) collective-permute-start(bf16[400,128]{1,0:T(8,128)(2,1)S(1)} %get-tuple-element.27), channel_id=1, source_target_pairs={{1,2},{3,4},{5,6},{2,1},{4,3},{6,5},{9,10},{11,12},{13,14},{10,9},... | collective-permute-start | bytes 307208 | tf_op jit(solution)/shard_map/ppermute | solution.py:456
  12.6 0.5 copy.8
  13.3 0.4 copy-done.6
  13.8 0.3 fusion.1.far_ref
  14.1 0.4 copy-done.5
  14.5 0.3 fusion.v_ref.near_ref
  14.8 0.9 %collective-permute-done.2.next_y_ref = bf16[400,128]{1,0:T(8,128)(2,1)S(1)} collective-permute-done((bf16[400,128]{1,0:T(8,128)(2,1)S(1)}, bf16[400,128]{1,0:T(8,128)(2,1)S(1)}, u32[]{:S(2)}, u32[]{:S(2)}) %collective-permute-start.2) | collective-permute-done | bytes 102432 | tf_op jit(solution)/shard_map/ppermute | solution.py:456
  15.7 2.3 %collective-permute-done.3.near_y_ref = bf16[400,128]{1,0:T(8,128)(2,1)S(1)} collective-permute-done((bf16[400,128]{1,0:T(8,128)(2,1)S(1)}, bf16[400,128]{1,0:T(8,128)(2,1)S(1)}, u32[]{:S(2)}, u32[]{:S(2)}) %collective-permute-start.3) | collective-permute-done | bytes 102432 | tf_op jit(solution)/shard_map/ppermute | solution.py:457
  18.0 2.0 %restrict.1 = (bf16[40,40,128]{2,1,0:T(8,128)(2,1)S(1)}, bf16[5,9,128]{2,1,0:T(8,128)(2,1)S(1)}, bf16[5,9,128]{2,1,0:T(8,128)(2,1)S(1)}, bf16[5,16,128]{2,1,0:T(8,128)(2,1)S(1)}, f32[32,8,128]{2,1,0:T(8,128)}) custom-call(s32[2]{0:T(128)S(1)} %pad_add_fusion.where_ref, bf16[20,20,128]{2,1,0:T(8,128)(2,1)S(1)} %copy-done, ...), custom_call_target="tpu_custom_call" | custom-call | bytes 65536 | tf_op jit(solution)/shard_map/restrict/pallas_call | solution.py:106
  20.0 11.5 %all-to-all-start = ((f32[32,8,128]{2,1,0:T(8,128)}), f32[32,8,128]{2,1,0:T(8,128)S(1)}, u32[]{:S(2)}, u32[]{:S(2)}) async-start(f32[32,8,128]{2,1,0:T(8,128)} %get-tuple-element.32), calls=%async_computation | async-start | bytes 262144 | tf_op jit(solution)/shard_map/all_to_all | solution.py:506
  31.5 0.4 collective-permute-start.4
  31.9 0.7 %collective-permute-start.5 = (bf16[5,9,128]{2,1,0:T(8,128)(2,1)S(1)}, bf16[5,9,128]{2,1,0:T(8,128)(2,1)S(1)}, u32[]{:S(2)}, u32[]{:S(2)}) collective-permute-start(bf16[5,9,128]{2,1,0:T(8,128)(2,1)S(1)} %get-tuple-element.39), channel_id=1, source_target_pairs={{8,16},{24,32},{40,48},{56,64},{72,80},{88,96},{104,112},{120,128}... | collective-permute-start | bytes 34568 | tf_op jit(solution)/shard_map/ppermute | solution.py:456
  32.8 2.6 %fine_sum.2.refs_0_ = f32[240,256]{1,0:T(8,128)S(1)} custom-call(bf16[40,40,128]{2,1,0:T(8,128)(2,1)S(1)} %get-tuple-element.33.d_in_ref, f32[882,128]{1,0:T(8,128)S(1)} %fusion.v_ref.near_ref), custom_call_target="tpu_custom_call" | custom-call | flops 2076180480 | bytes 65536 | tf_op jit(solution)/shard_map/fine_sum/pallas_call | solution.py:106
  35.4 6.9 %all-to-all-done.recv_ref = f32[32,8,128]{2,1,0:T(8,128)S(1)} async-done(((f32[32,8,128]{2,1,0:T(8,128)}), f32[32,8,128]{2,1,0:T(8,128)S(1)}, u32[]{:S(2)}, u32[]{:S(2)}) %all-to-all-start) | async-done | bytes 131104 | tf_op jit(solution)/shard_map/all_to_all | solution.py:506
  42.3 1.7 %spread.1 = bf16[8,208,128]{2,1,0:T(8,128)(2,1)} custom-call(s32[2]{0:T(128)S(1)} %pad_add_fusion.where_ref, f32[32,8,128]{2,1,0:T(8,128)S(1)} %all-to-all-done.recv_ref, f32[2,328,128]{2,1,0:T(8,128)S(1)} %copy-done.2, bf16[5,16,128]{2,1,0:T(8,128)(2,1)S(1)} %get-tuple-element.38.own_ref, bf16[5,9,128]{2,1,0:T(8,128)(2,1)S(1)} %collective-permute-done.5.next_ref, ...), custom_call_target="tpu_custom_call" | custom-call | bytes 65536 | tf_op jit(solution)/shard_map/spread/pallas_call | solution.py:106
  44.0 4.7 %all-to-all-start.1 = ((bf16[8,208,128]{2,1,0:T(8,128)(2,1)}), bf16[8,208,128]{2,1,0:T(8,128)(2,1)S(1)}, u32[]{:S(2)}, u32[]{:S(2)}) async-start(bf16[8,208,128]{2,1,0:T(8,128)(2,1)} %spread.1), calls=%async_computation.1 | async-start | bytes 851968 | tf_op jit(solution)/shard_map/all_to_all | solution.py:519
  48.7 6.6 %fine_sum.3.fine_ref = f32[240,256]{1,0:T(8,128)S(1)} custom-call(bf16[40,40,128]{2,1,0:T(8,128)(2,1)S(1)} %get-tuple-element.33.d_in_ref, f32[882,128]{1,0:T(8,128)S(1)} %fusion.v_ref.near_ref, f32[240,256]{1,0:T(8,128)S(1)} %fine_sum.2.refs_0_), custom_call_target="tpu_custom_call" | custom-call | flops 5190451200 | bytes 65536 | tf_op jit(solution)/shard_map/fine_sum/pallas_call | solution.py:106
  55.3 1.4 %all-to-all-done.1.recv_ref = bf16[8,208,128]{2,1,0:T(8,128)(2,1)S(1)} async-done(((bf16[8,208,128]{2,1,0:T(8,128)(2,1)}), bf16[8,208,128]{2,1,0:T(8,128)(2,1)S(1)}, u32[]{:S(2)}, u32[]{:S(2)}) %all-to-all-start.1) | async-done | bytes 426016 | tf_op jit(solution)/shard_map/all_to_all | solution.py:519
  56.8 4.6 %final.1 = f32[20,20,128]{2,1,0:T(8,128)} custom-call(s32[2]{0:T(128)S(1)} %pad_add_fusion.where_ref, bf16[8,208,128]{2,1,0:T(8,128)(2,1)S(1)} %all-to-all-done.1.recv_ref, f32[16,88,128]{2,1,0:T(8,128)S(1)} %copy-done.1, f32[512,128]{1,0:T(8,128)S(1)} %copy-done.3, f32[882,128]{1,0:T(8,128)S(1)} %fusion.v_ref.near_ref, f32[882,128]{1,0:T(8,128)S(1)} %fusion.1.far_ref, ...), custom_call_target="tpu_custom_call" | custom-call | bytes 65536 | tf_op jit(solution)/shard_map/final/pallas_call | solution.py:106
  (18 shorter events, 0.7 us)
Async XLA Ops:
  0.0 6.1 %copy-start = (bf16[20,20,128]{2,1,0:T(8,128)(2,1)S(1)}, bf16[20,20,128]{2,1,0:T(8,128)(2,1)}, u32[]{:S(2)}) copy-start(bf16[20,20,128]{2,1,0:T(8,128)(2,1)} %blk_ref.3) | copy-start | bytes 307204
  0.0 12.6 %copy-start.4 = (bf16[2,21,21,21]{3,0,2,1:T(2,128)(2,1)S(1)}, bf16[2,21,21,21]{3,0,2,1:T(2,128)(2,1)}, u32[]{:S(2)}) copy-start(bf16[2,21,21,21]{3,0,2,1:T(2,128)(2,1)} %param.8) | copy-start | bytes 111136
  0.9 4.3 %collective-permute-start.1 = (bf16[10,20,128]{2,1,0:T(8,128)(2,1)S(1)}, bf16[10,20,128]{2,1,0:T(8,128)(2,1)S(1)}, u32[]{:S(2)}, u32[]{:S(2)}) collective-permute-start(bf16[10,20,128]{2,1,0:T(8,128)(2,1)S(1)} %get-tuple-element.45), channel_id=1, source_target_pairs={{8,16},{24,32},{40,48},{56,64},{72,80},{88,96},{104,112},{120,128}... | collective-permute-start | bytes 153608 | tf_op jit(solution)/shard_map/ppermute | solution.py:456
  1.6 4.5 %collective-permute-start = (bf16[10,20,128]{2,1,0:T(8,128)(2,1)S(1)}, bf16[10,20,128]{2,1,0:T(8,128)(2,1)S(1)}, u32[]{:S(2)}, u32[]{:S(2)}) collective-permute-start(bf16[10,20,128]{2,1,0:T(8,128)(2,1)S(1)} %get-tuple-element.46), channel_id=1, source_target_pairs={{0,8},{16,24},{32,40},{48,56},{64,72},{80,88},{96,104},{112,120},{... | collective-permute-start | bytes 153608 | tf_op jit(solution)/shard_map/ppermute | solution.py:457
  6.7 9.0 %collective-permute-start.2 = (bf16[400,128]{1,0:T(8,128)(2,1)S(1)}, bf16[400,128]{1,0:T(8,128)(2,1)S(1)}, u32[]{:S(2)}, u32[]{:S(2)}) collective-permute-start(bf16[400,128]{1,0:T(8,128)(2,1)S(1)} %get-tuple-element.27), channel_id=1, source_target_pairs={{1,2},{3,4},{5,6},{2,1},{4,3},{6,5},{9,10},{11,12},{13,14},{10,9},... | collective-permute-start | bytes 307208 | tf_op jit(solution)/shard_map/ppermute | solution.py:456
  12.5 5.5 %collective-permute-start.3 = (bf16[400,128]{1,0:T(8,128)(2,1)S(1)}, bf16[400,128]{1,0:T(8,128)(2,1)S(1)}, u32[]{:S(2)}, u32[]{:S(2)}) collective-permute-start(bf16[400,128]{1,0:T(8,128)(2,1)S(1)} %get-tuple-element.28), channel_id=1, source_target_pairs={{0,1},{2,3},{4,5},{6,7},{1,0},{3,2},{5,4},{7,6},{8,9},{10,11},{12,... | collective-permute-start | bytes 307208 | tf_op jit(solution)/shard_map/ppermute | solution.py:457
  13.1 0.7 %copy-start.6 = (bf16[21,128]{1,0:T(8,128)(2,1)S(1)}, bf16[21,128]{1,0:T(8,128)(2,1)}, u32[]{:S(2)}) copy-start(bf16[21,128]{1,0:T(8,128)(2,1)} %constant.34.clone) | copy-start | bytes 16132
  13.8 0.7 %copy-start.5 = (bf16[21,128]{1,0:T(8,128)(2,1)S(1)}, bf16[21,128]{1,0:T(8,128)(2,1)}, u32[]{:S(2)}) copy-start(bf16[21,128]{1,0:T(8,128)(2,1)} %constant.33.clone) | copy-start | bytes 16132
  20.0 22.3 %all-to-all-start = ((f32[32,8,128]{2,1,0:T(8,128)}), f32[32,8,128]{2,1,0:T(8,128)S(1)}, u32[]{:S(2)}, u32[]{:S(2)}) async-start(f32[32,8,128]{2,1,0:T(8,128)} %get-tuple-element.32), calls=%async_computation | async-start | bytes 262144 | tf_op jit(solution)/shard_map/all_to_all | solution.py:506
  31.5 1.3 %collective-permute-start.4 = (bf16[5,9,128]{2,1,0:T(8,128)(2,1)S(1)}, bf16[5,9,128]{2,1,0:T(8,128)(2,1)S(1)}, u32[]{:S(2)}, u32[]{:S(2)}) collective-permute-start(bf16[5,9,128]{2,1,0:T(8,128)(2,1)S(1)} %get-tuple-element.35), channel_id=1, source_target_pairs={{0,8},{16,24},{32,40},{48,56},{64,72},{80,88},{96,104},{112,120},{... | collective-permute-start | bytes 34568 | tf_op jit(solution)/shard_map/ppermute | solution.py:457
  31.9 10.4 %collective-permute-start.5 = (bf16[5,9,128]{2,1,0:T(8,128)(2,1)S(1)}, bf16[5,9,128]{2,1,0:T(8,128)(2,1)S(1)}, u32[]{:S(2)}, u32[]{:S(2)}) collective-permute-start(bf16[5,9,128]{2,1,0:T(8,128)(2,1)S(1)} %get-tuple-element.39), channel_id=1, source_target_pairs={{8,16},{24,32},{40,48},{56,64},{72,80},{88,96},{104,112},{120,128}... | collective-permute-start | bytes 34568 | tf_op jit(solution)/shard_map/ppermute | solution.py:456
  32.8 9.5 %copy-start.2 = (f32[2,328,128]{2,1,0:T(8,128)S(1)}, f32[2,328,128]{2,1,0:T(8,128)}, u32[]{:S(2)}) copy-start(f32[2,328,128]{2,1,0:T(8,128)} %constant.35.clone.mx_ref) | copy-start | bytes 1007620
  44.0 12.7 %all-to-all-start.1 = ((bf16[8,208,128]{2,1,0:T(8,128)(2,1)}), bf16[8,208,128]{2,1,0:T(8,128)(2,1)S(1)}, u32[]{:S(2)}, u32[]{:S(2)}) async-start(bf16[8,208,128]{2,1,0:T(8,128)(2,1)} %spread.1), calls=%async_computation.1 | async-start | bytes 851968 | tf_op jit(solution)/shard_map/all_to_all | solution.py:519
  48.7 8.0 %copy-start.1 = (f32[16,88,128]{2,1,0:T(8,128)S(1)}, f32[16,88,128]{2,1,0:T(8,128)}, u32[]{:S(2)}) copy-start(f32[16,88,128]{2,1,0:T(8,128)} %constant.36.clone.my_ref) | copy-start | bytes 2162692
  48.7 8.0 %copy-start.3 = (f32[512,128]{1,0:T(8,128)S(1)}, f32[512,128]{1,0:T(8,128)}, u32[]{:S(2)}) copy-start(f32[512,128]{1,0:T(8,128)} %constant.37.clone.mz_ref) | copy-start | bytes 786436

commit v10 on v9

--- a/solution.py
+++ b/solution.py
@@ -119,17 +119,26 @@
     return index % 2 == 0
 
 
-def rim_kernel(where_ref, blk_ref, near_ref, next_ref, second_ref, first_ref, wide, dense):
-    even_x = even(where_ref[0])
-    wide[pl.ds(jnp.where(even_x, 30, 0), 10), 0:20, :] = near_ref[...].astype(f32)
-    wide[pl.ds(jnp.where(even_x, 0, 30), 10), 0:20, :] = next_ref[...].astype(f32)
-    wide[10:30, 0:20, :] = blk_ref[...].astype(f32)
+def rim_rows(where_ref, wide, dense, count):
     start = jnp.where(even(where_ref[1]), 10, 0)
-    for x in range(40):
+    for x in range(count):
         dense[0, 10 * x : 10 * x + 10, :] = wide[x, pl.ds(start, 10), :]
         dense[1, 10 * x : 10 * x + 10, :] = wide[x, pl.ds(10 - start, 10), :]
-    first_ref[...] = dense[0].astype(bf16)
-    second_ref[...] = dense[1].astype(bf16)
+
+
+def rim_own_kernel(where_ref, blk_ref, out_ref, wide, dense):
+    wide[:, 0:20, :] = blk_ref[...].astype(f32)
+    rim_rows(where_ref, wide, dense, 20)
+    out_ref[...] = dense[...]
+
+
+def rim_kernel(where_ref, own_ref, near_ref, next_ref, first_ref, second_ref, wide, dense):
+    even_x = even(where_ref[0])
+    wide[pl.ds(jnp.where(even_x, 10, 0), 10), 0:20, :] = near_ref[...].astype(f32)
+    wide[pl.ds(jnp.where(even_x, 0, 10), 10), 0:20, :] = next_ref[...].astype(f32)
+    rim_rows(where_ref, wide, dense, 20)
+    for k, out_ref in enumerate((first_ref, second_ref)):
+        out_ref[...] = jnp.concatenate([own_ref[k], dense[k]], axis=0).astype(bf16)
 
 
 def restrict_kernel(
@@ -147,8 +156,9 @@
     sides[1 - upper, :, 0:20, :] = next_x_ref[...].astype(f32)
     for x in range(40):
         p, i = x % 2, x // 2
-        d_ref[p, i, 0:10, :] = dense[0, 10 * x : 10 * x + 10, :]
-        d_ref[p, i, 30:40, :] = dense[1, 10 * x : 10 * x + 10, :]
+        at = 10 * (x - 10 if 10 <= x < 30 else x + 20 if x < 10 else x)
+        d_ref[p, i, 0:10, :] = dense[0, at : at + 10, :]
+        d_ref[p, i, 30:40, :] = dense[1, at : at + 10, :]
         if 10 <= x < 30:
             centre = blk_ref[x - 10].astype(f32)
         else:
@@ -466,12 +476,22 @@
     low, high = charges[:10], charges[10:]
     even_x = even(lax.axis_index("gx"))
     near_x, next_x = swap(jnp.where(even_x, high, low), jnp.where(even_x, low, high), "gx")
-    second, first = vmem_call(
+    scratch = [pltpu.VMEM((20, 24, 128), f32), pltpu.VMEM((2, 200, 128), f32)]
+    own = vmem_call(
+        rim_own_kernel,
+        [shape((2, 200, 128), f32)],
+        scratch,
+        "rim_own",
+        (where, charges),
+        smem=1,
+        flops=1 << 20,
+    )[0]
+    first, second = vmem_call(
         rim_kernel,
         [shape((400, 128), bf16)] * 2,
-        [pltpu.VMEM((40, 24, 128), f32), pltpu.VMEM((2, 400, 128), f32)],
+        scratch,
         "rim",
-        (where, charges, near_x, next_x),
+        (where, own, near_x, next_x),
         smem=1,
     )
     first, second, kernels = lax.optimization_barrier((first, second, kernels))

time: 61.8 us -> 61.7 us (level)
  waiting for transfers between devices: 12.7 us -> 12 us
    ppermute x3, waiting for transfers between devices: 3.36 us -> 2.74 us  [swap(): return (lax.ppermute(first, axis, both(pairs)), second)]
    pallas_call x6 -> x7, Pallas kernels: 18.1 us -> 18.6 us  [vmem_call(): pl.pallas_call(body, out_shape=out_shape, in_specs=[spec(pltpu.SMEM)] * s...]
  transfers between devices with their start and end apart: 8 -> 8, of which waited for: 6 -> 6; matrix products, arithmetic and copies ran while one was open for 2% -> 2% of each run, Pallas kernels for 15% -> 16%
where the time goes in v10:
time: 61.7 us; the launch traced here: 61.3 us
  starting transfers between devices  27.4 us (44%)
  Pallas kernels  18.6 us (30%)
  waiting for transfers between devices  12 us (19%)
  local copies, waits for them, and re-layouts  1.54 us (2%)
  other arithmetic  0.99 us (2%)
  matrix products  0.62 us (1%)
    pallas_call x7, Pallas kernels, vmem_call(): pl.pallas_call(body, out_shape=out_shape, in_specs=[spec(pltpu.SMEM)] * s...  18.6 us
    all_to_all x1, starting transfers between devices, per_device(): coarse = lax.all_to_all(coarse, 'gx', 0, 0)  11.5 us
    ppermute x3, starting transfers between devices, swap(): second = lax.ppermute(second, axis, both(others))  7.11 us
    all_to_all x1, waiting for transfers between devices, per_device(): coarse = lax.all_to_all(coarse, 'gx', 0, 0)  6.92 us
    all_to_all x1, starting transfers between devices, per_device(): parts = lax.all_to_all(parts, 'gy', 0, 0)  4.73 us
    ppermute x3, starting transfers between devices, swap(): return (lax.ppermute(first, axis, both(pairs)), second)  4.02 us
    ppermute x3, waiting for transfers between devices, swap(): return (lax.ppermute(first, axis, both(pairs)), second)  2.74 us
    all_to_all x1, waiting for transfers between devices, per_device(): parts = lax.all_to_all(parts, 'gy', 0, 0)  1.44 us
  transfers between devices with their start and end apart: 8, of which 6 were waited for; matrix products, arithmetic and copies ran while one was open for 2% of the time, Pallas kernels for 16%

profile of v10, /device:TPU:2, one launch (start us, length us, event | category | flops | bytes accessed | tf_op | source)
XLA Modules:
  0.0 61.3 jit_solution(12969144857537198508)
XLA Ops:
  0.0 0.9 %broadcast_select_fusion = (bf16[10,20,128]{2,1,0:T(8,128)(2,1)S(1)}, bf16[10,20,128]{2,1,0:T(8,128)(2,1)S(1)}) fusion(pred[]{:T(512)S(6)} %eq.5, bf16[20,20,128]{2,1,0:T(8,128)(2,1)} %blk_ref.3), kind=kLoop, calls=%fused_computation | loop fusion | flops 51200 | bytes 204801 | tf_op jit(solution)/shard_map/jit(_where)/select_n | solution.py:478
  0.9 0.7 %collective-permute-start.1 = (bf16[10,20,128]{2,1,0:T(8,128)(2,1)S(1)}, bf16[10,20,128]{2,1,0:T(8,128)(2,1)S(1)}, u32[]{:S(2)}, u32[]{:S(2)}) collective-permute-start(bf16[10,20,128]{2,1,0:T(8,128)(2,1)S(1)} %get-tuple-element.45), channel_id=1, source_target_pairs={{8,16},{24,32},{40,48},{56,64},{72,80},{88,96},{104,112},{120,128}... | collective-permute-start | bytes 153608 | tf_op jit(solution)/shard_map/ppermute | solution.py:466
  1.6 3.6 %collective-permute-start = (bf16[10,20,128]{2,1,0:T(8,128)(2,1)S(1)}, bf16[10,20,128]{2,1,0:T(8,128)(2,1)S(1)}, u32[]{:S(2)}, u32[]{:S(2)}) collective-permute-start(bf16[10,20,128]{2,1,0:T(8,128)(2,1)S(1)} %get-tuple-element.46), channel_id=1, source_target_pairs={{0,8},{16,24},{32,40},{48,56},{64,72},{80,88},{96,104},{112,120},{... | collective-permute-start | bytes 153608 | tf_op jit(solution)/shard_map/ppermute | solution.py:467
  5.2 0.6 rim_own.1.own_ref
  6.1 0.6 rim.1
  6.7 5.8 %collective-permute-start.2 = (bf16[400,128]{1,0:T(8,128)(2,1)S(1)}, bf16[400,128]{1,0:T(8,128)(2,1)S(1)}, u32[]{:S(2)}, u32[]{:S(2)}) collective-permute-start(bf16[400,128]{1,0:T(8,128)(2,1)S(1)} %get-tuple-element.27), channel_id=1, source_target_pairs={{1,2},{3,4},{5,6},{2,1},{4,3},{6,5},{9,10},{11,12},{13,14},{10,9},... | collective-permute-start | bytes 307208 | tf_op jit(solution)/shard_map/ppermute | solution.py:466
  12.6 0.5 copy.8
  13.3 0.4 copy-done.6
  13.7 0.3 fusion.1.far_ref
  14.1 0.4 copy-done.5
  14.4 0.3 fusion.v_ref.near_ref
  14.7 0.9 %collective-permute-done.2.next_y_ref = bf16[400,128]{1,0:T(8,128)(2,1)S(1)} collective-permute-done((bf16[400,128]{1,0:T(8,128)(2,1)S(1)}, bf16[400,128]{1,0:T(8,128)(2,1)S(1)}, u32[]{:S(2)}, u32[]{:S(2)}) %collective-permute-start.2) | collective-permute-done | bytes 102432 | tf_op jit(solution)/shard_map/ppermute | solution.py:466
  15.7 2.3 %collective-permute-done.3.near_y_ref = bf16[400,128]{1,0:T(8,128)(2,1)S(1)} collective-permute-done((bf16[400,128]{1,0:T(8,128)(2,1)S(1)}, bf16[400,128]{1,0:T(8,128)(2,1)S(1)}, u32[]{:S(2)}, u32[]{:S(2)}) %collective-permute-start.3) | collective-permute-done | bytes 102432 | tf_op jit(solution)/shard_map/ppermute | solution.py:467
  18.0 2.0 %restrict.1 = (bf16[40,40,128]{2,1,0:T(8,128)(2,1)S(1)}, bf16[5,9,128]{2,1,0:T(8,128)(2,1)S(1)}, bf16[5,9,128]{2,1,0:T(8,128)(2,1)S(1)}, bf16[5,16,128]{2,1,0:T(8,128)(2,1)S(1)}, f32[32,8,128]{2,1,0:T(8,128)}) custom-call(s32[2]{0:T(128)S(1)} %pad_add_fusion.where_ref, bf16[20,20,128]{2,1,0:T(8,128)(2,1)S(1)} %copy-done, ...), custom_call_target="tpu_custom_call" | custom-call | bytes 65536 | tf_op jit(solution)/shard_map/restrict/pallas_call | solution.py:106
  20.0 11.5 %all-to-all-start = ((f32[32,8,128]{2,1,0:T(8,128)}), f32[32,8,128]{2,1,0:T(8,128)S(1)}, u32[]{:S(2)}, u32[]{:S(2)}) async-start(f32[32,8,128]{2,1,0:T(8,128)} %get-tuple-element.32), calls=%async_computation | async-start | bytes 262144 | tf_op jit(solution)/shard_map/all_to_all | solution.py:526
  31.5 0.4 collective-permute-start.4
  31.9 0.7 %collective-permute-start.5 = (bf16[5,9,128]{2,1,0:T(8,128)(2,1)S(1)}, bf16[5,9,128]{2,1,0:T(8,128)(2,1)S(1)}, u32[]{:S(2)}, u32[]{:S(2)}) collective-permute-start(bf16[5,9,128]{2,1,0:T(8,128)(2,1)S(1)} %get-tuple-element.39), channel_id=1, source_target_pairs={{8,16},{24,32},{40,48},{56,64},{72,80},{88,96},{104,112},{120,128}... | collective-permute-start | bytes 34568 | tf_op jit(solution)/shard_map/ppermute | solution.py:466
  32.8 2.6 %fine_sum.2.refs_0_ = f32[240,256]{1,0:T(8,128)S(1)} custom-call(bf16[40,40,128]{2,1,0:T(8,128)(2,1)S(1)} %get-tuple-element.33.d_in_ref, f32[882,128]{1,0:T(8,128)S(1)} %fusion.v_ref.near_ref), custom_call_target="tpu_custom_call" | custom-call | flops 2076180480 | bytes 65536 | tf_op jit(solution)/shard_map/fine_sum/pallas_call | solution.py:106
  35.3 6.9 %all-to-all-done.recv_ref = f32[32,8,128]{2,1,0:T(8,128)S(1)} async-done(((f32[32,8,128]{2,1,0:T(8,128)}), f32[32,8,128]{2,1,0:T(8,128)S(1)}, u32[]{:S(2)}, u32[]{:S(2)}) %all-to-all-start) | async-done | bytes 131104 | tf_op jit(solution)/shard_map/all_to_all | solution.py:526
  42.3 1.7 %spread.1 = bf16[8,208,128]{2,1,0:T(8,128)(2,1)} custom-call(s32[2]{0:T(128)S(1)} %pad_add_fusion.where_ref, f32[32,8,128]{2,1,0:T(8,128)S(1)} %all-to-all-done.recv_ref, f32[2,328,128]{2,1,0:T(8,128)S(1)} %copy-done.2, bf16[5,16,128]{2,1,0:T(8,128)(2,1)S(1)} %get-tuple-element.38.own_ref, bf16[5,9,128]{2,1,0:T(8,128)(2,1)S(1)} %collective-permute-done.5.next_ref, ...), custom_call_target="tpu_custom_call" | custom-call | bytes 65536 | tf_op jit(solution)/shard_map/spread/pallas_call | solution.py:106
  44.0 4.7 %all-to-all-start.1 = ((bf16[8,208,128]{2,1,0:T(8,128)(2,1)}), bf16[8,208,128]{2,1,0:T(8,128)(2,1)S(1)}, u32[]{:S(2)}, u32[]{:S(2)}) async-start(bf16[8,208,128]{2,1,0:T(8,128)(2,1)} %spread.1), calls=%async_computation.1 | async-start | bytes 851968 | tf_op jit(solution)/shard_map/all_to_all | solution.py:539
  48.7 6.6 %fine_sum.3.fine_ref = f32[240,256]{1,0:T(8,128)S(1)} custom-call(bf16[40,40,128]{2,1,0:T(8,128)(2,1)S(1)} %get-tuple-element.33.d_in_ref, f32[882,128]{1,0:T(8,128)S(1)} %fusion.v_ref.near_ref, f32[240,256]{1,0:T(8,128)S(1)} %fine_sum.2.refs_0_), custom_call_target="tpu_custom_call" | custom-call | flops 5190451200 | bytes 65536 | tf_op jit(solution)/shard_map/fine_sum/pallas_call | solution.py:106
  55.3 1.4 %all-to-all-done.1.recv_ref = bf16[8,208,128]{2,1,0:T(8,128)(2,1)S(1)} async-done(((bf16[8,208,128]{2,1,0:T(8,128)(2,1)}), bf16[8,208,128]{2,1,0:T(8,128)(2,1)S(1)}, u32[]{:S(2)}, u32[]{:S(2)}) %all-to-all-start.1) | async-done | bytes 426016 | tf_op jit(solution)/shard_map/all_to_all | solution.py:539
  56.7 4.6 %final.1 = f32[20,20,128]{2,1,0:T(8,128)} custom-call(s32[2]{0:T(128)S(1)} %pad_add_fusion.where_ref, bf16[8,208,128]{2,1,0:T(8,128)(2,1)S(1)} %all-to-all-done.1.recv_ref, f32[16,88,128]{2,1,0:T(8,128)S(1)} %copy-done.1, f32[512,128]{1,0:T(8,128)S(1)} %copy-done.3, f32[882,128]{1,0:T(8,128)S(1)} %fusion.v_ref.near_ref, f32[882,128]{1,0:T(8,128)S(1)} %fusion.1.far_ref, ...), custom_call_target="tpu_custom_call" | custom-call | bytes 65536 | tf_op jit(solution)/shard_map/final/pallas_call | solution.py:106
  (19 shorter events, 0.9 us)
Async XLA Ops:
  0.0 5.2 %copy-start = (bf16[20,20,128]{2,1,0:T(8,128)(2,1)S(1)}, bf16[20,20,128]{2,1,0:T(8,128)(2,1)}, u32[]{:S(2)}) copy-start(bf16[20,20,128]{2,1,0:T(8,128)(2,1)} %blk_ref.3) | copy-start | bytes 307204
  0.9 4.9 %collective-permute-start.1 = (bf16[10,20,128]{2,1,0:T(8,128)(2,1)S(1)}, bf16[10,20,128]{2,1,0:T(8,128)(2,1)S(1)}, u32[]{:S(2)}, u32[]{:S(2)}) collective-permute-start(bf16[10,20,128]{2,1,0:T(8,128)(2,1)S(1)} %get-tuple-element.45), channel_id=1, source_target_pairs={{8,16},{24,32},{40,48},{56,64},{72,80},{88,96},{104,112},{120,128}... | collective-permute-start | bytes 153608 | tf_op jit(solution)/shard_map/ppermute | solution.py:466
  1.6 4.5 %collective-permute-start = (bf16[10,20,128]{2,1,0:T(8,128)(2,1)S(1)}, bf16[10,20,128]{2,1,0:T(8,128)(2,1)S(1)}, u32[]{:S(2)}, u32[]{:S(2)}) collective-permute-start(bf16[10,20,128]{2,1,0:T(8,128)(2,1)S(1)} %get-tuple-element.46), channel_id=1, source_target_pairs={{0,8},{16,24},{32,40},{48,56},{64,72},{80,88},{96,104},{112,120},{... | collective-permute-start | bytes 153608 | tf_op jit(solution)/shard_map/ppermute | solution.py:467
  5.8 6.7 %copy-start.4 = (bf16[2,21,21,21]{3,0,2,1:T(2,128)(2,1)S(1)}, bf16[2,21,21,21]{3,0,2,1:T(2,128)(2,1)}, u32[]{:S(2)}) copy-start(bf16[2,21,21,21]{3,0,2,1:T(2,128)(2,1)} %param.8) | copy-start | bytes 111136
  6.7 9.0 %collective-permute-start.2 = (bf16[400,128]{1,0:T(8,128)(2,1)S(1)}, bf16[400,128]{1,0:T(8,128)(2,1)S(1)}, u32[]{:S(2)}, u32[]{:S(2)}) collective-permute-start(bf16[400,128]{1,0:T(8,128)(2,1)S(1)} %get-tuple-element.27), channel_id=1, source_target_pairs={{1,2},{3,4},{5,6},{2,1},{4,3},{6,5},{9,10},{11,12},{13,14},{10,9},... | collective-permute-start | bytes 307208 | tf_op jit(solution)/shard_map/ppermute | solution.py:466
  12.5 5.5 %collective-permute-start.3 = (bf16[400,128]{1,0:T(8,128)(2,1)S(1)}, bf16[400,128]{1,0:T(8,128)(2,1)S(1)}, u32[]{:S(2)}, u32[]{:S(2)}) collective-permute-start(bf16[400,128]{1,0:T(8,128)(2,1)S(1)} %get-tuple-element.28), channel_id=1, source_target_pairs={{0,1},{2,3},{4,5},{6,7},{1,0},{3,2},{5,4},{7,6},{8,9},{10,11},{12,... | collective-permute-start | bytes 307208 | tf_op jit(solution)/shard_map/ppermute | solution.py:467
  13.0 0.7 %copy-start.6 = (bf16[21,128]{1,0:T(8,128)(2,1)S(1)}, bf16[21,128]{1,0:T(8,128)(2,1)}, u32[]{:S(2)}) copy-start(bf16[21,128]{1,0:T(8,128)(2,1)} %constant.34.clone) | copy-start | bytes 16132
  13.7 0.7 %copy-start.5 = (bf16[21,128]{1,0:T(8,128)(2,1)S(1)}, bf16[21,128]{1,0:T(8,128)(2,1)}, u32[]{:S(2)}) copy-start(bf16[21,128]{1,0:T(8,128)(2,1)} %constant.33.clone) | copy-start | bytes 16132
  20.0 22.3 %all-to-all-start = ((f32[32,8,128]{2,1,0:T(8,128)}), f32[32,8,128]{2,1,0:T(8,128)S(1)}, u32[]{:S(2)}, u32[]{:S(2)}) async-start(f32[32,8,128]{2,1,0:T(8,128)} %get-tuple-element.32), calls=%async_computation | async-start | bytes 262144 | tf_op jit(solution)/shard_map/all_to_all | solution.py:526
  31.5 1.3 %collective-permute-start.4 = (bf16[5,9,128]{2,1,0:T(8,128)(2,1)S(1)}, bf16[5,9,128]{2,1,0:T(8,128)(2,1)S(1)}, u32[]{:S(2)}, u32[]{:S(2)}) collective-permute-start(bf16[5,9,128]{2,1,0:T(8,128)(2,1)S(1)} %get-tuple-element.35), channel_id=1, source_target_pairs={{0,8},{16,24},{32,40},{48,56},{64,72},{80,88},{96,104},{112,120},{... | collective-permute-start | bytes 34568 | tf_op jit(solution)/shard_map/ppermute | solution.py:467
  31.9 10.4 %collective-permute-start.5 = (bf16[5,9,128]{2,1,0:T(8,128)(2,1)S(1)}, bf16[5,9,128]{2,1,0:T(8,128)(2,1)S(1)}, u32[]{:S(2)}, u32[]{:S(2)}) collective-permute-start(bf16[5,9,128]{2,1,0:T(8,128)(2,1)S(1)} %get-tuple-element.39), channel_id=1, source_target_pairs={{8,16},{24,32},{40,48},{56,64},{72,80},{88,96},{104,112},{120,128}... | collective-permute-start | bytes 34568 | tf_op jit(solution)/shard_map/ppermute | solution.py:466
  32.8 9.5 %copy-start.2 = (f32[2,328,128]{2,1,0:T(8,128)S(1)}, f32[2,328,128]{2,1,0:T(8,128)}, u32[]{:S(2)}) copy-start(f32[2,328,128]{2,1,0:T(8,128)} %constant.35.clone.mx_ref) | copy-start | bytes 1007620
  44.0 12.7 %all-to-all-start.1 = ((bf16[8,208,128]{2,1,0:T(8,128)(2,1)}), bf16[8,208,128]{2,1,0:T(8,128)(2,1)S(1)}, u32[]{:S(2)}, u32[]{:S(2)}) async-start(bf16[8,208,128]{2,1,0:T(8,128)(2,1)} %spread.1), calls=%async_computation.1 | async-start | bytes 851968 | tf_op jit(solution)/shard_map/all_to_all | solution.py:539
  48.7 8.0 %copy-start.1 = (f32[16,88,128]{2,1,0:T(8,128)S(1)}, f32[16,88,128]{2,1,0:T(8,128)}, u32[]{:S(2)}) copy-start(f32[16,88,128]{2,1,0:T(8,128)} %constant.36.clone.my_ref) | copy-start | bytes 2162692
  48.7 8.0 %copy-start.3 = (f32[512,128]{1,0:T(8,128)S(1)}, f32[512,128]{1,0:T(8,128)}, u32[]{:S(2)}) copy-start(f32[512,128]{1,0:T(8,128)} %constant.37.clone.mz_ref) | copy-start | bytes 786436

commit v11 on v10

--- a/solution.py
+++ b/solution.py
@@ -99,14 +99,14 @@
     return (lax.broadcasted_iota(jnp.int32, shape, 0), lax.broadcasted_iota(jnp.int32, shape, 1))
 
 
-def vmem_call(body, out_shape, scratch, name, args, smem=0, flops=0, limit=8):
+def vmem_call(body, out_shape, scratch, name, args, flops=0, limit=8):
     def spec(space):
         return pl.BlockSpec(memory_space=space)
 
     return pl.pallas_call(
         body,
         out_shape=out_shape,
-        in_specs=[spec(pltpu.SMEM)] * smem + [spec(pltpu.VMEM)] * (len(args) - smem),
+        in_specs=[spec(pltpu.VMEM)] * len(args),
         out_specs=[spec(pltpu.VMEM)] * len(out_shape),
         scratch_shapes=scratch,
         compiler_params=pltpu.CompilerParams(vmem_limit_bytes=limit << 20),
@@ -119,35 +119,35 @@
     return index % 2 == 0
 
 
-def rim_rows(where_ref, wide, dense, count):
-    start = jnp.where(even(where_ref[1]), 10, 0)
+def rim_rows(wide, dense, count):
+    start = jnp.where(even(lax.axis_index("gy")), 10, 0)
     for x in range(count):
         dense[0, 10 * x : 10 * x + 10, :] = wide[x, pl.ds(start, 10), :]
         dense[1, 10 * x : 10 * x + 10, :] = wide[x, pl.ds(10 - start, 10), :]
 
 
-def rim_own_kernel(where_ref, blk_ref, out_ref, wide, dense):
+def rim_own_kernel(blk_ref, out_ref, wide, dense):
     wide[:, 0:20, :] = blk_ref[...].astype(f32)
-    rim_rows(where_ref, wide, dense, 20)
+    rim_rows(wide, dense, 20)
     out_ref[...] = dense[...]
 
 
-def rim_kernel(where_ref, own_ref, near_ref, next_ref, first_ref, second_ref, wide, dense):
-    even_x = even(where_ref[0])
+def rim_kernel(own_ref, near_ref, next_ref, first_ref, second_ref, wide, dense):
+    even_x = even(lax.axis_index("gx"))
     wide[pl.ds(jnp.where(even_x, 10, 0), 10), 0:20, :] = near_ref[...].astype(f32)
     wide[pl.ds(jnp.where(even_x, 0, 10), 10), 0:20, :] = next_ref[...].astype(f32)
-    rim_rows(where_ref, wide, dense, 20)
+    rim_rows(wide, dense, 20)
     for k, out_ref in enumerate((first_ref, second_ref)):
         out_ref[...] = jnp.concatenate([own_ref[k], dense[k]], axis=0).astype(bf16)
 
 
 def restrict_kernel(
-    where_ref, blk_ref, near_x_ref, next_x_ref, next_y_ref, near_y_ref,
+    blk_ref, near_x_ref, next_x_ref, next_y_ref, near_y_ref,
     d_out_ref, second_ref, first_ref, own_ref, out_ref,
     d_ref, dense, sides, planes, cells, mid,
 ):
-    even_x = even(where_ref[0])
-    even_y = even(where_ref[1])
+    even_x = even(lax.axis_index("gx"))
+    even_y = even(lax.axis_index("gy"))
     upper = jnp.where(even_y, 1, 0)
     dense[upper] = near_y_ref[...].astype(f32)
     dense[1 - upper] = next_y_ref[...].astype(f32)
@@ -192,8 +192,8 @@
     down_z = jnp.where(r // 128 == c // 64, weight(r % 128 - 2 * (c % 64)), 0.0)
     value = exact_dot(jnp.concatenate(rows, axis=0), down_z)
     r, c = iota2((144, 128))
-    cell_x = 10 * where_ref[0] - 3 + r % 16
-    cell_y = 10 * where_ref[1] - 4 + 2 * (r // 16) + c // 64
+    cell_x = 10 * lax.axis_index("gx") - 3 + r % 16
+    cell_y = 10 * lax.axis_index("gy") - 4 + 2 * (r // 16) + c // 64
     inside = (cell_x >= 0) & (cell_x < 320) & (cell_y >= 0) & (cell_y < 80)
     value = jnp.where(inside, value, 0.0).astype(bf16).astype(f32)
     for n in range(9):
@@ -304,9 +304,9 @@
     )[0]
 
 
-def spread_kernel(where_ref, recv_ref, mx_ref, own_ref, next_ref, near_ref, out_ref, buf, tail):
-    even_x = even(where_ref[0])
-    start = 10 * where_ref[0]
+def spread_kernel(recv_ref, mx_ref, own_ref, next_ref, near_ref, out_ref, buf, tail):
+    even_x = even(lax.axis_index("gx"))
+    start = 10 * lax.axis_index("gx")
     halves = [mx_ref[h, pl.ds(start, 16), :] for h in range(2)]
     lane = lax.broadcasted_iota(jnp.int32, (16, 128), 1) % 8
     rows = [jnp.concatenate(halves, axis=1)]
@@ -340,11 +340,11 @@
 
 
 def final_kernel(
-    where_ref, recv_ref, my_ref, mz_ref, near_ref, far_ref, fine_ref, out_ref,
+    recv_ref, my_ref, mz_ref, near_ref, far_ref, fine_ref, out_ref,
     cells, w0, w1, acc, moved, wide, line, tail,
 ):
-    index_x = where_ref[0]
-    index_y = where_ref[1]
+    index_x = lax.axis_index("gx")
+    index_y = lax.axis_index("gy")
     count = recv_ref.shape[0]
     cells[:, 32:40, :] = jnp.zeros((17, 8, 128), f32)
     for step in range(-2, 3):
@@ -470,7 +470,6 @@
 def per_device(charges, kernels):
     count_x = lax.axis_size("gx")
     count_y = lax.axis_size("gy")
-    where = jnp.stack([lax.axis_index("gx"), lax.axis_index("gy")]).astype(jnp.int32)
     spread = charges.shape[0] * count_x / 16.0
     shape = jax.ShapeDtypeStruct
     low, high = charges[:10], charges[10:]
@@ -482,8 +481,7 @@
         [shape((2, 200, 128), f32)],
         scratch,
         "rim_own",
-        (where, charges),
-        smem=1,
+        (charges,),
         flops=1 << 20,
     )[0]
     first, second = vmem_call(
@@ -491,8 +489,7 @@
         [shape((400, 128), bf16)] * 2,
         scratch,
         "rim",
-        (where, own, near_x, next_x),
-        smem=1,
+        (own, near_x, next_x),
     )
     first, second, kernels = lax.optimization_barrier((first, second, kernels))
     near, far = (
@@ -519,8 +516,7 @@
             pltpu.VMEM((9, 24, 128), f32),
         ],
         "restrict",
-        (where, charges, near_x, next_x, next_y, near_y),
-        smem=1,
+        (charges, near_x, next_x, next_y, near_y),
     )
     near_m, next_m = swap(first, second, "gx")
     coarse = lax.all_to_all(coarse, "gx", 0, 0)
@@ -532,8 +528,7 @@
         [shape((count_y, 208, 128), bf16)],
         [pltpu.VMEM((208, 128), f32), pltpu.VMEM((16, 128), f32)],
         "spread",
-        (where, coarse, jnp.asarray(matrix_x_np(spread)), own, next_m, near_m),
-        smem=1,
+        (coarse, jnp.asarray(matrix_x_np(spread)), own, next_m, near_m),
     )[0]
     parts, near = lax.optimization_barrier((parts, near))
     parts = lax.all_to_all(parts, "gy", 0, 0)
@@ -553,7 +548,6 @@
         ],
         "final",
         (
-            where,
             parts,
             jnp.asarray(matrix_y_np(spread)),
             jnp.asarray(matrix_z_np(spread)),
@@ -561,7 +555,6 @@
             far,
             fine,
         ),
-        smem=1,
     )[0]
 
 

time: 61.7 us -> 59.6 us (0.966)
  Pallas kernels: 18.6 us -> 15.9 us
  waiting for transfers between devices: 12 us -> 12.7 us
    pallas_call x7, Pallas kernels: 18.6 us -> 15.9 us  [vmem_call(): pl.pallas_call(body, out_shape=out_shape, in_specs=[spec(pltpu.VMEM)] * l...]
where the time goes in v11:
time: 59.6 us; the launch traced here: 59.2 us
  starting transfers between devices  27.4 us (46%)
  Pallas kernels  15.9 us (27%)
  waiting for transfers between devices  12.7 us (21%)
  local copies, waits for them, and re-layouts  1.54 us (3%)
  other arithmetic  0.91 us (2%)
  matrix products  0.62 us (1%)
    pallas_call x7, Pallas kernels, vmem_call(): pl.pallas_call(body, out_shape=out_shape, in_specs=[spec(pltpu.VMEM)] * l...  15.9 us
    all_to_all x1, starting transfers between devices, per_device(): coarse = lax.all_to_all(coarse, 'gx', 0, 0)  11.5 us
    ppermute x3, starting transfers between devices, swap(): second = lax.ppermute(second, axis, both(others))  7.11 us
    all_to_all x1, waiting for transfers between devices, per_device(): coarse = lax.all_to_all(coarse, 'gx', 0, 0)  6.91 us
    all_to_all x1, starting transfers between devices, per_device(): parts = lax.all_to_all(parts, 'gy', 0, 0)  4.73 us
    ppermute x3, starting transfers between devices, swap(): return (lax.ppermute(first, axis, both(pairs)), second)  4.02 us
    ppermute x3, waiting for transfers between devices, swap(): return (lax.ppermute(first, axis, both(pairs)), second)  3.36 us
    all_to_all x1, waiting for transfers between devices, per_device(): parts = lax.all_to_all(parts, 'gy', 0, 0)  1.44 us
  transfers between devices with their start and end apart: 8, of which 6 were waited for; matrix products, arithmetic and copies ran while one was open for 2% of the time, Pallas kernels for 16%

profile of v11, /device:TPU:2, one launch (start us, length us, event | category | flops | bytes accessed | tf_op | source)
XLA Modules:
  0.0 59.2 jit_solution(18277899496653842303)
XLA Ops:
  0.0 0.9 %broadcast_select_fusion = (bf16[10,20,128]{2,1,0:T(8,128)(2,1)S(1)}, bf16[10,20,128]{2,1,0:T(8,128)(2,1)S(1)}) fusion(pred[]{:T(512)S(6)} %eq.5, bf16[20,20,128]{2,1,0:T(8,128)(2,1)} %blk_ref.3), kind=kLoop, calls=%fused_computation | loop fusion | flops 51200 | bytes 204801 | tf_op jit(solution)/shard_map/jit(_where)/select_n | solution.py:477
  0.9 0.7 %collective-permute-start.1 = (bf16[10,20,128]{2,1,0:T(8,128)(2,1)S(1)}, bf16[10,20,128]{2,1,0:T(8,128)(2,1)S(1)}, u32[]{:S(2)}, u32[]{:S(2)}) collective-permute-start(bf16[10,20,128]{2,1,0:T(8,128)(2,1)S(1)} %get-tuple-element.45), channel_id=1, source_target_pairs={{8,16},{24,32},{40,48},{56,64},{72,80},{88,96},{104,112},{120,128}... | collective-permute-start | bytes 153608 | tf_op jit(solution)/shard_map/ppermute | solution.py:466
  1.6 3.6 %collective-permute-start = (bf16[10,20,128]{2,1,0:T(8,128)(2,1)S(1)}, bf16[10,20,128]{2,1,0:T(8,128)(2,1)S(1)}, u32[]{:S(2)}, u32[]{:S(2)}) collective-permute-start(bf16[10,20,128]{2,1,0:T(8,128)(2,1)S(1)} %get-tuple-element.46), channel_id=1, source_target_pairs={{0,8},{16,24},{32,40},{48,56},{64,72},{80,88},{96,104},{112,120},{... | collective-permute-start | bytes 153608 | tf_op jit(solution)/shard_map/ppermute | solution.py:467
  5.2 0.8 %collective-permute-done.near_ref.near_x_ref = bf16[10,20,128]{2,1,0:T(8,128)(2,1)S(1)} collective-permute-done((bf16[10,20,128]{2,1,0:T(8,128)(2,1)S(1)}, bf16[10,20,128]{2,1,0:T(8,128)(2,1)S(1)}, u32[]{:S(2)}, u32[]{:S(2)}) %collective-permute-start) | collective-permute-done | bytes 51232 | tf_op jit(solution)/shard_map/ppermute | solution.py:467
  6.1 5.8 %collective-permute-start.2 = (bf16[400,128]{1,0:T(8,128)(2,1)S(1)}, bf16[400,128]{1,0:T(8,128)(2,1)S(1)}, u32[]{:S(2)}, u32[]{:S(2)}) collective-permute-start(bf16[400,128]{1,0:T(8,128)(2,1)S(1)} %get-tuple-element.27), channel_id=1, source_target_pairs={{1,2},{3,4},{5,6},{2,1},{4,3},{6,5},{9,10},{11,12},{13,14},{10,9},... | collective-permute-start | bytes 307208 | tf_op jit(solution)/shard_map/ppermute | solution.py:466
  12.0 0.5 copy.8
  12.5 0.3 reshape.4
  12.8 0.4 copy-done.6
  13.2 0.3 fusion.1.far_ref
  13.5 0.4 copy-done.5
  13.9 0.3 fusion.v_ref.near_ref
  14.2 0.9 %collective-permute-done.2.next_y_ref = bf16[400,128]{1,0:T(8,128)(2,1)S(1)} collective-permute-done((bf16[400,128]{1,0:T(8,128)(2,1)S(1)}, bf16[400,128]{1,0:T(8,128)(2,1)S(1)}, u32[]{:S(2)}, u32[]{:S(2)}) %collective-permute-start.2) | collective-permute-done | bytes 102432 | tf_op jit(solution)/shard_map/ppermute | solution.py:466
  15.2 2.3 %collective-permute-done.3.near_y_ref = bf16[400,128]{1,0:T(8,128)(2,1)S(1)} collective-permute-done((bf16[400,128]{1,0:T(8,128)(2,1)S(1)}, bf16[400,128]{1,0:T(8,128)(2,1)S(1)}, u32[]{:S(2)}, u32[]{:S(2)}) %collective-permute-start.3) | collective-permute-done | bytes 102432 | tf_op jit(solution)/shard_map/ppermute | solution.py:467
  17.4 1.4 %restrict.1 = (bf16[40,40,128]{2,1,0:T(8,128)(2,1)S(1)}, bf16[5,9,128]{2,1,0:T(8,128)(2,1)S(1)}, bf16[5,9,128]{2,1,0:T(8,128)(2,1)S(1)}, bf16[5,16,128]{2,1,0:T(8,128)(2,1)S(1)}, f32[32,8,128]{2,1,0:T(8,128)}) custom-call(bf16[20,20,128]{2,1,0:T(8,128)(2,1)S(1)} %copy-done, bf16[10,20,128]{2,1,0:T(8,128)(2,1)S(1)} %collective-permute-done.near_ref.near_x_ref, ...), custom_call_target="tpu_custom_call" | custom-call | bytes 65536 | tf_op jit(solution)/shard_map/restrict/pallas_call | solution.py:106
  18.9 11.5 %all-to-all-start = ((f32[32,8,128]{2,1,0:T(8,128)}), f32[32,8,128]{2,1,0:T(8,128)S(1)}, u32[]{:S(2)}, u32[]{:S(2)}) async-start(f32[32,8,128]{2,1,0:T(8,128)} %get-tuple-element.32), calls=%async_computation | async-start | bytes 262144 | tf_op jit(solution)/shard_map/all_to_all | solution.py:522
  30.4 0.4 collective-permute-start.4
  30.8 0.7 %collective-permute-start.5 = (bf16[5,9,128]{2,1,0:T(8,128)(2,1)S(1)}, bf16[5,9,128]{2,1,0:T(8,128)(2,1)S(1)}, u32[]{:S(2)}, u32[]{:S(2)}) collective-permute-start(bf16[5,9,128]{2,1,0:T(8,128)(2,1)S(1)} %get-tuple-element.39), channel_id=1, source_target_pairs={{8,16},{24,32},{40,48},{56,64},{72,80},{88,96},{104,112},{120,128}... | collective-permute-start | bytes 34568 | tf_op jit(solution)/shard_map/ppermute | solution.py:466
  31.7 2.6 %fine_sum.2.refs_0_ = f32[240,256]{1,0:T(8,128)S(1)} custom-call(bf16[40,40,128]{2,1,0:T(8,128)(2,1)S(1)} %get-tuple-element.33.d_in_ref, f32[882,128]{1,0:T(8,128)S(1)} %fusion.v_ref.near_ref), custom_call_target="tpu_custom_call" | custom-call | flops 2076180480 | bytes 65536 | tf_op jit(solution)/shard_map/fine_sum/pallas_call | solution.py:106
  34.3 6.9 %all-to-all-done.recv_ref = f32[32,8,128]{2,1,0:T(8,128)S(1)} async-done(((f32[32,8,128]{2,1,0:T(8,128)}), f32[32,8,128]{2,1,0:T(8,128)S(1)}, u32[]{:S(2)}, u32[]{:S(2)}) %all-to-all-start) | async-done | bytes 131104 | tf_op jit(solution)/shard_map/all_to_all | solution.py:522
  41.2 1.2 %spread.1 = bf16[8,208,128]{2,1,0:T(8,128)(2,1)} custom-call(f32[32,8,128]{2,1,0:T(8,128)S(1)} %all-to-all-done.recv_ref, f32[2,328,128]{2,1,0:T(8,128)S(1)} %copy-done.2, bf16[5,16,128]{2,1,0:T(8,128)(2,1)S(1)} %get-tuple-element.38.own_ref, bf16[5,9,128]{2,1,0:T(8,128)(2,1)S(1)} %collective-permute-done.5.next_ref, ...), custom_call_target="tpu_custom_call" | custom-call | bytes 65536 | tf_op jit(solution)/shard_map/spread/pallas_call | solution.py:106
  42.4 4.7 %all-to-all-start.1 = ((bf16[8,208,128]{2,1,0:T(8,128)(2,1)}), bf16[8,208,128]{2,1,0:T(8,128)(2,1)S(1)}, u32[]{:S(2)}, u32[]{:S(2)}) async-start(bf16[8,208,128]{2,1,0:T(8,128)(2,1)} %spread.1), calls=%async_computation.1 | async-start | bytes 851968 | tf_op jit(solution)/shard_map/all_to_all | solution.py:534
  47.1 6.6 %fine_sum.3.fine_ref = f32[240,256]{1,0:T(8,128)S(1)} custom-call(bf16[40,40,128]{2,1,0:T(8,128)(2,1)S(1)} %get-tuple-element.33.d_in_ref, f32[882,128]{1,0:T(8,128)S(1)} %fusion.v_ref.near_ref, f32[240,256]{1,0:T(8,128)S(1)} %fine_sum.2.refs_0_), custom_call_target="tpu_custom_call" | custom-call | flops 5190451200 | bytes 65536 | tf_op jit(solution)/shard_map/fine_sum/pallas_call | solution.py:106
  53.7 1.4 %all-to-all-done.1.recv_ref = bf16[8,208,128]{2,1,0:T(8,128)(2,1)S(1)} async-done(((bf16[8,208,128]{2,1,0:T(8,128)(2,1)}), bf16[8,208,128]{2,1,0:T(8,128)(2,1)S(1)}, u32[]{:S(2)}, u32[]{:S(2)}) %all-to-all-start.1) | async-done | bytes 426016 | tf_op jit(solution)/shard_map/all_to_all | solution.py:534
  55.1 4.1 %final.1 = f32[20,20,128]{2,1,0:T(8,128)} custom-call(bf16[8,208,128]{2,1,0:T(8,128)(2,1)S(1)} %all-to-all-done.1.recv_ref, f32[16,88,128]{2,1,0:T(8,128)S(1)} %copy-done.1, f32[512,128]{1,0:T(8,128)S(1)} %copy-done.3, f32[882,128]{1,0:T(8,128)S(1)} %fusion.v_ref.near_ref, f32[882,128]{1,0:T(8,128)S(1)} %fusion.1.far_ref, f32[240,256]{1,0:T(8,128)S(1)} %fine_sum.3.fine_ref), custom_call_target="tpu_custom_call" | custom-call | bytes 65536 | tf_op jit(solution)/shard_map/final/pallas_call | solution.py:106
  (18 shorter events, 0.5 us)
Async XLA Ops:
  0.0 5.2 %copy-start = (bf16[20,20,128]{2,1,0:T(8,128)(2,1)S(1)}, bf16[20,20,128]{2,1,0:T(8,128)(2,1)}, u32[]{:S(2)}) copy-start(bf16[20,20,128]{2,1,0:T(8,128)(2,1)} %blk_ref.3) | copy-start | bytes 307204
  0.9 4.3 %collective-permute-start.1 = (bf16[10,20,128]{2,1,0:T(8,128)(2,1)S(1)}, bf16[10,20,128]{2,1,0:T(8,128)(2,1)S(1)}, u32[]{:S(2)}, u32[]{:S(2)}) collective-permute-start(bf16[10,20,128]{2,1,0:T(8,128)(2,1)S(1)} %get-tuple-element.45), channel_id=1, source_target_pairs={{8,16},{24,32},{40,48},{56,64},{72,80},{88,96},{104,112},{120,128}... | collective-permute-start | bytes 153608 | tf_op jit(solution)/shard_map/ppermute | solution.py:466
  1.6 4.5 %collective-permute-start = (bf16[10,20,128]{2,1,0:T(8,128)(2,1)S(1)}, bf16[10,20,128]{2,1,0:T(8,128)(2,1)S(1)}, u32[]{:S(2)}, u32[]{:S(2)}) collective-permute-start(bf16[10,20,128]{2,1,0:T(8,128)(2,1)S(1)} %get-tuple-element.46), channel_id=1, source_target_pairs={{0,8},{16,24},{32,40},{48,56},{64,72},{80,88},{96,104},{112,120},{... | collective-permute-start | bytes 153608 | tf_op jit(solution)/shard_map/ppermute | solution.py:467
  5.2 6.8 %copy-start.4 = (bf16[2,21,21,21]{3,0,2,1:T(2,128)(2,1)S(1)}, bf16[2,21,21,21]{3,0,2,1:T(2,128)(2,1)}, u32[]{:S(2)}) copy-start(bf16[2,21,21,21]{3,0,2,1:T(2,128)(2,1)} %param.8) | copy-start | bytes 111136
  6.1 9.0 %collective-permute-start.2 = (bf16[400,128]{1,0:T(8,128)(2,1)S(1)}, bf16[400,128]{1,0:T(8,128)(2,1)S(1)}, u32[]{:S(2)}, u32[]{:S(2)}) collective-permute-start(bf16[400,128]{1,0:T(8,128)(2,1)S(1)} %get-tuple-element.27), channel_id=1, source_target_pairs={{1,2},{3,4},{5,6},{2,1},{4,3},{6,5},{9,10},{11,12},{13,14},{10,9},... | collective-permute-start | bytes 307208 | tf_op jit(solution)/shard_map/ppermute | solution.py:466
  11.9 5.5 %collective-permute-start.3 = (bf16[400,128]{1,0:T(8,128)(2,1)S(1)}, bf16[400,128]{1,0:T(8,128)(2,1)S(1)}, u32[]{:S(2)}, u32[]{:S(2)}) collective-permute-start(bf16[400,128]{1,0:T(8,128)(2,1)S(1)} %get-tuple-element.28), channel_id=1, source_target_pairs={{0,1},{2,3},{4,5},{6,7},{1,0},{3,2},{5,4},{7,6},{8,9},{10,11},{12,... | collective-permute-start | bytes 307208 | tf_op jit(solution)/shard_map/ppermute | solution.py:467
  12.5 0.7 %copy-start.6 = (bf16[21,128]{1,0:T(8,128)(2,1)S(1)}, bf16[21,128]{1,0:T(8,128)(2,1)}, u32[]{:S(2)}) copy-start(bf16[21,128]{1,0:T(8,128)(2,1)} %constant.31.clone) | copy-start | bytes 16132
  13.2 0.7 %copy-start.5 = (bf16[21,128]{1,0:T(8,128)(2,1)S(1)}, bf16[21,128]{1,0:T(8,128)(2,1)}, u32[]{:S(2)}) copy-start(bf16[21,128]{1,0:T(8,128)(2,1)} %constant.30.clone) | copy-start | bytes 16132
  18.9 22.3 %all-to-all-start = ((f32[32,8,128]{2,1,0:T(8,128)}), f32[32,8,128]{2,1,0:T(8,128)S(1)}, u32[]{:S(2)}, u32[]{:S(2)}) async-start(f32[32,8,128]{2,1,0:T(8,128)} %get-tuple-element.32), calls=%async_computation | async-start | bytes 262144 | tf_op jit(solution)/shard_map/all_to_all | solution.py:522
  30.4 1.3 %collective-permute-start.4 = (bf16[5,9,128]{2,1,0:T(8,128)(2,1)S(1)}, bf16[5,9,128]{2,1,0:T(8,128)(2,1)S(1)}, u32[]{:S(2)}, u32[]{:S(2)}) collective-permute-start(bf16[5,9,128]{2,1,0:T(8,128)(2,1)S(1)} %get-tuple-element.35), channel_id=1, source_target_pairs={{0,8},{16,24},{32,40},{48,56},{64,72},{80,88},{96,104},{112,120},{... | collective-permute-start | bytes 34568 | tf_op jit(solution)/shard_map/ppermute | solution.py:467
  30.8 10.4 %collective-permute-start.5 = (bf16[5,9,128]{2,1,0:T(8,128)(2,1)S(1)}, bf16[5,9,128]{2,1,0:T(8,128)(2,1)S(1)}, u32[]{:S(2)}, u32[]{:S(2)}) collective-permute-start(bf16[5,9,128]{2,1,0:T(8,128)(2,1)S(1)} %get-tuple-element.39), channel_id=1, source_target_pairs={{8,16},{24,32},{40,48},{56,64},{72,80},{88,96},{104,112},{120,128}... | collective-permute-start | bytes 34568 | tf_op jit(solution)/shard_map/ppermute | solution.py:466
  31.7 9.5 %copy-start.2 = (f32[2,328,128]{2,1,0:T(8,128)S(1)}, f32[2,328,128]{2,1,0:T(8,128)}, u32[]{:S(2)}) copy-start(f32[2,328,128]{2,1,0:T(8,128)} %constant.32.clone.mx_ref) | copy-start | bytes 1007620
  42.4 12.7 %all-to-all-start.1 = ((bf16[8,208,128]{2,1,0:T(8,128)(2,1)}), bf16[8,208,128]{2,1,0:T(8,128)(2,1)S(1)}, u32[]{:S(2)}, u32[]{:S(2)}) async-start(bf16[8,208,128]{2,1,0:T(8,128)(2,1)} %spread.1), calls=%async_computation.1 | async-start | bytes 851968 | tf_op jit(solution)/shard_map/all_to_all | solution.py:534
  47.1 8.0 %copy-start.1 = (f32[16,88,128]{2,1,0:T(8,128)S(1)}, f32[16,88,128]{2,1,0:T(8,128)}, u32[]{:S(2)}) copy-start(f32[16,88,128]{2,1,0:T(8,128)} %constant.33.clone.my_ref) | copy-start | bytes 2162692
  47.1 8.0 %copy-start.3 = (f32[512,128]{1,0:T(8,128)S(1)}, f32[512,128]{1,0:T(8,128)}, u32[]{:S(2)}) copy-start(f32[512,128]{1,0:T(8,128)} %constant.34.clone.mz_ref) | copy-start | bytes 786436

commit v12 on v11

--- a/solution.py
+++ b/solution.py
@@ -119,6 +119,16 @@
     return index % 2 == 0
 
 
+def edges_kernel(blk_ref, first_ref, second_ref, wide, dense):
+    wide[:, 0:20, :] = blk_ref[...].astype(f32)
+    start = jnp.where(even(lax.axis_index("gx")), 10, 0)
+    for x in range(10):
+        dense[0, 20 * x : 20 * x + 20, :] = wide[start + x, 0:20, :]
+        dense[1, 20 * x : 20 * x + 20, :] = wide[10 - start + x, 0:20, :]
+    first_ref[...] = dense[0].astype(bf16)
+    second_ref[...] = dense[1].astype(bf16)
+
+
 def rim_rows(wide, dense, count):
     start = jnp.where(even(lax.axis_index("gy")), 10, 0)
     for x in range(count):
@@ -132,10 +142,14 @@
     out_ref[...] = dense[...]
 
 
-def rim_kernel(own_ref, near_ref, next_ref, first_ref, second_ref, wide, dense):
+def rim_kernel(own_ref, next_ref, near_ref, first_ref, second_ref, wide, dense):
     even_x = even(lax.axis_index("gx"))
-    wide[pl.ds(jnp.where(even_x, 10, 0), 10), 0:20, :] = near_ref[...].astype(f32)
-    wide[pl.ds(jnp.where(even_x, 0, 10), 10), 0:20, :] = next_ref[...].astype(f32)
+    start = jnp.where(even_x, 10, 0)
+    dense[0] = near_ref[...].astype(f32)
+    dense[1] = next_ref[...].astype(f32)
+    for x in range(10):
+        wide[start + x, 0:20, :] = dense[0, 20 * x : 20 * x + 20, :]
+        wide[10 - start + x, 0:20, :] = dense[1, 20 * x : 20 * x + 20, :]
     rim_rows(wide, dense, 20)
     for k, out_ref in enumerate((first_ref, second_ref)):
         out_ref[...] = jnp.concatenate([own_ref[k], dense[k]], axis=0).astype(bf16)
@@ -152,8 +166,8 @@
     dense[upper] = near_y_ref[...].astype(f32)
     dense[1 - upper] = next_y_ref[...].astype(f32)
     upper = jnp.where(even_x, 1, 0)
-    sides[upper, :, 0:20, :] = near_x_ref[...].astype(f32)
-    sides[1 - upper, :, 0:20, :] = next_x_ref[...].astype(f32)
+    sides[upper] = near_x_ref[...].astype(f32)
+    sides[1 - upper] = next_x_ref[...].astype(f32)
     for x in range(40):
         p, i = x % 2, x // 2
         at = 10 * (x - 10 if 10 <= x < 30 else x + 20 if x < 10 else x)
@@ -162,7 +176,8 @@
         if 10 <= x < 30:
             centre = blk_ref[x - 10].astype(f32)
         else:
-            centre = sides[x // 30, x % 30, 0:20, :]
+            at = 20 * (x % 30)
+            centre = sides[x // 30, at : at + 20, :]
         d_ref[p, i, 10:30, :] = centre
         d_out_ref[x] = d_ref[p, i, 0:40, :].astype(bf16)
 
@@ -472,10 +487,11 @@
     count_y = lax.axis_size("gy")
     spread = charges.shape[0] * count_x / 16.0
     shape = jax.ShapeDtypeStruct
-    low, high = charges[:10], charges[10:]
-    even_x = even(lax.axis_index("gx"))
-    near_x, next_x = swap(jnp.where(even_x, high, low), jnp.where(even_x, low, high), "gx")
     scratch = [pltpu.VMEM((20, 24, 128), f32), pltpu.VMEM((2, 200, 128), f32)]
+    first, second = vmem_call(
+        edges_kernel, [shape((200, 128), bf16)] * 2, scratch, "edges", (charges,)
+    )
+    near_x, next_x = swap(first, second, "gx")
     own = vmem_call(
         rim_own_kernel,
         [shape((2, 200, 128), f32)],
@@ -489,7 +505,7 @@
         [shape((400, 128), bf16)] * 2,
         scratch,
         "rim",
-        (own, near_x, next_x),
+        (own, next_x, near_x),
     )
     first, second, kernels = lax.optimization_barrier((first, second, kernels))
     near, far = (
@@ -510,7 +526,7 @@
         [
             pltpu.VMEM((2, 20, 48, 128), f32),
             pltpu.VMEM((2, 400, 128), f32),
-            pltpu.VMEM((2, 10, 24, 128), f32),
+            pltpu.VMEM((2, 200, 128), f32),
             pltpu.VMEM((16, 48, 128), f32),
             pltpu.VMEM((256, 128), f32),
             pltpu.VMEM((9, 24, 128), f32),

time: 59.6 us -> 59.5 us (level)
  waiting for transfers between devices: 12.7 us -> 11.4 us
  starting transfers between devices: 27.4 us -> 28.5 us
  other arithmetic: 0.91 us -> 0 us
  local copies, waits for them, and re-layouts: 1.54 us -> 2.44 us
    all_to_all x1, starting transfers between devices: 11.5 us -> 17.4 us  [per_device(): coarse = lax.all_to_all(coarse, 'gx', 0, 0)]
    ppermute x3, starting transfers between devices: 4.02 us -> 0.71 us  [swap(): return (lax.ppermute(first, axis, both(pairs)), second)]
    ppermute x3, waiting for transfers between devices: 3.36 us -> 1.16 us  [swap(): return (lax.ppermute(first, axis, both(pairs)), second)]
    ppermute x3, waiting for transfers between devices: 0.95 us -> 1.9 us  [swap(): second = lax.ppermute(second, axis, both(others))]
    select_n x1 -> x0, other arithmetic: 0.91 us -> none  [per_device(): jnp.where(even_x, low, high)]
    ppermute x3, starting transfers between devices: 7.11 us -> 6.2 us  [swap(): second = lax.ppermute(second, axis, both(others))]
    unnamed x14 -> x16, local copies, waits for them, and re-layouts: 0.82 us -> 1.72 us
    pallas_call x7 -> x8, Pallas kernels: 15.9 us -> 16 us  [vmem_call(): pl.pallas_call(body, out_shape=out_shape, in_specs=[spec(pltpu.VMEM)] * l...]
where the time goes in v12:
time: 59.5 us; the launch traced here: 59.1 us
  starting transfers between devices  28.5 us (48%)
  Pallas kernels  16 us (27%)
  waiting for transfers between devices  11.4 us (19%)
  local copies, waits for them, and re-layouts  2.44 us (4%)
  matrix products  0.62 us (1%)
    all_to_all x1, starting transfers between devices, per_device(): coarse = lax.all_to_all(coarse, 'gx', 0, 0)  17.4 us
    pallas_call x8, Pallas kernels, vmem_call(): pl.pallas_call(body, out_shape=out_shape, in_specs=[spec(pltpu.VMEM)] * l...  16 us
    all_to_all x1, waiting for transfers between devices, per_device(): coarse = lax.all_to_all(coarse, 'gx', 0, 0)  6.91 us
    ppermute x3, starting transfers between devices, swap(): second = lax.ppermute(second, axis, both(others))  6.2 us
    all_to_all x1, starting transfers between devices, per_device(): parts = lax.all_to_all(parts, 'gy', 0, 0)  4.25 us
    ppermute x3, waiting for transfers between devices, swap(): second = lax.ppermute(second, axis, both(others))  1.9 us
    unnamed x16, local copies, waits for them, and re-layouts  1.72 us
    all_to_all x1, waiting for transfers between devices, per_device(): parts = lax.all_to_all(parts, 'gy', 0, 0)  1.44 us
  transfers between devices with their start and end apart: 8, of which 6 were waited for; matrix products, arithmetic and copies ran while one was open for 2% of the time, Pallas kernels for 16%

profile of v12, /device:TPU:2, one launch (start us, length us, event | category | flops | bytes accessed | tf_op | source)
XLA Modules:
  0.0 59.1 jit_solution(11316077574501991214)
XLA Ops:
  0.0 0.9 %copy-done = bf16[20,20,128]{2,1,0:T(8,128)(2,1)S(1)} copy-done((bf16[20,20,128]{2,1,0:T(8,128)(2,1)S(1)}, bf16[20,20,128]{2,1,0:T(8,128)(2,1)}, u32[]{:S(2)}) %copy-start) | copy-done | bytes 102424
  1.0 0.7 %collective-permute-start.1 = (bf16[200,128]{1,0:T(8,128)(2,1)S(1)}, bf16[200,128]{1,0:T(8,128)(2,1)S(1)}, u32[]{:S(2)}, u32[]{:S(2)}) collective-permute-start(bf16[200,128]{1,0:T(8,128)(2,1)S(1)} %get-tuple-element.28), channel_id=1, source_target_pairs={{8,16},{24,32},{40,48},{56,64},{72,80},{88,96},{104,112},{120,128}... | collective-permute-start | bytes 153608 | tf_op jit(solution)/shard_map/ppermute | solution.py:481
  1.8 0.5 collective-permute-done.near_ref.near_x_ref
  2.4 4.9 %collective-permute-start.2 = (bf16[400,128]{1,0:T(8,128)(2,1)S(1)}, bf16[400,128]{1,0:T(8,128)(2,1)S(1)}, u32[]{:S(2)}, u32[]{:S(2)}) collective-permute-start(bf16[400,128]{1,0:T(8,128)(2,1)S(1)} %get-tuple-element.31), channel_id=1, source_target_pairs={{1,2},{3,4},{5,6},{2,1},{4,3},{6,5},{9,10},{11,12},{13,14},{10,9},... | collective-permute-start | bytes 307208 | tf_op jit(solution)/shard_map/ppermute | solution.py:481
  7.3 0.3 collective-permute-start.3
  7.5 0.5 copy.8
  8.0 0.3 reshape.4
  8.2 0.4 copy-done.6
  8.7 0.3 fusion.1.far_ref
  9.0 0.4 copy-done.7
  9.4 0.3 fusion.v_ref.near_ref
  9.7 1.9 %collective-permute-done.2.next_y_ref = bf16[400,128]{1,0:T(8,128)(2,1)S(1)} collective-permute-done((bf16[400,128]{1,0:T(8,128)(2,1)S(1)}, bf16[400,128]{1,0:T(8,128)(2,1)S(1)}, u32[]{:S(2)}, u32[]{:S(2)}) %collective-permute-start.2) | collective-permute-done | bytes 102432 | tf_op jit(solution)/shard_map/ppermute | solution.py:481
  11.6 0.4 collective-permute-done.3.near_y_ref
  12.0 1.4 %restrict.1 = (bf16[40,40,128]{2,1,0:T(8,128)(2,1)S(1)}, bf16[5,9,128]{2,1,0:T(8,128)(2,1)S(1)}, bf16[5,9,128]{2,1,0:T(8,128)(2,1)S(1)}, bf16[5,16,128]{2,1,0:T(8,128)(2,1)S(1)}, f32[32,8,128]{2,1,0:T(8,128)}) custom-call(bf16[20,20,128]{2,1,0:T(8,128)(2,1)S(1)} %copy-done.1, bf16[200,128]{1,0:T(8,128)(2,1)S(1)} %collective-permute-done.near_ref.near_x_ref, ...), custom_call_target="tpu_custom_call" | custom-call | bytes 65536 | tf_op jit(solution)/shard_map/restrict/pallas_call | solution.py:106
  13.4 17.4 %all-to-all-start = ((f32[32,8,128]{2,1,0:T(8,128)}), f32[32,8,128]{2,1,0:T(8,128)S(1)}, u32[]{:S(2)}, u32[]{:S(2)}) async-start(f32[32,8,128]{2,1,0:T(8,128)} %get-tuple-element.36), calls=%async_computation | async-start | bytes 262144 | tf_op jit(solution)/shard_map/all_to_all | solution.py:538
  30.8 0.4 collective-permute-start.4
  31.2 0.7 %collective-permute-start.5 = (bf16[5,9,128]{2,1,0:T(8,128)(2,1)S(1)}, bf16[5,9,128]{2,1,0:T(8,128)(2,1)S(1)}, u32[]{:S(2)}, u32[]{:S(2)}) collective-permute-start(bf16[5,9,128]{2,1,0:T(8,128)(2,1)S(1)} %get-tuple-element.43), channel_id=1, source_target_pairs={{8,16},{24,32},{40,48},{56,64},{72,80},{88,96},{104,112},{120,128}... | collective-permute-start | bytes 34568 | tf_op jit(solution)/shard_map/ppermute | solution.py:481
  32.1 2.6 %fine_sum.2.refs_0_ = f32[240,256]{1,0:T(8,128)S(1)} custom-call(bf16[40,40,128]{2,1,0:T(8,128)(2,1)S(1)} %get-tuple-element.37.d_in_ref, f32[882,128]{1,0:T(8,128)S(1)} %fusion.v_ref.near_ref), custom_call_target="tpu_custom_call" | custom-call | flops 2076180480 | bytes 65536 | tf_op jit(solution)/shard_map/fine_sum/pallas_call | solution.py:106
  34.7 6.9 %all-to-all-done.recv_ref = f32[32,8,128]{2,1,0:T(8,128)S(1)} async-done(((f32[32,8,128]{2,1,0:T(8,128)}), f32[32,8,128]{2,1,0:T(8,128)S(1)}, u32[]{:S(2)}, u32[]{:S(2)}) %all-to-all-start) | async-done | bytes 131104 | tf_op jit(solution)/shard_map/all_to_all | solution.py:538
  41.6 1.2 %spread.1 = bf16[8,208,128]{2,1,0:T(8,128)(2,1)} custom-call(f32[32,8,128]{2,1,0:T(8,128)S(1)} %all-to-all-done.recv_ref, f32[2,328,128]{2,1,0:T(8,128)S(1)} %copy-done.3, bf16[5,16,128]{2,1,0:T(8,128)(2,1)S(1)} %get-tuple-element.42.own_ref, bf16[5,9,128]{2,1,0:T(8,128)(2,1)S(1)} %collective-permute-done.5.next_ref, ...), custom_call_target="tpu_custom_call" | custom-call | bytes 65536 | tf_op jit(solution)/shard_map/spread/pallas_call | solution.py:106
  42.8 4.2 %all-to-all-start.1 = ((bf16[8,208,128]{2,1,0:T(8,128)(2,1)}), bf16[8,208,128]{2,1,0:T(8,128)(2,1)S(1)}, u32[]{:S(2)}, u32[]{:S(2)}) async-start(bf16[8,208,128]{2,1,0:T(8,128)(2,1)} %spread.1), calls=%async_computation.1 | async-start | bytes 851968 | tf_op jit(solution)/shard_map/all_to_all | solution.py:550
  47.0 6.6 %fine_sum.3.fine_ref = f32[240,256]{1,0:T(8,128)S(1)} custom-call(bf16[40,40,128]{2,1,0:T(8,128)(2,1)S(1)} %get-tuple-element.37.d_in_ref, f32[882,128]{1,0:T(8,128)S(1)} %fusion.v_ref.near_ref, f32[240,256]{1,0:T(8,128)S(1)} %fine_sum.2.refs_0_), custom_call_target="tpu_custom_call" | custom-call | flops 5190451200 | bytes 65536 | tf_op jit(solution)/shard_map/fine_sum/pallas_call | solution.py:106
  53.6 1.4 %all-to-all-done.1.recv_ref = bf16[8,208,128]{2,1,0:T(8,128)(2,1)S(1)} async-done(((bf16[8,208,128]{2,1,0:T(8,128)(2,1)}), bf16[8,208,128]{2,1,0:T(8,128)(2,1)S(1)}, u32[]{:S(2)}, u32[]{:S(2)}) %all-to-all-start.1) | async-done | bytes 426016 | tf_op jit(solution)/shard_map/all_to_all | solution.py:550
  55.0 4.1 %final.1 = f32[20,20,128]{2,1,0:T(8,128)} custom-call(bf16[8,208,128]{2,1,0:T(8,128)(2,1)S(1)} %all-to-all-done.1.recv_ref, f32[16,88,128]{2,1,0:T(8,128)S(1)} %copy-done.2, f32[512,128]{1,0:T(8,128)S(1)} %copy-done.4, f32[882,128]{1,0:T(8,128)S(1)} %fusion.v_ref.near_ref, f32[882,128]{1,0:T(8,128)S(1)} %fusion.1.far_ref, f32[240,256]{1,0:T(8,128)S(1)} %fine_sum.3.fine_ref), custom_call_target="tpu_custom_call" | custom-call | bytes 65536 | tf_op jit(solution)/shard_map/final/pallas_call | solution.py:106
  (20 shorter events, 0.6 us)
Async XLA Ops:
  0.0 0.9 %copy-start = (bf16[20,20,128]{2,1,0:T(8,128)(2,1)S(1)}, bf16[20,20,128]{2,1,0:T(8,128)(2,1)}, u32[]{:S(2)}) copy-start(bf16[20,20,128]{2,1,0:T(8,128)(2,1)} %blk_ref.5) | copy-start | bytes 307204
  0.9 1.3 %collective-permute-start = (bf16[200,128]{1,0:T(8,128)(2,1)S(1)}, bf16[200,128]{1,0:T(8,128)(2,1)S(1)}, u32[]{:S(2)}, u32[]{:S(2)}) collective-permute-start(bf16[200,128]{1,0:T(8,128)(2,1)S(1)} %get-tuple-element.27), channel_id=1, source_target_pairs={{0,8},{16,24},{32,40},{48,56},{64,72},{80,88},{96,104},{112,120},{... | collective-permute-start | bytes 153608 | tf_op jit(solution)/shard_map/ppermute | solution.py:482
  1.0 1.2 %collective-permute-start.1 = (bf16[200,128]{1,0:T(8,128)(2,1)S(1)}, bf16[200,128]{1,0:T(8,128)(2,1)S(1)}, u32[]{:S(2)}, u32[]{:S(2)}) collective-permute-start(bf16[200,128]{1,0:T(8,128)(2,1)S(1)} %get-tuple-element.28), channel_id=1, source_target_pairs={{8,16},{24,32},{40,48},{56,64},{72,80},{88,96},{104,112},{120,128}... | collective-permute-start | bytes 153608 | tf_op jit(solution)/shard_map/ppermute | solution.py:481
  1.8 5.7 %copy-start.5 = (bf16[2,21,21,21]{3,0,2,1:T(2,128)(2,1)S(1)}, bf16[2,21,21,21]{3,0,2,1:T(2,128)(2,1)}, u32[]{:S(2)}) copy-start(bf16[2,21,21,21]{3,0,2,1:T(2,128)(2,1)} %param.8) | copy-start | bytes 111136
  2.4 9.2 %collective-permute-start.2 = (bf16[400,128]{1,0:T(8,128)(2,1)S(1)}, bf16[400,128]{1,0:T(8,128)(2,1)S(1)}, u32[]{:S(2)}, u32[]{:S(2)}) collective-permute-start(bf16[400,128]{1,0:T(8,128)(2,1)S(1)} %get-tuple-element.31), channel_id=1, source_target_pairs={{1,2},{3,4},{5,6},{2,1},{4,3},{6,5},{9,10},{11,12},{13,14},{10,9},... | collective-permute-start | bytes 307208 | tf_op jit(solution)/shard_map/ppermute | solution.py:481
  7.3 4.7 %collective-permute-start.3 = (bf16[400,128]{1,0:T(8,128)(2,1)S(1)}, bf16[400,128]{1,0:T(8,128)(2,1)S(1)}, u32[]{:S(2)}, u32[]{:S(2)}) collective-permute-start(bf16[400,128]{1,0:T(8,128)(2,1)S(1)} %get-tuple-element.32), channel_id=1, source_target_pairs={{0,1},{2,3},{4,5},{6,7},{1,0},{3,2},{5,4},{7,6},{8,9},{10,11},{12,... | collective-permute-start | bytes 307208 | tf_op jit(solution)/shard_map/ppermute | solution.py:482
  8.0 0.7 %copy-start.6 = (bf16[21,128]{1,0:T(8,128)(2,1)S(1)}, bf16[21,128]{1,0:T(8,128)(2,1)}, u32[]{:S(2)}) copy-start(bf16[21,128]{1,0:T(8,128)(2,1)} %constant.11.clone) | copy-start | bytes 16132
  8.7 0.7 %copy-start.7 = (bf16[21,128]{1,0:T(8,128)(2,1)S(1)}, bf16[21,128]{1,0:T(8,128)(2,1)}, u32[]{:S(2)}) copy-start(bf16[21,128]{1,0:T(8,128)(2,1)} %constant.10.clone) | copy-start | bytes 16132
  9.4 2.6 %copy-start.1 = (bf16[20,20,128]{2,1,0:T(8,128)(2,1)S(1)}, bf16[20,20,128]{2,1,0:T(8,128)(2,1)}, u32[]{:S(2)}) copy-start(bf16[20,20,128]{2,1,0:T(8,128)(2,1)} %blk_ref.5) | copy-start | bytes 307204
  13.4 28.1 %all-to-all-start = ((f32[32,8,128]{2,1,0:T(8,128)}), f32[32,8,128]{2,1,0:T(8,128)S(1)}, u32[]{:S(2)}, u32[]{:S(2)}) async-start(f32[32,8,128]{2,1,0:T(8,128)} %get-tuple-element.36), calls=%async_computation | async-start | bytes 262144 | tf_op jit(solution)/shard_map/all_to_all | solution.py:538
  30.8 1.3 %collective-permute-start.4 = (bf16[5,9,128]{2,1,0:T(8,128)(2,1)S(1)}, bf16[5,9,128]{2,1,0:T(8,128)(2,1)S(1)}, u32[]{:S(2)}, u32[]{:S(2)}) collective-permute-start(bf16[5,9,128]{2,1,0:T(8,128)(2,1)S(1)} %get-tuple-element.39), channel_id=1, source_target_pairs={{0,8},{16,24},{32,40},{48,56},{64,72},{80,88},{96,104},{112,120},{... | collective-permute-start | bytes 34568 | tf_op jit(solution)/shard_map/ppermute | solution.py:482
  31.2 10.4 %collective-permute-start.5 = (bf16[5,9,128]{2,1,0:T(8,128)(2,1)S(1)}, bf16[5,9,128]{2,1,0:T(8,128)(2,1)S(1)}, u32[]{:S(2)}, u32[]{:S(2)}) collective-permute-start(bf16[5,9,128]{2,1,0:T(8,128)(2,1)S(1)} %get-tuple-element.43), channel_id=1, source_target_pairs={{8,16},{24,32},{40,48},{56,64},{72,80},{88,96},{104,112},{120,128}... | collective-permute-start | bytes 34568 | tf_op jit(solution)/shard_map/ppermute | solution.py:481
  32.1 9.5 %copy-start.3 = (f32[2,328,128]{2,1,0:T(8,128)S(1)}, f32[2,328,128]{2,1,0:T(8,128)}, u32[]{:S(2)}) copy-start(f32[2,328,128]{2,1,0:T(8,128)} %constant.12.clone.mx_ref) | copy-start | bytes 1007620
  42.8 12.3 %all-to-all-start.1 = ((bf16[8,208,128]{2,1,0:T(8,128)(2,1)}), bf16[8,208,128]{2,1,0:T(8,128)(2,1)S(1)}, u32[]{:S(2)}, u32[]{:S(2)}) async-start(bf16[8,208,128]{2,1,0:T(8,128)(2,1)} %spread.1), calls=%async_computation.1 | async-start | bytes 851968 | tf_op jit(solution)/shard_map/all_to_all | solution.py:550
  47.0 8.0 %copy-start.2 = (f32[16,88,128]{2,1,0:T(8,128)S(1)}, f32[16,88,128]{2,1,0:T(8,128)}, u32[]{:S(2)}) copy-start(f32[16,88,128]{2,1,0:T(8,128)} %constant.13.clone.my_ref) | copy-start | bytes 2162692
  47.0 8.0 %copy-start.4 = (f32[512,128]{1,0:T(8,128)S(1)}, f32[512,128]{1,0:T(8,128)}, u32[]{:S(2)}) copy-start(f32[512,128]{1,0:T(8,128)} %constant.14.clone.mz_ref) | copy-start | bytes 786436

commit v13 on v12

--- a/solution.py
+++ b/solution.py
@@ -156,7 +156,7 @@
 
 
 def restrict_kernel(
-    blk_ref, near_x_ref, next_x_ref, next_y_ref, near_y_ref,
+    blk_ref, next_x_ref, near_x_ref, next_y_ref, near_y_ref,
     d_out_ref, second_ref, first_ref, own_ref, out_ref,
     d_ref, dense, sides, planes, cells, mid,
 ):
@@ -532,11 +532,10 @@
             pltpu.VMEM((9, 24, 128), f32),
         ],
         "restrict",
-        (charges, near_x, next_x, next_y, near_y),
+        (charges, next_x, near_x, next_y, near_y),
     )
     near_m, next_m = swap(first, second, "gx")
     coarse = lax.all_to_all(coarse, "gx", 0, 0)
-    near, near_m = lax.optimization_barrier((near, near_m))
     fine = fine_sum(0, SPLIT, d, near)
     coarse, fine = lax.optimization_barrier((coarse, fine))
     parts = vmem_call(

time: 59.5 us -> 59.5 us (level)
  starting transfers between devices: 28.5 us -> 31.8 us
  waiting for transfers between devices: 11.4 us -> 8.16 us
    ppermute x3, starting transfers between devices: 0.71 us -> 8.41 us  [swap(): return (lax.ppermute(first, axis, both(pairs)), second)]
    all_to_all x1, starting transfers between devices: 17.4 us -> 11.5 us  [per_device(): coarse = lax.all_to_all(coarse, 'gx', 0, 0)]
    all_to_all x1, waiting for transfers between devices: 6.91 us -> 2.77 us  [per_device(): coarse = lax.all_to_all(coarse, 'gx', 0, 0)]
    ppermute x3, waiting for transfers between devices: 1.16 us -> 2.88 us  [swap(): return (lax.ppermute(first, axis, both(pairs)), second)]
    ppermute x3, starting transfers between devices: 6.2 us -> 7.12 us  [swap(): second = lax.ppermute(second, axis, both(others))]
    ppermute x3, waiting for transfers between devices: 1.9 us -> 1.06 us  [swap(): second = lax.ppermute(second, axis, both(others))]
  transfers between devices with their start and end apart: 8 -> 8, of which waited for: 6 -> 5; matrix products, arithmetic and copies ran while one was open for 2% -> 2% of each run, Pallas kernels for 16% -> 16%
where the time goes in v13:
time: 59.5 us; the launch traced here: 59.1 us
  starting transfers between devices  31.8 us (53%)
  Pallas kernels  16 us (27%)
  waiting for transfers between devices  8.16 us (14%)
  local copies, waits for them, and re-layouts  2.44 us (4%)
  matrix products  0.62 us (1%)
    pallas_call x8, Pallas kernels, vmem_call(): pl.pallas_call(body, out_shape=out_shape, in_specs=[spec(pltpu.VMEM)] * l...  16 us
    all_to_all x1, starting transfers between devices, per_device(): coarse = lax.all_to_all(coarse, 'gx', 0, 0)  11.5 us
    ppermute x3, starting transfers between devices, swap(): return (lax.ppermute(first, axis, both(pairs)), second)  8.41 us
    ppermute x3, starting transfers between devices, swap(): second = lax.ppermute(second, axis, both(others))  7.12 us
    all_to_all x1, starting transfers between devices, per_device(): parts = lax.all_to_all(parts, 'gy', 0, 0)  4.73 us
    ppermute x3, waiting for transfers between devices, swap(): return (lax.ppermute(first, axis, both(pairs)), second)  2.88 us
    all_to_all x1, waiting for transfers between devices, per_device(): coarse = lax.all_to_all(coarse, 'gx', 0, 0)  2.77 us
    unnamed x16, local copies, waits for them, and re-layouts  1.72 us
  transfers between devices with their start and end apart: 8, of which 5 were waited for; matrix products, arithmetic and copies ran while one was open for 2% of the time, Pallas kernels for 16%

profile of v13, /device:TPU:2, one launch (start us, length us, event | category | flops | bytes accessed | tf_op | source)
XLA Modules:
  0.0 59.1 jit_solution(12992006325683274089)
XLA Ops:
  0.0 0.9 %copy-done = bf16[20,20,128]{2,1,0:T(8,128)(2,1)S(1)} copy-done((bf16[20,20,128]{2,1,0:T(8,128)(2,1)S(1)}, bf16[20,20,128]{2,1,0:T(8,128)(2,1)}, u32[]{:S(2)}) %copy-start) | copy-done | bytes 102424
  0.9 0.7 %collective-permute-start = (bf16[200,128]{1,0:T(8,128)(2,1)S(1)}, bf16[200,128]{1,0:T(8,128)(2,1)S(1)}, u32[]{:S(2)}, u32[]{:S(2)}) collective-permute-start(bf16[200,128]{1,0:T(8,128)(2,1)S(1)} %get-tuple-element.25), channel_id=1, source_target_pairs={{8,16},{24,32},{40,48},{56,64},{72,80},{88,96},{104,112},{120,128}... | collective-permute-start | bytes 153608 | tf_op jit(solution)/shard_map/ppermute | solution.py:481
  1.6 3.6 %collective-permute-start.1 = (bf16[200,128]{1,0:T(8,128)(2,1)S(1)}, bf16[200,128]{1,0:T(8,128)(2,1)S(1)}, u32[]{:S(2)}, u32[]{:S(2)}) collective-permute-start(bf16[200,128]{1,0:T(8,128)(2,1)S(1)} %get-tuple-element.26), channel_id=1, source_target_pairs={{0,8},{16,24},{32,40},{48,56},{64,72},{80,88},{96,104},{112,120},{... | collective-permute-start | bytes 153608 | tf_op jit(solution)/shard_map/ppermute | solution.py:482
  5.3 0.8 %collective-permute-done.1.near_ref.near_x_ref = bf16[200,128]{1,0:T(8,128)(2,1)S(1)} collective-permute-done((bf16[200,128]{1,0:T(8,128)(2,1)S(1)}, bf16[200,128]{1,0:T(8,128)(2,1)S(1)}, u32[]{:S(2)}, u32[]{:S(2)}) %collective-permute-start.1) | collective-permute-done | bytes 51232 | tf_op jit(solution)/shard_map/ppermute | solution.py:482
  6.2 5.8 %collective-permute-start.2 = (bf16[400,128]{1,0:T(8,128)(2,1)S(1)}, bf16[400,128]{1,0:T(8,128)(2,1)S(1)}, u32[]{:S(2)}, u32[]{:S(2)}) collective-permute-start(bf16[400,128]{1,0:T(8,128)(2,1)S(1)} %get-tuple-element.29), channel_id=1, source_target_pairs={{1,2},{3,4},{5,6},{2,1},{4,3},{6,5},{9,10},{11,12},{13,14},{10,9},... | collective-permute-start | bytes 307208 | tf_op jit(solution)/shard_map/ppermute | solution.py:481
  12.1 0.5 copy.8
  12.5 0.3 reshape.4
  12.8 0.4 copy-done.6
  13.2 0.3 fusion.1.far_ref
  13.5 0.4 copy-done.7
  13.9 0.3 fusion.v_ref.near_ref
  14.2 1.1 %collective-permute-done.2.next_y_ref = bf16[400,128]{1,0:T(8,128)(2,1)S(1)} collective-permute-done((bf16[400,128]{1,0:T(8,128)(2,1)S(1)}, bf16[400,128]{1,0:T(8,128)(2,1)S(1)}, u32[]{:S(2)}, u32[]{:S(2)}) %collective-permute-start.2) | collective-permute-done | bytes 102432 | tf_op jit(solution)/shard_map/ppermute | solution.py:481
  15.3 2.1 %collective-permute-done.3.near_y_ref = bf16[400,128]{1,0:T(8,128)(2,1)S(1)} collective-permute-done((bf16[400,128]{1,0:T(8,128)(2,1)S(1)}, bf16[400,128]{1,0:T(8,128)(2,1)S(1)}, u32[]{:S(2)}, u32[]{:S(2)}) %collective-permute-start.3) | collective-permute-done | bytes 102432 | tf_op jit(solution)/shard_map/ppermute | solution.py:482
  17.4 1.4 %restrict.1 = (bf16[40,40,128]{2,1,0:T(8,128)(2,1)S(1)}, bf16[5,9,128]{2,1,0:T(8,128)(2,1)S(1)}, bf16[5,9,128]{2,1,0:T(8,128)(2,1)S(1)}, bf16[5,16,128]{2,1,0:T(8,128)(2,1)S(1)}, f32[32,8,128]{2,1,0:T(8,128)}) custom-call(bf16[20,20,128]{2,1,0:T(8,128)(2,1)S(1)} %copy-done.1, bf16[200,128]{1,0:T(8,128)(2,1)S(1)} %collective-permute-done.next_ref.next_x_ref, ...), custom_call_target="tpu_custom_call" | custom-call | bytes 65536 | tf_op jit(solution)/shard_map/restrict/pallas_call | solution.py:106
  18.8 11.5 %all-to-all-start = ((f32[32,8,128]{2,1,0:T(8,128)}), f32[32,8,128]{2,1,0:T(8,128)S(1)}, u32[]{:S(2)}, u32[]{:S(2)}) async-start(f32[32,8,128]{2,1,0:T(8,128)} %get-tuple-element.34), calls=%async_computation | async-start | bytes 262144 | tf_op jit(solution)/shard_map/all_to_all | solution.py:538
  30.4 0.7 %collective-permute-start.4 = (bf16[5,9,128]{2,1,0:T(8,128)(2,1)S(1)}, bf16[5,9,128]{2,1,0:T(8,128)(2,1)S(1)}, u32[]{:S(2)}, u32[]{:S(2)}) collective-permute-start(bf16[5,9,128]{2,1,0:T(8,128)(2,1)S(1)} %get-tuple-element.39), channel_id=1, source_target_pairs={{8,16},{24,32},{40,48},{56,64},{72,80},{88,96},{104,112},{120,128}... | collective-permute-start | bytes 34568 | tf_op jit(solution)/shard_map/ppermute | solution.py:481
  31.0 4.7 %collective-permute-start.5 = (bf16[5,9,128]{2,1,0:T(8,128)(2,1)S(1)}, bf16[5,9,128]{2,1,0:T(8,128)(2,1)S(1)}, u32[]{:S(2)}, u32[]{:S(2)}) collective-permute-start(bf16[5,9,128]{2,1,0:T(8,128)(2,1)S(1)} %get-tuple-element.40), channel_id=1, source_target_pairs={{0,8},{16,24},{32,40},{48,56},{64,72},{80,88},{96,104},{112,120},{... | collective-permute-start | bytes 34568 | tf_op jit(solution)/shard_map/ppermute | solution.py:482
  35.8 2.6 %fine_sum.2.refs_0_ = f32[240,256]{1,0:T(8,128)S(1)} custom-call(bf16[40,40,128]{2,1,0:T(8,128)(2,1)S(1)} %get-tuple-element.35.d_in_ref, f32[882,128]{1,0:T(8,128)S(1)} %fusion.v_ref.near_ref), custom_call_target="tpu_custom_call" | custom-call | flops 2076180480 | bytes 65536 | tf_op jit(solution)/shard_map/fine_sum/pallas_call | solution.py:106
  38.3 2.8 %all-to-all-done.recv_ref = f32[32,8,128]{2,1,0:T(8,128)S(1)} async-done(((f32[32,8,128]{2,1,0:T(8,128)}), f32[32,8,128]{2,1,0:T(8,128)S(1)}, u32[]{:S(2)}, u32[]{:S(2)}) %all-to-all-start) | async-done | bytes 131104 | tf_op jit(solution)/shard_map/all_to_all | solution.py:538
  41.1 1.2 %spread.1 = bf16[8,208,128]{2,1,0:T(8,128)(2,1)} custom-call(f32[32,8,128]{2,1,0:T(8,128)S(1)} %all-to-all-done.recv_ref, f32[2,328,128]{2,1,0:T(8,128)S(1)} %copy-done.3, bf16[5,16,128]{2,1,0:T(8,128)(2,1)S(1)} %get-tuple-element.38.own_ref, bf16[5,9,128]{2,1,0:T(8,128)(2,1)S(1)} %collective-permute-done.4.next_ref, ...), custom_call_target="tpu_custom_call" | custom-call | bytes 65536 | tf_op jit(solution)/shard_map/spread/pallas_call | solution.py:106
  42.3 4.7 %all-to-all-start.1 = ((bf16[8,208,128]{2,1,0:T(8,128)(2,1)}), bf16[8,208,128]{2,1,0:T(8,128)(2,1)S(1)}, u32[]{:S(2)}, u32[]{:S(2)}) async-start(bf16[8,208,128]{2,1,0:T(8,128)(2,1)} %spread.1), calls=%async_computation.1 | async-start | bytes 851968 | tf_op jit(solution)/shard_map/all_to_all | solution.py:549
  47.0 6.6 %fine_sum.3.fine_ref = f32[240,256]{1,0:T(8,128)S(1)} custom-call(bf16[40,40,128]{2,1,0:T(8,128)(2,1)S(1)} %get-tuple-element.35.d_in_ref, f32[882,128]{1,0:T(8,128)S(1)} %fusion.v_ref.near_ref, f32[240,256]{1,0:T(8,128)S(1)} %fine_sum.2.refs_0_), custom_call_target="tpu_custom_call" | custom-call | flops 5190451200 | bytes 65536 | tf_op jit(solution)/shard_map/fine_sum/pallas_call | solution.py:106
  53.6 1.4 %all-to-all-done.1.recv_ref = bf16[8,208,128]{2,1,0:T(8,128)(2,1)S(1)} async-done(((bf16[8,208,128]{2,1,0:T(8,128)(2,1)}), bf16[8,208,128]{2,1,0:T(8,128)(2,1)S(1)}, u32[]{:S(2)}, u32[]{:S(2)}) %all-to-all-start.1) | async-done | bytes 426016 | tf_op jit(solution)/shard_map/all_to_all | solution.py:549
  55.0 4.1 %final.1 = f32[20,20,128]{2,1,0:T(8,128)} custom-call(bf16[8,208,128]{2,1,0:T(8,128)(2,1)S(1)} %all-to-all-done.1.recv_ref, f32[16,88,128]{2,1,0:T(8,128)S(1)} %copy-done.2, f32[512,128]{1,0:T(8,128)S(1)} %copy-done.4, f32[882,128]{1,0:T(8,128)S(1)} %fusion.v_ref.near_ref, f32[882,128]{1,0:T(8,128)S(1)} %fusion.1.far_ref, f32[240,256]{1,0:T(8,128)S(1)} %fine_sum.3.fine_ref), custom_call_target="tpu_custom_call" | custom-call | bytes 65536 | tf_op jit(solution)/shard_map/final/pallas_call | solution.py:106
  (20 shorter events, 0.3 us)
Async XLA Ops:
  0.0 0.9 %copy-start = (bf16[20,20,128]{2,1,0:T(8,128)(2,1)S(1)}, bf16[20,20,128]{2,1,0:T(8,128)(2,1)}, u32[]{:S(2)}) copy-start(bf16[20,20,128]{2,1,0:T(8,128)(2,1)} %blk_ref.5) | copy-start | bytes 307204
  0.9 4.3 %collective-permute-start = (bf16[200,128]{1,0:T(8,128)(2,1)S(1)}, bf16[200,128]{1,0:T(8,128)(2,1)S(1)}, u32[]{:S(2)}, u32[]{:S(2)}) collective-permute-start(bf16[200,128]{1,0:T(8,128)(2,1)S(1)} %get-tuple-element.25), channel_id=1, source_target_pairs={{8,16},{24,32},{40,48},{56,64},{72,80},{88,96},{104,112},{120,128}... | collective-permute-start | bytes 153608 | tf_op jit(solution)/shard_map/ppermute | solution.py:481
  1.6 4.5 %collective-permute-start.1 = (bf16[200,128]{1,0:T(8,128)(2,1)S(1)}, bf16[200,128]{1,0:T(8,128)(2,1)S(1)}, u32[]{:S(2)}, u32[]{:S(2)}) collective-permute-start(bf16[200,128]{1,0:T(8,128)(2,1)S(1)} %get-tuple-element.26), channel_id=1, source_target_pairs={{0,8},{16,24},{32,40},{48,56},{64,72},{80,88},{96,104},{112,120},{... | collective-permute-start | bytes 153608 | tf_op jit(solution)/shard_map/ppermute | solution.py:482
  5.3 6.8 %copy-start.5 = (bf16[2,21,21,21]{3,0,2,1:T(2,128)(2,1)S(1)}, bf16[2,21,21,21]{3,0,2,1:T(2,128)(2,1)}, u32[]{:S(2)}) copy-start(bf16[2,21,21,21]{3,0,2,1:T(2,128)(2,1)} %param.8) | copy-start | bytes 111136
  6.2 9.1 %collective-permute-start.2 = (bf16[400,128]{1,0:T(8,128)(2,1)S(1)}, bf16[400,128]{1,0:T(8,128)(2,1)S(1)}, u32[]{:S(2)}, u32[]{:S(2)}) collective-permute-start(bf16[400,128]{1,0:T(8,128)(2,1)S(1)} %get-tuple-element.29), channel_id=1, source_target_pairs={{1,2},{3,4},{5,6},{2,1},{4,3},{6,5},{9,10},{11,12},{13,14},{10,9},... | collective-permute-start | bytes 307208 | tf_op jit(solution)/shard_map/ppermute | solution.py:481
  12.0 5.4 %collective-permute-start.3 = (bf16[400,128]{1,0:T(8,128)(2,1)S(1)}, bf16[400,128]{1,0:T(8,128)(2,1)S(1)}, u32[]{:S(2)}, u32[]{:S(2)}) collective-permute-start(bf16[400,128]{1,0:T(8,128)(2,1)S(1)} %get-tuple-element.30), channel_id=1, source_target_pairs={{0,1},{2,3},{4,5},{6,7},{1,0},{3,2},{5,4},{7,6},{8,9},{10,11},{12,... | collective-permute-start | bytes 307208 | tf_op jit(solution)/shard_map/ppermute | solution.py:482
  12.5 0.7 %copy-start.6 = (bf16[21,128]{1,0:T(8,128)(2,1)S(1)}, bf16[21,128]{1,0:T(8,128)(2,1)}, u32[]{:S(2)}) copy-start(bf16[21,128]{1,0:T(8,128)(2,1)} %constant.11.clone) | copy-start | bytes 16132
  13.2 0.7 %copy-start.7 = (bf16[21,128]{1,0:T(8,128)(2,1)S(1)}, bf16[21,128]{1,0:T(8,128)(2,1)}, u32[]{:S(2)}) copy-start(bf16[21,128]{1,0:T(8,128)(2,1)} %constant.10.clone) | copy-start | bytes 16132
  13.9 3.5 %copy-start.1 = (bf16[20,20,128]{2,1,0:T(8,128)(2,1)S(1)}, bf16[20,20,128]{2,1,0:T(8,128)(2,1)}, u32[]{:S(2)}) copy-start(bf16[20,20,128]{2,1,0:T(8,128)(2,1)} %blk_ref.5) | copy-start | bytes 307204
  18.8 22.3 %all-to-all-start = ((f32[32,8,128]{2,1,0:T(8,128)}), f32[32,8,128]{2,1,0:T(8,128)S(1)}, u32[]{:S(2)}, u32[]{:S(2)}) async-start(f32[32,8,128]{2,1,0:T(8,128)} %get-tuple-element.34), calls=%async_computation | async-start | bytes 262144 | tf_op jit(solution)/shard_map/all_to_all | solution.py:538
  30.4 10.8 %collective-permute-start.4 = (bf16[5,9,128]{2,1,0:T(8,128)(2,1)S(1)}, bf16[5,9,128]{2,1,0:T(8,128)(2,1)S(1)}, u32[]{:S(2)}, u32[]{:S(2)}) collective-permute-start(bf16[5,9,128]{2,1,0:T(8,128)(2,1)S(1)} %get-tuple-element.39), channel_id=1, source_target_pairs={{8,16},{24,32},{40,48},{56,64},{72,80},{88,96},{104,112},{120,128}... | collective-permute-start | bytes 34568 | tf_op jit(solution)/shard_map/ppermute | solution.py:481
  31.0 10.1 %collective-permute-start.5 = (bf16[5,9,128]{2,1,0:T(8,128)(2,1)S(1)}, bf16[5,9,128]{2,1,0:T(8,128)(2,1)S(1)}, u32[]{:S(2)}, u32[]{:S(2)}) collective-permute-start(bf16[5,9,128]{2,1,0:T(8,128)(2,1)S(1)} %get-tuple-element.40), channel_id=1, source_target_pairs={{0,8},{16,24},{32,40},{48,56},{64,72},{80,88},{96,104},{112,120},{... | collective-permute-start | bytes 34568 | tf_op jit(solution)/shard_map/ppermute | solution.py:482
  35.8 5.4 %copy-start.3 = (f32[2,328,128]{2,1,0:T(8,128)S(1)}, f32[2,328,128]{2,1,0:T(8,128)}, u32[]{:S(2)}) copy-start(f32[2,328,128]{2,1,0:T(8,128)} %constant.12.clone.mx_ref) | copy-start | bytes 1007620
  42.3 12.7 %all-to-all-start.1 = ((bf16[8,208,128]{2,1,0:T(8,128)(2,1)}), bf16[8,208,128]{2,1,0:T(8,128)(2,1)S(1)}, u32[]{:S(2)}, u32[]{:S(2)}) async-start(bf16[8,208,128]{2,1,0:T(8,128)(2,1)} %spread.1), calls=%async_computation.1 | async-start | bytes 851968 | tf_op jit(solution)/shard_map/all_to_all | solution.py:549
  47.0 8.0 %copy-start.2 = (f32[16,88,128]{2,1,0:T(8,128)S(1)}, f32[16,88,128]{2,1,0:T(8,128)}, u32[]{:S(2)}) copy-start(f32[16,88,128]{2,1,0:T(8,128)} %constant.13.clone.my_ref) | copy-start | bytes 2162692
  47.0 8.0 %copy-start.4 = (f32[512,128]{1,0:T(8,128)S(1)}, f32[512,128]{1,0:T(8,128)}, u32[]{:S(2)}) copy-start(f32[512,128]{1,0:T(8,128)} %constant.14.clone.mz_ref) | copy-start | bytes 786436

commit v14 on v13

--- a/solution.py
+++ b/solution.py
@@ -13,7 +13,7 @@
 REACH = 10
 TAPS = 21
 GROUP = 3
-SPLIT = 6
+SPLIT = 9
 
 
 def weight_np(offset):

time: 59.5 us -> 59.5 us (level)
    all_to_all x1, waiting for transfers between devices: 2.77 us -> 0.89 us  [per_device(): coarse = lax.all_to_all(coarse, 'gx', 0, 0)]
    all_to_all x1, waiting for transfers between devices: 1.44 us -> 2.86 us  [per_device(): parts = lax.all_to_all(parts, 'gy', 0, 0)]
where the time goes in v14:
time: 59.5 us; the launch traced here: 59.1 us
  starting transfers between devices  31.8 us (53%)
  Pallas kernels  16.4 us (28%)
  waiting for transfers between devices  7.69 us (13%)
  local copies, waits for them, and re-layouts  2.44 us (4%)
  matrix products  0.62 us (1%)
    pallas_call x8, Pallas kernels, vmem_call(): pl.pallas_call(body, out_shape=out_shape, in_specs=[spec(pltpu.VMEM)] * l...  16.4 us
    all_to_all x1, starting transfers between devices, per_device(): coarse = lax.all_to_all(coarse, 'gx', 0, 0)  11.5 us
    ppermute x3, starting transfers between devices, swap(): return (lax.ppermute(first, axis, both(pairs)), second)  8.41 us
    ppermute x3, starting transfers between devices, swap(): second = lax.ppermute(second, axis, both(others))  7.12 us
    all_to_all x1, starting transfers between devices, per_device(): parts = lax.all_to_all(parts, 'gy', 0, 0)  4.73 us
    ppermute x3, waiting for transfers between devices, swap(): return (lax.ppermute(first, axis, both(pairs)), second)  2.88 us
    all_to_all x1, waiting for transfers between devices, per_device(): parts = lax.all_to_all(parts, 'gy', 0, 0)  2.86 us
    unnamed x16, local copies, waits for them, and re-layouts  1.72 us
  transfers between devices with their start and end apart: 8, of which 5 were waited for; matrix products, arithmetic and copies ran while one was open for 2% of the time, Pallas kernels for 16%

profile of v14, /device:TPU:2, one launch (start us, length us, event | category | flops | bytes accessed | tf_op | source)
XLA Modules:
  0.0 59.1 jit_solution(5655243881397656275)
XLA Ops:
  0.0 0.9 %copy-done = bf16[20,20,128]{2,1,0:T(8,128)(2,1)S(1)} copy-done((bf16[20,20,128]{2,1,0:T(8,128)(2,1)S(1)}, bf16[20,20,128]{2,1,0:T(8,128)(2,1)}, u32[]{:S(2)}) %copy-start) | copy-done | bytes 102424
  0.9 0.7 %collective-permute-start = (bf16[200,128]{1,0:T(8,128)(2,1)S(1)}, bf16[200,128]{1,0:T(8,128)(2,1)S(1)}, u32[]{:S(2)}, u32[]{:S(2)}) collective-permute-start(bf16[200,128]{1,0:T(8,128)(2,1)S(1)} %get-tuple-element.25), channel_id=1, source_target_pairs={{8,16},{24,32},{40,48},{56,64},{72,80},{88,96},{104,112},{120,128}... | collective-permute-start | bytes 153608 | tf_op jit(solution)/shard_map/ppermute | solution.py:481
  1.6 3.6 %collective-permute-start.1 = (bf16[200,128]{1,0:T(8,128)(2,1)S(1)}, bf16[200,128]{1,0:T(8,128)(2,1)S(1)}, u32[]{:S(2)}, u32[]{:S(2)}) collective-permute-start(bf16[200,128]{1,0:T(8,128)(2,1)S(1)} %get-tuple-element.26), channel_id=1, source_target_pairs={{0,8},{16,24},{32,40},{48,56},{64,72},{80,88},{96,104},{112,120},{... | collective-permute-start | bytes 153608 | tf_op jit(solution)/shard_map/ppermute | solution.py:482
  5.3 0.8 %collective-permute-done.1.near_ref.near_x_ref = bf16[200,128]{1,0:T(8,128)(2,1)S(1)} collective-permute-done((bf16[200,128]{1,0:T(8,128)(2,1)S(1)}, bf16[200,128]{1,0:T(8,128)(2,1)S(1)}, u32[]{:S(2)}, u32[]{:S(2)}) %collective-permute-start.1) | collective-permute-done | bytes 51232 | tf_op jit(solution)/shard_map/ppermute | solution.py:482
  6.2 5.8 %collective-permute-start.2 = (bf16[400,128]{1,0:T(8,128)(2,1)S(1)}, bf16[400,128]{1,0:T(8,128)(2,1)S(1)}, u32[]{:S(2)}, u32[]{:S(2)}) collective-permute-start(bf16[400,128]{1,0:T(8,128)(2,1)S(1)} %get-tuple-element.29), channel_id=1, source_target_pairs={{1,2},{3,4},{5,6},{2,1},{4,3},{6,5},{9,10},{11,12},{13,14},{10,9},... | collective-permute-start | bytes 307208 | tf_op jit(solution)/shard_map/ppermute | solution.py:481
  12.1 0.5 copy.8
  12.5 0.3 reshape.4
  12.8 0.4 copy-done.6
  13.2 0.3 fusion.1.far_ref
  13.5 0.4 copy-done.7
  13.9 0.3 fusion.v_ref.near_ref
  14.2 1.1 %collective-permute-done.2.next_y_ref = bf16[400,128]{1,0:T(8,128)(2,1)S(1)} collective-permute-done((bf16[400,128]{1,0:T(8,128)(2,1)S(1)}, bf16[400,128]{1,0:T(8,128)(2,1)S(1)}, u32[]{:S(2)}, u32[]{:S(2)}) %collective-permute-start.2) | collective-permute-done | bytes 102432 | tf_op jit(solution)/shard_map/ppermute | solution.py:481
  15.3 2.1 %collective-permute-done.3.near_y_ref = bf16[400,128]{1,0:T(8,128)(2,1)S(1)} collective-permute-done((bf16[400,128]{1,0:T(8,128)(2,1)S(1)}, bf16[400,128]{1,0:T(8,128)(2,1)S(1)}, u32[]{:S(2)}, u32[]{:S(2)}) %collective-permute-start.3) | collective-permute-done | bytes 102432 | tf_op jit(solution)/shard_map/ppermute | solution.py:482
  17.4 1.4 %restrict.1 = (bf16[40,40,128]{2,1,0:T(8,128)(2,1)S(1)}, bf16[5,9,128]{2,1,0:T(8,128)(2,1)S(1)}, bf16[5,9,128]{2,1,0:T(8,128)(2,1)S(1)}, bf16[5,16,128]{2,1,0:T(8,128)(2,1)S(1)}, f32[32,8,128]{2,1,0:T(8,128)}) custom-call(bf16[20,20,128]{2,1,0:T(8,128)(2,1)S(1)} %copy-done.1, bf16[200,128]{1,0:T(8,128)(2,1)S(1)} %collective-permute-done.next_ref.next_x_ref, ...), custom_call_target="tpu_custom_call" | custom-call | bytes 65536 | tf_op jit(solution)/shard_map/restrict/pallas_call | solution.py:106
  18.8 11.5 %all-to-all-start = ((f32[32,8,128]{2,1,0:T(8,128)}), f32[32,8,128]{2,1,0:T(8,128)S(1)}, u32[]{:S(2)}, u32[]{:S(2)}) async-start(f32[32,8,128]{2,1,0:T(8,128)} %get-tuple-element.34), calls=%async_computation | async-start | bytes 262144 | tf_op jit(solution)/shard_map/all_to_all | solution.py:538
  30.4 0.7 %collective-permute-start.4 = (bf16[5,9,128]{2,1,0:T(8,128)(2,1)S(1)}, bf16[5,9,128]{2,1,0:T(8,128)(2,1)S(1)}, u32[]{:S(2)}, u32[]{:S(2)}) collective-permute-start(bf16[5,9,128]{2,1,0:T(8,128)(2,1)S(1)} %get-tuple-element.39), channel_id=1, source_target_pairs={{8,16},{24,32},{40,48},{56,64},{72,80},{88,96},{104,112},{120,128}... | collective-permute-start | bytes 34568 | tf_op jit(solution)/shard_map/ppermute | solution.py:481
  31.0 4.7 %collective-permute-start.5 = (bf16[5,9,128]{2,1,0:T(8,128)(2,1)S(1)}, bf16[5,9,128]{2,1,0:T(8,128)(2,1)S(1)}, u32[]{:S(2)}, u32[]{:S(2)}) collective-permute-start(bf16[5,9,128]{2,1,0:T(8,128)(2,1)S(1)} %get-tuple-element.40), channel_id=1, source_target_pairs={{0,8},{16,24},{32,40},{48,56},{64,72},{80,88},{96,104},{112,120},{... | collective-permute-start | bytes 34568 | tf_op jit(solution)/shard_map/ppermute | solution.py:482
  35.8 4.4 %fine_sum.2.refs_0_ = f32[240,256]{1,0:T(8,128)S(1)} custom-call(bf16[40,40,128]{2,1,0:T(8,128)(2,1)S(1)} %get-tuple-element.35.d_in_ref, f32[882,128]{1,0:T(8,128)S(1)} %fusion.v_ref.near_ref), custom_call_target="tpu_custom_call" | custom-call | flops 3114270720 | bytes 65536 | tf_op jit(solution)/shard_map/fine_sum/pallas_call | solution.py:106
  40.2 0.9 %all-to-all-done.recv_ref = f32[32,8,128]{2,1,0:T(8,128)S(1)} async-done(((f32[32,8,128]{2,1,0:T(8,128)}), f32[32,8,128]{2,1,0:T(8,128)S(1)}, u32[]{:S(2)}, u32[]{:S(2)}) %all-to-all-start) | async-done | bytes 131104 | tf_op jit(solution)/shard_map/all_to_all | solution.py:538
  41.1 1.2 %spread.1 = bf16[8,208,128]{2,1,0:T(8,128)(2,1)} custom-call(f32[32,8,128]{2,1,0:T(8,128)S(1)} %all-to-all-done.recv_ref, f32[2,328,128]{2,1,0:T(8,128)S(1)} %copy-done.3, bf16[5,16,128]{2,1,0:T(8,128)(2,1)S(1)} %get-tuple-element.38.own_ref, bf16[5,9,128]{2,1,0:T(8,128)(2,1)S(1)} %collective-permute-done.4.next_ref, ...), custom_call_target="tpu_custom_call" | custom-call | bytes 65536 | tf_op jit(solution)/shard_map/spread/pallas_call | solution.py:106
  42.3 4.7 %all-to-all-start.1 = ((bf16[8,208,128]{2,1,0:T(8,128)(2,1)}), bf16[8,208,128]{2,1,0:T(8,128)(2,1)S(1)}, u32[]{:S(2)}, u32[]{:S(2)}) async-start(bf16[8,208,128]{2,1,0:T(8,128)(2,1)} %spread.1), calls=%async_computation.1 | async-start | bytes 851968 | tf_op jit(solution)/shard_map/all_to_all | solution.py:549
  47.0 5.1 %fine_sum.3.fine_ref = f32[240,256]{1,0:T(8,128)S(1)} custom-call(bf16[40,40,128]{2,1,0:T(8,128)(2,1)S(1)} %get-tuple-element.35.d_in_ref, f32[882,128]{1,0:T(8,128)S(1)} %fusion.v_ref.near_ref, f32[240,256]{1,0:T(8,128)S(1)} %fine_sum.2.refs_0_), custom_call_target="tpu_custom_call" | custom-call | flops 4152360960 | bytes 65536 | tf_op jit(solution)/shard_map/fine_sum/pallas_call | solution.py:106
  52.2 2.9 %all-to-all-done.1.recv_ref = bf16[8,208,128]{2,1,0:T(8,128)(2,1)S(1)} async-done(((bf16[8,208,128]{2,1,0:T(8,128)(2,1)}), bf16[8,208,128]{2,1,0:T(8,128)(2,1)S(1)}, u32[]{:S(2)}, u32[]{:S(2)}) %all-to-all-start.1) | async-done | bytes 426016 | tf_op jit(solution)/shard_map/all_to_all | solution.py:549
  55.0 4.1 %final.1 = f32[20,20,128]{2,1,0:T(8,128)} custom-call(bf16[8,208,128]{2,1,0:T(8,128)(2,1)S(1)} %all-to-all-done.1.recv_ref, f32[16,88,128]{2,1,0:T(8,128)S(1)} %copy-done.2, f32[512,128]{1,0:T(8,128)S(1)} %copy-done.4, f32[882,128]{1,0:T(8,128)S(1)} %fusion.v_ref.near_ref, f32[882,128]{1,0:T(8,128)S(1)} %fusion.1.far_ref, f32[240,256]{1,0:T(8,128)S(1)} %fine_sum.3.fine_ref), custom_call_target="tpu_custom_call" | custom-call | bytes 65536 | tf_op jit(solution)/shard_map/final/pallas_call | solution.py:106
  (20 shorter events, 0.3 us)
Async XLA Ops:
  0.0 0.9 %copy-start = (bf16[20,20,128]{2,1,0:T(8,128)(2,1)S(1)}, bf16[20,20,128]{2,1,0:T(8,128)(2,1)}, u32[]{:S(2)}) copy-start(bf16[20,20,128]{2,1,0:T(8,128)(2,1)} %blk_ref.5) | copy-start | bytes 307204
  0.9 4.3 %collective-permute-start = (bf16[200,128]{1,0:T(8,128)(2,1)S(1)}, bf16[200,128]{1,0:T(8,128)(2,1)S(1)}, u32[]{:S(2)}, u32[]{:S(2)}) collective-permute-start(bf16[200,128]{1,0:T(8,128)(2,1)S(1)} %get-tuple-element.25), channel_id=1, source_target_pairs={{8,16},{24,32},{40,48},{56,64},{72,80},{88,96},{104,112},{120,128}... | collective-permute-start | bytes 153608 | tf_op jit(solution)/shard_map/ppermute | solution.py:481
  1.6 4.5 %collective-permute-start.1 = (bf16[200,128]{1,0:T(8,128)(2,1)S(1)}, bf16[200,128]{1,0:T(8,128)(2,1)S(1)}, u32[]{:S(2)}, u32[]{:S(2)}) collective-permute-start(bf16[200,128]{1,0:T(8,128)(2,1)S(1)} %get-tuple-element.26), channel_id=1, source_target_pairs={{0,8},{16,24},{32,40},{48,56},{64,72},{80,88},{96,104},{112,120},{... | collective-permute-start | bytes 153608 | tf_op jit(solution)/shard_map/ppermute | solution.py:482
  5.3 6.8 %copy-start.5 = (bf16[2,21,21,21]{3,0,2,1:T(2,128)(2,1)S(1)}, bf16[2,21,21,21]{3,0,2,1:T(2,128)(2,1)}, u32[]{:S(2)}) copy-start(bf16[2,21,21,21]{3,0,2,1:T(2,128)(2,1)} %param.8) | copy-start | bytes 111136
  6.2 9.1 %collective-permute-start.2 = (bf16[400,128]{1,0:T(8,128)(2,1)S(1)}, bf16[400,128]{1,0:T(8,128)(2,1)S(1)}, u32[]{:S(2)}, u32[]{:S(2)}) collective-permute-start(bf16[400,128]{1,0:T(8,128)(2,1)S(1)} %get-tuple-element.29), channel_id=1, source_target_pairs={{1,2},{3,4},{5,6},{2,1},{4,3},{6,5},{9,10},{11,12},{13,14},{10,9},... | collective-permute-start | bytes 307208 | tf_op jit(solution)/shard_map/ppermute | solution.py:481
  12.0 5.4 %collective-permute-start.3 = (bf16[400,128]{1,0:T(8,128)(2,1)S(1)}, bf16[400,128]{1,0:T(8,128)(2,1)S(1)}, u32[]{:S(2)}, u32[]{:S(2)}) collective-permute-start(bf16[400,128]{1,0:T(8,128)(2,1)S(1)} %get-tuple-element.30), channel_id=1, source_target_pairs={{0,1},{2,3},{4,5},{6,7},{1,0},{3,2},{5,4},{7,6},{8,9},{10,11},{12,... | collective-permute-start | bytes 307208 | tf_op jit(solution)/shard_map/ppermute | solution.py:482
  12.5 0.7 %copy-start.6 = (bf16[21,128]{1,0:T(8,128)(2,1)S(1)}, bf16[21,128]{1,0:T(8,128)(2,1)}, u32[]{:S(2)}) copy-start(bf16[21,128]{1,0:T(8,128)(2,1)} %constant.11.clone) | copy-start | bytes 16132
  13.2 0.7 %copy-start.7 = (bf16[21,128]{1,0:T(8,128)(2,1)S(1)}, bf16[21,128]{1,0:T(8,128)(2,1)}, u32[]{:S(2)}) copy-start(bf16[21,128]{1,0:T(8,128)(2,1)} %constant.10.clone) | copy-start | bytes 16132
  13.9 3.5 %copy-start.1 = (bf16[20,20,128]{2,1,0:T(8,128)(2,1)S(1)}, bf16[20,20,128]{2,1,0:T(8,128)(2,1)}, u32[]{:S(2)}) copy-start(bf16[20,20,128]{2,1,0:T(8,128)(2,1)} %blk_ref.5) | copy-start | bytes 307204
  18.8 22.3 %all-to-all-start = ((f32[32,8,128]{2,1,0:T(8,128)}), f32[32,8,128]{2,1,0:T(8,128)S(1)}, u32[]{:S(2)}, u32[]{:S(2)}) async-start(f32[32,8,128]{2,1,0:T(8,128)} %get-tuple-element.34), calls=%async_computation | async-start | bytes 262144 | tf_op jit(solution)/shard_map/all_to_all | solution.py:538
  30.4 10.8 %collective-permute-start.4 = (bf16[5,9,128]{2,1,0:T(8,128)(2,1)S(1)}, bf16[5,9,128]{2,1,0:T(8,128)(2,1)S(1)}, u32[]{:S(2)}, u32[]{:S(2)}) collective-permute-start(bf16[5,9,128]{2,1,0:T(8,128)(2,1)S(1)} %get-tuple-element.39), channel_id=1, source_target_pairs={{8,16},{24,32},{40,48},{56,64},{72,80},{88,96},{104,112},{120,128}... | collective-permute-start | bytes 34568 | tf_op jit(solution)/shard_map/ppermute | solution.py:481
  31.0 10.1 %collective-permute-start.5 = (bf16[5,9,128]{2,1,0:T(8,128)(2,1)S(1)}, bf16[5,9,128]{2,1,0:T(8,128)(2,1)S(1)}, u32[]{:S(2)}, u32[]{:S(2)}) collective-permute-start(bf16[5,9,128]{2,1,0:T(8,128)(2,1)S(1)} %get-tuple-element.40), channel_id=1, source_target_pairs={{0,8},{16,24},{32,40},{48,56},{64,72},{80,88},{96,104},{112,120},{... | collective-permute-start | bytes 34568 | tf_op jit(solution)/shard_map/ppermute | solution.py:482
  35.8 5.4 %copy-start.3 = (f32[2,328,128]{2,1,0:T(8,128)S(1)}, f32[2,328,128]{2,1,0:T(8,128)}, u32[]{:S(2)}) copy-start(f32[2,328,128]{2,1,0:T(8,128)} %constant.12.clone.mx_ref) | copy-start | bytes 1007620
  42.3 12.7 %all-to-all-start.1 = ((bf16[8,208,128]{2,1,0:T(8,128)(2,1)}), bf16[8,208,128]{2,1,0:T(8,128)(2,1)S(1)}, u32[]{:S(2)}, u32[]{:S(2)}) async-start(bf16[8,208,128]{2,1,0:T(8,128)(2,1)} %spread.1), calls=%async_computation.1 | async-start | bytes 851968 | tf_op jit(solution)/shard_map/all_to_all | solution.py:549
  47.0 8.0 %copy-start.2 = (f32[16,88,128]{2,1,0:T(8,128)S(1)}, f32[16,88,128]{2,1,0:T(8,128)}, u32[]{:S(2)}) copy-start(f32[16,88,128]{2,1,0:T(8,128)} %constant.13.clone.my_ref) | copy-start | bytes 2162692
  47.0 8.0 %copy-start.4 = (f32[512,128]{1,0:T(8,128)S(1)}, f32[512,128]{1,0:T(8,128)}, u32[]{:S(2)}) copy-start(f32[512,128]{1,0:T(8,128)} %constant.14.clone.mz_ref) | copy-start | bytes 786436

commit v15 on v13

--- a/solution.py
+++ b/solution.py
@@ -155,11 +155,7 @@
         out_ref[...] = jnp.concatenate([own_ref[k], dense[k]], axis=0).astype(bf16)
 
 
-def restrict_kernel(
-    blk_ref, next_x_ref, near_x_ref, next_y_ref, near_y_ref,
-    d_out_ref, second_ref, first_ref, own_ref, out_ref,
-    d_ref, dense, sides, planes, cells, mid,
-):
+def assemble(blk_ref, next_x_ref, near_x_ref, next_y_ref, near_y_ref, d_ref, dense, sides):
     even_x = even(lax.axis_index("gx"))
     even_y = even(lax.axis_index("gy"))
     upper = jnp.where(even_y, 1, 0)
@@ -179,7 +175,30 @@
             at = 20 * (x % 30)
             centre = sides[x // 30, at : at + 20, :]
         d_ref[p, i, 10:30, :] = centre
-        d_out_ref[x] = d_ref[p, i, 0:40, :].astype(bf16)
+
+
+def pack_kernel(
+    blk_ref, next_x_ref, near_x_ref, next_y_ref, near_y_ref, mid_ref,
+    d_out_ref, second_ref, first_ref,
+    d_ref, dense, sides, mid,
+):
+    even_x = even(lax.axis_index("gx"))
+    for n in range(5):
+        mid[n] = mid_ref[n + 2].astype(f32)
+        right, left = mid[n, 1:10, :], mid[n, 6:15, :]
+        first_ref[n] = jnp.where(even_x, right, left).astype(bf16)
+        second_ref[n] = jnp.where(even_x, left, right).astype(bf16)
+    assemble(blk_ref, next_x_ref, near_x_ref, next_y_ref, near_y_ref, d_ref, dense, sides)
+    for x in range(40):
+        d_out_ref[x] = d_ref[x % 2, x // 2, 0:40, :].astype(bf16)
+
+
+def restrict_kernel(
+    blk_ref, next_x_ref, near_x_ref, next_y_ref, near_y_ref,
+    own_ref, out_ref,
+    d_ref, dense, sides, planes, cells, mid,
+):
+    assemble(blk_ref, next_x_ref, near_x_ref, next_y_ref, near_y_ref, d_ref, dense, sides)
 
     def fine(x):
         return d_ref[x % 2, x // 2]
@@ -214,11 +233,8 @@
     for n in range(9):
         mid[n, 0:16, :] = value[16 * n : 16 * n + 16]
         mid[n, 16:24, :] = jnp.zeros((8, 128), f32)
-    for n in range(5):
-        right, left = mid[n + 2, 1:10, :], mid[n + 2, 6:15, :]
-        first_ref[n] = jnp.where(even_x, right, left).astype(bf16)
-        second_ref[n] = jnp.where(even_x, left, right).astype(bf16)
-        own_ref[n] = mid[n + 2, 0:16, :].astype(bf16)
+    for n in range(9):
+        own_ref[n] = value[16 * n : 16 * n + 16].astype(bf16)
 
     lane = lax.broadcasted_iota(jnp.int32, (1, 128), 1)
     odd = lane >= 64
@@ -341,7 +357,7 @@
     for n in range(5):
         near, other = near_ref[n].astype(f32), next_ref[n].astype(f32)
         buf[33 * n : 33 * n + 8, :] = jnp.where(even_x, other, near)[1:9]
-        buf[33 * n + 8 : 33 * n + 24, :] = own_ref[n].astype(f32)
+        buf[33 * n + 8 : 33 * n + 24, :] = own_ref[n + 2].astype(f32)
         buf[33 * n + 24 : 33 * n + 33, :] = jnp.where(even_x, near, other)
     for at, part in ((165, last), (176, value[0:16])):
         rows = part.shape[0]
@@ -514,25 +530,34 @@
     )
     near_y, next_y = swap(first, second, "gy")
     next_y, near_y, near, far = lax.optimization_barrier((next_y, near_y, near, far))
-    d, second, first, own, coarse = vmem_call(
+    pieces = (charges, next_x, near_x, next_y, near_y)
+    scratch = [
+        pltpu.VMEM((2, 20, 48, 128), f32),
+        pltpu.VMEM((2, 400, 128), f32),
+        pltpu.VMEM((2, 200, 128), f32),
+    ]
+    own, coarse = vmem_call(
         restrict_kernel,
-        [
-            shape((40, 40, 128), bf16),
-            shape((5, 9, 128), bf16),
-            shape((5, 9, 128), bf16),
-            shape((5, 16, 128), bf16),
-            shape((count_x, 8, 128), f32),
-        ],
-        [
-            pltpu.VMEM((2, 20, 48, 128), f32),
-            pltpu.VMEM((2, 400, 128), f32),
-            pltpu.VMEM((2, 200, 128), f32),
+        [shape((9, 16, 128), bf16), shape((count_x, 8, 128), f32)],
+        scratch
+        + [
             pltpu.VMEM((16, 48, 128), f32),
             pltpu.VMEM((256, 128), f32),
             pltpu.VMEM((9, 24, 128), f32),
         ],
         "restrict",
-        (charges, next_x, near_x, next_y, near_y),
+        pieces,
+    )
+    d, second, first = vmem_call(
+        pack_kernel,
+        [
+            shape((40, 40, 128), bf16),
+            shape((5, 9, 128), bf16),
+            shape((5, 9, 128), bf16),
+        ],
+        scratch + [pltpu.VMEM((5, 16, 128), f32)],
+        "pack",
+        pieces + (own,),
     )
     near_m, next_m = swap(first, second, "gx")
     coarse = lax.all_to_all(coarse, "gx", 0, 0)

time: 59.5 us -> 59.5 us (level)
    pallas_call x8 -> x9, Pallas kernels: 16 us -> 16.1 us  [vmem_call(): pl.pallas_call(body, out_shape=out_shape, in_specs=[spec(pltpu.VMEM)] * l...]
where the time goes in v15:
time: 59.5 us; the launch traced here: 59 us
  starting transfers between devices  31.8 us (53%)
  Pallas kernels  16.1 us (27%)
  waiting for transfers between devices  7.97 us (13%)
  local copies, waits for them, and re-layouts  2.44 us (4%)
  matrix products  0.62 us (1%)
    pallas_call x9, Pallas kernels, vmem_call(): pl.pallas_call(body, out_shape=out_shape, in_specs=[spec(pltpu.VMEM)] * l...  16.1 us
    all_to_all x1, starting transfers between devices, per_device(): coarse = lax.all_to_all(coarse, 'gx', 0, 0)  11.5 us
    ppermute x3, starting transfers between devices, swap(): return (lax.ppermute(first, axis, both(pairs)), second)  8.41 us
    ppermute x3, starting transfers between devices, swap(): second = lax.ppermute(second, axis, both(others))  7.12 us
    all_to_all x1, starting transfers between devices, per_device(): parts = lax.all_to_all(parts, 'gy', 0, 0)  4.73 us
    ppermute x3, waiting for transfers between devices, swap(): return (lax.ppermute(first, axis, both(pairs)), second)  2.88 us
    all_to_all x1, waiting for transfers between devices, per_device(): coarse = lax.all_to_all(coarse, 'gx', 0, 0)  2.6 us
    unnamed x16, local copies, waits for them, and re-layouts  1.72 us
  transfers between devices with their start and end apart: 8, of which 5 were waited for; matrix products, arithmetic and copies ran while one was open for 2% of the time, Pallas kernels for 16%

profile of v15, /device:TPU:2, one launch (start us, length us, event | category | flops | bytes accessed | tf_op | source)
XLA Modules:
  0.0 59.0 jit_solution(17919717129700103336)
XLA Ops:
  0.0 0.9 %copy-done = bf16[20,20,128]{2,1,0:T(8,128)(2,1)S(1)} copy-done((bf16[20,20,128]{2,1,0:T(8,128)(2,1)S(1)}, bf16[20,20,128]{2,1,0:T(8,128)(2,1)}, u32[]{:S(2)}) %copy-start) | copy-done | bytes 102424
  0.9 0.7 %collective-permute-start = (bf16[200,128]{1,0:T(8,128)(2,1)S(1)}, bf16[200,128]{1,0:T(8,128)(2,1)S(1)}, u32[]{:S(2)}, u32[]{:S(2)}) collective-permute-start(bf16[200,128]{1,0:T(8,128)(2,1)S(1)} %get-tuple-element.25), channel_id=1, source_target_pairs={{8,16},{24,32},{40,48},{56,64},{72,80},{88,96},{104,112},{120,128}... | collective-permute-start | bytes 153608 | tf_op jit(solution)/shard_map/ppermute | solution.py:497
  1.6 3.6 %collective-permute-start.1 = (bf16[200,128]{1,0:T(8,128)(2,1)S(1)}, bf16[200,128]{1,0:T(8,128)(2,1)S(1)}, u32[]{:S(2)}, u32[]{:S(2)}) collective-permute-start(bf16[200,128]{1,0:T(8,128)(2,1)S(1)} %get-tuple-element.26), channel_id=1, source_target_pairs={{0,8},{16,24},{32,40},{48,56},{64,72},{80,88},{96,104},{112,120},{... | collective-permute-start | bytes 153608 | tf_op jit(solution)/shard_map/ppermute | solution.py:498
  5.3 0.8 %collective-permute-done.1.near_ref.near_x_ref = bf16[200,128]{1,0:T(8,128)(2,1)S(1)} collective-permute-done((bf16[200,128]{1,0:T(8,128)(2,1)S(1)}, bf16[200,128]{1,0:T(8,128)(2,1)S(1)}, u32[]{:S(2)}, u32[]{:S(2)}) %collective-permute-start.1) | collective-permute-done | bytes 51232 | tf_op jit(solution)/shard_map/ppermute | solution.py:498
  6.2 5.8 %collective-permute-start.2 = (bf16[400,128]{1,0:T(8,128)(2,1)S(1)}, bf16[400,128]{1,0:T(8,128)(2,1)S(1)}, u32[]{:S(2)}, u32[]{:S(2)}) collective-permute-start(bf16[400,128]{1,0:T(8,128)(2,1)S(1)} %get-tuple-element.29), channel_id=1, source_target_pairs={{1,2},{3,4},{5,6},{2,1},{4,3},{6,5},{9,10},{11,12},{13,14},{10,9},... | collective-permute-start | bytes 307208 | tf_op jit(solution)/shard_map/ppermute | solution.py:497
  12.1 0.5 copy.8
  12.5 0.3 reshape.4
  12.8 0.4 copy-done.6
  13.2 0.3 fusion.1.far_ref
  13.5 0.4 copy-done.7
  13.9 0.3 fusion.v_ref.near_ref
  14.2 1.1 %collective-permute-done.2.next_y_ref = bf16[400,128]{1,0:T(8,128)(2,1)S(1)} collective-permute-done((bf16[400,128]{1,0:T(8,128)(2,1)S(1)}, bf16[400,128]{1,0:T(8,128)(2,1)S(1)}, u32[]{:S(2)}, u32[]{:S(2)}) %collective-permute-start.2) | collective-permute-done | bytes 102432 | tf_op jit(solution)/shard_map/ppermute | solution.py:497
  15.3 2.1 %collective-permute-done.3.near_y_ref = bf16[400,128]{1,0:T(8,128)(2,1)S(1)} collective-permute-done((bf16[400,128]{1,0:T(8,128)(2,1)S(1)}, bf16[400,128]{1,0:T(8,128)(2,1)S(1)}, u32[]{:S(2)}, u32[]{:S(2)}) %collective-permute-start.3) | collective-permute-done | bytes 102432 | tf_op jit(solution)/shard_map/ppermute | solution.py:498
  17.4 1.4 %restrict.1 = (bf16[9,16,128]{2,1,0:T(8,128)(2,1)S(1)}, f32[32,8,128]{2,1,0:T(8,128)}) custom-call(bf16[20,20,128]{2,1,0:T(8,128)(2,1)S(1)} %copy-done.1, bf16[200,128]{1,0:T(8,128)(2,1)S(1)} %collective-permute-done.next_ref.next_x_ref, bf16[200,128]{1,0:T(8,128)(2,1)S(1)} %collective-permute-done.1.near_ref.near_x_ref, ...), custom_call_target="tpu_custom_call" | custom-call | bytes 65536 | tf_op jit(solution)/shard_map/restrict/pallas_call | solution.py:106
  18.7 11.5 %all-to-all-start = ((f32[32,8,128]{2,1,0:T(8,128)}), f32[32,8,128]{2,1,0:T(8,128)S(1)}, u32[]{:S(2)}, u32[]{:S(2)}) async-start(f32[32,8,128]{2,1,0:T(8,128)} %get-tuple-element.34), calls=%async_computation | async-start | bytes 262144 | tf_op jit(solution)/shard_map/all_to_all | solution.py:563
  30.5 0.7 %collective-permute-start.4 = (bf16[5,9,128]{2,1,0:T(8,128)(2,1)S(1)}, bf16[5,9,128]{2,1,0:T(8,128)(2,1)S(1)}, u32[]{:S(2)}, u32[]{:S(2)}) collective-permute-start(bf16[5,9,128]{2,1,0:T(8,128)(2,1)S(1)} %get-tuple-element.39), channel_id=1, source_target_pairs={{8,16},{24,32},{40,48},{56,64},{72,80},{88,96},{104,112},{120,128}... | collective-permute-start | bytes 34568 | tf_op jit(solution)/shard_map/ppermute | solution.py:497
  31.1 4.7 %collective-permute-start.5 = (bf16[5,9,128]{2,1,0:T(8,128)(2,1)S(1)}, bf16[5,9,128]{2,1,0:T(8,128)(2,1)S(1)}, u32[]{:S(2)}, u32[]{:S(2)}) collective-permute-start(bf16[5,9,128]{2,1,0:T(8,128)(2,1)S(1)} %get-tuple-element.40), channel_id=1, source_target_pairs={{0,8},{16,24},{32,40},{48,56},{64,72},{80,88},{96,104},{112,120},{... | collective-permute-start | bytes 34568 | tf_op jit(solution)/shard_map/ppermute | solution.py:498
  35.9 2.5 %fine_sum.2.refs_0_ = f32[240,256]{1,0:T(8,128)S(1)} custom-call(bf16[40,40,128]{2,1,0:T(8,128)(2,1)S(1)} %get-tuple-element.36.d_in_ref, f32[882,128]{1,0:T(8,128)S(1)} %fusion.v_ref.near_ref), custom_call_target="tpu_custom_call" | custom-call | flops 2076180480 | bytes 65536 | tf_op jit(solution)/shard_map/fine_sum/pallas_call | solution.py:106
  38.4 2.6 %all-to-all-done.recv_ref = f32[32,8,128]{2,1,0:T(8,128)S(1)} async-done(((f32[32,8,128]{2,1,0:T(8,128)}), f32[32,8,128]{2,1,0:T(8,128)S(1)}, u32[]{:S(2)}, u32[]{:S(2)}) %all-to-all-start) | async-done | bytes 131104 | tf_op jit(solution)/shard_map/all_to_all | solution.py:563
  41.1 1.2 %spread.1 = bf16[8,208,128]{2,1,0:T(8,128)(2,1)} custom-call(f32[32,8,128]{2,1,0:T(8,128)S(1)} %all-to-all-done.recv_ref, f32[2,328,128]{2,1,0:T(8,128)S(1)} %copy-done.3, bf16[9,16,128]{2,1,0:T(8,128)(2,1)S(1)} %get-tuple-element.35.mid_ref.own_ref, bf16[5,9,128]{2,1,0:T(8,128)(2,1)S(1)} %collective-permute-done.4.next_ref, ...), custom_call_target="tpu_custom_call" | custom-call | bytes 65536 | tf_op jit(solution)/shard_map/spread/pallas_call | solution.py:106
  42.2 4.7 %all-to-all-start.1 = ((bf16[8,208,128]{2,1,0:T(8,128)(2,1)}), bf16[8,208,128]{2,1,0:T(8,128)(2,1)S(1)}, u32[]{:S(2)}, u32[]{:S(2)}) async-start(bf16[8,208,128]{2,1,0:T(8,128)(2,1)} %spread.1), calls=%async_computation.1 | async-start | bytes 851968 | tf_op jit(solution)/shard_map/all_to_all | solution.py:574
  47.0 6.6 %fine_sum.3.fine_ref = f32[240,256]{1,0:T(8,128)S(1)} custom-call(bf16[40,40,128]{2,1,0:T(8,128)(2,1)S(1)} %get-tuple-element.36.d_in_ref, f32[882,128]{1,0:T(8,128)S(1)} %fusion.v_ref.near_ref, f32[240,256]{1,0:T(8,128)S(1)} %fine_sum.2.refs_0_), custom_call_target="tpu_custom_call" | custom-call | flops 5190451200 | bytes 65536 | tf_op jit(solution)/shard_map/fine_sum/pallas_call | solution.py:106
  53.5 1.4 %all-to-all-done.1.recv_ref = bf16[8,208,128]{2,1,0:T(8,128)(2,1)S(1)} async-done(((bf16[8,208,128]{2,1,0:T(8,128)(2,1)}), bf16[8,208,128]{2,1,0:T(8,128)(2,1)S(1)}, u32[]{:S(2)}, u32[]{:S(2)}) %all-to-all-start.1) | async-done | bytes 426016 | tf_op jit(solution)/shard_map/all_to_all | solution.py:574
  55.0 4.1 %final.1 = f32[20,20,128]{2,1,0:T(8,128)} custom-call(bf16[8,208,128]{2,1,0:T(8,128)(2,1)S(1)} %all-to-all-done.1.recv_ref, f32[16,88,128]{2,1,0:T(8,128)S(1)} %copy-done.2, f32[512,128]{1,0:T(8,128)S(1)} %copy-done.4, f32[882,128]{1,0:T(8,128)S(1)} %fusion.v_ref.near_ref, f32[882,128]{1,0:T(8,128)S(1)} %fusion.1.far_ref, f32[240,256]{1,0:T(8,128)S(1)} %fine_sum.3.fine_ref), custom_call_target="tpu_custom_call" | custom-call | bytes 65536 | tf_op jit(solution)/shard_map/final/pallas_call | solution.py:106
  (21 shorter events, 0.5 us)
Async XLA Ops:
  0.0 0.9 %copy-start = (bf16[20,20,128]{2,1,0:T(8,128)(2,1)S(1)}, bf16[20,20,128]{2,1,0:T(8,128)(2,1)}, u32[]{:S(2)}) copy-start(bf16[20,20,128]{2,1,0:T(8,128)(2,1)} %blk_ref.7) | copy-start | bytes 307204
  0.9 4.3 %collective-permute-start = (bf16[200,128]{1,0:T(8,128)(2,1)S(1)}, bf16[200,128]{1,0:T(8,128)(2,1)S(1)}, u32[]{:S(2)}, u32[]{:S(2)}) collective-permute-start(bf16[200,128]{1,0:T(8,128)(2,1)S(1)} %get-tuple-element.25), channel_id=1, source_target_pairs={{8,16},{24,32},{40,48},{56,64},{72,80},{88,96},{104,112},{120,128}... | collective-permute-start | bytes 153608 | tf_op jit(solution)/shard_map/ppermute | solution.py:497
  1.6 4.5 %collective-permute-start.1 = (bf16[200,128]{1,0:T(8,128)(2,1)S(1)}, bf16[200,128]{1,0:T(8,128)(2,1)S(1)}, u32[]{:S(2)}, u32[]{:S(2)}) collective-permute-start(bf16[200,128]{1,0:T(8,128)(2,1)S(1)} %get-tuple-element.26), channel_id=1, source_target_pairs={{0,8},{16,24},{32,40},{48,56},{64,72},{80,88},{96,104},{112,120},{... | collective-permute-start | bytes 153608 | tf_op jit(solution)/shard_map/ppermute | solution.py:498
  5.3 6.8 %copy-start.5 = (bf16[2,21,21,21]{3,0,2,1:T(2,128)(2,1)S(1)}, bf16[2,21,21,21]{3,0,2,1:T(2,128)(2,1)}, u32[]{:S(2)}) copy-start(bf16[2,21,21,21]{3,0,2,1:T(2,128)(2,1)} %param.8) | copy-start | bytes 111136
  6.2 9.1 %collective-permute-start.2 = (bf16[400,128]{1,0:T(8,128)(2,1)S(1)}, bf16[400,128]{1,0:T(8,128)(2,1)S(1)}, u32[]{:S(2)}, u32[]{:S(2)}) collective-permute-start(bf16[400,128]{1,0:T(8,128)(2,1)S(1)} %get-tuple-element.29), channel_id=1, source_target_pairs={{1,2},{3,4},{5,6},{2,1},{4,3},{6,5},{9,10},{11,12},{13,14},{10,9},... | collective-permute-start | bytes 307208 | tf_op jit(solution)/shard_map/ppermute | solution.py:497
  12.0 5.4 %collective-permute-start.3 = (bf16[400,128]{1,0:T(8,128)(2,1)S(1)}, bf16[400,128]{1,0:T(8,128)(2,1)S(1)}, u32[]{:S(2)}, u32[]{:S(2)}) collective-permute-start(bf16[400,128]{1,0:T(8,128)(2,1)S(1)} %get-tuple-element.30), channel_id=1, source_target_pairs={{0,1},{2,3},{4,5},{6,7},{1,0},{3,2},{5,4},{7,6},{8,9},{10,11},{12,... | collective-permute-start | bytes 307208 | tf_op jit(solution)/shard_map/ppermute | solution.py:498
  12.5 0.7 %copy-start.6 = (bf16[21,128]{1,0:T(8,128)(2,1)S(1)}, bf16[21,128]{1,0:T(8,128)(2,1)}, u32[]{:S(2)}) copy-start(bf16[21,128]{1,0:T(8,128)(2,1)} %constant.11.clone) | copy-start | bytes 16132
  13.2 0.7 %copy-start.7 = (bf16[21,128]{1,0:T(8,128)(2,1)S(1)}, bf16[21,128]{1,0:T(8,128)(2,1)}, u32[]{:S(2)}) copy-start(bf16[21,128]{1,0:T(8,128)(2,1)} %constant.10.clone) | copy-start | bytes 16132
  13.9 3.5 %copy-start.1 = (bf16[20,20,128]{2,1,0:T(8,128)(2,1)S(1)}, bf16[20,20,128]{2,1,0:T(8,128)(2,1)}, u32[]{:S(2)}) copy-start(bf16[20,20,128]{2,1,0:T(8,128)(2,1)} %blk_ref.7) | copy-start | bytes 307204
  18.7 22.3 %all-to-all-start = ((f32[32,8,128]{2,1,0:T(8,128)}), f32[32,8,128]{2,1,0:T(8,128)S(1)}, u32[]{:S(2)}, u32[]{:S(2)}) async-start(f32[32,8,128]{2,1,0:T(8,128)} %get-tuple-element.34), calls=%async_computation | async-start | bytes 262144 | tf_op jit(solution)/shard_map/all_to_all | solution.py:563
  30.5 10.6 %collective-permute-start.4 = (bf16[5,9,128]{2,1,0:T(8,128)(2,1)S(1)}, bf16[5,9,128]{2,1,0:T(8,128)(2,1)S(1)}, u32[]{:S(2)}, u32[]{:S(2)}) collective-permute-start(bf16[5,9,128]{2,1,0:T(8,128)(2,1)S(1)} %get-tuple-element.39), channel_id=1, source_target_pairs={{8,16},{24,32},{40,48},{56,64},{72,80},{88,96},{104,112},{120,128}... | collective-permute-start | bytes 34568 | tf_op jit(solution)/shard_map/ppermute | solution.py:497
  31.1 9.9 %collective-permute-start.5 = (bf16[5,9,128]{2,1,0:T(8,128)(2,1)S(1)}, bf16[5,9,128]{2,1,0:T(8,128)(2,1)S(1)}, u32[]{:S(2)}, u32[]{:S(2)}) collective-permute-start(bf16[5,9,128]{2,1,0:T(8,128)(2,1)S(1)} %get-tuple-element.40), channel_id=1, source_target_pairs={{0,8},{16,24},{32,40},{48,56},{64,72},{80,88},{96,104},{112,120},{... | collective-permute-start | bytes 34568 | tf_op jit(solution)/shard_map/ppermute | solution.py:498
  35.9 5.2 %copy-start.3 = (f32[2,328,128]{2,1,0:T(8,128)S(1)}, f32[2,328,128]{2,1,0:T(8,128)}, u32[]{:S(2)}) copy-start(f32[2,328,128]{2,1,0:T(8,128)} %constant.12.clone.mx_ref) | copy-start | bytes 1007620
  42.2 12.7 %all-to-all-start.1 = ((bf16[8,208,128]{2,1,0:T(8,128)(2,1)}), bf16[8,208,128]{2,1,0:T(8,128)(2,1)S(1)}, u32[]{:S(2)}, u32[]{:S(2)}) async-start(bf16[8,208,128]{2,1,0:T(8,128)(2,1)} %spread.1), calls=%async_computation.1 | async-start | bytes 851968 | tf_op jit(solution)/shard_map/all_to_all | solution.py:574
  46.9 8.0 %copy-start.2 = (f32[16,88,128]{2,1,0:T(8,128)S(1)}, f32[16,88,128]{2,1,0:T(8,128)}, u32[]{:S(2)}) copy-start(f32[16,88,128]{2,1,0:T(8,128)} %constant.13.clone.my_ref) | copy-start | bytes 2162692
  47.0 8.0 %copy-start.4 = (f32[512,128]{1,0:T(8,128)S(1)}, f32[512,128]{1,0:T(8,128)}, u32[]{:S(2)}) copy-start(f32[512,128]{1,0:T(8,128)} %constant.14.clone.mz_ref) | copy-start | bytes 786436

commit v16 on v15

--- a/solution.py
+++ b/solution.py
@@ -359,12 +359,12 @@
         buf[33 * n : 33 * n + 8, :] = jnp.where(even_x, other, near)[1:9]
         buf[33 * n + 8 : 33 * n + 24, :] = own_ref[n + 2].astype(f32)
         buf[33 * n + 24 : 33 * n + 33, :] = jnp.where(even_x, near, other)
-    for at, part in ((165, last), (176, value[0:16])):
+    for at, part in ((165, last), (173, value[0:13])):
         rows = part.shape[0]
         high = part.astype(bf16).astype(f32)
         buf[at : at + rows, :] = high
         buf[at + rows : at + 2 * rows, :] = part - high
-    buf[173:176, :] = jnp.zeros((3, 128), f32)
+    buf[199:200, :] = jnp.zeros((1, 128), f32)
     packed = buf[...].astype(bf16)
     for k in range(out_ref.shape[0]):
         out_ref[k] = packed
@@ -437,9 +437,9 @@
     start = 10 * index_y
     sums = [[None] * 14, [None] * 14]
     for k in range(count):
-        main = recv_ref[k, 176:192, :].astype(f32) + recv_ref[k, 192:208, :].astype(f32)
-        last = recv_ref[k, 160:176, :].astype(f32)
-        last = last[5:9] + last[9:13]
+        got = recv_ref[k].astype(f32)
+        main = jnp.concatenate([got[173:186] + got[186:199], jnp.zeros((3, 128), f32)], axis=0)
+        last = got[165:169] + got[169:173]
         tail[k, pl.ds(0, 4, stride=4), :] = last
         for r in range(1, 4):
             tail[k, pl.ds(r, 4, stride=4), :] = pltpu.roll(last, 128 - 32 * r, 1)
@@ -565,8 +565,8 @@
     coarse, fine = lax.optimization_barrier((coarse, fine))
     parts = vmem_call(
         spread_kernel,
-        [shape((count_y, 208, 128), bf16)],
-        [pltpu.VMEM((208, 128), f32), pltpu.VMEM((16, 128), f32)],
+        [shape((count_y, 200, 128), bf16)],
+        [pltpu.VMEM((200, 128), f32), pltpu.VMEM((16, 128), f32)],
         "spread",
         (coarse, jnp.asarray(matrix_x_np(spread)), own, next_m, near_m),
     )[0]

time: 59.5 us -> 59.3 us (level)
  no operation moved by 1% of the time
where the time goes in v16:
time: 59.3 us; the launch traced here: 58.9 us
  starting transfers between devices  31.8 us (54%)
  Pallas kernels  16.1 us (27%)
  waiting for transfers between devices  7.8 us (13%)
  local copies, waits for them, and re-layouts  2.44 us (4%)
  matrix products  0.62 us (1%)
    pallas_call x9, Pallas kernels, vmem_call(): pl.pallas_call(body, out_shape=out_shape, in_specs=[spec(pltpu.VMEM)] * l...  16.1 us
    all_to_all x1, starting transfers between devices, per_device(): coarse = lax.all_to_all(coarse, 'gx', 0, 0)  11.5 us
    ppermute x3, starting transfers between devices, swap(): return (lax.ppermute(first, axis, both(pairs)), second)  8.41 us
    ppermute x3, starting transfers between devices, swap(): second = lax.ppermute(second, axis, both(others))  7.12 us
    all_to_all x1, starting transfers between devices, per_device(): parts = lax.all_to_all(parts, 'gy', 0, 0)  4.73 us
    ppermute x3, waiting for transfers between devices, swap(): return (lax.ppermute(first, axis, both(pairs)), second)  2.88 us
    all_to_all x1, waiting for transfers between devices, per_device(): coarse = lax.all_to_all(coarse, 'gx', 0, 0)  2.6 us
    unnamed x16, local copies, waits for them, and re-layouts  1.72 us
  transfers between devices with their start and end apart: 8, of which 5 were waited for; matrix products, arithmetic and copies ran while one was open for 2% of the time, Pallas kernels for 16%

profile of v16, /device:TPU:2, one launch (start us, length us, event | category | flops | bytes accessed | tf_op | source)
XLA Modules:
  0.0 58.9 jit_solution(7096497187754902067)
XLA Ops:
  0.0 0.9 %copy-done = bf16[20,20,128]{2,1,0:T(8,128)(2,1)S(1)} copy-done((bf16[20,20,128]{2,1,0:T(8,128)(2,1)S(1)}, bf16[20,20,128]{2,1,0:T(8,128)(2,1)}, u32[]{:S(2)}) %copy-start) | copy-done | bytes 102424
  0.9 0.7 %collective-permute-start = (bf16[200,128]{1,0:T(8,128)(2,1)S(1)}, bf16[200,128]{1,0:T(8,128)(2,1)S(1)}, u32[]{:S(2)}, u32[]{:S(2)}) collective-permute-start(bf16[200,128]{1,0:T(8,128)(2,1)S(1)} %get-tuple-element.25), channel_id=1, source_target_pairs={{8,16},{24,32},{40,48},{56,64},{72,80},{88,96},{104,112},{120,128}... | collective-permute-start | bytes 153608 | tf_op jit(solution)/shard_map/ppermute | solution.py:497
  1.6 3.6 %collective-permute-start.1 = (bf16[200,128]{1,0:T(8,128)(2,1)S(1)}, bf16[200,128]{1,0:T(8,128)(2,1)S(1)}, u32[]{:S(2)}, u32[]{:S(2)}) collective-permute-start(bf16[200,128]{1,0:T(8,128)(2,1)S(1)} %get-tuple-element.26), channel_id=1, source_target_pairs={{0,8},{16,24},{32,40},{48,56},{64,72},{80,88},{96,104},{112,120},{... | collective-permute-start | bytes 153608 | tf_op jit(solution)/shard_map/ppermute | solution.py:498
  5.3 0.8 %collective-permute-done.1.near_ref.near_x_ref = bf16[200,128]{1,0:T(8,128)(2,1)S(1)} collective-permute-done((bf16[200,128]{1,0:T(8,128)(2,1)S(1)}, bf16[200,128]{1,0:T(8,128)(2,1)S(1)}, u32[]{:S(2)}, u32[]{:S(2)}) %collective-permute-start.1) | collective-permute-done | bytes 51232 | tf_op jit(solution)/shard_map/ppermute | solution.py:498
  6.2 5.8 %collective-permute-start.2 = (bf16[400,128]{1,0:T(8,128)(2,1)S(1)}, bf16[400,128]{1,0:T(8,128)(2,1)S(1)}, u32[]{:S(2)}, u32[]{:S(2)}) collective-permute-start(bf16[400,128]{1,0:T(8,128)(2,1)S(1)} %get-tuple-element.29), channel_id=1, source_target_pairs={{1,2},{3,4},{5,6},{2,1},{4,3},{6,5},{9,10},{11,12},{13,14},{10,9},... | collective-permute-start | bytes 307208 | tf_op jit(solution)/shard_map/ppermute | solution.py:497
  12.1 0.5 copy.8
  12.5 0.3 reshape.4
  12.8 0.4 copy-done.6
  13.2 0.3 fusion.1.far_ref
  13.5 0.4 copy-done.7
  13.9 0.3 fusion.v_ref.near_ref
  14.2 1.1 %collective-permute-done.2.next_y_ref = bf16[400,128]{1,0:T(8,128)(2,1)S(1)} collective-permute-done((bf16[400,128]{1,0:T(8,128)(2,1)S(1)}, bf16[400,128]{1,0:T(8,128)(2,1)S(1)}, u32[]{:S(2)}, u32[]{:S(2)}) %collective-permute-start.2) | collective-permute-done | bytes 102432 | tf_op jit(solution)/shard_map/ppermute | solution.py:497
  15.3 2.1 %collective-permute-done.3.near_y_ref = bf16[400,128]{1,0:T(8,128)(2,1)S(1)} collective-permute-done((bf16[400,128]{1,0:T(8,128)(2,1)S(1)}, bf16[400,128]{1,0:T(8,128)(2,1)S(1)}, u32[]{:S(2)}, u32[]{:S(2)}) %collective-permute-start.3) | collective-permute-done | bytes 102432 | tf_op jit(solution)/shard_map/ppermute | solution.py:498
  17.4 1.4 %restrict.1 = (bf16[9,16,128]{2,1,0:T(8,128)(2,1)S(1)}, f32[32,8,128]{2,1,0:T(8,128)}) custom-call(bf16[20,20,128]{2,1,0:T(8,128)(2,1)S(1)} %copy-done.1, bf16[200,128]{1,0:T(8,128)(2,1)S(1)} %collective-permute-done.next_ref.next_x_ref, bf16[200,128]{1,0:T(8,128)(2,1)S(1)} %collective-permute-done.1.near_ref.near_x_ref, ...), custom_call_target="tpu_custom_call" | custom-call | bytes 65536 | tf_op jit(solution)/shard_map/restrict/pallas_call | solution.py:106
  18.7 11.5 %all-to-all-start = ((f32[32,8,128]{2,1,0:T(8,128)}), f32[32,8,128]{2,1,0:T(8,128)S(1)}, u32[]{:S(2)}, u32[]{:S(2)}) async-start(f32[32,8,128]{2,1,0:T(8,128)} %get-tuple-element.34), calls=%async_computation | async-start | bytes 262144 | tf_op jit(solution)/shard_map/all_to_all | solution.py:563
  30.5 0.7 %collective-permute-start.4 = (bf16[5,9,128]{2,1,0:T(8,128)(2,1)S(1)}, bf16[5,9,128]{2,1,0:T(8,128)(2,1)S(1)}, u32[]{:S(2)}, u32[]{:S(2)}) collective-permute-start(bf16[5,9,128]{2,1,0:T(8,128)(2,1)S(1)} %get-tuple-element.39), channel_id=1, source_target_pairs={{8,16},{24,32},{40,48},{56,64},{72,80},{88,96},{104,112},{120,128}... | collective-permute-start | bytes 34568 | tf_op jit(solution)/shard_map/ppermute | solution.py:497
  31.1 4.7 %collective-permute-start.5 = (bf16[5,9,128]{2,1,0:T(8,128)(2,1)S(1)}, bf16[5,9,128]{2,1,0:T(8,128)(2,1)S(1)}, u32[]{:S(2)}, u32[]{:S(2)}) collective-permute-start(bf16[5,9,128]{2,1,0:T(8,128)(2,1)S(1)} %get-tuple-element.40), channel_id=1, source_target_pairs={{0,8},{16,24},{32,40},{48,56},{64,72},{80,88},{96,104},{112,120},{... | collective-permute-start | bytes 34568 | tf_op jit(solution)/shard_map/ppermute | solution.py:498
  35.9 2.5 %fine_sum.2.refs_0_ = f32[240,256]{1,0:T(8,128)S(1)} custom-call(bf16[40,40,128]{2,1,0:T(8,128)(2,1)S(1)} %get-tuple-element.36.d_in_ref, f32[882,128]{1,0:T(8,128)S(1)} %fusion.v_ref.near_ref), custom_call_target="tpu_custom_call" | custom-call | flops 2076180480 | bytes 65536 | tf_op jit(solution)/shard_map/fine_sum/pallas_call | solution.py:106
  38.4 2.6 %all-to-all-done.recv_ref = f32[32,8,128]{2,1,0:T(8,128)S(1)} async-done(((f32[32,8,128]{2,1,0:T(8,128)}), f32[32,8,128]{2,1,0:T(8,128)S(1)}, u32[]{:S(2)}, u32[]{:S(2)}) %all-to-all-start) | async-done | bytes 131104 | tf_op jit(solution)/shard_map/all_to_all | solution.py:563
  41.1 1.2 %spread.1 = bf16[8,200,128]{2,1,0:T(8,128)(2,1)} custom-call(f32[32,8,128]{2,1,0:T(8,128)S(1)} %all-to-all-done.recv_ref, f32[2,328,128]{2,1,0:T(8,128)S(1)} %copy-done.3, bf16[9,16,128]{2,1,0:T(8,128)(2,1)S(1)} %get-tuple-element.35.mid_ref.own_ref, bf16[5,9,128]{2,1,0:T(8,128)(2,1)S(1)} %collective-permute-done.4.next_ref, ...), custom_call_target="tpu_custom_call" | custom-call | bytes 65536 | tf_op jit(solution)/shard_map/spread/pallas_call | solution.py:106
  42.2 4.7 %all-to-all-start.1 = ((bf16[8,200,128]{2,1,0:T(8,128)(2,1)}), bf16[8,200,128]{2,1,0:T(8,128)(2,1)S(1)}, u32[]{:S(2)}, u32[]{:S(2)}) async-start(bf16[8,200,128]{2,1,0:T(8,128)(2,1)} %spread.1), calls=%async_computation.1 | async-start | bytes 819200 | tf_op jit(solution)/shard_map/all_to_all | solution.py:574
  47.0 6.6 %fine_sum.3.fine_ref = f32[240,256]{1,0:T(8,128)S(1)} custom-call(bf16[40,40,128]{2,1,0:T(8,128)(2,1)S(1)} %get-tuple-element.36.d_in_ref, f32[882,128]{1,0:T(8,128)S(1)} %fusion.v_ref.near_ref, f32[240,256]{1,0:T(8,128)S(1)} %fine_sum.2.refs_0_), custom_call_target="tpu_custom_call" | custom-call | flops 5190451200 | bytes 65536 | tf_op jit(solution)/shard_map/fine_sum/pallas_call | solution.py:106
  53.5 1.3 %all-to-all-done.1.recv_ref = bf16[8,200,128]{2,1,0:T(8,128)(2,1)S(1)} async-done(((bf16[8,200,128]{2,1,0:T(8,128)(2,1)}), bf16[8,200,128]{2,1,0:T(8,128)(2,1)S(1)}, u32[]{:S(2)}, u32[]{:S(2)}) %all-to-all-start.1) | async-done | bytes 409632 | tf_op jit(solution)/shard_map/all_to_all | solution.py:574
  54.8 4.1 %final.1 = f32[20,20,128]{2,1,0:T(8,128)} custom-call(bf16[8,200,128]{2,1,0:T(8,128)(2,1)S(1)} %all-to-all-done.1.recv_ref, f32[16,88,128]{2,1,0:T(8,128)S(1)} %copy-done.2, f32[512,128]{1,0:T(8,128)S(1)} %copy-done.4, f32[882,128]{1,0:T(8,128)S(1)} %fusion.v_ref.near_ref, f32[882,128]{1,0:T(8,128)S(1)} %fusion.1.far_ref, f32[240,256]{1,0:T(8,128)S(1)} %fine_sum.3.fine_ref), custom_call_target="tpu_custom_call" | custom-call | bytes 65536 | tf_op jit(solution)/shard_map/final/pallas_call | solution.py:106
  (21 shorter events, 0.5 us)
Async XLA Ops:
  0.0 0.9 %copy-start = (bf16[20,20,128]{2,1,0:T(8,128)(2,1)S(1)}, bf16[20,20,128]{2,1,0:T(8,128)(2,1)}, u32[]{:S(2)}) copy-start(bf16[20,20,128]{2,1,0:T(8,128)(2,1)} %blk_ref.7) | copy-start | bytes 307204
  0.9 4.3 %collective-permute-start = (bf16[200,128]{1,0:T(8,128)(2,1)S(1)}, bf16[200,128]{1,0:T(8,128)(2,1)S(1)}, u32[]{:S(2)}, u32[]{:S(2)}) collective-permute-start(bf16[200,128]{1,0:T(8,128)(2,1)S(1)} %get-tuple-element.25), channel_id=1, source_target_pairs={{8,16},{24,32},{40,48},{56,64},{72,80},{88,96},{104,112},{120,128}... | collective-permute-start | bytes 153608 | tf_op jit(solution)/shard_map/ppermute | solution.py:497
  1.6 4.5 %collective-permute-start.1 = (bf16[200,128]{1,0:T(8,128)(2,1)S(1)}, bf16[200,128]{1,0:T(8,128)(2,1)S(1)}, u32[]{:S(2)}, u32[]{:S(2)}) collective-permute-start(bf16[200,128]{1,0:T(8,128)(2,1)S(1)} %get-tuple-element.26), channel_id=1, source_target_pairs={{0,8},{16,24},{32,40},{48,56},{64,72},{80,88},{96,104},{112,120},{... | collective-permute-start | bytes 153608 | tf_op jit(solution)/shard_map/ppermute | solution.py:498
  5.3 6.8 %copy-start.5 = (bf16[2,21,21,21]{3,0,2,1:T(2,128)(2,1)S(1)}, bf16[2,21,21,21]{3,0,2,1:T(2,128)(2,1)}, u32[]{:S(2)}) copy-start(bf16[2,21,21,21]{3,0,2,1:T(2,128)(2,1)} %param.8) | copy-start | bytes 111136
  6.2 9.1 %collective-permute-start.2 = (bf16[400,128]{1,0:T(8,128)(2,1)S(1)}, bf16[400,128]{1,0:T(8,128)(2,1)S(1)}, u32[]{:S(2)}, u32[]{:S(2)}) collective-permute-start(bf16[400,128]{1,0:T(8,128)(2,1)S(1)} %get-tuple-element.29), channel_id=1, source_target_pairs={{1,2},{3,4},{5,6},{2,1},{4,3},{6,5},{9,10},{11,12},{13,14},{10,9},... | collective-permute-start | bytes 307208 | tf_op jit(solution)/shard_map/ppermute | solution.py:497
  12.0 5.4 %collective-permute-start.3 = (bf16[400,128]{1,0:T(8,128)(2,1)S(1)}, bf16[400,128]{1,0:T(8,128)(2,1)S(1)}, u32[]{:S(2)}, u32[]{:S(2)}) collective-permute-start(bf16[400,128]{1,0:T(8,128)(2,1)S(1)} %get-tuple-element.30), channel_id=1, source_target_pairs={{0,1},{2,3},{4,5},{6,7},{1,0},{3,2},{5,4},{7,6},{8,9},{10,11},{12,... | collective-permute-start | bytes 307208 | tf_op jit(solution)/shard_map/ppermute | solution.py:498
  12.5 0.7 %copy-start.6 = (bf16[21,128]{1,0:T(8,128)(2,1)S(1)}, bf16[21,128]{1,0:T(8,128)(2,1)}, u32[]{:S(2)}) copy-start(bf16[21,128]{1,0:T(8,128)(2,1)} %constant.11.clone) | copy-start | bytes 16132
  13.2 0.7 %copy-start.7 = (bf16[21,128]{1,0:T(8,128)(2,1)S(1)}, bf16[21,128]{1,0:T(8,128)(2,1)}, u32[]{:S(2)}) copy-start(bf16[21,128]{1,0:T(8,128)(2,1)} %constant.10.clone) | copy-start | bytes 16132
  13.9 3.5 %copy-start.1 = (bf16[20,20,128]{2,1,0:T(8,128)(2,1)S(1)}, bf16[20,20,128]{2,1,0:T(8,128)(2,1)}, u32[]{:S(2)}) copy-start(bf16[20,20,128]{2,1,0:T(8,128)(2,1)} %blk_ref.7) | copy-start | bytes 307204
  18.7 22.3 %all-to-all-start = ((f32[32,8,128]{2,1,0:T(8,128)}), f32[32,8,128]{2,1,0:T(8,128)S(1)}, u32[]{:S(2)}, u32[]{:S(2)}) async-start(f32[32,8,128]{2,1,0:T(8,128)} %get-tuple-element.34), calls=%async_computation | async-start | bytes 262144 | tf_op jit(solution)/shard_map/all_to_all | solution.py:563
  30.5 10.6 %collective-permute-start.4 = (bf16[5,9,128]{2,1,0:T(8,128)(2,1)S(1)}, bf16[5,9,128]{2,1,0:T(8,128)(2,1)S(1)}, u32[]{:S(2)}, u32[]{:S(2)}) collective-permute-start(bf16[5,9,128]{2,1,0:T(8,128)(2,1)S(1)} %get-tuple-element.39), channel_id=1, source_target_pairs={{8,16},{24,32},{40,48},{56,64},{72,80},{88,96},{104,112},{120,128}... | collective-permute-start | bytes 34568 | tf_op jit(solution)/shard_map/ppermute | solution.py:497
  31.1 9.9 %collective-permute-start.5 = (bf16[5,9,128]{2,1,0:T(8,128)(2,1)S(1)}, bf16[5,9,128]{2,1,0:T(8,128)(2,1)S(1)}, u32[]{:S(2)}, u32[]{:S(2)}) collective-permute-start(bf16[5,9,128]{2,1,0:T(8,128)(2,1)S(1)} %get-tuple-element.40), channel_id=1, source_target_pairs={{0,8},{16,24},{32,40},{48,56},{64,72},{80,88},{96,104},{112,120},{... | collective-permute-start | bytes 34568 | tf_op jit(solution)/shard_map/ppermute | solution.py:498
  35.9 5.2 %copy-start.3 = (f32[2,328,128]{2,1,0:T(8,128)S(1)}, f32[2,328,128]{2,1,0:T(8,128)}, u32[]{:S(2)}) copy-start(f32[2,328,128]{2,1,0:T(8,128)} %constant.12.clone.mx_ref) | copy-start | bytes 1007620
  42.2 12.6 %all-to-all-start.1 = ((bf16[8,200,128]{2,1,0:T(8,128)(2,1)}), bf16[8,200,128]{2,1,0:T(8,128)(2,1)S(1)}, u32[]{:S(2)}, u32[]{:S(2)}) async-start(bf16[8,200,128]{2,1,0:T(8,128)(2,1)} %spread.1), calls=%async_computation.1 | async-start | bytes 819200 | tf_op jit(solution)/shard_map/all_to_all | solution.py:574
  46.9 7.8 %copy-start.2 = (f32[16,88,128]{2,1,0:T(8,128)S(1)}, f32[16,88,128]{2,1,0:T(8,128)}, u32[]{:S(2)}) copy-start(f32[16,88,128]{2,1,0:T(8,128)} %constant.13.clone.my_ref) | copy-start | bytes 2162692
  46.9 7.8 %copy-start.4 = (f32[512,128]{1,0:T(8,128)S(1)}, f32[512,128]{1,0:T(8,128)}, u32[]{:S(2)}) copy-start(f32[512,128]{1,0:T(8,128)} %constant.14.clone.mz_ref) | copy-start | bytes 786436

commit v17 on v15

--- a/solution.py
+++ b/solution.py
@@ -13,7 +13,7 @@
 REACH = 10
 TAPS = 21
 GROUP = 3
-SPLIT = 6
+SPLIT = 9
 
 
 def weight_np(offset):

time: 59.5 us -> 59.5 us (level)
    all_to_all x1, waiting for transfers between devices: 2.6 us -> 0.72 us  [per_device(): coarse = lax.all_to_all(coarse, 'gx', 0, 0)]
    all_to_all x1, waiting for transfers between devices: 1.42 us -> 2.84 us  [per_device(): parts = lax.all_to_all(parts, 'gy', 0, 0)]
  transfers between devices with their start and end apart: 8 -> 8, of which waited for: 5 -> 5; matrix products, arithmetic and copies ran while one was open for 2% -> 2% of each run, Pallas kernels for 16% -> 17%
where the time goes in v17:
time: 59.5 us; the launch traced here: 59 us
  starting transfers between devices  31.8 us (53%)
  Pallas kernels  16.5 us (28%)
  waiting for transfers between devices  7.51 us (13%)
  local copies, waits for them, and re-layouts  2.44 us (4%)
  matrix products  0.62 us (1%)
    pallas_call x9, Pallas kernels, vmem_call(): pl.pallas_call(body, out_shape=out_shape, in_specs=[spec(pltpu.VMEM)] * l...  16.5 us
    all_to_all x1, starting transfers between devices, per_device(): coarse = lax.all_to_all(coarse, 'gx', 0, 0)  11.5 us
    ppermute x3, starting transfers between devices, swap(): return (lax.ppermute(first, axis, both(pairs)), second)  8.41 us
    ppermute x3, starting transfers between devices, swap(): second = lax.ppermute(second, axis, both(others))  7.12 us
    all_to_all x1, starting transfers between devices, per_device(): parts = lax.all_to_all(parts, 'gy', 0, 0)  4.73 us
    ppermute x3, waiting for transfers between devices, swap(): return (lax.ppermute(first, axis, both(pairs)), second)  2.88 us
    all_to_all x1, waiting for transfers between devices, per_device(): parts = lax.all_to_all(parts, 'gy', 0, 0)  2.84 us
    unnamed x16, local copies, waits for them, and re-layouts  1.72 us
  transfers between devices with their start and end apart: 8, of which 5 were waited for; matrix products, arithmetic and copies ran while one was open for 2% of the time, Pallas kernels for 17%

profile of v17, /device:TPU:2, one launch (start us, length us, event | category | flops | bytes accessed | tf_op | source)
XLA Modules:
  0.0 59.0 jit_solution(8314202598626377094)
XLA Ops:
  0.0 0.9 %copy-done = bf16[20,20,128]{2,1,0:T(8,128)(2,1)S(1)} copy-done((bf16[20,20,128]{2,1,0:T(8,128)(2,1)S(1)}, bf16[20,20,128]{2,1,0:T(8,128)(2,1)}, u32[]{:S(2)}) %copy-start) | copy-done | bytes 102424
  0.9 0.7 %collective-permute-start = (bf16[200,128]{1,0:T(8,128)(2,1)S(1)}, bf16[200,128]{1,0:T(8,128)(2,1)S(1)}, u32[]{:S(2)}, u32[]{:S(2)}) collective-permute-start(bf16[200,128]{1,0:T(8,128)(2,1)S(1)} %get-tuple-element.25), channel_id=1, source_target_pairs={{8,16},{24,32},{40,48},{56,64},{72,80},{88,96},{104,112},{120,128}... | collective-permute-start | bytes 153608 | tf_op jit(solution)/shard_map/ppermute | solution.py:497
  1.6 3.6 %collective-permute-start.1 = (bf16[200,128]{1,0:T(8,128)(2,1)S(1)}, bf16[200,128]{1,0:T(8,128)(2,1)S(1)}, u32[]{:S(2)}, u32[]{:S(2)}) collective-permute-start(bf16[200,128]{1,0:T(8,128)(2,1)S(1)} %get-tuple-element.26), channel_id=1, source_target_pairs={{0,8},{16,24},{32,40},{48,56},{64,72},{80,88},{96,104},{112,120},{... | collective-permute-start | bytes 153608 | tf_op jit(solution)/shard_map/ppermute | solution.py:498
  5.3 0.8 %collective-permute-done.1.near_ref.near_x_ref = bf16[200,128]{1,0:T(8,128)(2,1)S(1)} collective-permute-done((bf16[200,128]{1,0:T(8,128)(2,1)S(1)}, bf16[200,128]{1,0:T(8,128)(2,1)S(1)}, u32[]{:S(2)}, u32[]{:S(2)}) %collective-permute-start.1) | collective-permute-done | bytes 51232 | tf_op jit(solution)/shard_map/ppermute | solution.py:498
  6.2 5.8 %collective-permute-start.2 = (bf16[400,128]{1,0:T(8,128)(2,1)S(1)}, bf16[400,128]{1,0:T(8,128)(2,1)S(1)}, u32[]{:S(2)}, u32[]{:S(2)}) collective-permute-start(bf16[400,128]{1,0:T(8,128)(2,1)S(1)} %get-tuple-element.29), channel_id=1, source_target_pairs={{1,2},{3,4},{5,6},{2,1},{4,3},{6,5},{9,10},{11,12},{13,14},{10,9},... | collective-permute-start | bytes 307208 | tf_op jit(solution)/shard_map/ppermute | solution.py:497
  12.1 0.5 copy.8
  12.5 0.3 reshape.4
  12.8 0.4 copy-done.6
  13.2 0.3 fusion.1.far_ref
  13.5 0.4 copy-done.7
  13.9 0.3 fusion.v_ref.near_ref
  14.2 1.1 %collective-permute-done.2.next_y_ref = bf16[400,128]{1,0:T(8,128)(2,1)S(1)} collective-permute-done((bf16[400,128]{1,0:T(8,128)(2,1)S(1)}, bf16[400,128]{1,0:T(8,128)(2,1)S(1)}, u32[]{:S(2)}, u32[]{:S(2)}) %collective-permute-start.2) | collective-permute-done | bytes 102432 | tf_op jit(solution)/shard_map/ppermute | solution.py:497
  15.3 2.1 %collective-permute-done.3.near_y_ref = bf16[400,128]{1,0:T(8,128)(2,1)S(1)} collective-permute-done((bf16[400,128]{1,0:T(8,128)(2,1)S(1)}, bf16[400,128]{1,0:T(8,128)(2,1)S(1)}, u32[]{:S(2)}, u32[]{:S(2)}) %collective-permute-start.3) | collective-permute-done | bytes 102432 | tf_op jit(solution)/shard_map/ppermute | solution.py:498
  17.4 1.4 %restrict.1 = (bf16[9,16,128]{2,1,0:T(8,128)(2,1)S(1)}, f32[32,8,128]{2,1,0:T(8,128)}) custom-call(bf16[20,20,128]{2,1,0:T(8,128)(2,1)S(1)} %copy-done.1, bf16[200,128]{1,0:T(8,128)(2,1)S(1)} %collective-permute-done.next_ref.next_x_ref, bf16[200,128]{1,0:T(8,128)(2,1)S(1)} %collective-permute-done.1.near_ref.near_x_ref, ...), custom_call_target="tpu_custom_call" | custom-call | bytes 65536 | tf_op jit(solution)/shard_map/restrict/pallas_call | solution.py:106
  18.7 11.5 %all-to-all-start = ((f32[32,8,128]{2,1,0:T(8,128)}), f32[32,8,128]{2,1,0:T(8,128)S(1)}, u32[]{:S(2)}, u32[]{:S(2)}) async-start(f32[32,8,128]{2,1,0:T(8,128)} %get-tuple-element.34), calls=%async_computation | async-start | bytes 262144 | tf_op jit(solution)/shard_map/all_to_all | solution.py:563
  30.5 0.7 %collective-permute-start.4 = (bf16[5,9,128]{2,1,0:T(8,128)(2,1)S(1)}, bf16[5,9,128]{2,1,0:T(8,128)(2,1)S(1)}, u32[]{:S(2)}, u32[]{:S(2)}) collective-permute-start(bf16[5,9,128]{2,1,0:T(8,128)(2,1)S(1)} %get-tuple-element.39), channel_id=1, source_target_pairs={{8,16},{24,32},{40,48},{56,64},{72,80},{88,96},{104,112},{120,128}... | collective-permute-start | bytes 34568 | tf_op jit(solution)/shard_map/ppermute | solution.py:497
  31.1 4.7 %collective-permute-start.5 = (bf16[5,9,128]{2,1,0:T(8,128)(2,1)S(1)}, bf16[5,9,128]{2,1,0:T(8,128)(2,1)S(1)}, u32[]{:S(2)}, u32[]{:S(2)}) collective-permute-start(bf16[5,9,128]{2,1,0:T(8,128)(2,1)S(1)} %get-tuple-element.40), channel_id=1, source_target_pairs={{0,8},{16,24},{32,40},{48,56},{64,72},{80,88},{96,104},{112,120},{... | collective-permute-start | bytes 34568 | tf_op jit(solution)/shard_map/ppermute | solution.py:498
  35.9 4.4 %fine_sum.2.refs_0_ = f32[240,256]{1,0:T(8,128)S(1)} custom-call(bf16[40,40,128]{2,1,0:T(8,128)(2,1)S(1)} %get-tuple-element.36.d_in_ref, f32[882,128]{1,0:T(8,128)S(1)} %fusion.v_ref.near_ref), custom_call_target="tpu_custom_call" | custom-call | flops 3114270720 | bytes 65536 | tf_op jit(solution)/shard_map/fine_sum/pallas_call | solution.py:106
  40.3 0.7 %all-to-all-done.recv_ref = f32[32,8,128]{2,1,0:T(8,128)S(1)} async-done(((f32[32,8,128]{2,1,0:T(8,128)}), f32[32,8,128]{2,1,0:T(8,128)S(1)}, u32[]{:S(2)}, u32[]{:S(2)}) %all-to-all-start) | async-done | bytes 131104 | tf_op jit(solution)/shard_map/all_to_all | solution.py:563
  41.1 1.2 %spread.1 = bf16[8,208,128]{2,1,0:T(8,128)(2,1)} custom-call(f32[32,8,128]{2,1,0:T(8,128)S(1)} %all-to-all-done.recv_ref, f32[2,328,128]{2,1,0:T(8,128)S(1)} %copy-done.3, bf16[9,16,128]{2,1,0:T(8,128)(2,1)S(1)} %get-tuple-element.35.mid_ref.own_ref, bf16[5,9,128]{2,1,0:T(8,128)(2,1)S(1)} %collective-permute-done.4.next_ref, ...), custom_call_target="tpu_custom_call" | custom-call | bytes 65536 | tf_op jit(solution)/shard_map/spread/pallas_call | solution.py:106
  42.2 4.7 %all-to-all-start.1 = ((bf16[8,208,128]{2,1,0:T(8,128)(2,1)}), bf16[8,208,128]{2,1,0:T(8,128)(2,1)S(1)}, u32[]{:S(2)}, u32[]{:S(2)}) async-start(bf16[8,208,128]{2,1,0:T(8,128)(2,1)} %spread.1), calls=%async_computation.1 | async-start | bytes 851968 | tf_op jit(solution)/shard_map/all_to_all | solution.py:574
  47.0 5.2 %fine_sum.3.fine_ref = f32[240,256]{1,0:T(8,128)S(1)} custom-call(bf16[40,40,128]{2,1,0:T(8,128)(2,1)S(1)} %get-tuple-element.36.d_in_ref, f32[882,128]{1,0:T(8,128)S(1)} %fusion.v_ref.near_ref, f32[240,256]{1,0:T(8,128)S(1)} %fine_sum.2.refs_0_), custom_call_target="tpu_custom_call" | custom-call | flops 4152360960 | bytes 65536 | tf_op jit(solution)/shard_map/fine_sum/pallas_call | solution.py:106
  52.1 2.8 %all-to-all-done.1.recv_ref = bf16[8,208,128]{2,1,0:T(8,128)(2,1)S(1)} async-done(((bf16[8,208,128]{2,1,0:T(8,128)(2,1)}), bf16[8,208,128]{2,1,0:T(8,128)(2,1)S(1)}, u32[]{:S(2)}, u32[]{:S(2)}) %all-to-all-start.1) | async-done | bytes 426016 | tf_op jit(solution)/shard_map/all_to_all | solution.py:574
  55.0 4.1 %final.1 = f32[20,20,128]{2,1,0:T(8,128)} custom-call(bf16[8,208,128]{2,1,0:T(8,128)(2,1)S(1)} %all-to-all-done.1.recv_ref, f32[16,88,128]{2,1,0:T(8,128)S(1)} %copy-done.2, f32[512,128]{1,0:T(8,128)S(1)} %copy-done.4, f32[882,128]{1,0:T(8,128)S(1)} %fusion.v_ref.near_ref, f32[882,128]{1,0:T(8,128)S(1)} %fusion.1.far_ref, f32[240,256]{1,0:T(8,128)S(1)} %fine_sum.3.fine_ref), custom_call_target="tpu_custom_call" | custom-call | bytes 65536 | tf_op jit(solution)/shard_map/final/pallas_call | solution.py:106
  (21 shorter events, 0.5 us)
Async XLA Ops:
  0.0 0.9 %copy-start = (bf16[20,20,128]{2,1,0:T(8,128)(2,1)S(1)}, bf16[20,20,128]{2,1,0:T(8,128)(2,1)}, u32[]{:S(2)}) copy-start(bf16[20,20,128]{2,1,0:T(8,128)(2,1)} %blk_ref.7) | copy-start | bytes 307204
  0.9 4.3 %collective-permute-start = (bf16[200,128]{1,0:T(8,128)(2,1)S(1)}, bf16[200,128]{1,0:T(8,128)(2,1)S(1)}, u32[]{:S(2)}, u32[]{:S(2)}) collective-permute-start(bf16[200,128]{1,0:T(8,128)(2,1)S(1)} %get-tuple-element.25), channel_id=1, source_target_pairs={{8,16},{24,32},{40,48},{56,64},{72,80},{88,96},{104,112},{120,128}... | collective-permute-start | bytes 153608 | tf_op jit(solution)/shard_map/ppermute | solution.py:497
  1.6 4.5 %collective-permute-start.1 = (bf16[200,128]{1,0:T(8,128)(2,1)S(1)}, bf16[200,128]{1,0:T(8,128)(2,1)S(1)}, u32[]{:S(2)}, u32[]{:S(2)}) collective-permute-start(bf16[200,128]{1,0:T(8,128)(2,1)S(1)} %get-tuple-element.26), channel_id=1, source_target_pairs={{0,8},{16,24},{32,40},{48,56},{64,72},{80,88},{96,104},{112,120},{... | collective-permute-start | bytes 153608 | tf_op jit(solution)/shard_map/ppermute | solution.py:498
  5.3 6.8 %copy-start.5 = (bf16[2,21,21,21]{3,0,2,1:T(2,128)(2,1)S(1)}, bf16[2,21,21,21]{3,0,2,1:T(2,128)(2,1)}, u32[]{:S(2)}) copy-start(bf16[2,21,21,21]{3,0,2,1:T(2,128)(2,1)} %param.8) | copy-start | bytes 111136
  6.2 9.1 %collective-permute-start.2 = (bf16[400,128]{1,0:T(8,128)(2,1)S(1)}, bf16[400,128]{1,0:T(8,128)(2,1)S(1)}, u32[]{:S(2)}, u32[]{:S(2)}) collective-permute-start(bf16[400,128]{1,0:T(8,128)(2,1)S(1)} %get-tuple-element.29), channel_id=1, source_target_pairs={{1,2},{3,4},{5,6},{2,1},{4,3},{6,5},{9,10},{11,12},{13,14},{10,9},... | collective-permute-start | bytes 307208 | tf_op jit(solution)/shard_map/ppermute | solution.py:497
  12.0 5.4 %collective-permute-start.3 = (bf16[400,128]{1,0:T(8,128)(2,1)S(1)}, bf16[400,128]{1,0:T(8,128)(2,1)S(1)}, u32[]{:S(2)}, u32[]{:S(2)}) collective-permute-start(bf16[400,128]{1,0:T(8,128)(2,1)S(1)} %get-tuple-element.30), channel_id=1, source_target_pairs={{0,1},{2,3},{4,5},{6,7},{1,0},{3,2},{5,4},{7,6},{8,9},{10,11},{12,... | collective-permute-start | bytes 307208 | tf_op jit(solution)/shard_map/ppermute | solution.py:498
  12.5 0.7 %copy-start.6 = (bf16[21,128]{1,0:T(8,128)(2,1)S(1)}, bf16[21,128]{1,0:T(8,128)(2,1)}, u32[]{:S(2)}) copy-start(bf16[21,128]{1,0:T(8,128)(2,1)} %constant.11.clone) | copy-start | bytes 16132
  13.2 0.7 %copy-start.7 = (bf16[21,128]{1,0:T(8,128)(2,1)S(1)}, bf16[21,128]{1,0:T(8,128)(2,1)}, u32[]{:S(2)}) copy-start(bf16[21,128]{1,0:T(8,128)(2,1)} %constant.10.clone) | copy-start | bytes 16132
  13.9 3.5 %copy-start.1 = (bf16[20,20,128]{2,1,0:T(8,128)(2,1)S(1)}, bf16[20,20,128]{2,1,0:T(8,128)(2,1)}, u32[]{:S(2)}) copy-start(bf16[20,20,128]{2,1,0:T(8,128)(2,1)} %blk_ref.7) | copy-start | bytes 307204
  18.7 22.3 %all-to-all-start = ((f32[32,8,128]{2,1,0:T(8,128)}), f32[32,8,128]{2,1,0:T(8,128)S(1)}, u32[]{:S(2)}, u32[]{:S(2)}) async-start(f32[32,8,128]{2,1,0:T(8,128)} %get-tuple-element.34), calls=%async_computation | async-start | bytes 262144 | tf_op jit(solution)/shard_map/all_to_all | solution.py:563
  30.5 10.6 %collective-permute-start.4 = (bf16[5,9,128]{2,1,0:T(8,128)(2,1)S(1)}, bf16[5,9,128]{2,1,0:T(8,128)(2,1)S(1)}, u32[]{:S(2)}, u32[]{:S(2)}) collective-permute-start(bf16[5,9,128]{2,1,0:T(8,128)(2,1)S(1)} %get-tuple-element.39), channel_id=1, source_target_pairs={{8,16},{24,32},{40,48},{56,64},{72,80},{88,96},{104,112},{120,128}... | collective-permute-start | bytes 34568 | tf_op jit(solution)/shard_map/ppermute | solution.py:497
  31.1 9.9 %collective-permute-start.5 = (bf16[5,9,128]{2,1,0:T(8,128)(2,1)S(1)}, bf16[5,9,128]{2,1,0:T(8,128)(2,1)S(1)}, u32[]{:S(2)}, u32[]{:S(2)}) collective-permute-start(bf16[5,9,128]{2,1,0:T(8,128)(2,1)S(1)} %get-tuple-element.40), channel_id=1, source_target_pairs={{0,8},{16,24},{32,40},{48,56},{64,72},{80,88},{96,104},{112,120},{... | collective-permute-start | bytes 34568 | tf_op jit(solution)/shard_map/ppermute | solution.py:498
  35.9 5.2 %copy-start.3 = (f32[2,328,128]{2,1,0:T(8,128)S(1)}, f32[2,328,128]{2,1,0:T(8,128)}, u32[]{:S(2)}) copy-start(f32[2,328,128]{2,1,0:T(8,128)} %constant.12.clone.mx_ref) | copy-start | bytes 1007620
  42.2 12.7 %all-to-all-start.1 = ((bf16[8,208,128]{2,1,0:T(8,128)(2,1)}), bf16[8,208,128]{2,1,0:T(8,128)(2,1)S(1)}, u32[]{:S(2)}, u32[]{:S(2)}) async-start(bf16[8,208,128]{2,1,0:T(8,128)(2,1)} %spread.1), calls=%async_computation.1 | async-start | bytes 851968 | tf_op jit(solution)/shard_map/all_to_all | solution.py:574
  46.9 8.0 %copy-start.2 = (f32[16,88,128]{2,1,0:T(8,128)S(1)}, f32[16,88,128]{2,1,0:T(8,128)}, u32[]{:S(2)}) copy-start(f32[16,88,128]{2,1,0:T(8,128)} %constant.13.clone.my_ref) | copy-start | bytes 2162692
  47.0 8.0 %copy-start.4 = (f32[512,128]{1,0:T(8,128)S(1)}, f32[512,128]{1,0:T(8,128)}, u32[]{:S(2)}) copy-start(f32[512,128]{1,0:T(8,128)} %constant.14.clone.mz_ref) | copy-start | bytes 786436
